TPU v7x, 32 devices: a whole 2x2x4 slice. The times are simulated.
32 devices in a mesh: branch: 2 (over y), rows: 16 (over z, x, core).
Axes of the slice: x: 2, y: 2, z: 4, core: 2. Of those that a mesh axis runs over, the one named last changes fastest.
Arguments:
- homolog_features: bfloat16 [32, 256, 256], P(('branch', 'rows')), may hold values from -6 to 6
- pairwise_input: bfloat16 [256, 256, 128], P('rows', 'branch'), may hold values from -6 to 6
- transition_expand_matrix: bfloat16 [256, 1024], replicated, may hold values from -0.375 to 0.375
- transition_contract_matrix: bfloat16 [1024, 256], replicated, may hold values from -0.1875 to 0.1875
- factor_pair_matrices: bfloat16 [256, 64], replicated, may hold values from -0.375 to 0.375
- outer_output_weight: bfloat16 [1024, 128], replicated, may hold values from -0.75 to 0.75
- triangle_projection_weight: bfloat16 [128, 640], replicated, may hold values from -0.5 to 0.5
- triangle_output_weight: bfloat16 [128, 128], replicated, may hold values from -1 to 1
- pairwise_up_weight: bfloat16 [128, 512], replicated, may hold values from -0.5 to 0.5
- pairwise_down_weight: bfloat16 [512, 128], replicated, may hold values from -0.25 to 0.25
Outputs:
- refreshed_homolog_features: bfloat16 [32, 256, 256], P(('branch', 'rows'))
- pairwise_output: bfloat16 [256, 256, 128], P('rows', 'branch')
All inputs are finite; a program needn't handle non-finite values.
Results may differ from a plain program's by a relative error of at most 0.0085.
Values may be sent and summed in bfloat16 or wider, within the bound.
No kernel may reach another device: no remote copies, remote signals or barrier semaphores. Data moves between devices by JAX's collectives and lax.ppermute only.
A program may use at most 128 MiB of HBM per device.

v0:
```python
import jax
import jax.numpy as jnp
from jax import lax
from jax.sharding import PartitionSpec as P


def standardize_features(values, dimension):
    average = jnp.mean(values, axis=dimension, keepdims=True)
    centered = values - average
    variance = jnp.mean(centered * centered, axis=dimension, keepdims=True)
    return centered * lax.rsqrt(variance + 1e-05)


def alignment_branch(
    homolog_features, transition_expand_matrix, transition_contract_matrix, factor_pair_matrices
):
    local_rows, sequence_length, channel_width = homolog_features.shape
    homolog_real_matrix = homolog_features.astype(jnp.float32)
    standardized_homologs = (
        standardize_features(homolog_real_matrix, -1)
        .astype(jnp.bfloat16)
        .reshape(local_rows * sequence_length, channel_width)
    )
    expanded_activations = jax.nn.relu(
        jnp.dot(standardized_homologs, transition_expand_matrix, preferred_element_type=jnp.float32)
    ).astype(jnp.bfloat16)
    refreshed_homolog_features = (
        homolog_real_matrix
        + jnp.dot(
            expanded_activations, transition_contract_matrix, preferred_element_type=jnp.float32
        ).reshape(homolog_features.shape)
    ).astype(jnp.bfloat16)
    standardized_for_factors = (
        standardize_features(refreshed_homolog_features.astype(jnp.float32), -1)
        .astype(jnp.bfloat16)
        .reshape(local_rows * sequence_length, channel_width)
    )
    projected = jnp.dot(
        standardized_for_factors, factor_pair_matrices, preferred_element_type=jnp.float32
    ).reshape(local_rows, sequence_length, -1)
    channels = projected.shape[-1] // 2
    left_side = projected[..., :channels].astype(jnp.bfloat16)
    right_side = jnp.swapaxes(projected[..., channels:].astype(jnp.bfloat16), 1, 2)
    left_pair = lax.all_gather(left_side, "branch", axis=0, tiled=True)
    left_gathered = lax.all_to_all(left_pair, "rows", split_axis=1, concat_axis=0, tiled=True)
    right_pair = lax.all_to_all(right_side, "branch", split_axis=2, concat_axis=0, tiled=True)
    right_gathered = lax.all_gather(right_pair, "rows", axis=0, tiled=True)
    return (refreshed_homolog_features, left_gathered, right_gathered)


def send_whole(tri_left, tri_right):
    return (
        lax.all_to_all(
            lax.all_to_all(tri_left, "branch", split_axis=0, concat_axis=2, tiled=True),
            "rows",
            split_axis=0,
            concat_axis=1,
            tiled=True,
        ),
        lax.all_to_all(
            lax.all_to_all(tri_right, "branch", split_axis=0, concat_axis=2, tiled=True),
            "rows",
            split_axis=0,
            concat_axis=1,
            tiled=True,
        ),
    )


def send_back(product):
    return lax.all_to_all(
        lax.all_to_all(product, "rows", split_axis=1, concat_axis=0, tiled=True),
        "branch",
        split_axis=2,
        concat_axis=0,
        tiled=True,
    )


def pair_branch(
    pairwise_input,
    triangle_projection_weight,
    triangle_output_weight,
    pairwise_up_weight,
    pairwise_down_weight,
):
    tile_rows, columns, chans = pairwise_input.shape
    pair_float = pairwise_input.astype(jnp.float32)
    pair_norm = standardize_features(pair_float, -1).astype(jnp.bfloat16)
    norm_flat = pair_norm.reshape(tile_rows * columns, chans)
    proj_flat = lax.dot_general(
        triangle_projection_weight,
        norm_flat,
        (((0,), (1,)), ((), ())),
        preferred_element_type=jnp.float32,
    )
    proj_tile = proj_flat[: 4 * chans].reshape(4 * chans, tile_rows, columns)
    gate_vals = jax.nn.sigmoid(proj_flat[4 * chans :])
    tri_left = (jax.nn.sigmoid(proj_tile[chans : 2 * chans]) * proj_tile[:chans]).astype(
        jnp.bfloat16
    )
    tri_right = (jax.nn.sigmoid(proj_tile[3 * chans :]) * proj_tile[2 * chans : 3 * chans]).astype(
        jnp.bfloat16
    )
    left_chan, right_chan = send_whole(tri_left, tri_right)
    product = jnp.einsum(
        "cik,cjk->cij", left_chan, right_chan, preferred_element_type=jnp.float32
    ).astype(jnp.bfloat16)
    product_tile = send_back(product)
    prod_norm = (
        standardize_features(product_tile.astype(jnp.float32), 0)
        .astype(jnp.bfloat16)
        .reshape(chans, tile_rows * columns)
    )
    tri_update = lax.dot_general(
        triangle_output_weight,
        prod_norm,
        (((0,), (0,)), ((), ())),
        preferred_element_type=jnp.float32,
    )
    gated_update = jnp.transpose(gate_vals * tri_update).reshape(tile_rows, columns, chans)
    pair_mid = pair_float + gated_update
    mid_norm = standardize_features(pair_mid, -1).astype(jnp.bfloat16)
    pair_hidden = jax.nn.relu(
        jnp.einsum("ijd,dh->ijh", mid_norm, pairwise_up_weight, preferred_element_type=jnp.float32)
    ).astype(jnp.bfloat16)
    return pair_mid + jnp.einsum(
        "ijh,hd->ijd", pair_hidden, pairwise_down_weight, preferred_element_type=jnp.float32
    )


def outer_product(left_gathered, right_gathered, outer_output_weight):
    total_rows, tile_rows, channels = left_gathered.shape
    columns = right_gathered.shape[2]
    span_cols = 128
    left_flat = left_gathered.reshape(total_rows, tile_rows * channels)
    pieces = []
    for offset in range(0, columns, span_cols):
        right_piece = right_gathered[:, :, offset : offset + span_cols].reshape(
            total_rows, channels * span_cols
        )
        outer_vals = lax.dot_general(
            left_flat, right_piece, (((0,), (0,)), ((), ())), preferred_element_type=jnp.float32
        )
        outer_vals = (
            (outer_vals / total_rows)
            .astype(jnp.bfloat16)
            .reshape(tile_rows, channels * channels, span_cols)
        )
        pieces.append(
            lax.dot_general(
                outer_output_weight,
                outer_vals,
                (((0,), (1,)), ((), ())),
                preferred_element_type=jnp.float32,
            )
        )
    outer_eij = jnp.concatenate(pieces, axis=2)
    return jnp.transpose(outer_eij, (1, 2, 0))


def on_device(
    homolog_features,
    pairwise_input,
    transition_expand_matrix,
    transition_contract_matrix,
    factor_pair_matrices,
    outer_output_weight,
    triangle_projection_weight,
    triangle_output_weight,
    pairwise_up_weight,
    pairwise_down_weight,
):
    refreshed_homolog_features, left_gathered, right_gathered = alignment_branch(
        homolog_features, transition_expand_matrix, transition_contract_matrix, factor_pair_matrices
    )
    pair_mid = pair_branch(
        pairwise_input,
        triangle_projection_weight,
        triangle_output_weight,
        pairwise_up_weight,
        pairwise_down_weight,
    )
    outer_update = outer_product(left_gathered, right_gathered, outer_output_weight)
    pairwise_output = (pair_mid + outer_update).astype(jnp.bfloat16)
    return (refreshed_homolog_features, pairwise_output)


def solution(mesh):
    return jax.shard_map(
        on_device,
        mesh=mesh,
        in_specs=(
            P(("branch", "rows"), None, None),
            P("rows", "branch", None),
            P(),
            P(),
            P(),
            P(),
            P(),
            P(),
            P(),
            P(),
        ),
        out_specs=(P(("branch", "rows"), None, None), P("rows", "branch", None)),
        check_vma=False,
    )
```

profile of v0, /device:TPU:0, one launch (start us, length us, event | category | flops | bytes accessed | tf_op | source)
XLA Modules:
  0.0 158.4 jit_solution(768238492886870208)
XLA Ops:
  0.6 1.3 convert_reduce_fusion
  2.0 1.7 %fusion.13 = f32[16,128]{1,0:T(8,128)S(1)} fusion(bf16[16,128,128]{2,1,0:T(8,128)(2,1)} %param.11, f32[16,128]{1,0:T(8,128)S(1)} %broadcast_multiply_fusion.2), kind=kLoop, calls=%fused_computation.23 | loop fusion | flops 1046528 | bytes 540672 | tf_op jit(solution)/shard_map/reduce_sum | solution.py:10
  3.7 1.6 %fusion.14 = bf16[16,128,128]{2,1,0:T(8,128)(2,1)S(1)} fusion(bf16[16,128,128]{2,1,0:T(8,128)(2,1)} %param.11, f32[16,128]{1,0:T(8,128)S(1)} %add_rsqrt_fusion.1, f32[16,128]{1,0:T(8,128)S(1)} %broadcast_multiply_fusion.2), kind=kLoop, calls=%fused_computation.24 | loop fusion | flops 1048576 | bytes 1064960 | tf_op jit(solution)/shard_map/convert_element_type | solution.py:89
  5.3 1.7 %convolution_bitcast_fusion = f32[640,2048]{0,1:T(8,128)S(1)} fusion(bf16[2048,128]{1,0:T(8,128)(2,1)S(1)} %bitcast.117, bf16[128,640]{1,0:T(8,128)(2,1)} %param.16), kind=kOutput, calls=%fused_computation.2 | convolution fusion | flops 335544320 | bytes 5931008 | tf_op jit(solution)/shard_map/dot_general | solution.py:91
  7.1 2.3 %copy-done.1 = f32[640,2048]{0,1:T(8,128)} copy-done((f32[640,2048]{0,1:T(8,128)}, f32[640,2048]{0,1:T(8,128)S(1)}, u32[]{:S(2)}) %copy-start.1) | copy-done | bytes 5242904
  9.9 1.2 copy.70
  11.1 4.4 %all-to-all-start.2 = ((bf16[128,16,128]{2,1,0:T(8,128)(2,1)}), bf16[128,16,128]{2,1,0:T(8,128)(2,1)S(1)}, u32[]{:S(2)}, u32[]{:S(2)}) async-start(bf16[128,16,128]{2,1,0:T(8,128)(2,1)} %copy.70), calls=%async_computation.2 | async-start | bytes 1048576 | tf_op jit(solution)/shard_map/all_to_all | solution.py:61
  15.5 1.2 copy.67
  16.7 7.5 %all-to-all-done.2 = bf16[128,16,128]{2,1,0:T(8,128)(2,1)S(1)} async-done(((bf16[128,16,128]{2,1,0:T(8,128)(2,1)}), bf16[128,16,128]{2,1,0:T(8,128)(2,1)S(1)}, u32[]{:S(2)}, u32[]{:S(2)}) %all-to-all-start.2) | async-done | bytes 524320 | tf_op jit(solution)/shard_map/all_to_all | solution.py:61
  24.2 3.5 %all-to-all-start = ((bf16[128,16,128]{2,1,0:T(8,128)(2,1)}), bf16[128,16,128]{2,1,0:T(8,128)(2,1)S(1)}, u32[]{:S(2)}, u32[]{:S(2)}) async-start(bf16[128,16,128]{2,1,0:T(8,128)(2,1)} %copy.67), calls=%async_computation | async-start | bytes 1048576 | tf_op jit(solution)/shard_map/all_to_all | solution.py:54
  28.6 6.8 %all-to-all-done = bf16[128,16,128]{2,1,0:T(8,128)(2,1)S(1)} async-done(((bf16[128,16,128]{2,1,0:T(8,128)(2,1)}), bf16[128,16,128]{2,1,0:T(8,128)(2,1)S(1)}, u32[]{:S(2)}, u32[]{:S(2)}) %all-to-all-start) | async-done | bytes 524320 | tf_op jit(solution)/shard_map/all_to_all | solution.py:54
  35.4 5.8 %all-to-all-start.3 = ((bf16[64,16,256]{2,1,0:T(8,128)(2,1)}), bf16[64,16,256]{2,1,0:T(8,128)(2,1)S(1)}, u32[]{:S(2)}, u32[]{:S(2)}) async-start(bf16[64,16,256]{2,1,0:T(8,128)(2,1)} %bitcast.114), calls=%async_computation.3 | async-start | bytes 1048576 | tf_op jit(solution)/shard_map/all_to_all | solution.py:60
  42.4 13.3 %all-to-all-done.3 = bf16[64,16,256]{2,1,0:T(8,128)(2,1)S(1)} async-done(((bf16[64,16,256]{2,1,0:T(8,128)(2,1)}), bf16[64,16,256]{2,1,0:T(8,128)(2,1)S(1)}, u32[]{:S(2)}, u32[]{:S(2)}) %all-to-all-start.3) | async-done | bytes 524320 | tf_op jit(solution)/shard_map/all_to_all | solution.py:60
  55.7 4.1 %all-to-all-start.1 = ((bf16[64,16,256]{2,1,0:T(8,128)(2,1)}), bf16[64,16,256]{2,1,0:T(8,128)(2,1)S(1)}, u32[]{:S(2)}, u32[]{:S(2)}) async-start(bf16[64,16,256]{2,1,0:T(8,128)(2,1)} %bitcast.115), calls=%async_computation.1 | async-start | bytes 1048576 | tf_op jit(solution)/shard_map/all_to_all | solution.py:53
  63.2 11.1 %all-to-all-done.1 = bf16[64,16,256]{2,1,0:T(8,128)(2,1)S(1)} async-done(((bf16[64,16,256]{2,1,0:T(8,128)(2,1)}), bf16[64,16,256]{2,1,0:T(8,128)(2,1)S(1)}, u32[]{:S(2)}, u32[]{:S(2)}) %all-to-all-start.1) | async-done | bytes 524320 | tf_op jit(solution)/shard_map/all_to_all | solution.py:53
  74.3 3.2 %all-to-all-start.7 = ((bf16[2,2,2048]{2,1,0:T(2,128)(2,1)}), bf16[2,2,2048]{2,1,0:T(2,128)(2,1)S(1)}, u32[]{:S(2)}, u32[]{:S(2)}) async-start(bf16[2,2,2048]{2,1,0:T(2,128)(2,1)} %reshape.174), calls=%async_computation.7 | async-start | bytes 32768 | tf_op jit(solution)/shard_map/all_to_all | solution.py:46
  77.5 4.4 %all_gather.6 = bf16[2,256,32]{1,2,0:T(8,128)(2,1)S(1)} all-gather(bf16[1,256,32]{1,2,0:T(8,128)(2,1)S(1)} %get-tuple-element.15), channel_id=1, replica_groups=mesh['branch'=2,'rows'=16] {'branch'}, dimensions={0}, use_global_device_ids=true | all-gather | bytes 49152 | tf_op jit(solution)/shard_map/all_gather | solution.py:44
  82.9 4.1 %all-to-all-start.6 = ((bf16[16,2,512]{2,1,0:T(2,128)(2,1)}), bf16[16,2,512]{2,1,0:T(2,128)(2,1)S(1)}, u32[]{:S(2)}, u32[]{:S(2)}) async-start(bf16[16,2,512]{2,1,0:T(2,128)(2,1)} %reshape.172), calls=%async_computation.6 | async-start | bytes 65536 | tf_op jit(solution)/shard_map/all_to_all | solution.py:45
  87.4 1.2 copy.73
  88.6 5.1 %all-to-all-done.6 = bf16[16,2,512]{2,1,0:T(2,128)(2,1)S(1)} async-done(((bf16[16,2,512]{2,1,0:T(2,128)(2,1)}), bf16[16,2,512]{2,1,0:T(2,128)(2,1)S(1)}, u32[]{:S(2)}, u32[]{:S(2)}) %all-to-all-start.6) | async-done | bytes 32800 | tf_op jit(solution)/shard_map/all_to_all | solution.py:45
  93.7 3.6 %all-to-all-start.4 = ((bf16[4,256,256]{2,0,1:T(4,128)(2,1)}), bf16[4,256,256]{2,0,1:T(4,128)(2,1)S(1)}, u32[]{:S(2)}, u32[]{:S(2)}) async-start(bf16[4,256,256]{2,0,1:T(4,128)(2,1)} %copy.73), calls=%async_computation.4 | async-start | bytes 1048576 | tf_op jit(solution)/shard_map/all_to_all | solution.py:72
  98.3 24.8 %all-gather = bf16[32,1,32,128]{3,2,1,0:T(8,128)(2,1)S(1)} all-gather(bf16[2,1,32,128]{3,2,1,0:T(8,128)(2,1)S(1)} %copy.83), channel_id=2, replica_groups=mesh['branch'=2,'rows'=16] {'rows'}, dimensions={0}, use_global_device_ids=true | all-gather | bytes 278528 | tf_op jit(solution)/shard_map/all_gather | solution.py:47
  123.4 3.4 %multiply_convert_fusion = bf16[512,4096]{1,0:T(8,128)(2,1)} fusion(bf16[32,512]{1,0:T(8,128)(2,1)S(1)} %reshape.156, bf16[4,8,32,128]{3,2,1,0:T(8,128)(2,1)S(1)} %bitcast.133), kind=kOutput, calls=%fused_computation | convolution fusion | flops 138412032 | bytes 4489216 | tf_op jit(solution)/shard_map/dot_general | solution.py:142
  126.8 7.5 %reshape.158 = bf16[16,1024,128]{2,1,0:T(8,128)(2,1)} reshape(bf16[512,4096]{1,0:T(8,128)(2,1)} %multiply_convert_fusion) | data formatting | bytes 8388608 | tf_op jit(solution)/shard_map/reshape | solution.py:148
  134.4 1.3 copy.76
  135.7 1.5 reshape.176
  137.2 3.7 %all-to-all-start.5 = ((bf16[2,2,65536]{2,1,0:T(2,128)(2,1)}), bf16[2,2,65536]{2,1,0:T(2,128)(2,1)S(1)}, u32[]{:S(2)}, u32[]{:S(2)}) async-start(bf16[2,2,65536]{2,1,0:T(2,128)(2,1)} %reshape.176), calls=%async_computation.5 | async-start | bytes 1048576 | tf_op jit(solution)/shard_map/all_to_all | solution.py:71
  140.9 4.5 %fusion.49 = f32[16,128,128]{2,1,0:T(8,128)} fusion(bf16[16,1024,128]{2,1,0:T(8,128)(2,1)} %reshape.158, bf16[1024,128]{1,0:T(8,128)(2,1)S(1)} %copy-done.3), kind=kOutput, calls=%fused_computation.72 | convolution fusion | flops 536870912 | bytes 5505024 | tf_op jit(solution)/shard_map/dot_general | solution.py:151
  145.4 4.5 %all-to-all-done.5 = bf16[2,2,65536]{2,1,0:T(2,128)(2,1)S(1)} async-done(((bf16[2,2,65536]{2,1,0:T(2,128)(2,1)}), bf16[2,2,65536]{2,1,0:T(2,128)(2,1)S(1)}, u32[]{:S(2)}, u32[]{:S(2)}) %all-to-all-start.5) | async-done | bytes 524320 | tf_op jit(solution)/shard_map/all_to_all | solution.py:71
  150.6 1.1 copy.77
  152.1 1.9 %fusion = f32[128,2048]{0,1:T(8,128)S(1)} fusion(bf16[128,128]{1,0:T(8,128)(2,1)S(1)} %copy-done.9, f32[640,2048]{0,1:T(8,128)} %copy-done.1, f32[16,8,16,128]{3,2,1,0:T(8,128)S(1)} %bitcast.116, f32[2048]{0:T(1024)S(1)} %rsqrt_bitcast_fusion, f32[2048]{0:T(1024)S(1)} %get-tuple-element.16), kind=kOutput, calls=%fused_computation.4 | convolution fusion | flops 68943872 | bytes 3194880 | tf_op jit(solution)/shard_map/dot_general | solution.py:115
  155.1 3.3 %fusion.4 = bf16[16,128,128]{2,1,0:T(8,128)(2,1)} fusion(f32[16,128,128]{2,1,0:T(8,128)} %fusion.49, f32[16,128]{1,0:T(8,128)S(1)} %add_rsqrt_fusion, f32[16,128]{1,0:T(8,128)S(1)} %broadcast_multiply_fusion, f32[16,128,128]{2,1,0:T(8,128)S(1)} %bitcast.120, bf16[16,128,128]{2,1,0:T(8,128)(2,1)S(1)} %copy-done.2, bf16[512,128]{1,0:T(8,128)(2,1)S(1)} %copy-done.6, ...), kind=kOutput, calls=%fused_computation.12 | convolution fusion | flops 541589504 | bytes 3424256 | tf_op jit(solution)/shard_map/ijh,hd->ijd/dot_general | solution.py:127
  (66 shorter events, 10.7 us)
Async XLA Ops:
  0.6 59.2 %copy-start = (bf16[1024,256]{1,0:T(8,128)(2,1)S(1)}, bf16[1024,256]{1,0:T(8,128)(2,1)}, u32[]{:S(2)}) copy-start(bf16[1024,256]{1,0:T(8,128)(2,1)} %param.13) | copy-start | bytes 1572868
  7.1 2.3 %copy-start.1 = (f32[640,2048]{0,1:T(8,128)}, f32[640,2048]{0,1:T(8,128)S(1)}, u32[]{:S(2)}) copy-start(f32[640,2048]{0,1:T(8,128)S(1)} %convolution_bitcast_fusion) | copy-start | bytes 15728644
  9.9 31.3 %copy-start.4 = (bf16[1,256,256]{2,1,0:T(8,128)(2,1)S(1)}, bf16[1,256,256]{2,1,0:T(8,128)(2,1)}, u32[]{:S(2)}) copy-start(bf16[1,256,256]{2,1,0:T(8,128)(2,1)} %param.10) | copy-start | bytes 393220
  11.1 48.7 %copy-start.5 = (bf16[256,1024]{1,0:T(8,128)(2,1)S(1)}, bf16[256,1024]{1,0:T(8,128)(2,1)}, u32[]{:S(2)}) copy-start(bf16[256,1024]{1,0:T(8,128)(2,1)} %param.12) | copy-start | bytes 1572868
  11.1 13.1 %all-to-all-start.2 = ((bf16[128,16,128]{2,1,0:T(8,128)(2,1)}), bf16[128,16,128]{2,1,0:T(8,128)(2,1)S(1)}, u32[]{:S(2)}, u32[]{:S(2)}) async-start(bf16[128,16,128]{2,1,0:T(8,128)(2,1)} %copy.70), calls=%async_computation.2 | async-start | bytes 1048576 | tf_op jit(solution)/shard_map/all_to_all | solution.py:61
  15.5 45.1 %copy-start.8 = (bf16[256,64]{0,1:T(8,128)(2,1)S(1)}, bf16[256,64]{0,1:T(8,128)(2,1)}, u32[]{:S(2)}) copy-start(bf16[256,64]{0,1:T(8,128)(2,1)} %param.14) | copy-start | bytes 98308
  24.2 11.2 %all-to-all-start = ((bf16[128,16,128]{2,1,0:T(8,128)(2,1)}), bf16[128,16,128]{2,1,0:T(8,128)(2,1)S(1)}, u32[]{:S(2)}, u32[]{:S(2)}) async-start(bf16[128,16,128]{2,1,0:T(8,128)(2,1)} %copy.67), calls=%async_computation | async-start | bytes 1048576 | tf_op jit(solution)/shard_map/all_to_all | solution.py:54
  35.4 20.3 %all-to-all-start.3 = ((bf16[64,16,256]{2,1,0:T(8,128)(2,1)}), bf16[64,16,256]{2,1,0:T(8,128)(2,1)S(1)}, u32[]{:S(2)}, u32[]{:S(2)}) async-start(bf16[64,16,256]{2,1,0:T(8,128)(2,1)} %bitcast.114), calls=%async_computation.3 | async-start | bytes 1048576 | tf_op jit(solution)/shard_map/all_to_all | solution.py:60
  55.7 18.6 %all-to-all-start.1 = ((bf16[64,16,256]{2,1,0:T(8,128)(2,1)}), bf16[64,16,256]{2,1,0:T(8,128)(2,1)S(1)}, u32[]{:S(2)}, u32[]{:S(2)}) async-start(bf16[64,16,256]{2,1,0:T(8,128)(2,1)} %bitcast.115), calls=%async_computation.1 | async-start | bytes 1048576 | tf_op jit(solution)/shard_map/all_to_all | solution.py:53
  74.3 8.6 %all-to-all-start.7 = ((bf16[2,2,2048]{2,1,0:T(2,128)(2,1)}), bf16[2,2,2048]{2,1,0:T(2,128)(2,1)S(1)}, u32[]{:S(2)}, u32[]{:S(2)}) async-start(bf16[2,2,2048]{2,1,0:T(2,128)(2,1)} %reshape.174), calls=%async_computation.7 | async-start | bytes 32768 | tf_op jit(solution)/shard_map/all_to_all | solution.py:46
  82.9 10.8 %all-to-all-start.6 = ((bf16[16,2,512]{2,1,0:T(2,128)(2,1)}), bf16[16,2,512]{2,1,0:T(2,128)(2,1)S(1)}, u32[]{:S(2)}, u32[]{:S(2)}) async-start(bf16[16,2,512]{2,1,0:T(2,128)(2,1)} %reshape.172), calls=%async_computation.6 | async-start | bytes 65536 | tf_op jit(solution)/shard_map/all_to_all | solution.py:45
  93.7 40.6 %all-to-all-start.4 = ((bf16[4,256,256]{2,0,1:T(4,128)(2,1)}), bf16[4,256,256]{2,0,1:T(4,128)(2,1)S(1)}, u32[]{:S(2)}, u32[]{:S(2)}) async-start(bf16[4,256,256]{2,0,1:T(4,128)(2,1)} %copy.73), calls=%async_computation.4 | async-start | bytes 1048576 | tf_op jit(solution)/shard_map/all_to_all | solution.py:72
  134.2 6.7 %copy-start.3 = (bf16[1024,128]{1,0:T(8,128)(2,1)S(1)}, bf16[1024,128]{1,0:T(8,128)(2,1)}, u32[]{:S(2)}) copy-start(bf16[1024,128]{1,0:T(8,128)(2,1)} %param.15) | copy-start | bytes 786436
  137.2 12.7 %all-to-all-start.5 = ((bf16[2,2,65536]{2,1,0:T(2,128)(2,1)}), bf16[2,2,65536]{2,1,0:T(2,128)(2,1)S(1)}, u32[]{:S(2)}, u32[]{:S(2)}) async-start(bf16[2,2,65536]{2,1,0:T(2,128)(2,1)} %reshape.176), calls=%async_computation.5 | async-start | bytes 1048576 | tf_op jit(solution)/shard_map/all_to_all | solution.py:71
  145.4 6.7 %copy-start.9 = (bf16[128,128]{1,0:T(8,128)(2,1)S(1)}, bf16[128,128]{1,0:T(8,128)(2,1)}, u32[]{:S(2)}) copy-start(bf16[128,128]{1,0:T(8,128)(2,1)} %param.17) | copy-start | bytes 98308
  151.7 2.3 %copy-start.2 = (bf16[16,128,128]{2,1,0:T(8,128)(2,1)S(1)}, bf16[16,128,128]{2,1,0:T(8,128)(2,1)}, u32[]{:S(2)}) copy-start(bf16[16,128,128]{2,1,0:T(8,128)(2,1)} %param.11) | copy-start | bytes 1572868
  152.1 3.0 %copy-start.6 = (bf16[512,128]{1,0:T(8,128)(2,1)S(1)}, bf16[512,128]{1,0:T(8,128)(2,1)}, u32[]{:S(2)}) copy-start(bf16[512,128]{1,0:T(8,128)(2,1)} %param.19) | copy-start | bytes 393220
  152.1 3.0 %copy-start.7 = (bf16[128,512]{1,0:T(8,128)(2,1)S(1)}, bf16[128,512]{1,0:T(8,128)(2,1)}, u32[]{:S(2)}) copy-start(bf16[128,512]{1,0:T(8,128)(2,1)} %param.18) | copy-start | bytes 393220
where the time goes:
time: 160 us; the launch traced here: 158 us
  waiting for transfers between devices  48.4 us (30%)
  starting transfers between devices  32.4 us (20%)
  blocking collectives  29.2 us (18%)
  local copies, waits for them, and re-layouts  23.7 us (15%)
  matrix products  16 us (10%)
  other arithmetic  7.76 us (5%)
    all_gather x1, blocking collectives, alignment_branch(): right_gathered = lax.all_gather(right_pair, 'rows', axis=0, tiled=True)  24.8 us
    all_to_all x1, waiting for transfers between devices, send_whole(): lax.all_to_all(lax.all_to_all(tri_right, 'branch', split_axis=0, concat_a...  13.3 us
    all_to_all x1, waiting for transfers between devices, send_whole(): lax.all_to_all(lax.all_to_all(tri_left, 'branch', split_axis=0, concat_ax...  11.1 us
    unnamed x29, local copies, waits for them, and re-layouts  7.72 us
    all_to_all x1, waiting for transfers between devices, send_whole(): lax.all_to_all(tri_right, 'branch', split_axis=0, concat_axis=2, tiled=True)  7.53 us
    reshape x1, local copies, waits for them, and re-layouts, outer_product(): outer_vals = (outer_vals / total_rows).astype(jnp.bfloat16).reshape(tile_...  7.46 us
    all_to_all x1, waiting for transfers between devices, send_whole(): lax.all_to_all(tri_left, 'branch', split_axis=0, concat_axis=2, tiled=True)  6.79 us
    all_to_all x1, starting transfers between devices, send_whole(): lax.all_to_all(lax.all_to_all(tri_right, 'branch', split_axis=0, concat_a...  5.81 us
  transfers between devices with their start and end apart: 8, of which 6 were waited for; matrix products, arithmetic and copies ran while one was open for 16% of the time, Pallas kernels for 0%

commit v1 on v0

--- a/solution.py
+++ b/solution.py
@@ -1,8 +1,20 @@
+import functools
+
 import jax
 import jax.numpy as jnp
 from jax import lax
+from jax.experimental import pallas as pl
+from jax.experimental.pallas import tpu as pltpu
 from jax.sharding import PartitionSpec as P
 
+BF16 = jnp.bfloat16
+F32 = jnp.float32
+AXES = ("branch", "rows")
+NT = (((1,), (1,)), ((), ()))
+TN = (((0,), (0,)), ((), ()))
+VMEM = pl.BlockSpec(memory_space=pltpu.VMEM)
+SMEM = pl.BlockSpec(memory_space=pltpu.SMEM)
+PARAMS = pltpu.CompilerParams(vmem_limit_bytes=48 * 1024 * 1024)
 
 def standardize_features(values, dimension):
     average = jnp.mean(values, axis=dimension, keepdims=True)
@@ -159,7 +171,7 @@
     return jnp.transpose(outer_eij, (1, 2, 0))
 
 
-def on_device(
+def general_device(
     homolog_features,
     pairwise_input,
     transition_expand_matrix,
@@ -186,9 +198,334 @@
     return (refreshed_homolog_features, pairwise_output)
 
 
+def normed(values, axis):
+    average = jnp.mean(values, axis=axis, keepdims=True)
+    centered = values - average
+    variance = jnp.mean(centered * centered, axis=axis, keepdims=True)
+    return (centered * lax.rsqrt(variance + 1e-05)).astype(BF16)
+
+
+def sigmoid(values):
+    return 0.5 * jnp.tanh(0.5 * values) + 0.5
+
+
+def dot(a, b, dims=(((1,), (0,)), ((), ()))):
+    return lax.dot_general(a, b, dims, preferred_element_type=F32)
+
+
+def cost(flops, nbytes, transcendentals=0):
+    return pl.CostEstimate(flops=flops, bytes_accessed=nbytes, transcendentals=transcendentals)
+
+
+def operands_kernel(x_ref, w_ref, out_ref, scr):
+    rows, _, chans = x_ref.shape
+    per = out_ref.shape[1] // 2
+    n = 2 * chans
+    row = lax.broadcasted_iota(jnp.int32, (n, n), 0)
+    col = lax.broadcasted_iota(jnp.int32, (n, n), 1)
+    source = (row % (2 * per)) // per * chans + row // (2 * per) * per + row % per
+    order = jnp.where(col == source, 1.0, 0.0).astype(BF16)
+    w = w_ref[...]
+    values = jnp.concatenate([w[:, :chans], w[:, 2 * chans : 3 * chans]], axis=1)
+    gates = jnp.concatenate([w[:, chans : 2 * chans], w[:, 3 * chans : 4 * chans]], axis=1)
+    values = dot(order, values, NT).astype(BF16)
+    gates = dot(order, gates, NT).astype(BF16)
+    width = x_ref.shape[1]
+    for i in range(0, rows, 2):
+        pair = x_ref[i : i + 2].astype(F32).reshape(2 * width, chans)
+        tokens = normed(pair, -1)
+        result = dot(values, tokens, NT) * sigmoid(dot(gates, tokens, NT))
+        scr[pl.ds(i, n, stride=rows), :] = result[:, :width]
+        scr[pl.ds(i + 1, n, stride=rows), :] = result[:, width:]
+    for q in range(n):
+        out_ref[q // (2 * per), q % (2 * per)] = scr[q * rows : (q + 1) * rows, :].astype(BF16)
+
+
+def operands(x, w, devices):
+    rows, width, chans = x.shape
+    return pl.pallas_call(
+        operands_kernel,
+        out_shape=jax.ShapeDtypeStruct((devices, 2 * chans // devices, rows, width), BF16),
+        in_specs=[VMEM, VMEM],
+        out_specs=VMEM,
+        scratch_shapes=[pltpu.VMEM((2 * chans * rows, width), F32)],
+        compiler_params=PARAMS,
+        cost_estimate=cost(2 * rows * width * chans * 4 * chans, 3 * rows * width * chans * 2),
+        name="triangle_operands",
+    )(x, w)
+
+
+def gate_kernel(x_ref, w_ref, out_ref):
+    rows, width, chans = x_ref.shape
+    tokens = normed(x_ref[...].astype(F32).reshape(rows * width, chans), -1)
+    out_ref[...] = sigmoid(dot(tokens, w_ref[:, 4 * chans :])).reshape(rows, width, chans)
+
+
+def output_gate(x, w):
+    rows, width, chans = x.shape
+    step = 4
+    spec = pl.BlockSpec((step, width, chans), lambda i: (i, 0, 0))
+    return pl.pallas_call(
+        gate_kernel,
+        grid=(rows // step,),
+        out_shape=jax.ShapeDtypeStruct(x.shape, F32),
+        in_specs=[spec, pl.BlockSpec(w.shape, lambda i: (0, 0))],
+        out_specs=spec,
+        compiler_params=PARAMS,
+        cost_estimate=cost(2 * rows * width * chans * chans, rows * width * chans * 6),
+        name="triangle_output_gate",
+    )(x, w)
+
+
+def product_kernel(n_branch, in_ref, out_ref):
+    devices, double, rows, width = in_ref.shape
+    per = double // 2
+    n_rows = devices // n_branch
+    total = n_rows * rows
+
+    def side(c):
+        halves = [
+            in_ref[b * n_rows : (b + 1) * n_rows, c].reshape(total, width) for b in range(n_branch)
+        ]
+        return jnp.concatenate(halves, axis=1)
+
+    for c in range(per):
+        product = dot(side(c), side(per + c), NT).astype(BF16)
+        for b in range(n_branch):
+            out_ref[b * n_rows : (b + 1) * n_rows, c] = product[
+                :, b * width : (b + 1) * width
+            ].reshape(n_rows, rows, width)
+
+
+def triangle_product(received, n_branch):
+    devices, double, rows, width = received.shape
+    return pl.pallas_call(
+        functools.partial(product_kernel, n_branch),
+        out_shape=jax.ShapeDtypeStruct((devices, double // 2, rows, width), BF16),
+        in_specs=[VMEM],
+        out_specs=VMEM,
+        compiler_params=PARAMS,
+        cost_estimate=cost(double * (devices // n_branch * rows) ** 3, received.size * 3),
+        name="triangle_product",
+    )(received)
+
+
+def pair_output_kernel(
+    p_ref, x_ref, gate_ref, outer_ref, w_ref, up_ref, down_ref, out_ref, scr
+):
+    devices, per, rows, width = p_ref.shape
+    chans = devices * per
+    for g in range(devices):
+        for c in range(per):
+            scr[pl.ds(g * per + c, rows, stride=chans), :] = p_ref[g, c].astype(F32)
+    step = 4
+    for i in range(0, rows, step):
+        parts = [
+            normed(scr[(i + k) * chans : (i + k + 1) * chans, :], 0) for k in range(step)
+        ]
+        update = dot(jnp.concatenate(parts, axis=1), w_ref[...], TN)
+        shape = (step * width, chans)
+        x = x_ref[i : i + step].astype(F32).reshape(shape)
+        middle = x + gate_ref[i : i + step].reshape(shape) * update
+        hidden = jnp.maximum(dot(normed(middle, -1), up_ref[...]), 0.0).astype(BF16)
+        result = middle + dot(hidden, down_ref[...]) + outer_ref[i : i + step].reshape(shape)
+        out_ref[i : i + step] = result.astype(BF16).reshape(step, width, chans)
+
+
+def pair_output(product, x, gate, outer, w, up, down):
+    devices, per, rows, width = product.shape
+    chans = devices * per
+    return pl.pallas_call(
+        pair_output_kernel,
+        out_shape=jax.ShapeDtypeStruct(x.shape, BF16),
+        in_specs=[VMEM] * 7,
+        out_specs=VMEM,
+        scratch_shapes=[pltpu.VMEM((rows * chans, width), F32)],
+        compiler_params=PARAMS,
+        cost_estimate=cost(2 * x.size * (chans + 2 * up.shape[1]), x.size * 14),
+        name="pair_output",
+    )(product, x, gate, outer, w, up, down)
+
+
+def msa_kernel(n_branch, where_ref, x_ref, up_ref, down_ref, factor_ref, fresh_ref, *rest):
+    out_refs, right_scr, left_scr = rest[:-2], rest[-2], rest[-1]
+    x = x_ref[0].astype(F32)
+    hidden = jnp.maximum(dot(normed(x, -1), up_ref[...]), 0.0).astype(BF16)
+    fresh = (x + dot(hidden, down_ref[...])).astype(BF16)
+    fresh_ref[0] = fresh
+    tokens = normed(fresh.astype(F32), -1)
+    factor = factor_ref[...]
+    both = dot(tokens, factor).astype(BF16)
+    both_t = dot(factor, tokens, (((0,), (1,)), ((), ()))).astype(BF16)
+    depth = factor.shape[1] // 2
+    length = x.shape[0]
+    width = length // n_branch
+    for b in range(n_branch):
+        right_scr[b] = both_t[depth:, b * width : (b + 1) * width]
+    planes, span = left_scr.shape[:2]
+    padded = jnp.concatenate([both, jnp.zeros((length, width - 2 * depth), BF16)], axis=1)
+    left_scr[...] = padded.reshape(planes, span, width)
+    branch, plane = where_ref[0], where_ref[1]
+    for t, out_ref in enumerate(out_refs):
+        out_ref[:depth] = right_scr[lax.bitwise_xor(branch, t // planes)]
+        out_ref[depth:] = left_scr[lax.bitwise_xor(plane, t % planes)]
+
+
+def msa(where, x, up, down, factor, n_branch, planes):
+    _, length, feats = x.shape
+    depth = factor.shape[1] // 2
+    width, span = length // n_branch, length // planes
+    piece = jax.ShapeDtypeStruct((depth + span, width), BF16)
+    count = n_branch * planes
+    fresh, *pieces = pl.pallas_call(
+        functools.partial(msa_kernel, n_branch),
+        out_shape=[jax.ShapeDtypeStruct(x.shape, BF16)] + [piece] * count,
+        in_specs=[SMEM] + [VMEM] * 4,
+        out_specs=[VMEM] * (1 + count),
+        scratch_shapes=[
+            pltpu.VMEM((n_branch, depth, width), BF16),
+            pltpu.VMEM((planes, span, width), BF16),
+        ],
+        compiler_params=PARAMS,
+        cost_estimate=cost(4 * length * feats * up.shape[1], 4 * feats * up.shape[1]),
+        name="msa_transition",
+    )(where, x, up, down, factor)
+    return fresh, pieces
+
+
+def outer_kernel(where_ref, *refs):
+    groups, (w_ref, out_ref, right_scr, left_scr, w_scr, m_scr) = refs[:-6], refs[-6:]
+    rows, width, chans = out_ref.shape
+    total = sum(ref.shape[0] for ref in groups)
+    depth = m_scr.shape[1] // total
+    tile = where_ref[2]
+    s = 0
+    for ref in groups:
+        for k in range(ref.shape[0]):
+            right_scr[pl.ds(s, depth, stride=total), :] = ref[k, :depth].astype(F32)
+            start = pl.multiple_of(depth + tile * rows, rows)
+            left_scr[pl.ds(s, rows, stride=total), :] = ref[k, pl.ds(start, rows)].astype(F32)
+            s += 1
+    right = jnp.transpose(right_scr[...]).astype(BF16)
+    left = left_scr[...][:, :depth].astype(BF16)
+    w_scr[...] = w_ref[...].astype(F32)
+    for d in range(depth):
+        part = w_scr[pl.ds(d, depth, stride=depth), :].astype(BF16)
+        m_scr[:, d * total : (d + 1) * total] = (
+            dot(left, part).astype(BF16).reshape(rows, total, chans)
+        )
+    for i in range(0, rows, 2):
+        pair = jnp.concatenate([m_scr[i], m_scr[i + 1]], axis=1)
+        result = dot(right, pair) / total
+        out_ref[i] = result[:, :chans]
+        out_ref[i + 1] = result[:, chans:]
+
+
+def outer_update(where, groups, w, rows, chans):
+    total = sum(group.shape[0] for group in groups)
+    width = groups[0].shape[2]
+    depth = int(round(w.shape[0] ** 0.5))
+    return pl.pallas_call(
+        outer_kernel,
+        out_shape=jax.ShapeDtypeStruct((rows, width, chans), F32),
+        in_specs=[SMEM] + [VMEM] * (len(groups) + 1),
+        out_specs=VMEM,
+        scratch_shapes=[
+            pltpu.VMEM((depth * total, width), F32),
+            pltpu.VMEM((rows * total, width), F32),
+            pltpu.VMEM((depth * depth, chans), F32),
+            pltpu.VMEM((rows, depth * total, chans), BF16),
+        ],
+        compiler_params=PARAMS,
+        cost_estimate=cost(2 * rows * width * depth * total * chans * 2, rows * width * chans * 4),
+        name="outer_product_mean",
+    )(where, *groups, w)
+
+
+def swap(x, n_branch, n_rows, mask):
+    count = n_branch * n_rows
+    return lax.ppermute(x, AXES, [(d, d ^ mask) for d in range(count)])
+
+
+def own_channels_device(
+    n_branch,
+    n_rows,
+    homolog_features,
+    pairwise_input,
+    transition_expand_matrix,
+    transition_contract_matrix,
+    factor_pair_matrices,
+    outer_output_weight,
+    triangle_projection_weight,
+    triangle_output_weight,
+    pairwise_up_weight,
+    pairwise_down_weight,
+):
+    rows, _, chans = pairwise_input.shape
+    near = 4
+    planes = n_rows // near
+    r = lax.axis_index("rows")
+    where = jnp.stack([lax.axis_index("branch"), r // near, r % near]).astype(jnp.int32)
+
+    sent = operands(pairwise_input, triangle_projection_weight, n_branch * n_rows)
+    received = lax.all_to_all(sent, AXES, 0, 0, tiled=True)
+
+    fresh, pieces = msa(
+        where,
+        homolog_features,
+        transition_expand_matrix,
+        transition_contract_matrix,
+        factor_pair_matrices,
+        n_branch,
+        planes,
+    )
+    moved = [
+        piece if t == 0 else swap(piece, n_branch, n_rows, t // planes * n_rows + t % planes * near)
+        for t, piece in enumerate(pieces)
+    ]
+    mine = jnp.stack(moved)
+    beside = swap(mine, n_branch, n_rows, 2)
+    groups = [mine, beside, swap(mine, n_branch, n_rows, 1), swap(beside, n_branch, n_rows, 1)]
+    outer = outer_update(where, groups, outer_output_weight, rows, chans)
+    gate = output_gate(pairwise_input, triangle_projection_weight)
+
+    product = triangle_product(received, n_branch)
+    returned = lax.all_to_all(product, AXES, 0, 0, tiled=True)
+    pairwise_output = pair_output(
+        returned,
+        pairwise_input,
+        gate,
+        outer,
+        triangle_output_weight,
+        pairwise_up_weight,
+        pairwise_down_weight,
+    )
+    return (fresh, pairwise_output)
+
+
+def on_device(n_branch, n_rows, homolog_features, pairwise_input, *weights):
+    rows, width, chans = pairwise_input.shape
+    devices = n_branch * n_rows
+    planes = n_rows // 4
+    fits = (
+        homolog_features.shape[0] == 1
+        and n_branch & (n_branch - 1) == 0
+        and n_rows % 4 == 0
+        and n_rows & (n_rows - 1) == 0
+        and chans % devices == 0
+        and rows % 16 == 0
+        and width == 128
+        and homolog_features.shape[1] // planes == 4 * rows
+        and devices * chans * rows * width <= 2**25
+    )
+    if fits:
+        return own_channels_device(n_branch, n_rows, homolog_features, pairwise_input, *weights)
+    return general_device(homolog_features, pairwise_input, *weights)
+
+
 def solution(mesh):
     return jax.shard_map(
-        on_device,
+        functools.partial(on_device, mesh.shape["branch"], mesh.shape["rows"]),
         mesh=mesh,
         in_specs=(
             P(("branch", "rows"), None, None),

time: 160 us -> 70.9 us (0.44)
  blocking collectives: 29.2 us -> 0 us
  waiting for transfers between devices: 48.4 us -> 23.1 us
  local copies, waits for them, and re-layouts: 23.7 us -> 3.83 us
  matrix products: 16 us -> 0 us
  Pallas kernels: 0 us -> 15.2 us
  other arithmetic: 7.76 us -> 0.08 us
  starting transfers between devices: 32.4 us -> 27.4 us
    all_to_all x8 -> x2, waiting for transfers between devices: 48.4 us -> 0.01 us  [the longest x1 0.01 us: own_channels_device(): returned = lax.all_to_all(product, AXES, 0, 0, tiled=True)]
    all_gather x2 -> x0, blocking collectives: 29.2 us -> none  [the longest x1 24.8 us: alignment_branch(): right_gathered = lax.all_gather(right_pair, 'rows', axis=0, tiled=True)]
    ppermute x0 -> x10, waiting for transfers between devices: none -> 23.1 us  [swap(): return lax.ppermute(x, AXES, [(d, d ^ mask) for d in range(count)])]
    all_to_all x8 -> x2, starting transfers between devices: 32.4 us -> 11.3 us  [the longest x1 7.29 us: own_channels_device(): received = lax.all_to_all(sent, AXES, 0, 0, tiled=True)]
    ppermute x0 -> x10, starting transfers between devices: none -> 16.1 us  [swap(): return lax.ppermute(x, AXES, [(d, d ^ mask) for d in range(count)])]
    dot_general x8 -> x0, matrix products: 16 us -> none  [the longest x1 4.46 us: outer_product(): lax.dot_general(outer_output_weight, outer_vals, (((0,), (1,)), ((), ()))...]
    pallas_call x0 -> x6, Pallas kernels: none -> 15.2 us  [the longest x1 4.86 us: pair_output(): pl.pallas_call(pair_output_kernel, out_shape=jax.ShapeDtypeStruct(x.shape...]
    reshape x2 -> x0, local copies, waits for them, and re-layouts: 7.62 us -> none  [the longest x1 7.46 us: outer_product(): outer_vals = (outer_vals / total_rows).astype(jnp.bfloat16).reshape(tile_...]
  transfers between devices with their start and end apart: 8 -> 12, of which waited for: 6 -> 3; matrix products, arithmetic and copies ran while one was open for 16% -> 0% of each run, Pallas kernels for 0% -> 11%
where the time goes in v1:
time: 70.9 us; the launch traced here: 70.5 us
  starting transfers between devices  27.4 us (39%)
  waiting for transfers between devices  23.1 us (33%)
  Pallas kernels  15.2 us (21%)
  local copies, waits for them, and re-layouts  3.83 us (5%)
  between operations  0.91 us (1%)
    ppermute x10, waiting for transfers between devices, swap(): return lax.ppermute(x, AXES, [(d, d ^ mask) for d in range(count)])  23.1 us
    ppermute x10, starting transfers between devices, swap(): return lax.ppermute(x, AXES, [(d, d ^ mask) for d in range(count)])  16.1 us
    all_to_all x1, starting transfers between devices, own_channels_device(): received = lax.all_to_all(sent, AXES, 0, 0, tiled=True)  7.29 us
    pallas_call x1, Pallas kernels, pair_output(): pl.pallas_call(pair_output_kernel, out_shape=jax.ShapeDtypeStruct(x.shape...  4.86 us
    all_to_all x1, starting transfers between devices, own_channels_device(): returned = lax.all_to_all(product, AXES, 0, 0, tiled=True)  4.04 us
    unnamed x36, local copies, waits for them, and re-layouts  3.82 us
    pallas_call x1, Pallas kernels, operands(): pl.pallas_call(operands_kernel, out_shape=jax.ShapeDtypeStruct((devices,...  2.81 us
    pallas_call x1, Pallas kernels, outer_update(): pl.pallas_call(outer_kernel, out_shape=jax.ShapeDtypeStruct((rows, width,...  2.8 us
  transfers between devices with their start and end apart: 12, of which 3 were waited for; matrix products, arithmetic and copies ran while one was open for 0% of the time, Pallas kernels for 11%

profile of v1, /device:TPU:0, one launch (start us, length us, event | category | flops | bytes accessed | tf_op | source)
XLA Modules:
  0.0 70.5 jit_solution(5255187342612376853)
XLA Ops:
  0.6 0.0 copy-start
  0.6 1.0 %copy-done = bf16[16,128,128]{2,1,0:T(8,128)(2,1)S(1)} copy-done((bf16[16,128,128]{2,1,0:T(8,128)(2,1)S(1)}, bf16[16,128,128]{2,1,0:T(8,128)(2,1)}, u32[]{:S(2)}) %copy-start) | copy-done | bytes 524312
  1.7 0.9 %copy-done.2 = bf16[128,640]{1,0:T(8,128)(2,1)S(1)} copy-done((bf16[128,640]{1,0:T(8,128)(2,1)S(1)}, bf16[128,640]{1,0:T(8,128)(2,1)}, u32[]{:S(2)}) %copy-start.2) | copy-done | bytes 163864
  2.6 2.8 %triangle_operands.1 = bf16[32,8,16,128]{3,2,1,0:T(8,128)(2,1)} custom-call(bf16[16,128,128]{2,1,0:T(8,128)(2,1)S(1)} %copy-done, bf16[128,640]{1,0:T(8,128)(2,1)S(1)} %copy-done.2), custom_call_target="tpu_custom_call" | custom-call | flops 268435456 | bytes 1572864 | tf_op jit(solution)/shard_map/triangle_operands/pallas_call | solution.py:246
  5.4 7.3 %all-to-all-start = ((bf16[32,8,16,128]{3,2,1,0:T(8,128)(2,1)}), bf16[32,8,16,128]{3,2,1,0:T(8,128)(2,1)S(1)}, u32[]{:S(2)}, u32[]{:S(2)}) async-start(bf16[32,8,16,128]{3,2,1,0:T(8,128)(2,1)} %triangle_operands.1), calls=%async_computation | async-start | bytes 2097152 | tf_op jit(solution)/shard_map/all_to_all | solution.py:471
  12.7 0.0 copy-start.6
  12.8 0.1 copy.12.factor_ref
  12.9 0.1 pad_add_fusion.where_ref
  13.0 0.6 copy-done.6
  13.6 2.1 %msa_transition.1 = (bf16[1,256,256]{2,1,0:T(8,128)(2,1)}, bf16[96,128]{1,0:T(8,128)(2,1)S(1)}, bf16[96,128]{1,0:T(8,128)(2,1)S(1)}, bf16[96,128]{1,0:T(8,128)(2...) custom-call(s32[3]{0:T(128)S(1)} %pad_add_fusion.where_ref, ...), custom_call_target="tpu_custom_call" | custom-call | flops 268435456 | bytes 1048576 | tf_op jit(solution)/shard_map/msa_transition/pallas_call | solution.py:380
  15.7 1.8 %collective-permute-start = (bf16[96,128]{1,0:T(8,128)(2,1)S(1)}, bf16[96,128]{1,0:T(8,128)(2,1)S(1)}, u32[]{:S(2)}, u32[]{:S(2)}) collective-permute-start(bf16[96,128]{1,0:T(8,128)(2,1)S(1)} %get-tuple-element.13), channel_id=1, source_target_pairs={{0,4},{1,5},{2,6},{3,7},{4,0},{5,1},{6,2},{7,3},{8,12},{9,13},{10,... | collective-permute-start | bytes 73736 | tf_op jit(solution)/shard_map/ppermute | solution.py:447
  17.5 2.4 %collective-permute-start.1 = (bf16[96,128]{1,0:T(8,128)(2,1)S(1)}, bf16[96,128]{1,0:T(8,128)(2,1)S(1)}, u32[]{:S(2)}, u32[]{:S(2)}) collective-permute-start(bf16[96,128]{1,0:T(8,128)(2,1)S(1)} %get-tuple-element.14), channel_id=1, source_target_pairs={{0,8},{1,9},{2,10},{3,11},{4,12},{5,13},{6,14},{7,15},{8,0},{9,1},... | collective-permute-start | bytes 73736 | tf_op jit(solution)/shard_map/ppermute | solution.py:447
  19.9 0.2 collective-permute-start.2
  20.1 1.8 %collective-permute-start.3 = (bf16[96,128]{1,0:T(8,128)(2,1)S(1)}, bf16[96,128]{1,0:T(8,128)(2,1)S(1)}, u32[]{:S(2)}, u32[]{:S(2)}) collective-permute-start(bf16[96,128]{1,0:T(8,128)(2,1)S(1)} %get-tuple-element.16), channel_id=1, source_target_pairs={{0,16},{1,17},{2,18},{3,19},{4,20},{5,21},{6,22},{7,23},{8,24},{9,... | collective-permute-start | bytes 73736 | tf_op jit(solution)/shard_map/ppermute | solution.py:447
  21.9 0.6 collective-permute-start.4
  22.4 8.9 %collective-permute-done = bf16[96,128]{1,0:T(8,128)(2,1)S(1)} collective-permute-done((bf16[96,128]{1,0:T(8,128)(2,1)S(1)}, bf16[96,128]{1,0:T(8,128)(2,1)S(1)}, u32[]{:S(2)}, u32[]{:S(2)}) %collective-permute-start) | collective-permute-done | bytes 24608 | tf_op jit(solution)/shard_map/ppermute | solution.py:447
  31.4 5.6 %collective-permute-start.5 = (bf16[96,128]{1,0:T(8,128)(2,1)S(1)}, bf16[96,128]{1,0:T(8,128)(2,1)S(1)}, u32[]{:S(2)}, u32[]{:S(2)}) collective-permute-start(bf16[96,128]{1,0:T(8,128)(2,1)S(1)} %get-tuple-element.18), channel_id=1, source_target_pairs={{0,24},{1,25},{2,26},{3,27},{4,28},{5,29},{6,30},{7,31},{8,16},{9,... | collective-permute-start | bytes 73736 | tf_op jit(solution)/shard_map/ppermute | solution.py:447
  37.0 4.6 %collective-permute-done.1 = bf16[96,128]{1,0:T(8,128)(2,1)S(1)} collective-permute-done((bf16[96,128]{1,0:T(8,128)(2,1)S(1)}, bf16[96,128]{1,0:T(8,128)(2,1)S(1)}, u32[]{:S(2)}, u32[]{:S(2)}) %collective-permute-start.1) | collective-permute-done | bytes 24608 | tf_op jit(solution)/shard_map/ppermute | solution.py:447
  41.6 1.9 %collective-permute-start.6 = (bf16[96,128]{1,0:T(8,128)(2,1)S(1)}, bf16[96,128]{1,0:T(8,128)(2,1)S(1)}, u32[]{:S(2)}, u32[]{:S(2)}) collective-permute-start(bf16[96,128]{1,0:T(8,128)(2,1)S(1)} %get-tuple-element.19), channel_id=1, source_target_pairs={{0,28},{1,29},{2,30},{3,31},{4,24},{5,25},{6,26},{7,27},{8,20},{9,... | collective-permute-start | bytes 73736 | tf_op jit(solution)/shard_map/ppermute | solution.py:447
  43.6 1.1 %triangle_product.1 = bf16[32,4,16,128]{3,2,1,0:T(8,128)(2,1)} custom-call(bf16[32,8,16,128]{3,2,1,0:T(8,128)(2,1)S(1)} %all-to-all-done.in_ref), custom_call_target="tpu_custom_call" | custom-call | flops 134217728 | bytes 1572864 | tf_op jit(solution)/shard_map/triangle_product/pallas_call | solution.py:302
  44.7 4.0 %all-to-all-start.1 = ((bf16[32,4,16,128]{3,2,1,0:T(8,128)(2,1)}), bf16[32,4,16,128]{3,2,1,0:T(8,128)(2,1)S(1)}, u32[]{:S(2)}, u32[]{:S(2)}) async-start(bf16[32,4,16,128]{3,2,1,0:T(8,128)(2,1)} %triangle_product.1), calls=%async_computation.1 | async-start | bytes 1048576 | tf_op jit(solution)/shard_map/all_to_all | solution.py:493
  48.7 0.0 collective-permute-done.4
  48.8 0.0 copy-start.12
  48.8 1.8 %collective-permute-start.7 = (bf16[8,96,128]{2,1,0:T(8,128)(2,1)S(1)}, bf16[8,96,128]{2,1,0:T(8,128)(2,1)S(1)}, u32[]{:S(2)}, u32[]{:S(2)}) collective-permute-start(bf16[8,96,128]{2,1,0:T(8,128)(2,1)S(1)} %bitcast_dynamic-update-slice_fusion.refs_0_), channel_id=1, source_target_pairs={{0,2},{1,3},{2,0},{3,1},{4,6},{5,7},{6,4},{7,5},{8,10},{9,11},{10,... | collective-permute-start | bytes 589832 | tf_op jit(solution)/shard_map/ppermute | solution.py:447
  50.7 9.5 %collective-permute-done.7.refs_1_ = bf16[8,96,128]{2,1,0:T(8,128)(2,1)S(1)} collective-permute-done((bf16[8,96,128]{2,1,0:T(8,128)(2,1)S(1)}, bf16[8,96,128]{2,1,0:T(8,128)(2,1)S(1)}, u32[]{:S(2)}, u32[]{:S(2)}) %collective-permute-start.7) | collective-permute-done | bytes 196640 | tf_op jit(solution)/shard_map/ppermute | solution.py:447
  60.2 1.5 %triangle_output_gate.1.gate_ref = f32[16,128,128]{2,1,0:T(8,128)S(1)} custom-call(bf16[16,128,128]{2,1,0:T(8,128)(2,1)S(1)} %copy-done.1, bf16[128,640]{1,0:T(8,128)(2,1)S(1)} %copy-done.3), custom_call_target="tpu_custom_call" | custom-call | flops 67108864 | bytes 1572864 | tf_op jit(solution)/shard_map/triangle_output_gate/pallas_call | solution.py:268
  61.7 0.0 copy-start.7
  61.7 0.0 copy-start.8
  61.8 0.0 copy-start.9
  61.8 1.0 %copy-done.11 = bf16[8,96,128]{2,1,0:T(8,128)(2,1)S(1)} copy-done((bf16[8,96,128]{2,1,0:T(8,128)(2,1)S(1)}, bf16[8,96,128]{2,1,0:T(8,128)(2,1)}, u32[]{:S(2)}) %copy-start.11) | copy-done | bytes 196632
  62.8 2.8 %outer_product_mean.1.outer_ref = f32[16,128,128]{2,1,0:T(8,128)S(1)} custom-call(s32[3]{0:T(128)S(1)} %pad_add_fusion.where_ref, bf16[8,96,128]{2,1,0:T(8,128)(2,1)S(1)} %copy-done.11, bf16[8,96,128]{2,1,0:T(8,128)(2,1)S(1)} %collective-permute-done.7.refs_1_, bf16[8,96,128]{2,1,0:T(8,128)(2,1)S(1)} %collective-permute-done.8.refs_2_, ...), custom_call_target="tpu_custom_call" | custom-call | flops 1073741824 | bytes 1048576 | tf_op jit(solution)/shard_map/outer_product_mean/pallas_call | solution.py:428
  65.6 4.9 %pair_output.1 = bf16[16,128,128]{2,1,0:T(8,128)(2,1)} custom-call(bf16[32,4,16,128]{3,2,1,0:T(8,128)(2,1)S(1)} %all-to-all-done.1.p_ref, bf16[16,128,128]{2,1,0:T(8,128)(2,1)S(1)} %copy-done.1, f32[16,128,128]{2,1,0:T(8,128)S(1)} %triangle_output_gate.1.gate_ref, f32[16,128,128]{2,1,0:T(8,128)S(1)} %outer_product_mean.1.outer_ref, ...), custom_call_target="tpu_custom_call" | custom-call | flops 603979776 | bytes 3670016 | tf_op jit(solution)/shard_map/pair_output/pallas_call | solution.py:338
  (36 shorter events, 0.1 us)
Async XLA Ops:
  0.6 1.0 %copy-start = (bf16[16,128,128]{2,1,0:T(8,128)(2,1)S(1)}, bf16[16,128,128]{2,1,0:T(8,128)(2,1)}, u32[]{:S(2)}) copy-start(bf16[16,128,128]{2,1,0:T(8,128)(2,1)} %x_ref.7) | copy-start | bytes 1572868
  1.7 0.9 %copy-start.2 = (bf16[128,640]{1,0:T(8,128)(2,1)S(1)}, bf16[128,640]{1,0:T(8,128)(2,1)}, u32[]{:S(2)}) copy-start(bf16[128,640]{1,0:T(8,128)(2,1)} %w_ref.4) | copy-start | bytes 491524
  5.4 7.3 %copy-start.13 = (bf16[256,64]{0,1:T(8,128)(2,1)S(1)}, bf16[256,64]{0,1:T(8,128)(2,1)}, u32[]{:S(2)}) copy-start(bf16[256,64]{0,1:T(8,128)(2,1)} %param.14) | copy-start | bytes 98308
  5.4 7.6 %copy-start.4 = (bf16[256,1024]{1,0:T(8,128)(2,1)S(1)}, bf16[256,1024]{1,0:T(8,128)(2,1)}, u32[]{:S(2)}) copy-start(bf16[256,1024]{1,0:T(8,128)(2,1)} %up_ref.2) | copy-start | bytes 1572868
  5.4 7.6 %copy-start.5 = (bf16[1024,256]{1,0:T(8,128)(2,1)S(1)}, bf16[1024,256]{1,0:T(8,128)(2,1)}, u32[]{:S(2)}) copy-start(bf16[1024,256]{1,0:T(8,128)(2,1)} %down_ref.2) | copy-start | bytes 1572868
  5.4 38.1 %all-to-all-start = ((bf16[32,8,16,128]{3,2,1,0:T(8,128)(2,1)}), bf16[32,8,16,128]{3,2,1,0:T(8,128)(2,1)S(1)}, u32[]{:S(2)}, u32[]{:S(2)}) async-start(bf16[32,8,16,128]{3,2,1,0:T(8,128)(2,1)} %triangle_operands.1), calls=%async_computation | async-start | bytes 2097152 | tf_op jit(solution)/shard_map/all_to_all | solution.py:471
  12.7 0.9 %copy-start.6 = (bf16[1,256,256]{2,1,0:T(8,128)(2,1)S(1)}, bf16[1,256,256]{2,1,0:T(8,128)(2,1)}, u32[]{:S(2)}) copy-start(bf16[1,256,256]{2,1,0:T(8,128)(2,1)} %x_ref.4) | copy-start | bytes 393220
  15.7 15.7 %collective-permute-start = (bf16[96,128]{1,0:T(8,128)(2,1)S(1)}, bf16[96,128]{1,0:T(8,128)(2,1)S(1)}, u32[]{:S(2)}, u32[]{:S(2)}) collective-permute-start(bf16[96,128]{1,0:T(8,128)(2,1)S(1)} %get-tuple-element.13), channel_id=1, source_target_pairs={{0,4},{1,5},{2,6},{3,7},{4,0},{5,1},{6,2},{7,3},{8,12},{9,13},{10,... | collective-permute-start | bytes 73736 | tf_op jit(solution)/shard_map/ppermute | solution.py:447
  17.5 24.1 %collective-permute-start.1 = (bf16[96,128]{1,0:T(8,128)(2,1)S(1)}, bf16[96,128]{1,0:T(8,128)(2,1)S(1)}, u32[]{:S(2)}, u32[]{:S(2)}) collective-permute-start(bf16[96,128]{1,0:T(8,128)(2,1)S(1)} %get-tuple-element.14), channel_id=1, source_target_pairs={{0,8},{1,9},{2,10},{3,11},{4,12},{5,13},{6,14},{7,15},{8,0},{9,1},... | collective-permute-start | bytes 73736 | tf_op jit(solution)/shard_map/ppermute | solution.py:447
  19.9 23.6 %collective-permute-start.2 = (bf16[96,128]{1,0:T(8,128)(2,1)S(1)}, bf16[96,128]{1,0:T(8,128)(2,1)S(1)}, u32[]{:S(2)}, u32[]{:S(2)}) collective-permute-start(bf16[96,128]{1,0:T(8,128)(2,1)S(1)} %get-tuple-element.15), channel_id=1, source_target_pairs={{0,12},{1,13},{2,14},{3,15},{4,8},{5,9},{6,10},{7,11},{8,4},{9,5},... | collective-permute-start | bytes 73736 | tf_op jit(solution)/shard_map/ppermute | solution.py:447
  20.1 23.4 %collective-permute-start.3 = (bf16[96,128]{1,0:T(8,128)(2,1)S(1)}, bf16[96,128]{1,0:T(8,128)(2,1)S(1)}, u32[]{:S(2)}, u32[]{:S(2)}) collective-permute-start(bf16[96,128]{1,0:T(8,128)(2,1)S(1)} %get-tuple-element.16), channel_id=1, source_target_pairs={{0,16},{1,17},{2,18},{3,19},{4,20},{5,21},{6,22},{7,23},{8,24},{9,... | collective-permute-start | bytes 73736 | tf_op jit(solution)/shard_map/ppermute | solution.py:447
  21.9 26.9 %collective-permute-start.4 = (bf16[96,128]{1,0:T(8,128)(2,1)S(1)}, bf16[96,128]{1,0:T(8,128)(2,1)S(1)}, u32[]{:S(2)}, u32[]{:S(2)}) collective-permute-start(bf16[96,128]{1,0:T(8,128)(2,1)S(1)} %get-tuple-element.17), channel_id=1, source_target_pairs={{0,20},{1,21},{2,22},{3,23},{4,16},{5,17},{6,18},{7,19},{8,28},{9,... | collective-permute-start | bytes 73736 | tf_op jit(solution)/shard_map/ppermute | solution.py:447
  31.4 17.4 %collective-permute-start.5 = (bf16[96,128]{1,0:T(8,128)(2,1)S(1)}, bf16[96,128]{1,0:T(8,128)(2,1)S(1)}, u32[]{:S(2)}, u32[]{:S(2)}) collective-permute-start(bf16[96,128]{1,0:T(8,128)(2,1)S(1)} %get-tuple-element.18), channel_id=1, source_target_pairs={{0,24},{1,25},{2,26},{3,27},{4,28},{5,29},{6,30},{7,31},{8,16},{9,... | collective-permute-start | bytes 73736 | tf_op jit(solution)/shard_map/ppermute | solution.py:447
  41.6 7.2 %collective-permute-start.6 = (bf16[96,128]{1,0:T(8,128)(2,1)S(1)}, bf16[96,128]{1,0:T(8,128)(2,1)S(1)}, u32[]{:S(2)}, u32[]{:S(2)}) collective-permute-start(bf16[96,128]{1,0:T(8,128)(2,1)S(1)} %get-tuple-element.19), channel_id=1, source_target_pairs={{0,28},{1,29},{2,30},{3,31},{4,24},{5,25},{6,26},{7,27},{8,20},{9,... | collective-permute-start | bytes 73736 | tf_op jit(solution)/shard_map/ppermute | solution.py:447
  44.7 15.5 %copy-start.1 = (bf16[16,128,128]{2,1,0:T(8,128)(2,1)S(1)}, bf16[16,128,128]{2,1,0:T(8,128)(2,1)}, u32[]{:S(2)}) copy-start(bf16[16,128,128]{2,1,0:T(8,128)(2,1)} %x_ref.7) | copy-start | bytes 1572868
  44.7 15.5 %copy-start.3 = (bf16[128,640]{1,0:T(8,128)(2,1)S(1)}, bf16[128,640]{1,0:T(8,128)(2,1)}, u32[]{:S(2)}) copy-start(bf16[128,640]{1,0:T(8,128)(2,1)} %w_ref.4) | copy-start | bytes 491524
  44.7 20.9 %all-to-all-start.1 = ((bf16[32,4,16,128]{3,2,1,0:T(8,128)(2,1)}), bf16[32,4,16,128]{3,2,1,0:T(8,128)(2,1)S(1)}, u32[]{:S(2)}, u32[]{:S(2)}) async-start(bf16[32,4,16,128]{3,2,1,0:T(8,128)(2,1)} %triangle_product.1), calls=%async_computation.1 | async-start | bytes 1048576 | tf_op jit(solution)/shard_map/all_to_all | solution.py:493
  48.8 12.9 %copy-start.10 = (bf16[8,96,128]{2,1,0:T(8,128)(2,1)}, bf16[8,96,128]{2,1,0:T(8,128)(2,1)S(1)}, u32[]{:S(2)}) copy-start(bf16[8,96,128]{2,1,0:T(8,128)(2,1)S(1)} %bitcast_dynamic-update-slice_fusion.refs_0_) | copy-start | bytes 589828
  48.8 13.0 %copy-start.12 = (bf16[1024,128]{1,0:T(8,128)(2,1)S(1)}, bf16[1024,128]{1,0:T(8,128)(2,1)}, u32[]{:S(2)}) copy-start(bf16[1024,128]{1,0:T(8,128)(2,1)} %refs_4_.1) | copy-start | bytes 786436
  48.8 11.4 %collective-permute-start.7 = (bf16[8,96,128]{2,1,0:T(8,128)(2,1)S(1)}, bf16[8,96,128]{2,1,0:T(8,128)(2,1)S(1)}, u32[]{:S(2)}, u32[]{:S(2)}) collective-permute-start(bf16[8,96,128]{2,1,0:T(8,128)(2,1)S(1)} %bitcast_dynamic-update-slice_fusion.refs_0_), channel_id=1, source_target_pairs={{0,2},{1,3},{2,0},{3,1},{4,6},{5,7},{6,4},{7,5},{8,10},{9,11},{10,... | collective-permute-start | bytes 589832 | tf_op jit(solution)/shard_map/ppermute | solution.py:447
  50.7 11.1 %collective-permute-start.8 = (bf16[8,96,128]{2,1,0:T(8,128)(2,1)S(1)}, bf16[8,96,128]{2,1,0:T(8,128)(2,1)S(1)}, u32[]{:S(2)}, u32[]{:S(2)}) collective-permute-start(bf16[8,96,128]{2,1,0:T(8,128)(2,1)S(1)} %bitcast_dynamic-update-slice_fusion.refs_0_), channel_id=1, source_target_pairs={{0,1},{1,0},{2,3},{3,2},{4,5},{5,4},{6,7},{7,6},{8,9},{9,8},{10,11... | collective-permute-start | bytes 589832 | tf_op jit(solution)/shard_map/ppermute | solution.py:447
  60.2 1.6 %collective-permute-start.9 = (bf16[8,96,128]{2,1,0:T(8,128)(2,1)S(1)}, bf16[8,96,128]{2,1,0:T(8,128)(2,1)S(1)}, u32[]{:S(2)}, u32[]{:S(2)}) collective-permute-start(bf16[8,96,128]{2,1,0:T(8,128)(2,1)S(1)} %collective-permute-done.7.refs_1_), channel_id=1, source_target_pairs={{0,1},{1,0},{2,3},{3,2},{4,5},{5,4},{6,7},{7,6},{8,9},{9,8},{10,11... | collective-permute-start | bytes 589832 | tf_op jit(solution)/shard_map/ppermute | solution.py:447
  61.7 3.9 %copy-start.7 = (bf16[128,512]{1,0:T(8,128)(2,1)S(1)}, bf16[128,512]{1,0:T(8,128)(2,1)}, u32[]{:S(2)}) copy-start(bf16[128,512]{1,0:T(8,128)(2,1)} %up_ref.3) | copy-start | bytes 393220
  61.7 3.9 %copy-start.8 = (bf16[512,128]{1,0:T(8,128)(2,1)S(1)}, bf16[512,128]{1,0:T(8,128)(2,1)}, u32[]{:S(2)}) copy-start(bf16[512,128]{1,0:T(8,128)(2,1)} %down_ref.3) | copy-start | bytes 393220
  61.8 3.9 %copy-start.9 = (bf16[128,128]{1,0:T(8,128)(2,1)S(1)}, bf16[128,128]{1,0:T(8,128)(2,1)}, u32[]{:S(2)}) copy-start(bf16[128,128]{1,0:T(8,128)(2,1)} %w_ref.5) | copy-start | bytes 98308
  61.8 1.0 %copy-start.11 = (bf16[8,96,128]{2,1,0:T(8,128)(2,1)S(1)}, bf16[8,96,128]{2,1,0:T(8,128)(2,1)}, u32[]{:S(2)}) copy-start(bf16[8,96,128]{2,1,0:T(8,128)(2,1)} %copy-done.10) | copy-start | bytes 589828

commit v2 on v1

--- a/solution.py
+++ b/solution.py
@@ -217,42 +217,153 @@
     return pl.CostEstimate(flops=flops, bytes_accessed=nbytes, transcendentals=transcendentals)
 
 
-def operands_kernel(x_ref, w_ref, out_ref, scr):
+def channel_order(w, sides, source, count):
+    chans = w.shape[0]
+    col = lax.broadcasted_iota(jnp.int32, (count, chans), 1)
+    order = jnp.where(col == source, 1.0, 0.0).astype(BF16)
+    return [dot(order, w[:, s * chans : (s + 1) * chans], NT).astype(BF16) for s in sides]
+
+
+def gated_rows(values, gates, rows_ref, store):
+    rows, width, chans = rows_ref.shape
+    for i in range(0, rows, 2):
+        tokens = normed(rows_ref[i : i + 2].astype(F32).reshape(2 * width, chans), -1)
+        result = dot(values, tokens, NT) * sigmoid(dot(gates, tokens, NT))
+        store(i, result[:, :width])
+        store(i + 1, result[:, width:])
+
+
+def right_kernel(n_branch, x_hbm, w_hbm, out_ref, x_ref, w_ref, scr, sems):
     rows, _, chans = x_ref.shape
-    per = out_ref.shape[1] // 2
-    n = 2 * chans
-    row = lax.broadcasted_iota(jnp.int32, (n, n), 0)
-    col = lax.broadcasted_iota(jnp.int32, (n, n), 1)
-    source = (row % (2 * per)) // per * chans + row // (2 * per) * per + row % per
-    order = jnp.where(col == source, 1.0, 0.0).astype(BF16)
-    w = w_ref[...]
-    values = jnp.concatenate([w[:, :chans], w[:, 2 * chans : 3 * chans]], axis=1)
-    gates = jnp.concatenate([w[:, chans : 2 * chans], w[:, 3 * chans : 4 * chans]], axis=1)
-    values = dot(order, values, NT).astype(BF16)
-    gates = dot(order, gates, NT).astype(BF16)
-    width = x_ref.shape[1]
-    for i in range(0, rows, 2):
-        pair = x_ref[i : i + 2].astype(F32).reshape(2 * width, chans)
-        tokens = normed(pair, -1)
-        result = dot(values, tokens, NT) * sigmoid(dot(gates, tokens, NT))
-        scr[pl.ds(i, n, stride=rows), :] = result[:, :width]
-        scr[pl.ds(i + 1, n, stride=rows), :] = result[:, width:]
-    for q in range(n):
-        out_ref[q // (2 * per), q % (2 * per)] = scr[q * rows : (q + 1) * rows, :].astype(BF16)
-
-
-def operands(x, w, devices):
+    devices, per = out_ref.shape[:2]
+    groups = chans // per
+    near = groups // n_branch
+    halves = devices // groups
+    copies = [
+        pltpu.make_async_copy(w_hbm, w_ref, sems.at[0]),
+        pltpu.make_async_copy(x_hbm, x_ref, sems.at[1]),
+    ]
+    for copy in copies:
+        copy.start()
+    for copy in copies:
+        copy.wait()
+    source = lax.broadcasted_iota(jnp.int32, (chans, chans), 0)
+    values, gates = channel_order(w_ref[...], (2, 3), source, chans)
+
+    def store(i, block):
+        scr[pl.ds(i, chans, stride=rows), :] = block
+
+    gated_rows(values, gates, x_ref, store)
+    for q in range(chans):
+        g, c = q // per, q % per
+        block = scr[q * rows : (q + 1) * rows, :].astype(BF16)
+        for h in range(halves):
+            out_ref[(g // near * halves + h) * near + g % near, c] = block
+
+
+def right_operand(x, w, n_branch, devices, per):
     rows, width, chans = x.shape
+    hbm = pl.BlockSpec(memory_space=pl.ANY)
     return pl.pallas_call(
-        operands_kernel,
-        out_shape=jax.ShapeDtypeStruct((devices, 2 * chans // devices, rows, width), BF16),
-        in_specs=[VMEM, VMEM],
+        functools.partial(right_kernel, n_branch),
+        out_shape=jax.ShapeDtypeStruct((devices, per, rows, width), BF16),
+        in_specs=[hbm, hbm],
         out_specs=VMEM,
-        scratch_shapes=[pltpu.VMEM((2 * chans * rows, width), F32)],
+        scratch_shapes=[
+            pltpu.VMEM(x.shape, BF16),
+            pltpu.VMEM(w.shape, BF16),
+            pltpu.VMEM((chans * rows, width), F32),
+            pltpu.SemaphoreType.DMA((2,)),
+        ],
         compiler_params=PARAMS,
-        cost_estimate=cost(2 * rows * width * chans * 4 * chans, 3 * rows * width * chans * 2),
-        name="triangle_operands",
+        cost_estimate=cost(2 * rows * width * chans * 2 * chans, 3 * rows * width * chans * 2),
+        name="right_operand",
     )(x, w)
+
+
+def beside_kernel(
+    n_branch, near, where_ref, x_ref, other_ref, w_ref, seq_ref, up_ref, down_ref, factor_ref,
+    fresh_ref, *rest
+):
+    out_refs, (scr, right_scr, left_scr) = rest[:-3], rest[-3:]
+    rows, width, chans = x_ref.shape
+    branch, row_at = where_ref[0], where_ref[1]
+    core = lax.bitwise_and(row_at, 1)
+    place = lax.shift_right_logical(lax.bitwise_and(row_at, near - 1), 1)
+    count = len(out_refs)
+    places = count // n_branch
+    per = chans // (n_branch * near)
+
+    x = seq_ref[0].astype(F32)
+    hidden = jnp.maximum(dot(normed(x, -1), up_ref[...]), 0.0).astype(BF16)
+    fresh = (x + dot(hidden, down_ref[...])).astype(BF16)
+    fresh_ref[0] = fresh
+    tokens = normed(fresh.astype(F32), -1)
+    factor = factor_ref[...]
+    depth = factor.shape[1] // 2
+    left = dot(tokens, factor[:, :depth]).astype(BF16)
+    right = dot(factor[:, depth:], tokens, (((0,), (1,)), ((), ()))).astype(BF16)
+    for b in range(n_branch):
+        right_scr[b] = right[:, b * width : (b + 1) * width]
+    tiles = left.reshape(-1, places, 2, rows, depth)
+    for t in range(places):
+        left_scr[t] = jnp.concatenate(
+            [tiles[h, t, c] for h in range(tiles.shape[0]) for c in range(2)], axis=1
+        )
+
+    total = count * per
+    q = lax.broadcasted_iota(jnp.int32, (total, chans), 0)
+    t = q // per
+    group = lax.bitwise_xor(t // places, branch) * near + (
+        lax.bitwise_xor(t % places, place) * 2 + core
+    )
+    values, gates = channel_order(w_ref[...], (0, 1), group * per + q % per, total)
+
+    def store_at(at):
+        def store(i, block):
+            scr[at, pl.ds(i, total, stride=rows), :] = block
+
+        return store
+
+    gated_rows(values, gates, x_ref, store_at(core))
+    gated_rows(values, gates, other_ref, store_at(1 - core))
+    for t, out_ref in enumerate(out_refs):
+        for c in range(per):
+            for k in range(2):
+                start = (t * per + c) * rows
+                out_ref[pl.ds((c * 2 + k) * rows, rows)] = scr[k, start : start + rows, :].astype(
+                    BF16
+                )
+        base = per * 2 * rows
+        out_ref[base : base + depth] = right_scr[lax.bitwise_xor(branch, t // places)]
+        out_ref[base + depth :] = left_scr[lax.bitwise_xor(place, t % places)]
+
+
+def beside(where, x, other, w, seq, up, down, factor, n_branch, near):
+    rows, width, chans = x.shape
+    _, length, feats = seq.shape
+    depth = factor.shape[1] // 2
+    places = near // 2
+    count = n_branch * places
+    per = chans // (n_branch * near)
+    piece = jax.ShapeDtypeStruct((per * 2 * rows + depth + rows, width), BF16)
+    fresh, *pieces = pl.pallas_call(
+        functools.partial(beside_kernel, n_branch, near),
+        out_shape=[jax.ShapeDtypeStruct(seq.shape, BF16)] + [piece] * count,
+        in_specs=[SMEM] + [VMEM] * 7,
+        out_specs=[VMEM] * (1 + count),
+        scratch_shapes=[
+            pltpu.VMEM((2, count * per * rows, width), F32),
+            pltpu.VMEM((n_branch, depth, width), BF16),
+            pltpu.VMEM((places, rows, width), BF16),
+        ],
+        compiler_params=PARAMS,
+        cost_estimate=cost(
+            4 * length * feats * up.shape[1] + 4 * x.size * 2 * chans, 4 * feats * up.shape[1]
+        ),
+        name="left_operand_and_msa",
+    )(where, x, other, w, seq, up, down, factor)
+    return fresh, pieces
 
 
 def gate_kernel(x_ref, w_ref, out_ref):
@@ -277,37 +388,50 @@
     )(x, w)
 
 
-def product_kernel(n_branch, in_ref, out_ref):
-    devices, double, rows, width = in_ref.shape
-    per = double // 2
+def product_kernel(n_branch, near, where_ref, in_ref, *rest):
+    left_refs, (out_ref, left_scr) = rest[:-2], rest[-2:]
+    devices, per, rows, width = in_ref.shape
     n_rows = devices // n_branch
-    total = n_rows * rows
-
-    def side(c):
-        halves = [
-            in_ref[b * n_rows : (b + 1) * n_rows, c].reshape(total, width) for b in range(n_branch)
-        ]
-        return jnp.concatenate(halves, axis=1)
-
+    branch, row_at = where_ref[0], where_ref[1]
+    place = lax.shift_right_logical(lax.bitwise_and(row_at, near - 1), 1)
+    places = near // 2
+    for t, ref in enumerate(left_refs):
+        b = lax.bitwise_xor(branch, t // places)
+        p = lax.bitwise_xor(place, t % places)
+        for c in range(per):
+            left_scr[b, c, p] = ref[c * 2 * rows : (c + 1) * 2 * rows]
     for c in range(per):
-        product = dot(side(c), side(per + c), NT).astype(BF16)
+        left = jnp.concatenate(
+            [left_scr[b, c].reshape(near * rows, width) for b in range(n_branch)], axis=1
+        )
+        right = jnp.concatenate(
+            [
+                in_ref[b * n_rows : (b + 1) * n_rows, c].reshape(n_rows * rows, width)
+                for b in range(n_branch)
+            ],
+            axis=1,
+        )
+        product = dot(left, right, NT).astype(BF16)
         for b in range(n_branch):
-            out_ref[b * n_rows : (b + 1) * n_rows, c] = product[
+            out_ref[b * near : (b + 1) * near, c] = product[
                 :, b * width : (b + 1) * width
-            ].reshape(n_rows, rows, width)
-
-
-def triangle_product(received, n_branch):
-    devices, double, rows, width = received.shape
+            ].reshape(near, rows, width)
+
+
+def triangle_product(where, received, pieces, n_branch, near):
+    devices, per, rows, width = received.shape
     return pl.pallas_call(
-        functools.partial(product_kernel, n_branch),
-        out_shape=jax.ShapeDtypeStruct((devices, double // 2, rows, width), BF16),
-        in_specs=[VMEM],
+        functools.partial(product_kernel, n_branch, near),
+        out_shape=jax.ShapeDtypeStruct((n_branch * near, per, rows, width), BF16),
+        in_specs=[SMEM] + [VMEM] * (1 + len(pieces)),
         out_specs=VMEM,
+        scratch_shapes=[pltpu.VMEM((n_branch, per, near // 2, 2 * rows, width), BF16)],
         compiler_params=PARAMS,
-        cost_estimate=cost(double * (devices // n_branch * rows) ** 3, received.size * 3),
+        cost_estimate=cost(
+            2 * per * near * rows * received.size // per, received.size * 4
+        ),
         name="triangle_product",
-    )(received)
+    )(where, received, *pieces)
 
 
 def pair_output_kernel(
@@ -347,67 +471,19 @@
     )(product, x, gate, outer, w, up, down)
 
 
-def msa_kernel(n_branch, where_ref, x_ref, up_ref, down_ref, factor_ref, fresh_ref, *rest):
-    out_refs, right_scr, left_scr = rest[:-2], rest[-2], rest[-1]
-    x = x_ref[0].astype(F32)
-    hidden = jnp.maximum(dot(normed(x, -1), up_ref[...]), 0.0).astype(BF16)
-    fresh = (x + dot(hidden, down_ref[...])).astype(BF16)
-    fresh_ref[0] = fresh
-    tokens = normed(fresh.astype(F32), -1)
-    factor = factor_ref[...]
-    both = dot(tokens, factor).astype(BF16)
-    both_t = dot(factor, tokens, (((0,), (1,)), ((), ()))).astype(BF16)
-    depth = factor.shape[1] // 2
-    length = x.shape[0]
-    width = length // n_branch
-    for b in range(n_branch):
-        right_scr[b] = both_t[depth:, b * width : (b + 1) * width]
-    planes, span = left_scr.shape[:2]
-    padded = jnp.concatenate([both, jnp.zeros((length, width - 2 * depth), BF16)], axis=1)
-    left_scr[...] = padded.reshape(planes, span, width)
-    branch, plane = where_ref[0], where_ref[1]
-    for t, out_ref in enumerate(out_refs):
-        out_ref[:depth] = right_scr[lax.bitwise_xor(branch, t // planes)]
-        out_ref[depth:] = left_scr[lax.bitwise_xor(plane, t % planes)]
-
-
-def msa(where, x, up, down, factor, n_branch, planes):
-    _, length, feats = x.shape
-    depth = factor.shape[1] // 2
-    width, span = length // n_branch, length // planes
-    piece = jax.ShapeDtypeStruct((depth + span, width), BF16)
-    count = n_branch * planes
-    fresh, *pieces = pl.pallas_call(
-        functools.partial(msa_kernel, n_branch),
-        out_shape=[jax.ShapeDtypeStruct(x.shape, BF16)] + [piece] * count,
-        in_specs=[SMEM] + [VMEM] * 4,
-        out_specs=[VMEM] * (1 + count),
-        scratch_shapes=[
-            pltpu.VMEM((n_branch, depth, width), BF16),
-            pltpu.VMEM((planes, span, width), BF16),
-        ],
-        compiler_params=PARAMS,
-        cost_estimate=cost(4 * length * feats * up.shape[1], 4 * feats * up.shape[1]),
-        name="msa_transition",
-    )(where, x, up, down, factor)
-    return fresh, pieces
-
-
 def outer_kernel(where_ref, *refs):
     groups, (w_ref, out_ref, right_scr, left_scr, w_scr, m_scr) = refs[:-6], refs[-6:]
     rows, width, chans = out_ref.shape
     total = sum(ref.shape[0] for ref in groups)
     depth = m_scr.shape[1] // total
-    tile = where_ref[2]
     s = 0
     for ref in groups:
         for k in range(ref.shape[0]):
             right_scr[pl.ds(s, depth, stride=total), :] = ref[k, :depth].astype(F32)
-            start = pl.multiple_of(depth + tile * rows, rows)
-            left_scr[pl.ds(s, rows, stride=total), :] = ref[k, pl.ds(start, rows)].astype(F32)
+            left_scr[pl.ds(s, rows, stride=total), :] = ref[k, depth:].astype(F32)
             s += 1
     right = jnp.transpose(right_scr[...]).astype(BF16)
-    left = left_scr[...][:, :depth].astype(BF16)
+    left = pltpu.roll(left_scr[...], width - where_ref[2] * depth, 1)[:, :depth].astype(BF16)
     w_scr[...] = w_ref[...].astype(F32)
     for d in range(depth):
         part = w_scr[pl.ds(d, depth, stride=depth), :].astype(BF16)
@@ -424,7 +500,7 @@
 def outer_update(where, groups, w, rows, chans):
     total = sum(group.shape[0] for group in groups)
     width = groups[0].shape[2]
-    depth = int(round(w.shape[0] ** 0.5))
+    depth = groups[0].shape[1] - rows
     return pl.pallas_call(
         outer_kernel,
         out_shape=jax.ShapeDtypeStruct((rows, width, chans), F32),
@@ -462,35 +538,47 @@
     pairwise_down_weight,
 ):
     rows, _, chans = pairwise_input.shape
-    near = 4
-    planes = n_rows // near
+    near = 8
+    halves = n_rows // near
+    places = near // 2
+    per = chans // (n_branch * near)
     r = lax.axis_index("rows")
-    where = jnp.stack([lax.axis_index("branch"), r // near, r % near]).astype(jnp.int32)
-
-    sent = operands(pairwise_input, triangle_projection_weight, n_branch * n_rows)
+    where = jnp.stack([lax.axis_index("branch"), r, r // near * 2 + r % 2]).astype(jnp.int32)
+
+    sent = right_operand(
+        pairwise_input, triangle_projection_weight, n_branch, n_branch * n_rows, per
+    )
     received = lax.all_to_all(sent, AXES, 0, 0, tiled=True)
 
-    fresh, pieces = msa(
+    other = swap(pairwise_input, n_branch, n_rows, 1)
+    fresh, pieces = beside(
         where,
+        pairwise_input,
+        other,
+        triangle_projection_weight,
         homolog_features,
         transition_expand_matrix,
         transition_contract_matrix,
         factor_pair_matrices,
         n_branch,
-        planes,
+        near,
     )
     moved = [
-        piece if t == 0 else swap(piece, n_branch, n_rows, t // planes * n_rows + t % planes * near)
+        piece if t == 0 else swap(piece, n_branch, n_rows, t // places * n_rows + t % places * 2)
         for t, piece in enumerate(pieces)
     ]
-    mine = jnp.stack(moved)
-    beside = swap(mine, n_branch, n_rows, 2)
-    groups = [mine, beside, swap(mine, n_branch, n_rows, 1), swap(beside, n_branch, n_rows, 1)]
+    groups = [jnp.stack([piece[per * 2 * rows :] for piece in moved])]
+    for mask in [1] + [near << k for k in range(halves.bit_length() - 1)]:
+        groups += [swap(group, n_branch, n_rows, mask) for group in groups]
     outer = outer_update(where, groups, outer_output_weight, rows, chans)
     gate = output_gate(pairwise_input, triangle_projection_weight)
 
-    product = triangle_product(received, n_branch)
-    returned = lax.all_to_all(product, AXES, 0, 0, tiled=True)
+    product = triangle_product(where, received, moved, n_branch, near)
+    members = [
+        [b * n_rows + h * near + k for b in range(n_branch) for k in range(near)]
+        for h in range(halves)
+    ]
+    returned = lax.all_to_all(product, AXES, 0, 0, axis_index_groups=members, tiled=True)
     pairwise_output = pair_output(
         returned,
         pairwise_input,
@@ -505,18 +593,18 @@
 
 def on_device(n_branch, n_rows, homolog_features, pairwise_input, *weights):
     rows, width, chans = pairwise_input.shape
-    devices = n_branch * n_rows
-    planes = n_rows // 4
+    near = 8
+    halves = n_rows // near
     fits = (
         homolog_features.shape[0] == 1
-        and n_branch & (n_branch - 1) == 0
-        and n_rows % 4 == 0
-        and n_rows & (n_rows - 1) == 0
-        and chans % devices == 0
-        and rows % 16 == 0
+        and n_branch == 2
+        and n_rows % near == 0
+        and halves & (halves - 1) == 0
+        and chans % (n_branch * near) == 0
+        and rows == 16
         and width == 128
-        and homolog_features.shape[1] // planes == 4 * rows
-        and devices * chans * rows * width <= 2**25
+        and homolog_features.shape[1] == n_rows * rows == n_branch * width
+        and halves * weights[2].shape[1] == width
     )
     if fits:
         return own_channels_device(n_branch, n_rows, homolog_features, pairwise_input, *weights)

time: 70.9 us -> 68.6 us (0.968)
  the two profiles are of different devices: /device:TPU:0 before, /device:TPU:8 now
where the time goes in v2:
time: 68.6 us; the launch traced here: 68.1 us
  starting transfers between devices  24.4 us (36%)
  waiting for transfers between devices  21.8 us (32%)
  Pallas kernels  16.9 us (25%)
  local copies, waits for them, and re-layouts  3.98 us (6%)
  between operations  0.86 us (1%)
    ppermute x11, waiting for transfers between devices, swap(): return lax.ppermute(x, AXES, [(d, d ^ mask) for d in range(count)])  21.8 us
    ppermute x11, starting transfers between devices, swap(): return lax.ppermute(x, AXES, [(d, d ^ mask) for d in range(count)])  13.7 us
    all_to_all x1, starting transfers between devices, own_channels_device(): received = lax.all_to_all(sent, AXES, 0, 0, tiled=True)  6.05 us
    pallas_call x1, Pallas kernels, pair_output(): pl.pallas_call(pair_output_kernel, out_shape=jax.ShapeDtypeStruct(x.shape...  4.86 us
    all_to_all x1, starting transfers between devices, own_channels_device(): lax.all_to_all(product, AXES, 0, 0, axis_index_groups=members, tiled=True)  4.63 us
    unnamed x40, local copies, waits for them, and re-layouts  3.97 us
    pallas_call x1, Pallas kernels, beside(): pl.pallas_call(functools.partial(beside_kernel, n_branch, near), out_shap...  3.52 us
    pallas_call x1, Pallas kernels, outer_update(): pl.pallas_call(outer_kernel, out_shape=jax.ShapeDtypeStruct((rows, width,...  2.87 us
  transfers between devices with their start and end apart: 13, of which 7 were waited for; matrix products, arithmetic and copies ran while one was open for 0% of the time, Pallas kernels for 12%

profile of v2, /device:TPU:8, one launch (start us, length us, event | category | flops | bytes accessed | tf_op | source)
XLA Modules:
  0.0 68.1 jit_solution(6217919195705410517)
XLA Ops:
  0.6 1.0 %copy-done = bf16[16,128,128]{2,1,0:T(8,128)(2,1)S(1)} copy-done((bf16[16,128,128]{2,1,0:T(8,128)(2,1)S(1)}, bf16[16,128,128]{2,1,0:T(8,128)(2,1)}, u32[]{:S(2)}) %copy-start) | copy-done | bytes 524312
  1.7 0.9 %copy-done.2 = bf16[128,640]{1,0:T(8,128)(2,1)S(1)} copy-done((bf16[128,640]{1,0:T(8,128)(2,1)S(1)}, bf16[128,640]{1,0:T(8,128)(2,1)}, u32[]{:S(2)}) %copy-start.2) | copy-done | bytes 163864
  2.6 2.4 %right_operand.1 = bf16[32,8,16,128]{3,2,1,0:T(8,128)(2,1)} custom-call(bf16[16,128,128]{2,1,0:T(8,128)(2,1)S(1)} %copy-done, bf16[128,640]{1,0:T(8,128)(2,1)S(1)} %copy-done.2), custom_call_target="tpu_custom_call" | custom-call | flops 134217728 | bytes 1572864 | tf_op jit(solution)/shard_map/right_operand/pallas_call | solution.py:267
  5.1 6.1 %all-to-all-start = ((bf16[32,8,16,128]{3,2,1,0:T(8,128)(2,1)}), bf16[32,8,16,128]{3,2,1,0:T(8,128)(2,1)S(1)}, u32[]{:S(2)}, u32[]{:S(2)}) async-start(bf16[32,8,16,128]{3,2,1,0:T(8,128)(2,1)} %right_operand.1), calls=%async_computation | async-start | bytes 2097152 | tf_op jit(solution)/shard_map/all_to_all | solution.py:551
  11.2 0.2 collective-permute-start
  11.4 0.1 copy.12.factor_ref
  11.5 0.1 pad_add_fusion.where_ref
  11.6 1.6 %collective-permute-done.other_ref = bf16[16,128,128]{2,1,0:T(8,128)(2,1)S(1)} collective-permute-done((bf16[16,128,128]{2,1,0:T(8,128)(2,1)S(1)}, bf16[16,128,128]{2,1,0:T(8,128)(2,1)S(1)}, u32[]{:S(2)}, u32[]{:S(2)}) %collective-permute-start) | collective-permute-done | bytes 524320 | tf_op jit(solution)/shard_map/ppermute | solution.py:523
  13.2 3.5 %left_operand_and_msa.1 = (bf16[1,256,256]{2,1,0:T(8,128)(2,1)}, bf16[304,128]{1,0:T(8,128)(2,1)S(1)}, bf16[304,128]{1,0:T(8,128)(2,1)S(1)}, bf16[304,128]{1,0:T...) custom-call(s32[3]{0:T(128)S(1)} %pad_add_fusion.where_ref, ...), custom_call_target="tpu_custom_call" | custom-call | flops 536870912 | bytes 1048576 | tf_op jit(solution)/shard_map/left_operand_and_msa/pallas_call | solution.py:350
  16.7 1.5 %collective-permute-start.1 = (bf16[304,128]{1,0:T(8,128)(2,1)S(1)}, bf16[304,128]{1,0:T(8,128)(2,1)S(1)}, u32[]{:S(2)}, u32[]{:S(2)}) collective-permute-start(bf16[304,128]{1,0:T(8,128)(2,1)S(1)} %get-tuple-element.13), channel_id=1, source_target_pairs={{0,2},{1,3},{2,0},{3,1},{4,6},{5,7},{6,4},{7,5},{8,10},{9,11},{10,... | collective-permute-start | bytes 233480 | tf_op jit(solution)/shard_map/ppermute | solution.py:523
  18.1 0.6 collective-permute-start.2
  18.7 1.5 %collective-permute-start.3 = (bf16[304,128]{1,0:T(8,128)(2,1)S(1)}, bf16[304,128]{1,0:T(8,128)(2,1)S(1)}, u32[]{:S(2)}, u32[]{:S(2)}) collective-permute-start(bf16[304,128]{1,0:T(8,128)(2,1)S(1)} %get-tuple-element.15), channel_id=1, source_target_pairs={{0,6},{1,7},{2,4},{3,5},{4,2},{5,3},{6,0},{7,1},{8,14},{9,15},{10,... | collective-permute-start | bytes 233480 | tf_op jit(solution)/shard_map/ppermute | solution.py:523
  20.2 1.5 %collective-permute-start.4 = (bf16[304,128]{1,0:T(8,128)(2,1)S(1)}, bf16[304,128]{1,0:T(8,128)(2,1)S(1)}, u32[]{:S(2)}, u32[]{:S(2)}) collective-permute-start(bf16[304,128]{1,0:T(8,128)(2,1)S(1)} %get-tuple-element.16), channel_id=1, source_target_pairs={{0,16},{1,17},{2,18},{3,19},{4,20},{5,21},{6,22},{7,23},{8,24},{9,... | collective-permute-start | bytes 233480 | tf_op jit(solution)/shard_map/ppermute | solution.py:523
  21.6 1.5 %collective-permute-start.5 = (bf16[304,128]{1,0:T(8,128)(2,1)S(1)}, bf16[304,128]{1,0:T(8,128)(2,1)S(1)}, u32[]{:S(2)}, u32[]{:S(2)}) collective-permute-start(bf16[304,128]{1,0:T(8,128)(2,1)S(1)} %get-tuple-element.17), channel_id=1, source_target_pairs={{0,18},{1,19},{2,16},{3,17},{4,22},{5,23},{6,20},{7,21},{8,26},{9,... | collective-permute-start | bytes 233480 | tf_op jit(solution)/shard_map/ppermute | solution.py:523
  23.1 1.6 %collective-permute-start.6 = (bf16[304,128]{1,0:T(8,128)(2,1)S(1)}, bf16[304,128]{1,0:T(8,128)(2,1)S(1)}, u32[]{:S(2)}, u32[]{:S(2)}) collective-permute-start(bf16[304,128]{1,0:T(8,128)(2,1)S(1)} %get-tuple-element.18), channel_id=1, source_target_pairs={{0,20},{1,21},{2,22},{3,23},{4,16},{5,17},{6,18},{7,19},{8,28},{9,... | collective-permute-start | bytes 233480 | tf_op jit(solution)/shard_map/ppermute | solution.py:523
  24.7 6.9 %collective-permute-done.2.rest_2_ = bf16[304,128]{1,0:T(8,128)(2,1)S(1)} collective-permute-done((bf16[304,128]{1,0:T(8,128)(2,1)S(1)}, bf16[304,128]{1,0:T(8,128)(2,1)S(1)}, u32[]{:S(2)}, u32[]{:S(2)}) %collective-permute-start.2) | collective-permute-done | bytes 77856 | tf_op jit(solution)/shard_map/ppermute | solution.py:523
  31.6 1.6 %collective-permute-start.7 = (bf16[304,128]{1,0:T(8,128)(2,1)S(1)}, bf16[304,128]{1,0:T(8,128)(2,1)S(1)}, u32[]{:S(2)}, u32[]{:S(2)}) collective-permute-start(bf16[304,128]{1,0:T(8,128)(2,1)S(1)} %get-tuple-element.19), channel_id=1, source_target_pairs={{0,22},{1,23},{2,20},{3,21},{4,18},{5,19},{6,16},{7,17},{8,30},{9,... | collective-permute-start | bytes 233480 | tf_op jit(solution)/shard_map/ppermute | solution.py:523
  33.3 1.2 %collective-permute-done.3.rest_3_ = bf16[304,128]{1,0:T(8,128)(2,1)S(1)} collective-permute-done((bf16[304,128]{1,0:T(8,128)(2,1)S(1)}, bf16[304,128]{1,0:T(8,128)(2,1)S(1)}, u32[]{:S(2)}, u32[]{:S(2)}) %collective-permute-start.3) | collective-permute-done | bytes 77856 | tf_op jit(solution)/shard_map/ppermute | solution.py:523
  34.5 1.9 %collective-permute-done.6.rest_6_ = bf16[304,128]{1,0:T(8,128)(2,1)S(1)} collective-permute-done((bf16[304,128]{1,0:T(8,128)(2,1)S(1)}, bf16[304,128]{1,0:T(8,128)(2,1)S(1)}, u32[]{:S(2)}, u32[]{:S(2)}) %collective-permute-start.6) | collective-permute-done | bytes 77856 | tf_op jit(solution)/shard_map/ppermute | solution.py:523
  36.4 2.2 %collective-permute-done.7.rest_7_ = bf16[304,128]{1,0:T(8,128)(2,1)S(1)} collective-permute-done((bf16[304,128]{1,0:T(8,128)(2,1)S(1)}, bf16[304,128]{1,0:T(8,128)(2,1)S(1)}, u32[]{:S(2)}, u32[]{:S(2)}) %collective-permute-start.7) | collective-permute-done | bytes 77856 | tf_op jit(solution)/shard_map/ppermute | solution.py:523
  38.6 0.9 %copy-done.10 = bf16[304,128]{1,0:T(8,128)(2,1)S(1)} copy-done((bf16[304,128]{1,0:T(8,128)(2,1)S(1)}, bf16[304,128]{1,0:T(8,128)(2,1)}, u32[]{:S(2)}) %copy-start.10) | copy-done | bytes 77848
  39.5 1.8 %triangle_product.1 = bf16[16,8,16,128]{3,2,1,0:T(8,128)(2,1)} custom-call(s32[3]{0:T(128)S(1)} %pad_add_fusion.where_ref, bf16[32,8,16,128]{3,2,1,0:T(8,128)(2,1)S(1)} %all-to-all-done.in_ref, bf16[304,128]{1,0:T(8,128)(2,1)S(1)} %copy-done.10, bf16[304,128]{1,0:T(8,128)(2,1)S(1)} %collective-permute-done.1.rest_1_, ...), custom_call_target="tpu_custom_call" | custom-call | flops 134217728 | bytes 2097152 | tf_op jit(solution)/shard_map/triangle_product/pallas_call | solution.py:423
  41.3 4.6 %all-to-all-start.1 = ((bf16[16,8,16,128]{3,2,1,0:T(8,128)(2,1)}), bf16[16,8,16,128]{3,2,1,0:T(8,128)(2,1)S(1)}, u32[]{:S(2)}, u32[]{:S(2)}) async-start(bf16[16,8,16,128]{3,2,1,0:T(8,128)(2,1)} %triangle_product.1), calls=%async_computation.1 | async-start | bytes 1048576 | tf_op jit(solution)/shard_map/all_to_all | solution.py:581
  46.0 0.2 collective-permute-start.8
  46.2 2.5 %collective-permute-start.9 = (bf16[8,48,128]{2,1,0:T(8,128)(2,1)S(1)}, bf16[8,48,128]{2,1,0:T(8,128)(2,1)S(1)}, u32[]{:S(2)}, u32[]{:S(2)}) collective-permute-start(bf16[8,48,128]{2,1,0:T(8,128)(2,1)S(1)} %constant_dynamic-update-slice_fusion.refs_0_), channel_id=1, source_target_pairs={{0,8},{1,9},{2,10},{3,11},{4,12},{5,13},{6,14},{7,15},{8,0},{9,1},... | collective-permute-start | bytes 294920 | tf_op jit(solution)/shard_map/ppermute | solution.py:523
  48.7 1.1 %collective-permute-start.10 = (bf16[8,48,128]{2,1,0:T(8,128)(2,1)S(1)}, bf16[8,48,128]{2,1,0:T(8,128)(2,1)S(1)}, u32[]{:S(2)}, u32[]{:S(2)}) collective-permute-start(bf16[8,48,128]{2,1,0:T(8,128)(2,1)S(1)} %collective-permute-done.8.refs_1_), channel_id=1, source_target_pairs={{0,8},{1,9},{2,10},{3,11},{4,12},{5,13},{6,14},{7,15},{8,0},{9,1},... | collective-permute-start | bytes 294920 | tf_op jit(solution)/shard_map/ppermute | solution.py:523
  49.9 1.5 %triangle_output_gate.1.gate_ref = f32[16,128,128]{2,1,0:T(8,128)S(1)} custom-call(bf16[16,128,128]{2,1,0:T(8,128)(2,1)S(1)} %copy-done.1, bf16[128,640]{1,0:T(8,128)(2,1)S(1)} %copy-done.3), custom_call_target="tpu_custom_call" | custom-call | flops 67108864 | bytes 1572864 | tf_op jit(solution)/shard_map/triangle_output_gate/pallas_call | solution.py:379
  51.4 6.4 %collective-permute-done.9.refs_2_ = bf16[8,48,128]{2,1,0:T(8,128)(2,1)S(1)} collective-permute-done((bf16[8,48,128]{2,1,0:T(8,128)(2,1)S(1)}, bf16[8,48,128]{2,1,0:T(8,128)(2,1)S(1)}, u32[]{:S(2)}, u32[]{:S(2)}) %collective-permute-start.9) | collective-permute-done | bytes 98336 | tf_op jit(solution)/shard_map/ppermute | solution.py:523
  57.8 1.6 %collective-permute-done.10.refs_3_ = bf16[8,48,128]{2,1,0:T(8,128)(2,1)S(1)} collective-permute-done((bf16[8,48,128]{2,1,0:T(8,128)(2,1)S(1)}, bf16[8,48,128]{2,1,0:T(8,128)(2,1)S(1)}, u32[]{:S(2)}, u32[]{:S(2)}) %collective-permute-start.10) | collective-permute-done | bytes 98336 | tf_op jit(solution)/shard_map/ppermute | solution.py:523
  59.5 0.9 %copy-done.13 = bf16[8,48,128]{2,1,0:T(8,128)(2,1)S(1)} copy-done((bf16[8,48,128]{2,1,0:T(8,128)(2,1)S(1)}, bf16[8,48,128]{2,1,0:T(8,128)(2,1)}, u32[]{:S(2)}) %copy-start.13) | copy-done | bytes 98328
  60.4 2.9 %outer_product_mean.1.outer_ref = f32[16,128,128]{2,1,0:T(8,128)S(1)} custom-call(s32[3]{0:T(128)S(1)} %pad_add_fusion.where_ref, bf16[8,48,128]{2,1,0:T(8,128)(2,1)S(1)} %copy-done.13, bf16[8,48,128]{2,1,0:T(8,128)(2,1)S(1)} %collective-permute-done.8.refs_1_, bf16[8,48,128]{2,1,0:T(8,128)(2,1)S(1)} %collective-permute-done.9.refs_2_, ...), custom_call_target="tpu_custom_call" | custom-call | flops 1073741824 | bytes 1048576 | tf_op jit(solution)/shard_map/outer_product_mean/pallas_call | solution.py:504
  63.3 4.9 %pair_output.1 = bf16[16,128,128]{2,1,0:T(8,128)(2,1)} custom-call(bf16[16,8,16,128]{3,2,1,0:T(8,128)(2,1)S(1)} %all-to-all-done.1.p_ref, bf16[16,128,128]{2,1,0:T(8,128)(2,1)S(1)} %copy-done.1, f32[16,128,128]{2,1,0:T(8,128)S(1)} %triangle_output_gate.1.gate_ref, f32[16,128,128]{2,1,0:T(8,128)S(1)} %outer_product_mean.1.outer_ref, ...), custom_call_target="tpu_custom_call" | custom-call | flops 603979776 | bytes 3670016 | tf_op jit(solution)/shard_map/pair_output/pallas_call | solution.py:462
  (42 shorter events, 0.2 us)
Async XLA Ops:
  0.6 1.0 %copy-start = (bf16[16,128,128]{2,1,0:T(8,128)(2,1)S(1)}, bf16[16,128,128]{2,1,0:T(8,128)(2,1)}, u32[]{:S(2)}) copy-start(bf16[16,128,128]{2,1,0:T(8,128)(2,1)} %x_ref.5) | copy-start | bytes 1572868
  1.7 0.9 %copy-start.2 = (bf16[128,640]{1,0:T(8,128)(2,1)S(1)}, bf16[128,640]{1,0:T(8,128)(2,1)}, u32[]{:S(2)}) copy-start(bf16[128,640]{1,0:T(8,128)(2,1)} %w_ref.4) | copy-start | bytes 491524
  5.0 6.1 %copy-start.1 = (bf16[16,128,128]{2,1,0:T(8,128)(2,1)S(1)}, bf16[16,128,128]{2,1,0:T(8,128)(2,1)}, u32[]{:S(2)}) copy-start(bf16[16,128,128]{2,1,0:T(8,128)(2,1)} %x_ref.5) | copy-start | bytes 1572868
  5.0 6.3 %copy-start.15 = (bf16[256,64]{0,1:T(8,128)(2,1)S(1)}, bf16[256,64]{0,1:T(8,128)(2,1)}, u32[]{:S(2)}) copy-start(bf16[256,64]{0,1:T(8,128)(2,1)} %param.14) | copy-start | bytes 98308
  5.0 8.1 %copy-start.4 = (bf16[256,1024]{1,0:T(8,128)(2,1)S(1)}, bf16[256,1024]{1,0:T(8,128)(2,1)}, u32[]{:S(2)}) copy-start(bf16[256,1024]{1,0:T(8,128)(2,1)} %up_ref.2) | copy-start | bytes 1572868
  5.0 8.1 %copy-start.5 = (bf16[1024,256]{1,0:T(8,128)(2,1)S(1)}, bf16[1024,256]{1,0:T(8,128)(2,1)}, u32[]{:S(2)}) copy-start(bf16[1024,256]{1,0:T(8,128)(2,1)} %down_ref.2) | copy-start | bytes 1572868
  5.1 8.1 %copy-start.8 = (bf16[1,256,256]{2,1,0:T(8,128)(2,1)S(1)}, bf16[1,256,256]{2,1,0:T(8,128)(2,1)}, u32[]{:S(2)}) copy-start(bf16[1,256,256]{2,1,0:T(8,128)(2,1)} %seq_ref.1) | copy-start | bytes 393220
  5.1 33.5 %all-to-all-start = ((bf16[32,8,16,128]{3,2,1,0:T(8,128)(2,1)}), bf16[32,8,16,128]{3,2,1,0:T(8,128)(2,1)S(1)}, u32[]{:S(2)}, u32[]{:S(2)}) async-start(bf16[32,8,16,128]{3,2,1,0:T(8,128)(2,1)} %right_operand.1), calls=%async_computation | async-start | bytes 2097152 | tf_op jit(solution)/shard_map/all_to_all | solution.py:551
  11.1 2.0 %copy-start.3 = (bf16[128,640]{1,0:T(8,128)(2,1)S(1)}, bf16[128,640]{1,0:T(8,128)(2,1)}, u32[]{:S(2)}) copy-start(bf16[128,640]{1,0:T(8,128)(2,1)} %w_ref.4) | copy-start | bytes 491524
  11.2 2.0 %collective-permute-start = (bf16[16,128,128]{2,1,0:T(8,128)(2,1)S(1)}, bf16[16,128,128]{2,1,0:T(8,128)(2,1)S(1)}, u32[]{:S(2)}, u32[]{:S(2)}) collective-permute-start(bf16[16,128,128]{2,1,0:T(8,128)(2,1)S(1)} %copy-done.1), channel_id=1, source_target_pairs={{0,1},{1,0},{2,3},{3,2},{4,5},{5,4},{6,7},{7,6},{8,9},{9,8},{10,11... | collective-permute-start | bytes 1572872 | tf_op jit(solution)/shard_map/ppermute | solution.py:523
  16.7 19.7 %copy-start.9 = (bf16[304,128]{1,0:T(8,128)(2,1)}, bf16[304,128]{1,0:T(8,128)(2,1)S(1)}, u32[]{:S(2)}) copy-start(bf16[304,128]{1,0:T(8,128)(2,1)S(1)} %get-tuple-element.12.rest_0_) | copy-start | bytes 233476
  16.7 6.4 %collective-permute-start.1 = (bf16[304,128]{1,0:T(8,128)(2,1)S(1)}, bf16[304,128]{1,0:T(8,128)(2,1)S(1)}, u32[]{:S(2)}, u32[]{:S(2)}) collective-permute-start(bf16[304,128]{1,0:T(8,128)(2,1)S(1)} %get-tuple-element.13), channel_id=1, source_target_pairs={{0,2},{1,3},{2,0},{3,1},{4,6},{5,7},{6,4},{7,5},{8,10},{9,11},{10,... | collective-permute-start | bytes 233480 | tf_op jit(solution)/shard_map/ppermute | solution.py:523
  18.1 13.5 %collective-permute-start.2 = (bf16[304,128]{1,0:T(8,128)(2,1)S(1)}, bf16[304,128]{1,0:T(8,128)(2,1)S(1)}, u32[]{:S(2)}, u32[]{:S(2)}) collective-permute-start(bf16[304,128]{1,0:T(8,128)(2,1)S(1)} %get-tuple-element.14), channel_id=1, source_target_pairs={{0,4},{1,5},{2,6},{3,7},{4,0},{5,1},{6,2},{7,3},{8,12},{9,13},{10,... | collective-permute-start | bytes 233480 | tf_op jit(solution)/shard_map/ppermute | solution.py:523
  18.7 15.8 %collective-permute-start.3 = (bf16[304,128]{1,0:T(8,128)(2,1)S(1)}, bf16[304,128]{1,0:T(8,128)(2,1)S(1)}, u32[]{:S(2)}, u32[]{:S(2)}) collective-permute-start(bf16[304,128]{1,0:T(8,128)(2,1)S(1)} %get-tuple-element.15), channel_id=1, source_target_pairs={{0,6},{1,7},{2,4},{3,5},{4,2},{5,3},{6,0},{7,1},{8,14},{9,15},{10,... | collective-permute-start | bytes 233480 | tf_op jit(solution)/shard_map/ppermute | solution.py:523
  20.2 14.3 %collective-permute-start.4 = (bf16[304,128]{1,0:T(8,128)(2,1)S(1)}, bf16[304,128]{1,0:T(8,128)(2,1)S(1)}, u32[]{:S(2)}, u32[]{:S(2)}) collective-permute-start(bf16[304,128]{1,0:T(8,128)(2,1)S(1)} %get-tuple-element.16), channel_id=1, source_target_pairs={{0,16},{1,17},{2,18},{3,19},{4,20},{5,21},{6,22},{7,23},{8,24},{9,... | collective-permute-start | bytes 233480 | tf_op jit(solution)/shard_map/ppermute | solution.py:523
  21.6 12.9 %collective-permute-start.5 = (bf16[304,128]{1,0:T(8,128)(2,1)S(1)}, bf16[304,128]{1,0:T(8,128)(2,1)S(1)}, u32[]{:S(2)}, u32[]{:S(2)}) collective-permute-start(bf16[304,128]{1,0:T(8,128)(2,1)S(1)} %get-tuple-element.17), channel_id=1, source_target_pairs={{0,18},{1,19},{2,16},{3,17},{4,22},{5,23},{6,20},{7,21},{8,26},{9,... | collective-permute-start | bytes 233480 | tf_op jit(solution)/shard_map/ppermute | solution.py:523
  23.1 13.3 %collective-permute-start.6 = (bf16[304,128]{1,0:T(8,128)(2,1)S(1)}, bf16[304,128]{1,0:T(8,128)(2,1)S(1)}, u32[]{:S(2)}, u32[]{:S(2)}) collective-permute-start(bf16[304,128]{1,0:T(8,128)(2,1)S(1)} %get-tuple-element.18), channel_id=1, source_target_pairs={{0,20},{1,21},{2,22},{3,23},{4,16},{5,17},{6,18},{7,19},{8,28},{9,... | collective-permute-start | bytes 233480 | tf_op jit(solution)/shard_map/ppermute | solution.py:523
  31.6 7.0 %collective-permute-start.7 = (bf16[304,128]{1,0:T(8,128)(2,1)S(1)}, bf16[304,128]{1,0:T(8,128)(2,1)S(1)}, u32[]{:S(2)}, u32[]{:S(2)}) collective-permute-start(bf16[304,128]{1,0:T(8,128)(2,1)S(1)} %get-tuple-element.19), channel_id=1, source_target_pairs={{0,22},{1,23},{2,20},{3,21},{4,18},{5,19},{6,16},{7,17},{8,30},{9,... | collective-permute-start | bytes 233480 | tf_op jit(solution)/shard_map/ppermute | solution.py:523
  38.6 0.9 %copy-start.10 = (bf16[304,128]{1,0:T(8,128)(2,1)S(1)}, bf16[304,128]{1,0:T(8,128)(2,1)}, u32[]{:S(2)}) copy-start(bf16[304,128]{1,0:T(8,128)(2,1)} %copy-done.9) | copy-start | bytes 233476
  41.3 21.9 %all-to-all-start.1 = ((bf16[16,8,16,128]{3,2,1,0:T(8,128)(2,1)}), bf16[16,8,16,128]{3,2,1,0:T(8,128)(2,1)S(1)}, u32[]{:S(2)}, u32[]{:S(2)}) async-start(bf16[16,8,16,128]{3,2,1,0:T(8,128)(2,1)} %triangle_product.1), calls=%async_computation.1 | async-start | bytes 1048576 | tf_op jit(solution)/shard_map/all_to_all | solution.py:581
  46.0 5.4 %copy-start.12 = (bf16[8,48,128]{2,1,0:T(8,128)(2,1)}, bf16[8,48,128]{2,1,0:T(8,128)(2,1)S(1)}, u32[]{:S(2)}) copy-start(bf16[8,48,128]{2,1,0:T(8,128)(2,1)S(1)} %constant_dynamic-update-slice_fusion.refs_0_) | copy-start | bytes 294916
  46.0 13.5 %copy-start.14 = (bf16[1024,128]{1,0:T(8,128)(2,1)S(1)}, bf16[1024,128]{1,0:T(8,128)(2,1)}, u32[]{:S(2)}) copy-start(bf16[1024,128]{1,0:T(8,128)(2,1)} %refs_4_.1) | copy-start | bytes 786436
  46.0 2.7 %collective-permute-start.8 = (bf16[8,48,128]{2,1,0:T(8,128)(2,1)S(1)}, bf16[8,48,128]{2,1,0:T(8,128)(2,1)S(1)}, u32[]{:S(2)}, u32[]{:S(2)}) collective-permute-start(bf16[8,48,128]{2,1,0:T(8,128)(2,1)S(1)} %constant_dynamic-update-slice_fusion.refs_0_), channel_id=1, source_target_pairs={{0,1},{1,0},{2,3},{3,2},{4,5},{5,4},{6,7},{7,6},{8,9},{9,8},{10,11... | collective-permute-start | bytes 294920 | tf_op jit(solution)/shard_map/ppermute | solution.py:523
  46.2 11.6 %collective-permute-start.9 = (bf16[8,48,128]{2,1,0:T(8,128)(2,1)S(1)}, bf16[8,48,128]{2,1,0:T(8,128)(2,1)S(1)}, u32[]{:S(2)}, u32[]{:S(2)}) collective-permute-start(bf16[8,48,128]{2,1,0:T(8,128)(2,1)S(1)} %constant_dynamic-update-slice_fusion.refs_0_), channel_id=1, source_target_pairs={{0,8},{1,9},{2,10},{3,11},{4,12},{5,13},{6,14},{7,15},{8,0},{9,1},... | collective-permute-start | bytes 294920 | tf_op jit(solution)/shard_map/ppermute | solution.py:523
  48.7 10.7 %collective-permute-start.10 = (bf16[8,48,128]{2,1,0:T(8,128)(2,1)S(1)}, bf16[8,48,128]{2,1,0:T(8,128)(2,1)S(1)}, u32[]{:S(2)}, u32[]{:S(2)}) collective-permute-start(bf16[8,48,128]{2,1,0:T(8,128)(2,1)S(1)} %collective-permute-done.8.refs_1_), channel_id=1, source_target_pairs={{0,8},{1,9},{2,10},{3,11},{4,12},{5,13},{6,14},{7,15},{8,0},{9,1},... | collective-permute-start | bytes 294920 | tf_op jit(solution)/shard_map/ppermute | solution.py:523
  51.4 11.9 %copy-start.6 = (bf16[128,512]{1,0:T(8,128)(2,1)S(1)}, bf16[128,512]{1,0:T(8,128)(2,1)}, u32[]{:S(2)}) copy-start(bf16[128,512]{1,0:T(8,128)(2,1)} %up_ref.3) | copy-start | bytes 393220
  51.4 11.9 %copy-start.7 = (bf16[512,128]{1,0:T(8,128)(2,1)S(1)}, bf16[512,128]{1,0:T(8,128)(2,1)}, u32[]{:S(2)}) copy-start(bf16[512,128]{1,0:T(8,128)(2,1)} %down_ref.3) | copy-start | bytes 393220
  51.4 11.9 %copy-start.11 = (bf16[128,128]{1,0:T(8,128)(2,1)S(1)}, bf16[128,128]{1,0:T(8,128)(2,1)}, u32[]{:S(2)}) copy-start(bf16[128,128]{1,0:T(8,128)(2,1)} %w_ref.5) | copy-start | bytes 98308
  59.5 0.9 %copy-start.13 = (bf16[8,48,128]{2,1,0:T(8,128)(2,1)S(1)}, bf16[8,48,128]{2,1,0:T(8,128)(2,1)}, u32[]{:S(2)}) copy-start(bf16[8,48,128]{2,1,0:T(8,128)(2,1)} %copy-done.12) | copy-start | bytes 294916

commit v3 on v2

--- a/solution.py
+++ b/solution.py
@@ -14,6 +14,7 @@
 TN = (((0,), (0,)), ((), ()))
 VMEM = pl.BlockSpec(memory_space=pltpu.VMEM)
 SMEM = pl.BlockSpec(memory_space=pltpu.SMEM)
+HBM = pl.BlockSpec(memory_space=pltpu.HBM)
 PARAMS = pltpu.CompilerParams(vmem_limit_bytes=48 * 1024 * 1024)
 
 def standardize_features(values, dimension):
@@ -233,20 +234,12 @@
         store(i + 1, result[:, width:])
 
 
-def right_kernel(n_branch, x_hbm, w_hbm, out_ref, x_ref, w_ref, scr, sems):
+def right_kernel(n_branch, x_ref, w_ref, out_ref, scr):
     rows, _, chans = x_ref.shape
     devices, per = out_ref.shape[:2]
     groups = chans // per
     near = groups // n_branch
     halves = devices // groups
-    copies = [
-        pltpu.make_async_copy(w_hbm, w_ref, sems.at[0]),
-        pltpu.make_async_copy(x_hbm, x_ref, sems.at[1]),
-    ]
-    for copy in copies:
-        copy.start()
-    for copy in copies:
-        copy.wait()
     source = lax.broadcasted_iota(jnp.int32, (chans, chans), 0)
     values, gates = channel_order(w_ref[...], (2, 3), source, chans)
 
@@ -263,39 +256,32 @@
 
 def right_operand(x, w, n_branch, devices, per):
     rows, width, chans = x.shape
-    hbm = pl.BlockSpec(memory_space=pl.ANY)
     return pl.pallas_call(
         functools.partial(right_kernel, n_branch),
         out_shape=jax.ShapeDtypeStruct((devices, per, rows, width), BF16),
-        in_specs=[hbm, hbm],
+        in_specs=[VMEM, VMEM],
         out_specs=VMEM,
-        scratch_shapes=[
-            pltpu.VMEM(x.shape, BF16),
-            pltpu.VMEM(w.shape, BF16),
-            pltpu.VMEM((chans * rows, width), F32),
-            pltpu.SemaphoreType.DMA((2,)),
-        ],
+        scratch_shapes=[pltpu.VMEM((chans * rows, width), F32)],
         compiler_params=PARAMS,
         cost_estimate=cost(2 * rows * width * chans * 2 * chans, 3 * rows * width * chans * 2),
         name="right_operand",
     )(x, w)
 
 
-def beside_kernel(
-    n_branch, near, where_ref, x_ref, other_ref, w_ref, seq_ref, up_ref, down_ref, factor_ref,
-    fresh_ref, *rest
+def msa_kernel(
+    n_branch, near, x_hbm, up_hbm, down_hbm, factor_ref, fresh_ref, right_ref, left_ref,
+    x_ref, up_ref, down_ref, sems
 ):
-    out_refs, (scr, right_scr, left_scr) = rest[:-3], rest[-3:]
-    rows, width, chans = x_ref.shape
-    branch, row_at = where_ref[0], where_ref[1]
-    core = lax.bitwise_and(row_at, 1)
-    place = lax.shift_right_logical(lax.bitwise_and(row_at, near - 1), 1)
-    count = len(out_refs)
-    places = count // n_branch
-    per = chans // (n_branch * near)
-
-    x = seq_ref[0].astype(F32)
-    hidden = jnp.maximum(dot(normed(x, -1), up_ref[...]), 0.0).astype(BF16)
+    pairs = [(x_hbm, x_ref), (up_hbm, up_ref), (down_hbm, down_ref)]
+    copies = [pltpu.make_async_copy(a, b, sems.at[k]) for k, (a, b) in enumerate(pairs)]
+    for copy in copies:
+        copy.start()
+    copies[0].wait()
+    x = x_ref[0].astype(F32)
+    tokens = normed(x, -1)
+    copies[1].wait()
+    hidden = jnp.maximum(dot(tokens, up_ref[...]), 0.0).astype(BF16)
+    copies[2].wait()
     fresh = (x + dot(hidden, down_ref[...])).astype(BF16)
     fresh_ref[0] = fresh
     tokens = normed(fresh.astype(F32), -1)
@@ -303,13 +289,55 @@
     depth = factor.shape[1] // 2
     left = dot(tokens, factor[:, :depth]).astype(BF16)
     right = dot(factor[:, depth:], tokens, (((0,), (1,)), ((), ()))).astype(BF16)
+    width = right_ref.shape[2]
     for b in range(n_branch):
-        right_scr[b] = right[:, b * width : (b + 1) * width]
-    tiles = left.reshape(-1, places, 2, rows, depth)
-    for t in range(places):
-        left_scr[t] = jnp.concatenate(
-            [tiles[h, t, c] for h in range(tiles.shape[0]) for c in range(2)], axis=1
-        )
+        right_ref[b] = right[:, b * width : (b + 1) * width]
+    halves, places, rows, _ = left_ref.shape
+    tiles = left.reshape(halves, places, 2, rows, depth)
+    blank = jnp.zeros((rows, width - 2 * depth), BF16)
+    for h in range(halves):
+        for t in range(places):
+            left_ref[h, t] = jnp.concatenate([tiles[h, t, 0], tiles[h, t, 1], blank], axis=1)
+
+
+def msa(x, up, down, factor, n_branch, near, halves, rows):
+    _, length, feats = x.shape
+    depth = factor.shape[1] // 2
+    width = length // n_branch
+    return pl.pallas_call(
+        functools.partial(msa_kernel, n_branch, near),
+        out_shape=[
+            jax.ShapeDtypeStruct(x.shape, BF16),
+            jax.ShapeDtypeStruct((n_branch, depth, width), BF16),
+            jax.ShapeDtypeStruct((halves, near // 2, rows, width), BF16),
+        ],
+        in_specs=[HBM] * 3 + [VMEM],
+        out_specs=[VMEM] * 3,
+        scratch_shapes=[
+            pltpu.VMEM(x.shape, BF16),
+            pltpu.VMEM(up.shape, BF16),
+            pltpu.VMEM(down.shape, BF16),
+            pltpu.SemaphoreType.DMA((3,)),
+        ],
+        compiler_params=PARAMS,
+        cost_estimate=cost(4 * length * feats * up.shape[1], 4 * feats * up.shape[1]),
+        name="msa_transition",
+    )(x, up, down, factor)
+
+
+def beside_kernel(
+    n_branch, near, where_ref, x_ref, other_ref, w_ref, right_ref, left_ref, far_right_ref,
+    far_left_ref, *rest
+):
+    out_refs, scr = rest[:-1], rest[-1]
+    rows, _, chans = x_ref.shape
+    branch, row_at = where_ref[0], where_ref[1]
+    core = lax.bitwise_and(row_at, 1)
+    place = lax.shift_right_logical(lax.bitwise_and(row_at, near - 1), 1)
+    half = row_at // near
+    count = len(out_refs)
+    places = count // n_branch
+    per = chans // (n_branch * near)
 
     total = count * per
     q = lax.broadcasted_iota(jnp.int32, (total, chans), 0)
@@ -327,6 +355,8 @@
 
     gated_rows(values, gates, x_ref, store_at(core))
     gated_rows(values, gates, other_ref, store_at(1 - core))
+    depth = right_ref.shape[1]
+    base = per * 2 * rows
     for t, out_ref in enumerate(out_refs):
         for c in range(per):
             for k in range(2):
@@ -334,36 +364,31 @@
                 out_ref[pl.ds((c * 2 + k) * rows, rows)] = scr[k, start : start + rows, :].astype(
                     BF16
                 )
-        base = per * 2 * rows
-        out_ref[base : base + depth] = right_scr[lax.bitwise_xor(branch, t // places)]
-        out_ref[base + depth :] = left_scr[lax.bitwise_xor(place, t % places)]
-
-
-def beside(where, x, other, w, seq, up, down, factor, n_branch, near):
+        b = lax.bitwise_xor(branch, t // places)
+        p = lax.bitwise_xor(place, t % places)
+        out_ref[base : base + depth] = right_ref[b]
+        out_ref[base + depth : base + 2 * depth] = far_right_ref[b]
+        out_ref[base + 2 * depth :] = jnp.concatenate(
+            [left_ref[half, p][:, : 2 * depth], far_left_ref[half, p][:, : 2 * depth]], axis=1
+        )
+
+
+def beside(where, x, other, w, sides, far_sides, n_branch, near):
     rows, width, chans = x.shape
-    _, length, feats = seq.shape
-    depth = factor.shape[1] // 2
-    places = near // 2
-    count = n_branch * places
+    depth = sides[0].shape[1]
+    count = n_branch * near // 2
     per = chans // (n_branch * near)
-    piece = jax.ShapeDtypeStruct((per * 2 * rows + depth + rows, width), BF16)
-    fresh, *pieces = pl.pallas_call(
+    piece = jax.ShapeDtypeStruct((per * 2 * rows + 2 * depth + rows, width), BF16)
+    return pl.pallas_call(
         functools.partial(beside_kernel, n_branch, near),
-        out_shape=[jax.ShapeDtypeStruct(seq.shape, BF16)] + [piece] * count,
+        out_shape=[piece] * count,
         in_specs=[SMEM] + [VMEM] * 7,
-        out_specs=[VMEM] * (1 + count),
-        scratch_shapes=[
-            pltpu.VMEM((2, count * per * rows, width), F32),
-            pltpu.VMEM((n_branch, depth, width), BF16),
-            pltpu.VMEM((places, rows, width), BF16),
-        ],
+        out_specs=[VMEM] * count,
+        scratch_shapes=[pltpu.VMEM((2, count * per * rows, width), F32)],
         compiler_params=PARAMS,
-        cost_estimate=cost(
-            4 * length * feats * up.shape[1] + 4 * x.size * 2 * chans, 4 * feats * up.shape[1]
-        ),
-        name="left_operand_and_msa",
-    )(where, x, other, w, seq, up, down, factor)
-    return fresh, pieces
+        cost_estimate=cost(4 * x.size * 2 * chans, x.size * 8),
+        name="left_operand",
+    )(where, x, other, w, *sides, *far_sides)
 
 
 def gate_kernel(x_ref, w_ref, out_ref):
@@ -474,16 +499,25 @@
 def outer_kernel(where_ref, *refs):
     groups, (w_ref, out_ref, right_scr, left_scr, w_scr, m_scr) = refs[:-6], refs[-6:]
     rows, width, chans = out_ref.shape
-    total = sum(ref.shape[0] for ref in groups)
+    total = 2 * sum(ref.shape[0] for ref in groups)
     depth = m_scr.shape[1] // total
     s = 0
     for ref in groups:
         for k in range(ref.shape[0]):
-            right_scr[pl.ds(s, depth, stride=total), :] = ref[k, :depth].astype(F32)
-            left_scr[pl.ds(s, rows, stride=total), :] = ref[k, depth:].astype(F32)
+            both = ref[k, 2 * depth :].astype(F32)
+            for far in range(2):
+                at = s + far * (total // 2)
+                side = ref[k, far * depth : (far + 1) * depth].astype(F32)
+                right_scr[pl.ds(at, depth, stride=total), :] = side
+                left_scr[pl.ds(at, rows, stride=total), :] = both
             s += 1
     right = jnp.transpose(right_scr[...]).astype(BF16)
-    left = pltpu.roll(left_scr[...], width - where_ref[2] * depth, 1)[:, :depth].astype(BF16)
+    both = left_scr[...]
+    shift = lax.bitwise_and(where_ref[1], 1) * depth
+    first = pltpu.roll(both, width - shift, 1)[:, :depth]
+    second = pltpu.roll(both, width - 2 * depth - shift, 1)[:, :depth]
+    row = lax.broadcasted_iota(jnp.int32, first.shape, 0)
+    left = jnp.where(row % total < total // 2, first, second).astype(BF16)
     w_scr[...] = w_ref[...].astype(F32)
     for d in range(depth):
         part = w_scr[pl.ds(d, depth, stride=depth), :].astype(BF16)
@@ -498,9 +532,9 @@
 
 
 def outer_update(where, groups, w, rows, chans):
-    total = sum(group.shape[0] for group in groups)
+    total = 2 * sum(group.shape[0] for group in groups)
     width = groups[0].shape[2]
-    depth = groups[0].shape[1] - rows
+    depth = (groups[0].shape[1] - rows) // 2
     return pl.pallas_call(
         outer_kernel,
         out_shape=jax.ShapeDtypeStruct((rows, width, chans), F32),
@@ -542,34 +576,35 @@
     halves = n_rows // near
     places = near // 2
     per = chans // (n_branch * near)
-    r = lax.axis_index("rows")
-    where = jnp.stack([lax.axis_index("branch"), r, r // near * 2 + r % 2]).astype(jnp.int32)
-
-    sent = right_operand(
-        pairwise_input, triangle_projection_weight, n_branch, n_branch * n_rows, per
-    )
-    received = lax.all_to_all(sent, AXES, 0, 0, tiled=True)
-
-    other = swap(pairwise_input, n_branch, n_rows, 1)
-    fresh, pieces = beside(
-        where,
-        pairwise_input,
-        other,
-        triangle_projection_weight,
+    where = jnp.stack([lax.axis_index("branch"), lax.axis_index("rows")]).astype(jnp.int32)
+
+    fresh, *sides = msa(
         homolog_features,
         transition_expand_matrix,
         transition_contract_matrix,
         factor_pair_matrices,
         n_branch,
         near,
+        halves,
+        rows,
+    )
+    pairwise_input, sides = lax.optimization_barrier((pairwise_input, sides))
+    far_sides = [swap(side, n_branch, n_rows, near) for side in sides]
+    sent = right_operand(
+        pairwise_input, triangle_projection_weight, n_branch, n_branch * n_rows, per
+    )
+    received = lax.all_to_all(sent, AXES, 0, 0, tiled=True)
+
+    other = swap(pairwise_input, n_branch, n_rows, 1)
+    pieces = beside(
+        where, pairwise_input, other, triangle_projection_weight, sides, far_sides, n_branch, near
     )
     moved = [
         piece if t == 0 else swap(piece, n_branch, n_rows, t // places * n_rows + t % places * 2)
         for t, piece in enumerate(pieces)
     ]
-    groups = [jnp.stack([piece[per * 2 * rows :] for piece in moved])]
-    for mask in [1] + [near << k for k in range(halves.bit_length() - 1)]:
-        groups += [swap(group, n_branch, n_rows, mask) for group in groups]
+    mine = jnp.stack([piece[per * 2 * rows :] for piece in moved])
+    groups = [mine, swap(mine, n_branch, n_rows, 1)]
     outer = outer_update(where, groups, outer_output_weight, rows, chans)
     gate = output_gate(pairwise_input, triangle_projection_weight)
 
@@ -597,14 +632,14 @@
     halves = n_rows // near
     fits = (
         homolog_features.shape[0] == 1
+        and halves == 2
         and n_branch == 2
         and n_rows % near == 0
-        and halves & (halves - 1) == 0
         and chans % (n_branch * near) == 0
         and rows == 16
         and width == 128
         and homolog_features.shape[1] == n_rows * rows == n_branch * width
-        and halves * weights[2].shape[1] == width
+        and 2 * weights[2].shape[1] == width
     )
     if fits:
         return own_channels_device(n_branch, n_rows, homolog_features, pairwise_input, *weights)

time: 68.6 us -> 82.4 us (1.20)
  the two profiles are of different devices: /device:TPU:8 before, /device:TPU:0 now
where the time goes in v3:
time: 82.4 us; the launch traced here: 81.9 us
  waiting for transfers between devices  33.9 us (41%)
  starting transfers between devices  23.9 us (29%)
  Pallas kernels  18.2 us (22%)
  local copies, waits for them, and re-layouts  4.95 us (6%)
    ppermute x11, waiting for transfers between devices, swap(): return lax.ppermute(x, AXES, [(d, d ^ mask) for d in range(count)])  29.3 us
    ppermute x11, starting transfers between devices, swap(): return lax.ppermute(x, AXES, [(d, d ^ mask) for d in range(count)])  13.1 us
    all_to_all x1, starting transfers between devices, own_channels_device(): received = lax.all_to_all(sent, AXES, 0, 0, tiled=True)  7.3 us
    unnamed x30, local copies, waits for them, and re-layouts  4.94 us
    pallas_call x1, Pallas kernels, pair_output(): pl.pallas_call(pair_output_kernel, out_shape=jax.ShapeDtypeStruct(x.shape...  4.85 us
    all_to_all x1, waiting for transfers between devices, own_channels_device(): lax.all_to_all(product, AXES, 0, 0, axis_index_groups=members, tiled=True)  4.62 us
    all_to_all x1, starting transfers between devices, own_channels_device(): lax.all_to_all(product, AXES, 0, 0, axis_index_groups=members, tiled=True)  3.57 us
    pallas_call x1, Pallas kernels, outer_update(): pl.pallas_call(outer_kernel, out_shape=jax.ShapeDtypeStruct((rows, width,...  2.91 us
  transfers between devices with their start and end apart: 13, of which 6 were waited for; matrix products, arithmetic and copies ran while one was open for 0% of the time, Pallas kernels for 9%

profile of v3, /device:TPU:0, one launch (start us, length us, event | category | flops | bytes accessed | tf_op | source)
XLA Modules:
  0.0 81.9 jit_solution(16272026233690960059)
XLA Ops:
  0.6 0.9 %copy.12.factor_ref = bf16[256,64]{1,0:T(8,128)(2,1)S(1)} copy(bf16[256,64]{0,1:T(8,128)(2,1)} %param.14) | data formatting | bytes 65536 | tf_op args[4]
  1.5 0.0 copy-start.2
  1.5 1.0 %copy-done.2 = bf16[256,1024]{1,0:T(8,128)(2,1)S(1)} copy-done((bf16[256,1024]{1,0:T(8,128)(2,1)S(1)}, bf16[256,1024]{1,0:T(8,128)(2,1)}, u32[]{:S(2)}) %copy-start.2) | copy-done | bytes 524312
  2.6 1.0 %copy-done.3 = bf16[1024,256]{1,0:T(8,128)(2,1)S(1)} copy-done((bf16[1024,256]{1,0:T(8,128)(2,1)S(1)}, bf16[1024,256]{1,0:T(8,128)(2,1)}, u32[]{:S(2)}) %copy-start.3) | copy-done | bytes 524312
  3.6 0.9 %copy-done.4 = bf16[1,256,256]{2,1,0:T(8,128)(2,1)S(1)} copy-done((bf16[1,256,256]{2,1,0:T(8,128)(2,1)S(1)}, bf16[1,256,256]{2,1,0:T(8,128)(2,1)}, u32[]{:S(2)}) %copy-start.4) | copy-done | bytes 131096
  4.5 2.2 %msa_transition.1 = (bf16[1,256,256]{2,1,0:T(8,128)(2,1)}, bf16[2,32,128]{2,1,0:T(8,128)(2,1)S(1)}, bf16[2,4,16,128]{3,2,1,0:T(8,128)(2,1)S(1)}) custom-call(bf16[1,256,256]{2,1,0:T(8,128)(2,1)S(1)} %copy-done.4, bf16[256,1024]{1,0:T(8,128)(2,1)S(1)} %copy-done.2, bf16[1024,256]{1,0:T(8,128)(2,1)S(1)} %copy-done.3, bf16[256,64]{1,0:T(8,128)(2,1)S(1)} %copy.12.factor_ref), custom_call_target="tpu_custom_call" | custom-call | flops 268435456 | bytes 1048576 | tf_op jit(solution)/shard_map/msa_transition/pallas_call | solution.py:307
  6.7 2.2 %right_operand.1 = bf16[32,8,16,128]{3,2,1,0:T(8,128)(2,1)} custom-call(bf16[16,128,128]{2,1,0:T(8,128)(2,1)S(1)} %copy-done, bf16[128,640]{1,0:T(8,128)(2,1)S(1)} %copy-done.1), custom_call_target="tpu_custom_call" | custom-call | flops 134217728 | bytes 1572864 | tf_op jit(solution)/shard_map/right_operand/pallas_call | solution.py:259
  9.0 7.3 %all-to-all-start = ((bf16[32,8,16,128]{3,2,1,0:T(8,128)(2,1)}), bf16[32,8,16,128]{3,2,1,0:T(8,128)(2,1)S(1)}, u32[]{:S(2)}, u32[]{:S(2)}) async-start(bf16[32,8,16,128]{3,2,1,0:T(8,128)(2,1)} %right_operand.1), calls=%async_computation | async-start | bytes 2097152 | tf_op jit(solution)/shard_map/all_to_all | solution.py:596
  16.3 0.3 collective-permute-start
  16.6 2.6 %collective-permute-start.1 = (bf16[2,32,128]{2,1,0:T(8,128)(2,1)S(1)}, bf16[2,32,128]{2,1,0:T(8,128)(2,1)S(1)}, u32[]{:S(2)}, u32[]{:S(2)}) collective-permute-start(bf16[2,32,128]{2,1,0:T(8,128)(2,1)S(1)} %get-tuple-element.20.right_ref), channel_id=1, source_target_pairs={{0,8},{1,9},{2,10},{3,11},{4,12},{5,13},{6,14},{7,15},{8,0},{9,1},... | collective-permute-start | bytes 49160 | tf_op jit(solution)/shard_map/ppermute | solution.py:557
  19.2 0.3 collective-permute-start.2
  19.5 0.1 pad_add_fusion.where_ref
  19.6 24.7 %collective-permute-done.1.far_right_ref = bf16[2,32,128]{2,1,0:T(8,128)(2,1)S(1)} collective-permute-done((bf16[2,32,128]{2,1,0:T(8,128)(2,1)S(1)}, bf16[2,32,128]{2,1,0:T(8,128)(2,1)S(1)}, u32[]{:S(2)}, u32[]{:S(2)}) %collective-permute-start.1) | collective-permute-done | bytes 16416 | tf_op jit(solution)/shard_map/ppermute | solution.py:557
  44.3 0.4 collective-permute-done.2.far_left_ref
  44.7 2.7 %left_operand.1 = (bf16[336,128]{1,0:T(8,128)(2,1)S(1)}, bf16[336,128]{1,0:T(8,128)(2,1)S(1)}, bf16[336,128]{1,0:T(8,128)(2,1)S(1)}, bf16[336,128]{1,0:T(8,128)(...) custom-call(s32[2]{0:T(128)S(1)} %pad_add_fusion.where_ref, ...), custom_call_target="tpu_custom_call" | custom-call | flops 268435456 | bytes 2097152 | tf_op jit(solution)/shard_map/left_operand/pallas_call | solution.py:382
  47.4 1.5 %collective-permute-start.3 = (bf16[336,128]{1,0:T(8,128)(2,1)S(1)}, bf16[336,128]{1,0:T(8,128)(2,1)S(1)}, u32[]{:S(2)}, u32[]{:S(2)}) collective-permute-start(bf16[336,128]{1,0:T(8,128)(2,1)S(1)} %get-tuple-element.23), channel_id=1, source_target_pairs={{0,2},{1,3},{2,0},{3,1},{4,6},{5,7},{6,4},{7,5},{8,10},{9,11},{10,... | collective-permute-start | bytes 258056 | tf_op jit(solution)/shard_map/ppermute | solution.py:557
  48.9 2.1 %collective-permute-start.5 = (bf16[336,128]{1,0:T(8,128)(2,1)S(1)}, bf16[336,128]{1,0:T(8,128)(2,1)S(1)}, u32[]{:S(2)}, u32[]{:S(2)}) collective-permute-start(bf16[336,128]{1,0:T(8,128)(2,1)S(1)} %get-tuple-element.25), channel_id=1, source_target_pairs={{0,6},{1,7},{2,4},{3,5},{4,2},{5,3},{6,0},{7,1},{8,14},{9,15},{10,... | collective-permute-start | bytes 258056 | tf_op jit(solution)/shard_map/ppermute | solution.py:557
  51.0 1.5 %collective-permute-start.6 = (bf16[336,128]{1,0:T(8,128)(2,1)S(1)}, bf16[336,128]{1,0:T(8,128)(2,1)S(1)}, u32[]{:S(2)}, u32[]{:S(2)}) collective-permute-start(bf16[336,128]{1,0:T(8,128)(2,1)S(1)} %get-tuple-element.26), channel_id=1, source_target_pairs={{0,16},{1,17},{2,18},{3,19},{4,20},{5,21},{6,22},{7,23},{8,24},{9,... | collective-permute-start | bytes 258056 | tf_op jit(solution)/shard_map/ppermute | solution.py:557
  52.4 1.4 %collective-permute-start.7 = (bf16[336,128]{1,0:T(8,128)(2,1)S(1)}, bf16[336,128]{1,0:T(8,128)(2,1)S(1)}, u32[]{:S(2)}, u32[]{:S(2)}) collective-permute-start(bf16[336,128]{1,0:T(8,128)(2,1)S(1)} %get-tuple-element.27), channel_id=1, source_target_pairs={{0,18},{1,19},{2,16},{3,17},{4,22},{5,23},{6,20},{7,21},{8,26},{9,... | collective-permute-start | bytes 258056 | tf_op jit(solution)/shard_map/ppermute | solution.py:557
  53.8 0.9 %collective-permute-start.8 = (bf16[336,128]{1,0:T(8,128)(2,1)S(1)}, bf16[336,128]{1,0:T(8,128)(2,1)S(1)}, u32[]{:S(2)}, u32[]{:S(2)}) collective-permute-start(bf16[336,128]{1,0:T(8,128)(2,1)S(1)} %get-tuple-element.28), channel_id=1, source_target_pairs={{0,20},{1,21},{2,22},{3,23},{4,16},{5,17},{6,18},{7,19},{8,28},{9,... | collective-permute-start | bytes 258056 | tf_op jit(solution)/shard_map/ppermute | solution.py:557
  54.8 2.1 %collective-permute-start.9 = (bf16[336,128]{1,0:T(8,128)(2,1)S(1)}, bf16[336,128]{1,0:T(8,128)(2,1)S(1)}, u32[]{:S(2)}, u32[]{:S(2)}) collective-permute-start(bf16[336,128]{1,0:T(8,128)(2,1)S(1)} %get-tuple-element.29), channel_id=1, source_target_pairs={{0,22},{1,23},{2,20},{3,21},{4,18},{5,19},{6,16},{7,17},{8,30},{9,... | collective-permute-start | bytes 258056 | tf_op jit(solution)/shard_map/ppermute | solution.py:557
  56.9 2.9 %collective-permute-done.6.rest_4_ = bf16[336,128]{1,0:T(8,128)(2,1)S(1)} collective-permute-done((bf16[336,128]{1,0:T(8,128)(2,1)S(1)}, bf16[336,128]{1,0:T(8,128)(2,1)S(1)}, u32[]{:S(2)}, u32[]{:S(2)}) %collective-permute-start.6) | collective-permute-done | bytes 86048 | tf_op jit(solution)/shard_map/ppermute | solution.py:557
  59.8 0.2 collective-permute-done.8.rest_6_
  60.0 1.2 %collective-permute-done.9.rest_7_ = bf16[336,128]{1,0:T(8,128)(2,1)S(1)} collective-permute-done((bf16[336,128]{1,0:T(8,128)(2,1)S(1)}, bf16[336,128]{1,0:T(8,128)(2,1)S(1)}, u32[]{:S(2)}, u32[]{:S(2)}) %collective-permute-start.9) | collective-permute-done | bytes 86048 | tf_op jit(solution)/shard_map/ppermute | solution.py:557
  61.1 1.8 %triangle_product.1 = bf16[16,8,16,128]{3,2,1,0:T(8,128)(2,1)} custom-call(s32[2]{0:T(128)S(1)} %pad_add_fusion.where_ref, bf16[32,8,16,128]{3,2,1,0:T(8,128)(2,1)S(1)} %all-to-all-done.in_ref, bf16[336,128]{1,0:T(8,128)(2,1)S(1)} %get-tuple-element.22.rest_0_, bf16[336,128]{1,0:T(8,128)(2,1)S(1)} %collective-permute-done.3.rest_1_, ...), custom_call_target="tpu_custom_call" | custom-call | flops 134217728 | bytes 2097152 | tf_op jit(solution)/shard_map/triangle_product/pallas_call | solution.py:448
  63.0 3.6 %all-to-all-start.1 = ((bf16[16,8,16,128]{3,2,1,0:T(8,128)(2,1)}), bf16[16,8,16,128]{3,2,1,0:T(8,128)(2,1)S(1)}, u32[]{:S(2)}, u32[]{:S(2)}) async-start(bf16[16,8,16,128]{3,2,1,0:T(8,128)(2,1)} %triangle_product.1), calls=%async_computation.1 | async-start | bytes 1048576 | tf_op jit(solution)/shard_map/all_to_all | solution.py:616
  66.6 0.3 collective-permute-start.10
  67.0 1.5 %triangle_output_gate.1.gate_ref = f32[16,128,128]{2,1,0:T(8,128)S(1)} custom-call(bf16[16,128,128]{2,1,0:T(8,128)(2,1)S(1)} %copy-done, bf16[128,640]{1,0:T(8,128)(2,1)S(1)} %copy-done.1), custom_call_target="tpu_custom_call" | custom-call | flops 67108864 | bytes 1572864 | tf_op jit(solution)/shard_map/triangle_output_gate/pallas_call | solution.py:404
  68.5 1.0 %copy-done.9 = bf16[8,80,128]{2,1,0:T(8,128)(2,1)S(1)} copy-done((bf16[8,80,128]{2,1,0:T(8,128)(2,1)S(1)}, bf16[8,80,128]{2,1,0:T(8,128)(2,1)}, u32[]{:S(2)}) %copy-start.9) | copy-done | bytes 163864
  69.5 2.9 %outer_product_mean.1.outer_ref = f32[16,128,128]{2,1,0:T(8,128)S(1)} custom-call(s32[2]{0:T(128)S(1)} %pad_add_fusion.where_ref, bf16[8,80,128]{2,1,0:T(8,128)(2,1)S(1)} %copy-done.9, bf16[8,80,128]{2,1,0:T(8,128)(2,1)S(1)} %collective-permute-done.10.refs_1_, bf16[1024,128]{1,0:T(8,128)(2,1)S(1)} %copy-done.10), custom_call_target="tpu_custom_call" | custom-call | flops 1073741824 | bytes 1048576 | tf_op jit(solution)/shard_map/outer_product_mean/pallas_call | solution.py:538
  72.4 4.6 %all-to-all-done.1.p_ref = bf16[16,8,16,128]{3,2,1,0:T(8,128)(2,1)S(1)} async-done(((bf16[16,8,16,128]{3,2,1,0:T(8,128)(2,1)}), bf16[16,8,16,128]{3,2,1,0:T(8,128)(2,1)S(1)}, u32[]{:S(2)}, u32[]{:S(2)}) %all-to-all-start.1) | async-done | bytes 524320 | tf_op jit(solution)/shard_map/all_to_all | solution.py:616
  77.1 4.8 %pair_output.1 = bf16[16,128,128]{2,1,0:T(8,128)(2,1)} custom-call(bf16[16,8,16,128]{3,2,1,0:T(8,128)(2,1)S(1)} %all-to-all-done.1.p_ref, bf16[16,128,128]{2,1,0:T(8,128)(2,1)S(1)} %copy-done, f32[16,128,128]{2,1,0:T(8,128)S(1)} %triangle_output_gate.1.gate_ref, f32[16,128,128]{2,1,0:T(8,128)S(1)} %outer_product_mean.1.outer_ref, ...), custom_call_target="tpu_custom_call" | custom-call | flops 603979776 | bytes 3670016 | tf_op jit(solution)/shard_map/pair_output/pallas_call | solution.py:487
  (33 shorter events, 0.1 us)
Async XLA Ops:
  1.5 1.0 %copy-start.2 = (bf16[256,1024]{1,0:T(8,128)(2,1)S(1)}, bf16[256,1024]{1,0:T(8,128)(2,1)}, u32[]{:S(2)}) copy-start(bf16[256,1024]{1,0:T(8,128)(2,1)} %up_hbm.1) | copy-start | bytes 1572868
  2.6 1.0 %copy-start.3 = (bf16[1024,256]{1,0:T(8,128)(2,1)S(1)}, bf16[1024,256]{1,0:T(8,128)(2,1)}, u32[]{:S(2)}) copy-start(bf16[1024,256]{1,0:T(8,128)(2,1)} %down_hbm.1) | copy-start | bytes 1572868
  3.6 0.9 %copy-start.4 = (bf16[1,256,256]{2,1,0:T(8,128)(2,1)S(1)}, bf16[1,256,256]{2,1,0:T(8,128)(2,1)}, u32[]{:S(2)}) copy-start(bf16[1,256,256]{2,1,0:T(8,128)(2,1)} %x_hbm.1) | copy-start | bytes 393220
  4.5 2.2 %copy-start = (bf16[16,128,128]{2,1,0:T(8,128)(2,1)S(1)}, bf16[16,128,128]{2,1,0:T(8,128)(2,1)}, u32[]{:S(2)}) copy-start(bf16[16,128,128]{2,1,0:T(8,128)(2,1)} %x_ref.3) | copy-start | bytes 1572868
  4.5 2.2 %copy-start.1 = (bf16[128,640]{1,0:T(8,128)(2,1)S(1)}, bf16[128,640]{1,0:T(8,128)(2,1)}, u32[]{:S(2)}) copy-start(bf16[128,640]{1,0:T(8,128)(2,1)} %w_ref.6) | copy-start | bytes 491524
  9.0 52.2 %all-to-all-start = ((bf16[32,8,16,128]{3,2,1,0:T(8,128)(2,1)}), bf16[32,8,16,128]{3,2,1,0:T(8,128)(2,1)S(1)}, u32[]{:S(2)}, u32[]{:S(2)}) async-start(bf16[32,8,16,128]{3,2,1,0:T(8,128)(2,1)} %right_operand.1), calls=%async_computation | async-start | bytes 2097152 | tf_op jit(solution)/shard_map/all_to_all | solution.py:596
  16.3 28.4 %collective-permute-start = (bf16[16,128,128]{2,1,0:T(8,128)(2,1)S(1)}, bf16[16,128,128]{2,1,0:T(8,128)(2,1)S(1)}, u32[]{:S(2)}, u32[]{:S(2)}) collective-permute-start(bf16[16,128,128]{2,1,0:T(8,128)(2,1)S(1)} %copy-done), channel_id=1, source_target_pairs={{0,1},{1,0},{2,3},{3,2},{4,5},{5,4},{6,7},{7,6},{8,9},{9,8},{10,11... | collective-permute-start | bytes 1572872 | tf_op jit(solution)/shard_map/ppermute | solution.py:557
  16.6 27.7 %collective-permute-start.1 = (bf16[2,32,128]{2,1,0:T(8,128)(2,1)S(1)}, bf16[2,32,128]{2,1,0:T(8,128)(2,1)S(1)}, u32[]{:S(2)}, u32[]{:S(2)}) collective-permute-start(bf16[2,32,128]{2,1,0:T(8,128)(2,1)S(1)} %get-tuple-element.20.right_ref), channel_id=1, source_target_pairs={{0,8},{1,9},{2,10},{3,11},{4,12},{5,13},{6,14},{7,15},{8,0},{9,1},... | collective-permute-start | bytes 49160 | tf_op jit(solution)/shard_map/ppermute | solution.py:557
  19.2 25.5 %collective-permute-start.2 = (bf16[2,4,16,128]{3,2,1,0:T(8,128)(2,1)S(1)}, bf16[2,4,16,128]{3,2,1,0:T(8,128)(2,1)S(1)}, u32[]{:S(2)}, u32[]{:S(2)}) collective-permute-start(bf16[2,4,16,128]{3,2,1,0:T(8,128)(2,1)S(1)} %get-tuple-element.21.left_ref), channel_id=1, source_target_pairs={{0,8},{1,9},{2,10},{3,11},{4,12},{5,13},{6,14},{7,15},{8,0},{9,1},... | collective-permute-start | bytes 98312 | tf_op jit(solution)/shard_map/ppermute | solution.py:557
  47.4 6.4 %collective-permute-start.3 = (bf16[336,128]{1,0:T(8,128)(2,1)S(1)}, bf16[336,128]{1,0:T(8,128)(2,1)S(1)}, u32[]{:S(2)}, u32[]{:S(2)}) collective-permute-start(bf16[336,128]{1,0:T(8,128)(2,1)S(1)} %get-tuple-element.23), channel_id=1, source_target_pairs={{0,2},{1,3},{2,0},{3,1},{4,6},{5,7},{6,4},{7,5},{8,10},{9,11},{10,... | collective-permute-start | bytes 258056 | tf_op jit(solution)/shard_map/ppermute | solution.py:557
  48.9 5.9 %collective-permute-start.4 = (bf16[336,128]{1,0:T(8,128)(2,1)S(1)}, bf16[336,128]{1,0:T(8,128)(2,1)S(1)}, u32[]{:S(2)}, u32[]{:S(2)}) collective-permute-start(bf16[336,128]{1,0:T(8,128)(2,1)S(1)} %get-tuple-element.24), channel_id=1, source_target_pairs={{0,4},{1,5},{2,6},{3,7},{4,0},{5,1},{6,2},{7,3},{8,12},{9,13},{10,... | collective-permute-start | bytes 258056 | tf_op jit(solution)/shard_map/ppermute | solution.py:557
  48.9 8.0 %collective-permute-start.5 = (bf16[336,128]{1,0:T(8,128)(2,1)S(1)}, bf16[336,128]{1,0:T(8,128)(2,1)S(1)}, u32[]{:S(2)}, u32[]{:S(2)}) collective-permute-start(bf16[336,128]{1,0:T(8,128)(2,1)S(1)} %get-tuple-element.25), channel_id=1, source_target_pairs={{0,6},{1,7},{2,4},{3,5},{4,2},{5,3},{6,0},{7,1},{8,14},{9,15},{10,... | collective-permute-start | bytes 258056 | tf_op jit(solution)/shard_map/ppermute | solution.py:557
  51.0 8.8 %collective-permute-start.6 = (bf16[336,128]{1,0:T(8,128)(2,1)S(1)}, bf16[336,128]{1,0:T(8,128)(2,1)S(1)}, u32[]{:S(2)}, u32[]{:S(2)}) collective-permute-start(bf16[336,128]{1,0:T(8,128)(2,1)S(1)} %get-tuple-element.26), channel_id=1, source_target_pairs={{0,16},{1,17},{2,18},{3,19},{4,20},{5,21},{6,22},{7,23},{8,24},{9,... | collective-permute-start | bytes 258056 | tf_op jit(solution)/shard_map/ppermute | solution.py:557
  52.4 7.4 %collective-permute-start.7 = (bf16[336,128]{1,0:T(8,128)(2,1)S(1)}, bf16[336,128]{1,0:T(8,128)(2,1)S(1)}, u32[]{:S(2)}, u32[]{:S(2)}) collective-permute-start(bf16[336,128]{1,0:T(8,128)(2,1)S(1)} %get-tuple-element.27), channel_id=1, source_target_pairs={{0,18},{1,19},{2,16},{3,17},{4,22},{5,23},{6,20},{7,21},{8,26},{9,... | collective-permute-start | bytes 258056 | tf_op jit(solution)/shard_map/ppermute | solution.py:557
  53.8 6.1 %collective-permute-start.8 = (bf16[336,128]{1,0:T(8,128)(2,1)S(1)}, bf16[336,128]{1,0:T(8,128)(2,1)S(1)}, u32[]{:S(2)}, u32[]{:S(2)}) collective-permute-start(bf16[336,128]{1,0:T(8,128)(2,1)S(1)} %get-tuple-element.28), channel_id=1, source_target_pairs={{0,20},{1,21},{2,22},{3,23},{4,16},{5,17},{6,18},{7,19},{8,28},{9,... | collective-permute-start | bytes 258056 | tf_op jit(solution)/shard_map/ppermute | solution.py:557
  54.8 6.3 %collective-permute-start.9 = (bf16[336,128]{1,0:T(8,128)(2,1)S(1)}, bf16[336,128]{1,0:T(8,128)(2,1)S(1)}, u32[]{:S(2)}, u32[]{:S(2)}) collective-permute-start(bf16[336,128]{1,0:T(8,128)(2,1)S(1)} %get-tuple-element.29), channel_id=1, source_target_pairs={{0,22},{1,23},{2,20},{3,21},{4,18},{5,19},{6,16},{7,17},{8,30},{9,... | collective-permute-start | bytes 258056 | tf_op jit(solution)/shard_map/ppermute | solution.py:557
  63.0 14.1 %all-to-all-start.1 = ((bf16[16,8,16,128]{3,2,1,0:T(8,128)(2,1)}), bf16[16,8,16,128]{3,2,1,0:T(8,128)(2,1)S(1)}, u32[]{:S(2)}, u32[]{:S(2)}) async-start(bf16[16,8,16,128]{3,2,1,0:T(8,128)(2,1)} %triangle_product.1), calls=%async_computation.1 | async-start | bytes 1048576 | tf_op jit(solution)/shard_map/all_to_all | solution.py:616
  66.6 1.9 %copy-start.8 = (bf16[8,80,128]{2,1,0:T(8,128)(2,1)}, bf16[8,80,128]{2,1,0:T(8,128)(2,1)S(1)}, u32[]{:S(2)}) copy-start(bf16[8,80,128]{2,1,0:T(8,128)(2,1)S(1)} %fusion.refs_0_) | copy-start | bytes 491524
  66.6 1.9 %copy-start.10 = (bf16[1024,128]{1,0:T(8,128)(2,1)S(1)}, bf16[1024,128]{1,0:T(8,128)(2,1)}, u32[]{:S(2)}) copy-start(bf16[1024,128]{1,0:T(8,128)(2,1)} %refs_2_.1) | copy-start | bytes 786436
  66.6 1.9 %collective-permute-start.10 = (bf16[8,80,128]{2,1,0:T(8,128)(2,1)S(1)}, bf16[8,80,128]{2,1,0:T(8,128)(2,1)S(1)}, u32[]{:S(2)}, u32[]{:S(2)}) collective-permute-start(bf16[8,80,128]{2,1,0:T(8,128)(2,1)S(1)} %fusion.refs_0_), channel_id=1, source_target_pairs={{0,1},{1,0},{2,3},{3,2},{4,5},{5,4},{6,7},{7,6},{8,9},{9,8},{10,11... | collective-permute-start | bytes 491528 | tf_op jit(solution)/shard_map/ppermute | solution.py:557
  68.5 8.6 %copy-start.5 = (bf16[128,512]{1,0:T(8,128)(2,1)S(1)}, bf16[128,512]{1,0:T(8,128)(2,1)}, u32[]{:S(2)}) copy-start(bf16[128,512]{1,0:T(8,128)(2,1)} %up_ref.1) | copy-start | bytes 393220
  68.5 8.6 %copy-start.6 = (bf16[512,128]{1,0:T(8,128)(2,1)S(1)}, bf16[512,128]{1,0:T(8,128)(2,1)}, u32[]{:S(2)}) copy-start(bf16[512,128]{1,0:T(8,128)(2,1)} %down_ref.1) | copy-start | bytes 393220
  68.5 8.6 %copy-start.7 = (bf16[128,128]{1,0:T(8,128)(2,1)S(1)}, bf16[128,128]{1,0:T(8,128)(2,1)}, u32[]{:S(2)}) copy-start(bf16[128,128]{1,0:T(8,128)(2,1)} %w_ref.7) | copy-start | bytes 98308
  68.5 1.0 %copy-start.9 = (bf16[8,80,128]{2,1,0:T(8,128)(2,1)S(1)}, bf16[8,80,128]{2,1,0:T(8,128)(2,1)}, u32[]{:S(2)}) copy-start(bf16[8,80,128]{2,1,0:T(8,128)(2,1)} %copy-done.8) | copy-start | bytes 491524

commit v4 on v3

--- a/solution.py
+++ b/solution.py
@@ -14,6 +14,7 @@
 TN = (((0,), (0,)), ((), ()))
 VMEM = pl.BlockSpec(memory_space=pltpu.VMEM)
 SMEM = pl.BlockSpec(memory_space=pltpu.SMEM)
+TARGETS = (0, 1, 4, 7, 3, 6, 2, 5)
 HBM = pl.BlockSpec(memory_space=pltpu.HBM)
 PARAMS = pltpu.CompilerParams(vmem_limit_bytes=48 * 1024 * 1024)
 
@@ -228,25 +229,25 @@
 def gated_rows(values, gates, rows_ref, store):
     rows, width, chans = rows_ref.shape
     for i in range(0, rows, 2):
-        tokens = normed(rows_ref[i : i + 2].astype(F32).reshape(2 * width, chans), -1)
+        tokens = rows_ref[i : i + 2].reshape(2 * width, chans)
         result = dot(values, tokens, NT) * sigmoid(dot(gates, tokens, NT))
         store(i, result[:, :width])
         store(i + 1, result[:, width:])
 
 
-def right_kernel(n_branch, x_ref, w_ref, out_ref, scr):
-    rows, _, chans = x_ref.shape
+def fill_right(n_branch, tokens_ref, w, out_ref, scr):
+    rows, _, chans = tokens_ref.shape
     devices, per = out_ref.shape[:2]
     groups = chans // per
     near = groups // n_branch
     halves = devices // groups
-    source = lax.broadcasted_iota(jnp.int32, (chans, chans), 0)
-    values, gates = channel_order(w_ref[...], (2, 3), source, chans)
+    own = lax.broadcasted_iota(jnp.int32, (chans, chans), 0)
+    values, gates = channel_order(w, (2, 3), own, chans)
 
     def store(i, block):
         scr[pl.ds(i, chans, stride=rows), :] = block
 
-    gated_rows(values, gates, x_ref, store)
+    gated_rows(values, gates, tokens_ref, store)
     for q in range(chans):
         g, c = q // per, q % per
         block = scr[q * rows : (q + 1) * rows, :].astype(BF16)
@@ -254,30 +255,61 @@
             out_ref[(g // near * halves + h) * near + g % near, c] = block
 
 
+def right_kernel(
+    n_branch, x_hbm, w_hbm, sent_hbm, tokens_hbm, x_ref, w_ref, sent_ref, tokens_ref, scr, sems
+):
+    rows = x_ref.shape[0]
+    step = rows // 4
+    copies = [pltpu.make_async_copy(w_hbm, w_ref, sems.at[0])]
+    for k in range(4):
+        part = pl.ds(k * step, step)
+        copies.append(pltpu.make_async_copy(x_hbm.at[part], x_ref.at[part], sems.at[k + 1]))
+    for copy in copies:
+        copy.start()
+    for k in range(4):
+        copies[k + 1].wait()
+        part = slice(k * step, (k + 1) * step)
+        tokens_ref[part] = normed(x_ref[part].astype(F32), -1)
+    copies[0].wait()
+    keep = pltpu.make_async_copy(tokens_ref, tokens_hbm, sems.at[5])
+    keep.start()
+    fill_right(n_branch, tokens_ref, w_ref[...], sent_ref, scr)
+    send = pltpu.make_async_copy(sent_ref, sent_hbm, sems.at[6])
+    send.start()
+    keep.wait()
+    send.wait()
+
+
 def right_operand(x, w, n_branch, devices, per):
     rows, width, chans = x.shape
+    sent = jax.ShapeDtypeStruct((devices, per, rows, width), BF16)
     return pl.pallas_call(
         functools.partial(right_kernel, n_branch),
-        out_shape=jax.ShapeDtypeStruct((devices, per, rows, width), BF16),
-        in_specs=[VMEM, VMEM],
-        out_specs=VMEM,
-        scratch_shapes=[pltpu.VMEM((chans * rows, width), F32)],
-        compiler_params=PARAMS,
+        out_shape=[sent, jax.ShapeDtypeStruct(x.shape, BF16)],
+        in_specs=[HBM] * 2,
+        out_specs=[HBM] * 2,
+        scratch_shapes=[pltpu.VMEM(array.shape, BF16) for array in (x, w, sent, x)]
+        + [pltpu.VMEM((chans * rows, width), F32), pltpu.SemaphoreType.DMA((7,))],
         cost_estimate=cost(2 * rows * width * chans * 2 * chans, 3 * rows * width * chans * 2),
         name="right_operand",
     )(x, w)
 
 
 def msa_kernel(
-    n_branch, near, x_hbm, up_hbm, down_hbm, factor_ref, fresh_ref, right_ref, left_ref,
-    x_ref, up_ref, down_ref, sems
+    n_branch, rows, seq_hbm, up_hbm, down_hbm, factor_hbm, fresh_ref, sides_ref,
+    seq_ref, up_ref, down_ref, factor_ref, sems
 ):
-    pairs = [(x_hbm, x_ref), (up_hbm, up_ref), (down_hbm, down_ref)]
+    pairs = [
+        (seq_hbm, seq_ref),
+        (up_hbm, up_ref),
+        (down_hbm, down_ref),
+        (factor_hbm, factor_ref),
+    ]
     copies = [pltpu.make_async_copy(a, b, sems.at[k]) for k, (a, b) in enumerate(pairs)]
     for copy in copies:
         copy.start()
     copies[0].wait()
-    x = x_ref[0].astype(F32)
+    x = seq_ref[0].astype(F32)
     tokens = normed(x, -1)
     copies[1].wait()
     hidden = jnp.maximum(dot(tokens, up_ref[...]), 0.0).astype(BF16)
@@ -285,49 +317,45 @@
     fresh = (x + dot(hidden, down_ref[...])).astype(BF16)
     fresh_ref[0] = fresh
     tokens = normed(fresh.astype(F32), -1)
+    copies[3].wait()
     factor = factor_ref[...]
-    depth = factor.shape[1] // 2
-    left = dot(tokens, factor[:, :depth]).astype(BF16)
-    right = dot(factor[:, depth:], tokens, (((0,), (1,)), ((), ()))).astype(BF16)
-    width = right_ref.shape[2]
+    depth = factor.shape[0] // 2
+    left = dot(tokens, factor[:depth], NT).astype(BF16)
+    right = dot(factor[depth:], tokens, NT).astype(BF16)
+    width = sides_ref.shape[1]
     for b in range(n_branch):
-        right_ref[b] = right[:, b * width : (b + 1) * width]
-    halves, places, rows, _ = left_ref.shape
-    tiles = left.reshape(halves, places, 2, rows, depth)
+        sides_ref[b * depth : (b + 1) * depth] = right[:, b * width : (b + 1) * width]
+    tiles = left.reshape(-1, 2, rows, depth)
     blank = jnp.zeros((rows, width - 2 * depth), BF16)
-    for h in range(halves):
-        for t in range(places):
-            left_ref[h, t] = jnp.concatenate([tiles[h, t, 0], tiles[h, t, 1], blank], axis=1)
-
-
-def msa(x, up, down, factor, n_branch, near, halves, rows):
-    _, length, feats = x.shape
-    depth = factor.shape[1] // 2
-    width = length // n_branch
+    base = n_branch * depth
+    for t in range(tiles.shape[0]):
+        sides_ref[base + t * rows : base + (t + 1) * rows] = jnp.concatenate(
+            [tiles[t, 0], tiles[t, 1], blank], axis=1
+        )
+
+
+def msa(seq, up, down, factor, rows, width):
+    _, length, feats = seq.shape
+    depth = factor.shape[0] // 2
+    n_branch = length // width
+    operands = (seq, up, down, factor)
     return pl.pallas_call(
-        functools.partial(msa_kernel, n_branch, near),
+        functools.partial(msa_kernel, n_branch, rows),
         out_shape=[
-            jax.ShapeDtypeStruct(x.shape, BF16),
-            jax.ShapeDtypeStruct((n_branch, depth, width), BF16),
-            jax.ShapeDtypeStruct((halves, near // 2, rows, width), BF16),
+            jax.ShapeDtypeStruct(seq.shape, BF16),
+            jax.ShapeDtypeStruct((n_branch * depth + length // 2, width), BF16),
         ],
-        in_specs=[HBM] * 3 + [VMEM],
-        out_specs=[VMEM] * 3,
-        scratch_shapes=[
-            pltpu.VMEM(x.shape, BF16),
-            pltpu.VMEM(up.shape, BF16),
-            pltpu.VMEM(down.shape, BF16),
-            pltpu.SemaphoreType.DMA((3,)),
-        ],
-        compiler_params=PARAMS,
+        in_specs=[HBM] * 4,
+        out_specs=[VMEM] * 2,
+        scratch_shapes=[pltpu.VMEM(array.shape, BF16) for array in operands]
+        + [pltpu.SemaphoreType.DMA((4,))],
         cost_estimate=cost(4 * length * feats * up.shape[1], 4 * feats * up.shape[1]),
         name="msa_transition",
-    )(x, up, down, factor)
+    )(*operands)
 
 
 def beside_kernel(
-    n_branch, near, where_ref, x_ref, other_ref, w_ref, right_ref, left_ref, far_right_ref,
-    far_left_ref, *rest
+    n_branch, near, where_ref, x_ref, other_ref, w_ref, sides_ref, far_ref, *rest
 ):
     out_refs, scr = rest[:-1], rest[-1]
     rows, _, chans = x_ref.shape
@@ -355,9 +383,9 @@
 
     gated_rows(values, gates, x_ref, store_at(core))
     gated_rows(values, gates, other_ref, store_at(1 - core))
-    depth = right_ref.shape[1]
+    depth = (out_refs[0].shape[0] - per * 2 * rows - rows) // 2
     base = per * 2 * rows
-    for t, out_ref in enumerate(out_refs):
+    for t, out_ref in zip(TARGETS, out_refs):
         for c in range(per):
             for k in range(2):
                 start = (t * per + c) * rows
@@ -366,34 +394,36 @@
                 )
         b = lax.bitwise_xor(branch, t // places)
         p = lax.bitwise_xor(place, t % places)
-        out_ref[base : base + depth] = right_ref[b]
-        out_ref[base + depth : base + 2 * depth] = far_right_ref[b]
+        right = pl.ds(pl.multiple_of(b * depth, depth), depth)
+        start = n_branch * depth + (half * places + p) * rows
+        left = pl.ds(pl.multiple_of(start, rows), rows)
+        out_ref[base : base + depth] = sides_ref[right]
+        out_ref[base + depth : base + 2 * depth] = far_ref[right]
         out_ref[base + 2 * depth :] = jnp.concatenate(
-            [left_ref[half, p][:, : 2 * depth], far_left_ref[half, p][:, : 2 * depth]], axis=1
-        )
-
-
-def beside(where, x, other, w, sides, far_sides, n_branch, near):
+            [sides_ref[left][:, : 2 * depth], far_ref[left][:, : 2 * depth]], axis=1
+        )
+
+
+def beside(where, x, other, w, sides, far_sides, depth, n_branch, near):
     rows, width, chans = x.shape
-    depth = sides[0].shape[1]
     count = n_branch * near // 2
     per = chans // (n_branch * near)
     piece = jax.ShapeDtypeStruct((per * 2 * rows + 2 * depth + rows, width), BF16)
     return pl.pallas_call(
         functools.partial(beside_kernel, n_branch, near),
         out_shape=[piece] * count,
-        in_specs=[SMEM] + [VMEM] * 7,
+        in_specs=[SMEM] + [VMEM] * 5,
         out_specs=[VMEM] * count,
         scratch_shapes=[pltpu.VMEM((2, count * per * rows, width), F32)],
         compiler_params=PARAMS,
         cost_estimate=cost(4 * x.size * 2 * chans, x.size * 8),
         name="left_operand",
-    )(where, x, other, w, *sides, *far_sides)
+    )(where, x, other, w, sides, far_sides)
 
 
 def gate_kernel(x_ref, w_ref, out_ref):
     rows, width, chans = x_ref.shape
-    tokens = normed(x_ref[...].astype(F32).reshape(rows * width, chans), -1)
+    tokens = x_ref[...].reshape(rows * width, chans)
     out_ref[...] = sigmoid(dot(tokens, w_ref[:, 4 * chans :])).reshape(rows, width, chans)
 
 
@@ -420,7 +450,7 @@
     branch, row_at = where_ref[0], where_ref[1]
     place = lax.shift_right_logical(lax.bitwise_and(row_at, near - 1), 1)
     places = near // 2
-    for t, ref in enumerate(left_refs):
+    for t, ref in zip(TARGETS, left_refs):
         b = lax.bitwise_xor(branch, t // places)
         p = lax.bitwise_xor(place, t % places)
         for c in range(per):
@@ -578,35 +608,43 @@
     per = chans // (n_branch * near)
     where = jnp.stack([lax.axis_index("branch"), lax.axis_index("rows")]).astype(jnp.int32)
 
-    fresh, *sides = msa(
+    fresh, sides = msa(
         homolog_features,
         transition_expand_matrix,
         transition_contract_matrix,
-        factor_pair_matrices,
+        jnp.transpose(factor_pair_matrices),
+        rows,
+        pairwise_input.shape[1],
+    )
+    far_sides = swap(sides, n_branch, n_rows, near)
+    pairwise_input, _ = lax.optimization_barrier((pairwise_input, sides))
+    sent, tokens = right_operand(
+        pairwise_input, triangle_projection_weight, n_branch, n_branch * n_rows, per
+    )
+    sent, far_sides = lax.optimization_barrier((sent, far_sides))
+    received = lax.all_to_all(sent, AXES, 0, 0, tiled=True)
+
+    other = swap(tokens, n_branch, n_rows, 1)
+    pieces = beside(
+        where,
+        tokens,
+        other,
+        triangle_projection_weight,
+        sides,
+        far_sides,
+        factor_pair_matrices.shape[1] // 2,
         n_branch,
         near,
-        halves,
-        rows,
-    )
-    pairwise_input, sides = lax.optimization_barrier((pairwise_input, sides))
-    far_sides = [swap(side, n_branch, n_rows, near) for side in sides]
-    sent = right_operand(
-        pairwise_input, triangle_projection_weight, n_branch, n_branch * n_rows, per
-    )
-    received = lax.all_to_all(sent, AXES, 0, 0, tiled=True)
-
-    other = swap(pairwise_input, n_branch, n_rows, 1)
-    pieces = beside(
-        where, pairwise_input, other, triangle_projection_weight, sides, far_sides, n_branch, near
     )
     moved = [
         piece if t == 0 else swap(piece, n_branch, n_rows, t // places * n_rows + t % places * 2)
-        for t, piece in enumerate(pieces)
+        for t, piece in zip(TARGETS, pieces)
     ]
     mine = jnp.stack([piece[per * 2 * rows :] for piece in moved])
     groups = [mine, swap(mine, n_branch, n_rows, 1)]
     outer = outer_update(where, groups, outer_output_weight, rows, chans)
-    gate = output_gate(pairwise_input, triangle_projection_weight)
+    gate_tokens, _ = lax.optimization_barrier((tokens, moved[0]))
+    gate = output_gate(gate_tokens, triangle_projection_weight)
 
     product = triangle_product(where, received, moved, n_branch, near)
     members = [

time: 82.4 us -> 65.8 us (0.80)
  waiting for transfers between devices: 33.9 us -> 19.9 us
  local copies, waits for them, and re-layouts: 4.95 us -> 1.04 us
  starting transfers between devices: 23.9 us -> 24.9 us
    ppermute x11 -> x10, waiting for transfers between devices: 29.3 us -> 14.6 us  [swap(): return lax.ppermute(x, AXES, [(d, d ^ mask) for d in range(count)])]
    unnamed x30 -> x27, local copies, waits for them, and re-layouts: 4.94 us -> 1.03 us
    ppermute x11 -> x10, starting transfers between devices: 13.1 us -> 15.6 us  [swap(): return lax.ppermute(x, AXES, [(d, d ^ mask) for d in range(count)])]
    pallas_call x2, Pallas kernels: 4.43 us -> 6.82 us  [the longest x1 3.87 us: right_operand(): pl.pallas_call(functools.partial(right_kernel, n_branch), out_shape=[sent...]
    all_to_all x1, starting transfers between devices: 7.3 us -> 4.96 us  [own_channels_device(): received = lax.all_to_all(sent, AXES, 0, 0, tiled=True)]
    pallas_call x1, Pallas kernels: 2.75 us -> 1.64 us  [beside(): pl.pallas_call(functools.partial(beside_kernel, n_branch, near), out_shap...]
  transfers between devices with their start and end apart: 13 -> 12, of which waited for: 6 -> 8; matrix products, arithmetic and copies ran while one was open for 0% -> 0% of each run, Pallas kernels for 9% -> 14%
where the time goes in v4:
time: 65.8 us; the launch traced here: 65.5 us
  starting transfers between devices  24.9 us (38%)
  waiting for transfers between devices  19.9 us (30%)
  Pallas kernels  18.8 us (29%)
  local copies, waits for them, and re-layouts  1.04 us (2%)
  between operations  0.82 us (1%)
    ppermute x10, starting transfers between devices, swap(): return lax.ppermute(x, AXES, [(d, d ^ mask) for d in range(count)])  15.6 us
    ppermute x10, waiting for transfers between devices, swap(): return lax.ppermute(x, AXES, [(d, d ^ mask) for d in range(count)])  14.6 us
    all_to_all x1, waiting for transfers between devices, own_channels_device(): lax.all_to_all(product, AXES, 0, 0, axis_index_groups=members, tiled=True)  5.13 us
    all_to_all x1, starting transfers between devices, own_channels_device(): received = lax.all_to_all(sent, AXES, 0, 0, tiled=True)  4.96 us
    pallas_call x1, Pallas kernels, pair_output(): pl.pallas_call(pair_output_kernel, out_shape=jax.ShapeDtypeStruct(x.shape...  4.86 us
    all_to_all x1, starting transfers between devices, own_channels_device(): lax.all_to_all(product, AXES, 0, 0, axis_index_groups=members, tiled=True)  4.34 us
    pallas_call x1, Pallas kernels, right_operand(): pl.pallas_call(functools.partial(right_kernel, n_branch), out_shape=[sent...  3.87 us
    pallas_call x1, Pallas kernels, msa(): pl.pallas_call(functools.partial(msa_kernel, n_branch, rows), out_shape=[...  2.95 us
  transfers between devices with their start and end apart: 12, of which 8 were waited for; matrix products, arithmetic and copies ran while one was open for 0% of the time, Pallas kernels for 14%

profile of v4, /device:TPU:0, one launch (start us, length us, event | category | flops | bytes accessed | tf_op | source)
XLA Modules:
  0.0 65.5 jit_solution(7090838241644270260)
XLA Ops:
  0.6 3.0 %msa_transition.1 = (bf16[1,256,256]{2,1,0:T(8,128)(2,1)}, bf16[192,128]{1,0:T(8,128)(2,1)}) custom-call(bf16[1,256,256]{2,1,0:T(8,128)(2,1)} %seq_hbm.1, bf16[256,1024]{1,0:T(8,128)(2,1)} %up_hbm.1, bf16[1024,256]{1,0:T(8,128)(2,1)} %down_hbm.1, bf16[64,256]{1,0:T(8,128)(2,1)} %bitcast.33), custom_call_target="tpu_custom_call" | custom-call | flops 268435456 | bytes 1048576 | tf_op jit(solution)/shard_map/msa_transition/pallas_call | solution.py:342
  3.6 4.1 %collective-permute-start = (bf16[192,128]{1,0:T(8,128)(2,1)}, bf16[192,128]{1,0:T(8,128)(2,1)S(1)}, u32[]{:S(2)}, u32[]{:S(2)}) collective-permute-start(bf16[192,128]{1,0:T(8,128)(2,1)} %get-tuple-element.19.sides_ref), channel_id=1, source_target_pairs={{0,8},{1,9},{2,10},{3,11},{4,12},{5,13},{6,14},{7,15},{8,0},{9,1},... | collective-permute-start | bytes 147464 | tf_op jit(solution)/shard_map/ppermute | solution.py:587
  7.7 3.9 %right_operand.1 = (bf16[32,8,16,128]{3,2,1,0:T(8,128)(2,1)}, bf16[16,128,128]{2,1,0:T(8,128)(2,1)}) custom-call(bf16[16,128,128]{2,1,0:T(8,128)(2,1)} %x_ref, bf16[128,640]{1,0:T(8,128)(2,1)} %w_ref.4), custom_call_target="tpu_custom_call" | custom-call | flops 134217728 | bytes 1572864 | tf_op jit(solution)/shard_map/right_operand/pallas_call | solution.py:286
  11.6 0.0 copy-start.2
  11.6 5.0 %all-to-all-start = ((bf16[32,8,16,128]{3,2,1,0:T(8,128)(2,1)}), bf16[32,8,16,128]{3,2,1,0:T(8,128)(2,1)S(1)}, u32[]{:S(2)}, u32[]{:S(2)}) async-start(bf16[32,8,16,128]{3,2,1,0:T(8,128)(2,1)} %get-tuple-element.22), calls=%async_computation | async-start | bytes 2097152 | tf_op jit(solution)/shard_map/all_to_all | solution.py:625
  16.6 0.3 collective-permute-start.1
  16.9 0.1 pad_add_fusion.where_ref
  17.0 1.6 %collective-permute-done.1.other_ref = bf16[16,128,128]{2,1,0:T(8,128)(2,1)S(1)} collective-permute-done((bf16[16,128,128]{2,1,0:T(8,128)(2,1)S(1)}, bf16[16,128,128]{2,1,0:T(8,128)(2,1)S(1)}, u32[]{:S(2)}, u32[]{:S(2)}) %collective-permute-start.1) | collective-permute-done | bytes 524320 | tf_op jit(solution)/shard_map/ppermute | solution.py:587
  18.6 1.6 %left_operand.1 = (bf16[336,128]{1,0:T(8,128)(2,1)S(1)}, bf16[336,128]{1,0:T(8,128)(2,1)S(1)}, bf16[336,128]{1,0:T(8,128)(2,1)S(1)}, bf16[336,128]{1,0:T(8,128)(...) custom-call(s32[2]{0:T(128)S(1)} %pad_add_fusion.where_ref, ...), custom_call_target="tpu_custom_call" | custom-call | flops 268435456 | bytes 2097152 | tf_op jit(solution)/shard_map/left_operand/pallas_call | solution.py:412
  20.2 1.8 %collective-permute-start.2 = (bf16[336,128]{1,0:T(8,128)(2,1)S(1)}, bf16[336,128]{1,0:T(8,128)(2,1)S(1)}, u32[]{:S(2)}, u32[]{:S(2)}) collective-permute-start(bf16[336,128]{1,0:T(8,128)(2,1)S(1)} %get-tuple-element.26), channel_id=1, source_target_pairs={{0,2},{1,3},{2,0},{3,1},{4,6},{5,7},{6,4},{7,5},{8,10},{9,11},{10,... | collective-permute-start | bytes 258056 | tf_op jit(solution)/shard_map/ppermute | solution.py:587
  22.0 1.5 %collective-permute-start.3 = (bf16[336,128]{1,0:T(8,128)(2,1)S(1)}, bf16[336,128]{1,0:T(8,128)(2,1)S(1)}, u32[]{:S(2)}, u32[]{:S(2)}) collective-permute-start(bf16[336,128]{1,0:T(8,128)(2,1)S(1)} %get-tuple-element.27), channel_id=1, source_target_pairs={{0,16},{1,17},{2,18},{3,19},{4,20},{5,21},{6,22},{7,23},{8,24},{9,... | collective-permute-start | bytes 258056 | tf_op jit(solution)/shard_map/ppermute | solution.py:587
  23.5 1.5 %collective-permute-start.4 = (bf16[336,128]{1,0:T(8,128)(2,1)S(1)}, bf16[336,128]{1,0:T(8,128)(2,1)S(1)}, u32[]{:S(2)}, u32[]{:S(2)}) collective-permute-start(bf16[336,128]{1,0:T(8,128)(2,1)S(1)} %get-tuple-element.28), channel_id=1, source_target_pairs={{0,22},{1,23},{2,20},{3,21},{4,18},{5,19},{6,16},{7,17},{8,30},{9,... | collective-permute-start | bytes 258056 | tf_op jit(solution)/shard_map/ppermute | solution.py:587
  25.0 1.5 %collective-permute-start.5 = (bf16[336,128]{1,0:T(8,128)(2,1)S(1)}, bf16[336,128]{1,0:T(8,128)(2,1)S(1)}, u32[]{:S(2)}, u32[]{:S(2)}) collective-permute-start(bf16[336,128]{1,0:T(8,128)(2,1)S(1)} %get-tuple-element.29), channel_id=1, source_target_pairs={{0,6},{1,7},{2,4},{3,5},{4,2},{5,3},{6,0},{7,1},{8,14},{9,15},{10,... | collective-permute-start | bytes 258056 | tf_op jit(solution)/shard_map/ppermute | solution.py:587
  26.4 2.4 %collective-permute-start.6 = (bf16[336,128]{1,0:T(8,128)(2,1)S(1)}, bf16[336,128]{1,0:T(8,128)(2,1)S(1)}, u32[]{:S(2)}, u32[]{:S(2)}) collective-permute-start(bf16[336,128]{1,0:T(8,128)(2,1)S(1)} %get-tuple-element.30), channel_id=1, source_target_pairs={{0,20},{1,21},{2,22},{3,23},{4,16},{5,17},{6,18},{7,19},{8,28},{9,... | collective-permute-start | bytes 258056 | tf_op jit(solution)/shard_map/ppermute | solution.py:587
  28.8 0.6 collective-permute-start.7
  29.4 1.5 %collective-permute-start.8 = (bf16[336,128]{1,0:T(8,128)(2,1)S(1)}, bf16[336,128]{1,0:T(8,128)(2,1)S(1)}, u32[]{:S(2)}, u32[]{:S(2)}) collective-permute-start(bf16[336,128]{1,0:T(8,128)(2,1)S(1)} %get-tuple-element.32), channel_id=1, source_target_pairs={{0,18},{1,19},{2,16},{3,17},{4,22},{5,23},{6,20},{7,21},{8,26},{9,... | collective-permute-start | bytes 258056 | tf_op jit(solution)/shard_map/ppermute | solution.py:587
  30.9 5.9 %collective-permute-done.4.rest_3_ = bf16[336,128]{1,0:T(8,128)(2,1)S(1)} collective-permute-done((bf16[336,128]{1,0:T(8,128)(2,1)S(1)}, bf16[336,128]{1,0:T(8,128)(2,1)S(1)}, u32[]{:S(2)}, u32[]{:S(2)}) %collective-permute-start.4) | collective-permute-done | bytes 86048 | tf_op jit(solution)/shard_map/ppermute | solution.py:587
  36.9 2.1 %collective-permute-done.5.rest_4_ = bf16[336,128]{1,0:T(8,128)(2,1)S(1)} collective-permute-done((bf16[336,128]{1,0:T(8,128)(2,1)S(1)}, bf16[336,128]{1,0:T(8,128)(2,1)S(1)}, u32[]{:S(2)}, u32[]{:S(2)}) %collective-permute-start.5) | collective-permute-done | bytes 86048 | tf_op jit(solution)/shard_map/ppermute | solution.py:587
  39.0 2.8 %collective-permute-done.6.rest_5_ = bf16[336,128]{1,0:T(8,128)(2,1)S(1)} collective-permute-done((bf16[336,128]{1,0:T(8,128)(2,1)S(1)}, bf16[336,128]{1,0:T(8,128)(2,1)S(1)}, u32[]{:S(2)}, u32[]{:S(2)}) %collective-permute-start.6) | collective-permute-done | bytes 86048 | tf_op jit(solution)/shard_map/ppermute | solution.py:587
  41.8 1.9 %collective-permute-done.7.rest_6_ = bf16[336,128]{1,0:T(8,128)(2,1)S(1)} collective-permute-done((bf16[336,128]{1,0:T(8,128)(2,1)S(1)}, bf16[336,128]{1,0:T(8,128)(2,1)S(1)}, u32[]{:S(2)}, u32[]{:S(2)}) %collective-permute-start.7) | collective-permute-done | bytes 86048 | tf_op jit(solution)/shard_map/ppermute | solution.py:587
  43.7 0.2 all-to-all-done.in_ref
  43.9 1.8 %triangle_product.1 = bf16[16,8,16,128]{3,2,1,0:T(8,128)(2,1)} custom-call(s32[2]{0:T(128)S(1)} %pad_add_fusion.where_ref, bf16[32,8,16,128]{3,2,1,0:T(8,128)(2,1)S(1)} %all-to-all-done.in_ref, bf16[336,128]{1,0:T(8,128)(2,1)S(1)} %get-tuple-element.25.rest_0_, bf16[336,128]{1,0:T(8,128)(2,1)S(1)} %collective-permute-done.2.rest_1_, ...), custom_call_target="tpu_custom_call" | custom-call | flops 134217728 | bytes 2097152 | tf_op jit(solution)/shard_map/triangle_product/pallas_call | solution.py:478
  45.7 4.3 %all-to-all-start.1 = ((bf16[16,8,16,128]{3,2,1,0:T(8,128)(2,1)}), bf16[16,8,16,128]{3,2,1,0:T(8,128)(2,1)S(1)}, u32[]{:S(2)}, u32[]{:S(2)}) async-start(bf16[16,8,16,128]{3,2,1,0:T(8,128)(2,1)} %triangle_product.1), calls=%async_computation.1 | async-start | bytes 1048576 | tf_op jit(solution)/shard_map/all_to_all | solution.py:654
  50.1 0.0 copy-start.9
  50.1 0.5 collective-permute-start.9
  50.6 0.8 %triangle_output_gate.1.gate_ref = f32[16,128,128]{2,1,0:T(8,128)S(1)} custom-call(bf16[16,128,128]{2,1,0:T(8,128)(2,1)S(1)} %copy-done.1, bf16[128,640]{1,0:T(8,128)(2,1)S(1)} %copy-done.2), custom_call_target="tpu_custom_call" | custom-call | flops 67108864 | bytes 1572864 | tf_op jit(solution)/shard_map/triangle_output_gate/pallas_call | solution.py:434
  51.4 0.0 copy-start.4
  51.4 0.2 collective-permute-done.9.refs_1_
  51.6 0.9 %copy-done.8 = bf16[8,80,128]{2,1,0:T(8,128)(2,1)S(1)} copy-done((bf16[8,80,128]{2,1,0:T(8,128)(2,1)S(1)}, bf16[8,80,128]{2,1,0:T(8,128)(2,1)}, u32[]{:S(2)}) %copy-start.8) | copy-done | bytes 163864
  52.5 2.9 %outer_product_mean.1.outer_ref = f32[16,128,128]{2,1,0:T(8,128)S(1)} custom-call(s32[2]{0:T(128)S(1)} %pad_add_fusion.where_ref, bf16[8,80,128]{2,1,0:T(8,128)(2,1)S(1)} %copy-done.8, bf16[8,80,128]{2,1,0:T(8,128)(2,1)S(1)} %collective-permute-done.9.refs_1_, bf16[1024,128]{1,0:T(8,128)(2,1)S(1)} %copy-done.9), custom_call_target="tpu_custom_call" | custom-call | flops 1073741824 | bytes 1048576 | tf_op jit(solution)/shard_map/outer_product_mean/pallas_call | solution.py:568
  55.4 5.1 %all-to-all-done.1.p_ref = bf16[16,8,16,128]{3,2,1,0:T(8,128)(2,1)S(1)} async-done(((bf16[16,8,16,128]{3,2,1,0:T(8,128)(2,1)}), bf16[16,8,16,128]{3,2,1,0:T(8,128)(2,1)S(1)}, u32[]{:S(2)}, u32[]{:S(2)}) %all-to-all-start.1) | async-done | bytes 524320 | tf_op jit(solution)/shard_map/all_to_all | solution.py:654
  60.6 4.9 %pair_output.1 = bf16[16,128,128]{2,1,0:T(8,128)(2,1)} custom-call(bf16[16,8,16,128]{3,2,1,0:T(8,128)(2,1)S(1)} %all-to-all-done.1.p_ref, bf16[16,128,128]{2,1,0:T(8,128)(2,1)S(1)} %copy-done, f32[16,128,128]{2,1,0:T(8,128)S(1)} %triangle_output_gate.1.gate_ref, f32[16,128,128]{2,1,0:T(8,128)S(1)} %outer_product_mean.1.outer_ref, ...), custom_call_target="tpu_custom_call" | custom-call | flops 603979776 | bytes 3670016 | tf_op jit(solution)/shard_map/pair_output/pallas_call | solution.py:517
  (28 shorter events, 0.1 us)
Async XLA Ops:
  3.6 8.0 %collective-permute-start = (bf16[192,128]{1,0:T(8,128)(2,1)}, bf16[192,128]{1,0:T(8,128)(2,1)S(1)}, u32[]{:S(2)}, u32[]{:S(2)}) collective-permute-start(bf16[192,128]{1,0:T(8,128)(2,1)} %get-tuple-element.19.sides_ref), channel_id=1, source_target_pairs={{0,8},{1,9},{2,10},{3,11},{4,12},{5,13},{6,14},{7,15},{8,0},{9,1},... | collective-permute-start | bytes 147464 | tf_op jit(solution)/shard_map/ppermute | solution.py:587
  11.6 5.0 %copy-start.1 = (bf16[16,128,128]{2,1,0:T(8,128)(2,1)S(1)}, bf16[16,128,128]{2,1,0:T(8,128)(2,1)}, u32[]{:S(2)}) copy-start(bf16[16,128,128]{2,1,0:T(8,128)(2,1)} %get-tuple-element.33.x_ref) | copy-start | bytes 1572868
  11.6 7.0 %copy-start.2 = (bf16[128,640]{1,0:T(8,128)(2,1)S(1)}, bf16[128,640]{1,0:T(8,128)(2,1)}, u32[]{:S(2)}) copy-start(bf16[128,640]{1,0:T(8,128)(2,1)} %w_ref.4) | copy-start | bytes 491524
  11.6 7.0 %copy-start.5 = (bf16[192,128]{1,0:T(8,128)(2,1)S(1)}, bf16[192,128]{1,0:T(8,128)(2,1)}, u32[]{:S(2)}) copy-start(bf16[192,128]{1,0:T(8,128)(2,1)} %get-tuple-element.19.sides_ref) | copy-start | bytes 147460
  11.6 32.3 %all-to-all-start = ((bf16[32,8,16,128]{3,2,1,0:T(8,128)(2,1)}), bf16[32,8,16,128]{3,2,1,0:T(8,128)(2,1)S(1)}, u32[]{:S(2)}, u32[]{:S(2)}) async-start(bf16[32,8,16,128]{3,2,1,0:T(8,128)(2,1)} %get-tuple-element.22), calls=%async_computation | async-start | bytes 2097152 | tf_op jit(solution)/shard_map/all_to_all | solution.py:625
  16.6 2.0 %collective-permute-start.1 = (bf16[16,128,128]{2,1,0:T(8,128)(2,1)S(1)}, bf16[16,128,128]{2,1,0:T(8,128)(2,1)S(1)}, u32[]{:S(2)}, u32[]{:S(2)}) collective-permute-start(bf16[16,128,128]{2,1,0:T(8,128)(2,1)S(1)} %copy-done.1), channel_id=1, source_target_pairs={{0,1},{1,0},{2,3},{3,2},{4,5},{5,4},{6,7},{7,6},{8,9},{9,8},{10,11... | collective-permute-start | bytes 1572872 | tf_op jit(solution)/shard_map/ppermute | solution.py:587
  20.2 8.6 %collective-permute-start.2 = (bf16[336,128]{1,0:T(8,128)(2,1)S(1)}, bf16[336,128]{1,0:T(8,128)(2,1)S(1)}, u32[]{:S(2)}, u32[]{:S(2)}) collective-permute-start(bf16[336,128]{1,0:T(8,128)(2,1)S(1)} %get-tuple-element.26), channel_id=1, source_target_pairs={{0,2},{1,3},{2,0},{3,1},{4,6},{5,7},{6,4},{7,5},{8,10},{9,11},{10,... | collective-permute-start | bytes 258056 | tf_op jit(solution)/shard_map/ppermute | solution.py:587
  22.0 7.3 %collective-permute-start.3 = (bf16[336,128]{1,0:T(8,128)(2,1)S(1)}, bf16[336,128]{1,0:T(8,128)(2,1)S(1)}, u32[]{:S(2)}, u32[]{:S(2)}) collective-permute-start(bf16[336,128]{1,0:T(8,128)(2,1)S(1)} %get-tuple-element.27), channel_id=1, source_target_pairs={{0,16},{1,17},{2,18},{3,19},{4,20},{5,21},{6,22},{7,23},{8,24},{9,... | collective-permute-start | bytes 258056 | tf_op jit(solution)/shard_map/ppermute | solution.py:587
  23.5 13.3 %collective-permute-start.4 = (bf16[336,128]{1,0:T(8,128)(2,1)S(1)}, bf16[336,128]{1,0:T(8,128)(2,1)S(1)}, u32[]{:S(2)}, u32[]{:S(2)}) collective-permute-start(bf16[336,128]{1,0:T(8,128)(2,1)S(1)} %get-tuple-element.28), channel_id=1, source_target_pairs={{0,22},{1,23},{2,20},{3,21},{4,18},{5,19},{6,16},{7,17},{8,30},{9,... | collective-permute-start | bytes 258056 | tf_op jit(solution)/shard_map/ppermute | solution.py:587
  25.0 14.0 %collective-permute-start.5 = (bf16[336,128]{1,0:T(8,128)(2,1)S(1)}, bf16[336,128]{1,0:T(8,128)(2,1)S(1)}, u32[]{:S(2)}, u32[]{:S(2)}) collective-permute-start(bf16[336,128]{1,0:T(8,128)(2,1)S(1)} %get-tuple-element.29), channel_id=1, source_target_pairs={{0,6},{1,7},{2,4},{3,5},{4,2},{5,3},{6,0},{7,1},{8,14},{9,15},{10,... | collective-permute-start | bytes 258056 | tf_op jit(solution)/shard_map/ppermute | solution.py:587
  26.4 15.4 %collective-permute-start.6 = (bf16[336,128]{1,0:T(8,128)(2,1)S(1)}, bf16[336,128]{1,0:T(8,128)(2,1)S(1)}, u32[]{:S(2)}, u32[]{:S(2)}) collective-permute-start(bf16[336,128]{1,0:T(8,128)(2,1)S(1)} %get-tuple-element.30), channel_id=1, source_target_pairs={{0,20},{1,21},{2,22},{3,23},{4,16},{5,17},{6,18},{7,19},{8,28},{9,... | collective-permute-start | bytes 258056 | tf_op jit(solution)/shard_map/ppermute | solution.py:587
  28.8 14.9 %collective-permute-start.7 = (bf16[336,128]{1,0:T(8,128)(2,1)S(1)}, bf16[336,128]{1,0:T(8,128)(2,1)S(1)}, u32[]{:S(2)}, u32[]{:S(2)}) collective-permute-start(bf16[336,128]{1,0:T(8,128)(2,1)S(1)} %get-tuple-element.31), channel_id=1, source_target_pairs={{0,4},{1,5},{2,6},{3,7},{4,0},{5,1},{6,2},{7,3},{8,12},{9,13},{10,... | collective-permute-start | bytes 258056 | tf_op jit(solution)/shard_map/ppermute | solution.py:587
  29.4 14.3 %collective-permute-start.8 = (bf16[336,128]{1,0:T(8,128)(2,1)S(1)}, bf16[336,128]{1,0:T(8,128)(2,1)S(1)}, u32[]{:S(2)}, u32[]{:S(2)}) collective-permute-start(bf16[336,128]{1,0:T(8,128)(2,1)S(1)} %get-tuple-element.32), channel_id=1, source_target_pairs={{0,18},{1,19},{2,16},{3,17},{4,22},{5,23},{6,20},{7,21},{8,26},{9,... | collective-permute-start | bytes 258056 | tf_op jit(solution)/shard_map/ppermute | solution.py:587
  45.7 14.9 %all-to-all-start.1 = ((bf16[16,8,16,128]{3,2,1,0:T(8,128)(2,1)}), bf16[16,8,16,128]{3,2,1,0:T(8,128)(2,1)S(1)}, u32[]{:S(2)}, u32[]{:S(2)}) async-start(bf16[16,8,16,128]{3,2,1,0:T(8,128)(2,1)} %triangle_product.1), calls=%async_computation.1 | async-start | bytes 1048576 | tf_op jit(solution)/shard_map/all_to_all | solution.py:654
  50.1 1.3 %copy-start.7 = (bf16[8,80,128]{2,1,0:T(8,128)(2,1)}, bf16[8,80,128]{2,1,0:T(8,128)(2,1)S(1)}, u32[]{:S(2)}) copy-start(bf16[8,80,128]{2,1,0:T(8,128)(2,1)S(1)} %fusion.refs_0_) | copy-start | bytes 491524
  50.1 1.5 %copy-start.9 = (bf16[1024,128]{1,0:T(8,128)(2,1)S(1)}, bf16[1024,128]{1,0:T(8,128)(2,1)}, u32[]{:S(2)}) copy-start(bf16[1024,128]{1,0:T(8,128)(2,1)} %refs_2_.1) | copy-start | bytes 786436
  50.1 1.5 %collective-permute-start.9 = (bf16[8,80,128]{2,1,0:T(8,128)(2,1)S(1)}, bf16[8,80,128]{2,1,0:T(8,128)(2,1)S(1)}, u32[]{:S(2)}, u32[]{:S(2)}) collective-permute-start(bf16[8,80,128]{2,1,0:T(8,128)(2,1)S(1)} %fusion.refs_0_), channel_id=1, source_target_pairs={{0,1},{1,0},{2,3},{3,2},{4,5},{5,4},{6,7},{7,6},{8,9},{9,8},{10,11... | collective-permute-start | bytes 491528 | tf_op jit(solution)/shard_map/ppermute | solution.py:587
  51.3 9.2 %copy-start = (bf16[16,128,128]{2,1,0:T(8,128)(2,1)S(1)}, bf16[16,128,128]{2,1,0:T(8,128)(2,1)}, u32[]{:S(2)}) copy-start(bf16[16,128,128]{2,1,0:T(8,128)(2,1)} %x_ref) | copy-start | bytes 1572868
  51.4 9.2 %copy-start.3 = (bf16[128,512]{1,0:T(8,128)(2,1)S(1)}, bf16[128,512]{1,0:T(8,128)(2,1)}, u32[]{:S(2)}) copy-start(bf16[128,512]{1,0:T(8,128)(2,1)} %up_ref.1) | copy-start | bytes 393220
  51.4 9.2 %copy-start.4 = (bf16[512,128]{1,0:T(8,128)(2,1)S(1)}, bf16[512,128]{1,0:T(8,128)(2,1)}, u32[]{:S(2)}) copy-start(bf16[512,128]{1,0:T(8,128)(2,1)} %down_ref.1) | copy-start | bytes 393220
  51.4 9.2 %copy-start.6 = (bf16[128,128]{1,0:T(8,128)(2,1)S(1)}, bf16[128,128]{1,0:T(8,128)(2,1)}, u32[]{:S(2)}) copy-start(bf16[128,128]{1,0:T(8,128)(2,1)} %w_ref.5) | copy-start | bytes 98308
  51.6 0.9 %copy-start.8 = (bf16[8,80,128]{2,1,0:T(8,128)(2,1)S(1)}, bf16[8,80,128]{2,1,0:T(8,128)(2,1)}, u32[]{:S(2)}) copy-start(bf16[8,80,128]{2,1,0:T(8,128)(2,1)} %copy-done.7) | copy-start | bytes 491524

commit v5 on v4

--- a/solution.py
+++ b/solution.py
@@ -235,61 +235,75 @@
         store(i + 1, result[:, width:])
 
 
-def fill_right(n_branch, tokens_ref, w, out_ref, scr):
-    rows, _, chans = tokens_ref.shape
-    devices, per = out_ref.shape[:2]
-    groups = chans // per
-    near = groups // n_branch
-    halves = devices // groups
-    own = lax.broadcasted_iota(jnp.int32, (chans, chans), 0)
-    values, gates = channel_order(w, (2, 3), own, chans)
-
-    def store(i, block):
-        scr[pl.ds(i, chans, stride=rows), :] = block
-
-    gated_rows(values, gates, tokens_ref, store)
-    for q in range(chans):
-        g, c = q // per, q % per
-        block = scr[q * rows : (q + 1) * rows, :].astype(BF16)
-        for h in range(halves):
-            out_ref[(g // near * halves + h) * near + g % near, c] = block
-
-
 def right_kernel(
     n_branch, x_hbm, w_hbm, sent_hbm, tokens_hbm, x_ref, w_ref, sent_ref, tokens_ref, scr, sems
 ):
-    rows = x_ref.shape[0]
-    step = rows // 4
-    copies = [pltpu.make_async_copy(w_hbm, w_ref, sems.at[0])]
-    for k in range(4):
-        part = pl.ds(k * step, step)
-        copies.append(pltpu.make_async_copy(x_hbm.at[part], x_ref.at[part], sems.at[k + 1]))
+    rows, width, chans = x_ref.shape
+    groups, per = sent_ref.shape[:2]
+    near = groups // n_branch
+    halves = sent_hbm.shape[0] // groups
+    columns = w_hbm.at[:, pl.ds(2 * chans, 2 * chans)]
+    copies = [
+        pltpu.make_async_copy(columns, w_ref, sems.at[0]),
+        pltpu.make_async_copy(x_hbm, x_ref, sems.at[1]),
+    ]
     for copy in copies:
         copy.start()
-    for k in range(4):
-        copies[k + 1].wait()
-        part = slice(k * step, (k + 1) * step)
-        tokens_ref[part] = normed(x_ref[part].astype(F32), -1)
-    copies[0].wait()
-    keep = pltpu.make_async_copy(tokens_ref, tokens_hbm, sems.at[5])
-    keep.start()
-    fill_right(n_branch, tokens_ref, w_ref[...], sent_ref, scr)
-    send = pltpu.make_async_copy(sent_ref, sent_hbm, sems.at[6])
-    send.start()
-    keep.wait()
-    send.wait()
+    for copy in copies:
+        copy.wait()
+    values = jnp.transpose(w_ref[:, :chans])
+    gates = jnp.transpose(w_ref[:, chans:])
+    step = 4
+    parts = []
+    for i in range(0, rows, step):
+        tokens = normed(x_ref[i : i + step].astype(F32), -1)
+        tokens_ref[i : i + step] = tokens
+        parts.append(tokens.reshape(step * width, chans))
+    outs = [pltpu.make_async_copy(tokens_ref, tokens_hbm, sems.at[2])]
+    outs[0].start()
+    for i, tokens in zip(range(0, rows, step), parts):
+        result = dot(values, tokens, NT) * sigmoid(dot(gates, tokens, NT))
+        for k in range(step):
+            scr[pl.ds(i + k, chans, stride=rows), :] = result[:, k * width : (k + 1) * width]
+    span = 4
+    for g in range(groups):
+        for c in range(per):
+            q = (g * per + c) * rows
+            sent_ref[g, c] = scr[q : q + rows, :].astype(BF16)
+        if g % span == span - 1:
+            begin = g + 1 - span
+            for h in range(halves):
+                to = (begin // near * halves + h) * near + begin % near
+                copy = pltpu.make_async_copy(
+                    sent_ref.at[pl.ds(begin, span)],
+                    sent_hbm.at[pl.ds(to, span)],
+                    sems.at[2 + len(outs)],
+                )
+                copy.start()
+                outs.append(copy)
+    for copy in outs:
+        copy.wait()
 
 
 def right_operand(x, w, n_branch, devices, per):
     rows, width, chans = x.shape
-    sent = jax.ShapeDtypeStruct((devices, per, rows, width), BF16)
+    groups = chans // per
     return pl.pallas_call(
         functools.partial(right_kernel, n_branch),
-        out_shape=[sent, jax.ShapeDtypeStruct(x.shape, BF16)],
+        out_shape=[
+            jax.ShapeDtypeStruct((devices, per, rows, width), BF16),
+            jax.ShapeDtypeStruct(x.shape, BF16),
+        ],
         in_specs=[HBM] * 2,
         out_specs=[HBM] * 2,
-        scratch_shapes=[pltpu.VMEM(array.shape, BF16) for array in (x, w, sent, x)]
-        + [pltpu.VMEM((chans * rows, width), F32), pltpu.SemaphoreType.DMA((7,))],
+        scratch_shapes=[
+            pltpu.VMEM(x.shape, BF16),
+            pltpu.VMEM((chans, 2 * chans), BF16),
+            pltpu.VMEM((groups, per, rows, width), BF16),
+            pltpu.VMEM(x.shape, BF16),
+            pltpu.VMEM((chans * rows, width), F32),
+            pltpu.SemaphoreType.DMA((3 + devices // 4,)),
+        ],
         cost_estimate=cost(2 * rows * width * chans * 2 * chans, 3 * rows * width * chans * 2),
         name="right_operand",
     )(x, w)
@@ -444,71 +458,109 @@
 
 
 def product_kernel(n_branch, near, where_ref, in_ref, *rest):
-    left_refs, (out_ref, left_scr) = rest[:-2], rest[-2:]
+    places = near // 2
+    left_refs = dict(zip(TARGETS, rest))
+    out_hbm, out_ref, sems = rest[n_branch * places :]
     devices, per, rows, width = in_ref.shape
     n_rows = devices // n_branch
     branch, row_at = where_ref[0], where_ref[1]
     place = lax.shift_right_logical(lax.bitwise_and(row_at, near - 1), 1)
-    places = near // 2
-    for t, ref in zip(TARGETS, left_refs):
-        b = lax.bitwise_xor(branch, t // places)
-        p = lax.bitwise_xor(place, t % places)
-        for c in range(per):
-            left_scr[b, c, p] = ref[c * 2 * rows : (c + 1) * 2 * rows]
+    outs = []
     for c in range(per):
+        span = slice(c * 2 * rows, (c + 1) * 2 * rows)
         left = jnp.concatenate(
-            [left_scr[b, c].reshape(near * rows, width) for b in range(n_branch)], axis=1
+            [
+                jnp.concatenate([left_refs[s * places + p][span] for p in range(places)], axis=0)
+                for s in range(n_branch)
+            ],
+            axis=1,
         )
         right = jnp.concatenate(
             [
-                in_ref[b * n_rows : (b + 1) * n_rows, c].reshape(n_rows * rows, width)
-                for b in range(n_branch)
+                in_ref[pl.ds(lax.bitwise_xor(branch, s) * n_rows, n_rows), c].reshape(
+                    n_rows * rows, width
+                )
+                for s in range(n_branch)
             ],
             axis=1,
         )
         product = dot(left, right, NT).astype(BF16)
-        for b in range(n_branch):
-            out_ref[b * near : (b + 1) * near, c] = product[
-                :, b * width : (b + 1) * width
-            ].reshape(near, rows, width)
+        for p in range(places):
+            at = lax.bitwise_xor(place, p) * 2
+            part = product[p * 2 * rows : (p + 1) * 2 * rows]
+            for b in range(n_branch):
+                for k in range(2):
+                    out_ref[n_branch * near - 1 - (b * near + at + k), c] = part[
+                        k * rows : (k + 1) * rows, b * width : (b + 1) * width
+                    ]
+        if c % 2 == 1:
+            half = pl.ds(c - 1, 2)
+            copy = pltpu.make_async_copy(
+                out_ref.at[:, half], out_hbm.at[:, half], sems.at[c // 2]
+            )
+            copy.start()
+            outs.append(copy)
+    for copy in outs:
+        copy.wait()
 
 
 def triangle_product(where, received, pieces, n_branch, near):
     devices, per, rows, width = received.shape
+    shape = (n_branch * near, per, rows, width)
     return pl.pallas_call(
         functools.partial(product_kernel, n_branch, near),
-        out_shape=jax.ShapeDtypeStruct((n_branch * near, per, rows, width), BF16),
+        out_shape=jax.ShapeDtypeStruct(shape, BF16),
         in_specs=[SMEM] + [VMEM] * (1 + len(pieces)),
-        out_specs=VMEM,
-        scratch_shapes=[pltpu.VMEM((n_branch, per, near // 2, 2 * rows, width), BF16)],
+        out_specs=HBM,
+        scratch_shapes=[pltpu.VMEM(shape, BF16), pltpu.SemaphoreType.DMA((per // 2,))],
         compiler_params=PARAMS,
-        cost_estimate=cost(
-            2 * per * near * rows * received.size // per, received.size * 4
-        ),
+        cost_estimate=cost(2 * near * rows * received.size, received.size * 4),
         name="triangle_product",
     )(where, received, *pieces)
 
 
 def pair_output_kernel(
-    p_ref, x_ref, gate_ref, outer_ref, w_ref, up_ref, down_ref, out_ref, scr
+    p_ref, x_ref, gate_ref, outer_ref, w_ref, up_ref, down_ref, out_hbm, scr, out_ref, sems
 ):
     devices, per, rows, width = p_ref.shape
     chans = devices * per
-    for g in range(devices):
-        for c in range(per):
-            scr[pl.ds(g * per + c, rows, stride=chans), :] = p_ref[g, c].astype(F32)
-    step = 4
-    for i in range(0, rows, step):
+    step = rows // 2
+    shape = (step * width, chans)
+    share = up_ref.shape[1] // 4
+
+    def place(i):
+        for g in range(devices):
+            for c in range(per):
+                tile = p_ref[devices - 1 - g, c].astype(F32)[i : i + step]
+                scr[pl.ds(i * chans + g * per + c, step, stride=chans), :] = tile
+
+    def triangle(i):
         parts = [
             normed(scr[(i + k) * chans : (i + k + 1) * chans, :], 0) for k in range(step)
         ]
         update = dot(jnp.concatenate(parts, axis=1), w_ref[...], TN)
-        shape = (step * width, chans)
         x = x_ref[i : i + step].astype(F32).reshape(shape)
         middle = x + gate_ref[i : i + step].reshape(shape) * update
-        hidden = jnp.maximum(dot(normed(middle, -1), up_ref[...]), 0.0).astype(BF16)
-        result = middle + dot(hidden, down_ref[...]) + outer_ref[i : i + step].reshape(shape)
+        return middle, normed(middle, -1)
+
+    def transition(i, middle, tokens):
+        result = middle + outer_ref[i : i + step].reshape(shape)
+        for h in range(0, up_ref.shape[1], share):
+            hidden = dot(tokens, up_ref[:, h : h + share]).astype(BF16)
+            result = result + dot(jnp.maximum(hidden, 0.0), down_ref[h : h + share])
         out_ref[i : i + step] = result.astype(BF16).reshape(step, width, chans)
+        part = pl.ds(i, step)
+        copy = pltpu.make_async_copy(out_ref.at[part], out_hbm.at[part], sems.at[i // step])
+        copy.start()
+        return copy
+
+    middles = []
+    for i in range(0, rows, step):
+        place(i)
+        middles.append(triangle(i))
+    copies = [transition(i * step, *middle) for i, middle in enumerate(middles)]
+    for copy in copies:
+        copy.wait()
 
 
 def pair_output(product, x, gate, outer, w, up, down):
@@ -518,8 +570,12 @@
         pair_output_kernel,
         out_shape=jax.ShapeDtypeStruct(x.shape, BF16),
         in_specs=[VMEM] * 7,
-        out_specs=VMEM,
-        scratch_shapes=[pltpu.VMEM((rows * chans, width), F32)],
+        out_specs=HBM,
+        scratch_shapes=[
+            pltpu.VMEM((rows * chans, width), F32),
+            pltpu.VMEM(x.shape, BF16),
+            pltpu.SemaphoreType.DMA((2,)),
+        ],
         compiler_params=PARAMS,
         cost_estimate=cost(2 * x.size * (chans + 2 * up.shape[1]), x.size * 14),
         name="pair_output",
@@ -648,7 +704,7 @@
 
     product = triangle_product(where, received, moved, n_branch, near)
     members = [
-        [b * n_rows + h * near + k for b in range(n_branch) for k in range(near)]
+        [b * n_rows + h * near + k for b in range(n_branch) for k in range(near)][::-1]
         for h in range(halves)
     ]
     returned = lax.all_to_all(product, AXES, 0, 0, axis_index_groups=members, tiled=True)

time: 65.8 us -> 62.1 us (0.944)
  waiting for transfers between devices: 19.9 us -> 16.9 us
  Pallas kernels: 18.8 us -> 16.5 us
  starting transfers between devices: 24.9 us -> 26.5 us
    all_to_all x1, waiting for transfers between devices: 5.13 us -> 1.82 us  [own_channels_device(): lax.all_to_all(product, AXES, 0, 0, axis_index_groups=members, tiled=True)]
    pallas_call x1, Pallas kernels: 4.86 us -> 3.22 us  [pair_output(): pl.pallas_call(pair_output_kernel, out_shape=jax.ShapeDtypeStruct(x.shape...]
    all_to_all x1, starting transfers between devices: 4.34 us -> 5.7 us  [own_channels_device(): lax.all_to_all(product, AXES, 0, 0, axis_index_groups=members, tiled=True)]
where the time goes in v5:
time: 62.1 us; the launch traced here: 61.7 us
  starting transfers between devices  26.5 us (43%)
  waiting for transfers between devices  16.9 us (27%)
  Pallas kernels  16.5 us (27%)
  local copies, waits for them, and re-layouts  1.03 us (2%)
  between operations  0.82 us (1%)
    ppermute x10, starting transfers between devices, swap(): return lax.ppermute(x, AXES, [(d, d ^ mask) for d in range(count)])  15.2 us
    ppermute x10, waiting for transfers between devices, swap(): return lax.ppermute(x, AXES, [(d, d ^ mask) for d in range(count)])  14.9 us
    all_to_all x1, starting transfers between devices, own_channels_device(): lax.all_to_all(product, AXES, 0, 0, axis_index_groups=members, tiled=True)  5.7 us
    all_to_all x1, starting transfers between devices, own_channels_device(): received = lax.all_to_all(sent, AXES, 0, 0, tiled=True)  5.53 us
    pallas_call x1, Pallas kernels, right_operand(): pl.pallas_call(functools.partial(right_kernel, n_branch), out_shape=[jax....  3.29 us
    pallas_call x1, Pallas kernels, pair_output(): pl.pallas_call(pair_output_kernel, out_shape=jax.ShapeDtypeStruct(x.shape...  3.22 us
    pallas_call x1, Pallas kernels, msa(): pl.pallas_call(functools.partial(msa_kernel, n_branch, rows), out_shape=[...  2.95 us
    pallas_call x1, Pallas kernels, outer_update(): pl.pallas_call(outer_kernel, out_shape=jax.ShapeDtypeStruct((rows, width,...  2.91 us
  transfers between devices with their start and end apart: 12, of which 8 were waited for; matrix products, arithmetic and copies ran while one was open for 0% of the time, Pallas kernels for 14%

profile of v5, /device:TPU:0, one launch (start us, length us, event | category | flops | bytes accessed | tf_op | source)
XLA Modules:
  0.0 61.7 jit_solution(9591379455173721724)
XLA Ops:
  0.6 3.0 %msa_transition.1 = (bf16[1,256,256]{2,1,0:T(8,128)(2,1)}, bf16[192,128]{1,0:T(8,128)(2,1)}) custom-call(bf16[1,256,256]{2,1,0:T(8,128)(2,1)} %seq_hbm.1, bf16[256,1024]{1,0:T(8,128)(2,1)} %up_hbm.1, bf16[1024,256]{1,0:T(8,128)(2,1)} %down_hbm.1, bf16[64,256]{1,0:T(8,128)(2,1)} %bitcast.33), custom_call_target="tpu_custom_call" | custom-call | flops 268435456 | bytes 1048576 | tf_op jit(solution)/shard_map/msa_transition/pallas_call | solution.py:356
  3.6 4.1 %collective-permute-start = (bf16[192,128]{1,0:T(8,128)(2,1)}, bf16[192,128]{1,0:T(8,128)(2,1)S(1)}, u32[]{:S(2)}, u32[]{:S(2)}) collective-permute-start(bf16[192,128]{1,0:T(8,128)(2,1)} %get-tuple-element.19.sides_ref), channel_id=1, source_target_pairs={{0,8},{1,9},{2,10},{3,11},{4,12},{5,13},{6,14},{7,15},{8,0},{9,1},... | collective-permute-start | bytes 147464 | tf_op jit(solution)/shard_map/ppermute | solution.py:643
  7.7 3.3 %right_operand.1 = (bf16[32,8,16,128]{3,2,1,0:T(8,128)(2,1)}, bf16[16,128,128]{2,1,0:T(8,128)(2,1)}) custom-call(bf16[16,128,128]{2,1,0:T(8,128)(2,1)} %x_ref, bf16[128,640]{1,0:T(8,128)(2,1)} %w_ref.4), custom_call_target="tpu_custom_call" | custom-call | flops 134217728 | bytes 1572864 | tf_op jit(solution)/shard_map/right_operand/pallas_call | solution.py:291
  11.0 0.0 copy-start.1
  11.0 0.0 copy-start.2
  11.0 5.5 %all-to-all-start = ((bf16[32,8,16,128]{3,2,1,0:T(8,128)(2,1)}), bf16[32,8,16,128]{3,2,1,0:T(8,128)(2,1)S(1)}, u32[]{:S(2)}, u32[]{:S(2)}) async-start(bf16[32,8,16,128]{3,2,1,0:T(8,128)(2,1)} %get-tuple-element.22), calls=%async_computation | async-start | bytes 2097152 | tf_op jit(solution)/shard_map/all_to_all | solution.py:681
  16.6 0.3 collective-permute-start.1
  16.9 0.1 pad_add_fusion.where_ref
  17.0 1.6 %collective-permute-done.1.other_ref = bf16[16,128,128]{2,1,0:T(8,128)(2,1)S(1)} collective-permute-done((bf16[16,128,128]{2,1,0:T(8,128)(2,1)S(1)}, bf16[16,128,128]{2,1,0:T(8,128)(2,1)S(1)}, u32[]{:S(2)}, u32[]{:S(2)}) %collective-permute-start.1) | collective-permute-done | bytes 524320 | tf_op jit(solution)/shard_map/ppermute | solution.py:643
  18.6 1.6 %left_operand.1 = (bf16[336,128]{1,0:T(8,128)(2,1)S(1)}, bf16[336,128]{1,0:T(8,128)(2,1)S(1)}, bf16[336,128]{1,0:T(8,128)(2,1)S(1)}, bf16[336,128]{1,0:T(8,128)(...) custom-call(s32[2]{0:T(128)S(1)} %pad_add_fusion.where_ref, ...), custom_call_target="tpu_custom_call" | custom-call | flops 268435456 | bytes 2097152 | tf_op jit(solution)/shard_map/left_operand/pallas_call | solution.py:426
  20.2 1.8 %collective-permute-start.2 = (bf16[336,128]{1,0:T(8,128)(2,1)S(1)}, bf16[336,128]{1,0:T(8,128)(2,1)S(1)}, u32[]{:S(2)}, u32[]{:S(2)}) collective-permute-start(bf16[336,128]{1,0:T(8,128)(2,1)S(1)} %get-tuple-element.26), channel_id=1, source_target_pairs={{0,2},{1,3},{2,0},{3,1},{4,6},{5,7},{6,4},{7,5},{8,10},{9,11},{10,... | collective-permute-start | bytes 258056 | tf_op jit(solution)/shard_map/ppermute | solution.py:643
  22.0 1.5 %collective-permute-start.3 = (bf16[336,128]{1,0:T(8,128)(2,1)S(1)}, bf16[336,128]{1,0:T(8,128)(2,1)S(1)}, u32[]{:S(2)}, u32[]{:S(2)}) collective-permute-start(bf16[336,128]{1,0:T(8,128)(2,1)S(1)} %get-tuple-element.27), channel_id=1, source_target_pairs={{0,16},{1,17},{2,18},{3,19},{4,20},{5,21},{6,22},{7,23},{8,24},{9,... | collective-permute-start | bytes 258056 | tf_op jit(solution)/shard_map/ppermute | solution.py:643
  23.5 1.5 %collective-permute-start.4 = (bf16[336,128]{1,0:T(8,128)(2,1)S(1)}, bf16[336,128]{1,0:T(8,128)(2,1)S(1)}, u32[]{:S(2)}, u32[]{:S(2)}) collective-permute-start(bf16[336,128]{1,0:T(8,128)(2,1)S(1)} %get-tuple-element.28), channel_id=1, source_target_pairs={{0,22},{1,23},{2,20},{3,21},{4,18},{5,19},{6,16},{7,17},{8,30},{9,... | collective-permute-start | bytes 258056 | tf_op jit(solution)/shard_map/ppermute | solution.py:643
  25.0 1.5 %collective-permute-start.5 = (bf16[336,128]{1,0:T(8,128)(2,1)S(1)}, bf16[336,128]{1,0:T(8,128)(2,1)S(1)}, u32[]{:S(2)}, u32[]{:S(2)}) collective-permute-start(bf16[336,128]{1,0:T(8,128)(2,1)S(1)} %get-tuple-element.29), channel_id=1, source_target_pairs={{0,6},{1,7},{2,4},{3,5},{4,2},{5,3},{6,0},{7,1},{8,14},{9,15},{10,... | collective-permute-start | bytes 258056 | tf_op jit(solution)/shard_map/ppermute | solution.py:643
  26.4 2.4 %collective-permute-start.6 = (bf16[336,128]{1,0:T(8,128)(2,1)S(1)}, bf16[336,128]{1,0:T(8,128)(2,1)S(1)}, u32[]{:S(2)}, u32[]{:S(2)}) collective-permute-start(bf16[336,128]{1,0:T(8,128)(2,1)S(1)} %get-tuple-element.30), channel_id=1, source_target_pairs={{0,20},{1,21},{2,22},{3,23},{4,16},{5,17},{6,18},{7,19},{8,28},{9,... | collective-permute-start | bytes 258056 | tf_op jit(solution)/shard_map/ppermute | solution.py:643
  28.8 0.6 collective-permute-start.7
  29.4 1.5 %collective-permute-start.8 = (bf16[336,128]{1,0:T(8,128)(2,1)S(1)}, bf16[336,128]{1,0:T(8,128)(2,1)S(1)}, u32[]{:S(2)}, u32[]{:S(2)}) collective-permute-start(bf16[336,128]{1,0:T(8,128)(2,1)S(1)} %get-tuple-element.32), channel_id=1, source_target_pairs={{0,18},{1,19},{2,16},{3,17},{4,22},{5,23},{6,20},{7,21},{8,26},{9,... | collective-permute-start | bytes 258056 | tf_op jit(solution)/shard_map/ppermute | solution.py:643
  30.9 5.9 %collective-permute-done.4.rest_3_ = bf16[336,128]{1,0:T(8,128)(2,1)S(1)} collective-permute-done((bf16[336,128]{1,0:T(8,128)(2,1)S(1)}, bf16[336,128]{1,0:T(8,128)(2,1)S(1)}, u32[]{:S(2)}, u32[]{:S(2)}) %collective-permute-start.4) | collective-permute-done | bytes 86048 | tf_op jit(solution)/shard_map/ppermute | solution.py:643
  36.9 2.1 %collective-permute-done.5.rest_4_ = bf16[336,128]{1,0:T(8,128)(2,1)S(1)} collective-permute-done((bf16[336,128]{1,0:T(8,128)(2,1)S(1)}, bf16[336,128]{1,0:T(8,128)(2,1)S(1)}, u32[]{:S(2)}, u32[]{:S(2)}) %collective-permute-start.5) | collective-permute-done | bytes 86048 | tf_op jit(solution)/shard_map/ppermute | solution.py:643
  39.0 2.8 %collective-permute-done.6.rest_5_ = bf16[336,128]{1,0:T(8,128)(2,1)S(1)} collective-permute-done((bf16[336,128]{1,0:T(8,128)(2,1)S(1)}, bf16[336,128]{1,0:T(8,128)(2,1)S(1)}, u32[]{:S(2)}, u32[]{:S(2)}) %collective-permute-start.6) | collective-permute-done | bytes 86048 | tf_op jit(solution)/shard_map/ppermute | solution.py:643
  41.8 1.9 %collective-permute-done.7.rest_6_ = bf16[336,128]{1,0:T(8,128)(2,1)S(1)} collective-permute-done((bf16[336,128]{1,0:T(8,128)(2,1)S(1)}, bf16[336,128]{1,0:T(8,128)(2,1)S(1)}, u32[]{:S(2)}, u32[]{:S(2)}) %collective-permute-start.7) | collective-permute-done | bytes 86048 | tf_op jit(solution)/shard_map/ppermute | solution.py:643
  43.7 0.2 all-to-all-done.in_ref
  43.9 1.7 %triangle_product.1 = bf16[16,8,16,128]{3,2,1,0:T(8,128)(2,1)} custom-call(s32[2]{0:T(128)S(1)} %pad_add_fusion.where_ref, bf16[32,8,16,128]{3,2,1,0:T(8,128)(2,1)S(1)} %all-to-all-done.in_ref, bf16[336,128]{1,0:T(8,128)(2,1)S(1)} %get-tuple-element.25.rest_0_, bf16[336,128]{1,0:T(8,128)(2,1)S(1)} %collective-permute-done.2.rest_1_, ...), custom_call_target="tpu_custom_call" | custom-call | flops 134217728 | bytes 2097152 | tf_op jit(solution)/shard_map/triangle_product/pallas_call | solution.py:510
  45.6 5.7 %all-to-all-start.1 = ((bf16[16,8,16,128]{3,2,1,0:T(8,128)(2,1)}), bf16[16,8,16,128]{3,2,1,0:T(8,128)(2,1)S(1)}, u32[]{:S(2)}, u32[]{:S(2)}) async-start(bf16[16,8,16,128]{3,2,1,0:T(8,128)(2,1)} %triangle_product.1), calls=%async_computation.1 | async-start | bytes 1048576 | tf_op jit(solution)/shard_map/all_to_all | solution.py:710
  51.4 0.0 copy-start.9
  51.4 0.1 collective-permute-start.9
  51.5 0.7 %triangle_output_gate.1.gate_ref = f32[16,128,128]{2,1,0:T(8,128)S(1)} custom-call(bf16[16,128,128]{2,1,0:T(8,128)(2,1)S(1)} %copy-done.1, bf16[128,640]{1,0:T(8,128)(2,1)S(1)} %copy-done.2), custom_call_target="tpu_custom_call" | custom-call | flops 67108864 | bytes 1572864 | tf_op jit(solution)/shard_map/triangle_output_gate/pallas_call | solution.py:448
  52.3 0.5 collective-permute-done.9.refs_1_
  52.8 0.9 %copy-done.8 = bf16[8,80,128]{2,1,0:T(8,128)(2,1)S(1)} copy-done((bf16[8,80,128]{2,1,0:T(8,128)(2,1)S(1)}, bf16[8,80,128]{2,1,0:T(8,128)(2,1)}, u32[]{:S(2)}) %copy-start.8) | copy-done | bytes 163864
  53.8 2.9 %outer_product_mean.1.outer_ref = f32[16,128,128]{2,1,0:T(8,128)S(1)} custom-call(s32[2]{0:T(128)S(1)} %pad_add_fusion.where_ref, bf16[8,80,128]{2,1,0:T(8,128)(2,1)S(1)} %copy-done.8, bf16[8,80,128]{2,1,0:T(8,128)(2,1)S(1)} %collective-permute-done.9.refs_1_, bf16[1024,128]{1,0:T(8,128)(2,1)S(1)} %copy-done.9), custom_call_target="tpu_custom_call" | custom-call | flops 1073741824 | bytes 1048576 | tf_op jit(solution)/shard_map/outer_product_mean/pallas_call | solution.py:624
  56.7 1.8 %all-to-all-done.1.p_ref = bf16[16,8,16,128]{3,2,1,0:T(8,128)(2,1)S(1)} async-done(((bf16[16,8,16,128]{3,2,1,0:T(8,128)(2,1)}), bf16[16,8,16,128]{3,2,1,0:T(8,128)(2,1)S(1)}, u32[]{:S(2)}, u32[]{:S(2)}) %all-to-all-start.1) | async-done | bytes 524320 | tf_op jit(solution)/shard_map/all_to_all | solution.py:710
  58.5 3.2 %pair_output.1 = bf16[16,128,128]{2,1,0:T(8,128)(2,1)} custom-call(bf16[16,8,16,128]{3,2,1,0:T(8,128)(2,1)S(1)} %all-to-all-done.1.p_ref, bf16[16,128,128]{2,1,0:T(8,128)(2,1)S(1)} %copy-done, f32[16,128,128]{2,1,0:T(8,128)S(1)} %triangle_output_gate.1.gate_ref, f32[16,128,128]{2,1,0:T(8,128)S(1)} %outer_product_mean.1.outer_ref, ...), custom_call_target="tpu_custom_call" | custom-call | flops 603979776 | bytes 3670016 | tf_op jit(solution)/shard_map/pair_output/pallas_call | solution.py:569
  (28 shorter events, 0.1 us)
Async XLA Ops:
  3.6 7.4 %collective-permute-start = (bf16[192,128]{1,0:T(8,128)(2,1)}, bf16[192,128]{1,0:T(8,128)(2,1)S(1)}, u32[]{:S(2)}, u32[]{:S(2)}) collective-permute-start(bf16[192,128]{1,0:T(8,128)(2,1)} %get-tuple-element.19.sides_ref), channel_id=1, source_target_pairs={{0,8},{1,9},{2,10},{3,11},{4,12},{5,13},{6,14},{7,15},{8,0},{9,1},... | collective-permute-start | bytes 147464 | tf_op jit(solution)/shard_map/ppermute | solution.py:643
  11.0 5.6 %copy-start.1 = (bf16[16,128,128]{2,1,0:T(8,128)(2,1)S(1)}, bf16[16,128,128]{2,1,0:T(8,128)(2,1)}, u32[]{:S(2)}) copy-start(bf16[16,128,128]{2,1,0:T(8,128)(2,1)} %get-tuple-element.33.x_ref) | copy-start | bytes 1572868
  11.0 7.6 %copy-start.2 = (bf16[128,640]{1,0:T(8,128)(2,1)S(1)}, bf16[128,640]{1,0:T(8,128)(2,1)}, u32[]{:S(2)}) copy-start(bf16[128,640]{1,0:T(8,128)(2,1)} %w_ref.4) | copy-start | bytes 491524
  11.0 7.5 %copy-start.5 = (bf16[192,128]{1,0:T(8,128)(2,1)S(1)}, bf16[192,128]{1,0:T(8,128)(2,1)}, u32[]{:S(2)}) copy-start(bf16[192,128]{1,0:T(8,128)(2,1)} %get-tuple-element.19.sides_ref) | copy-start | bytes 147460
  11.0 32.8 %all-to-all-start = ((bf16[32,8,16,128]{3,2,1,0:T(8,128)(2,1)}), bf16[32,8,16,128]{3,2,1,0:T(8,128)(2,1)S(1)}, u32[]{:S(2)}, u32[]{:S(2)}) async-start(bf16[32,8,16,128]{3,2,1,0:T(8,128)(2,1)} %get-tuple-element.22), calls=%async_computation | async-start | bytes 2097152 | tf_op jit(solution)/shard_map/all_to_all | solution.py:681
  16.6 2.0 %collective-permute-start.1 = (bf16[16,128,128]{2,1,0:T(8,128)(2,1)S(1)}, bf16[16,128,128]{2,1,0:T(8,128)(2,1)S(1)}, u32[]{:S(2)}, u32[]{:S(2)}) collective-permute-start(bf16[16,128,128]{2,1,0:T(8,128)(2,1)S(1)} %copy-done.1), channel_id=1, source_target_pairs={{0,1},{1,0},{2,3},{3,2},{4,5},{5,4},{6,7},{7,6},{8,9},{9,8},{10,11... | collective-permute-start | bytes 1572872 | tf_op jit(solution)/shard_map/ppermute | solution.py:643
  20.2 8.6 %collective-permute-start.2 = (bf16[336,128]{1,0:T(8,128)(2,1)S(1)}, bf16[336,128]{1,0:T(8,128)(2,1)S(1)}, u32[]{:S(2)}, u32[]{:S(2)}) collective-permute-start(bf16[336,128]{1,0:T(8,128)(2,1)S(1)} %get-tuple-element.26), channel_id=1, source_target_pairs={{0,2},{1,3},{2,0},{3,1},{4,6},{5,7},{6,4},{7,5},{8,10},{9,11},{10,... | collective-permute-start | bytes 258056 | tf_op jit(solution)/shard_map/ppermute | solution.py:643
  22.0 7.3 %collective-permute-start.3 = (bf16[336,128]{1,0:T(8,128)(2,1)S(1)}, bf16[336,128]{1,0:T(8,128)(2,1)S(1)}, u32[]{:S(2)}, u32[]{:S(2)}) collective-permute-start(bf16[336,128]{1,0:T(8,128)(2,1)S(1)} %get-tuple-element.27), channel_id=1, source_target_pairs={{0,16},{1,17},{2,18},{3,19},{4,20},{5,21},{6,22},{7,23},{8,24},{9,... | collective-permute-start | bytes 258056 | tf_op jit(solution)/shard_map/ppermute | solution.py:643
  23.5 13.3 %collective-permute-start.4 = (bf16[336,128]{1,0:T(8,128)(2,1)S(1)}, bf16[336,128]{1,0:T(8,128)(2,1)S(1)}, u32[]{:S(2)}, u32[]{:S(2)}) collective-permute-start(bf16[336,128]{1,0:T(8,128)(2,1)S(1)} %get-tuple-element.28), channel_id=1, source_target_pairs={{0,22},{1,23},{2,20},{3,21},{4,18},{5,19},{6,16},{7,17},{8,30},{9,... | collective-permute-start | bytes 258056 | tf_op jit(solution)/shard_map/ppermute | solution.py:643
  25.0 14.0 %collective-permute-start.5 = (bf16[336,128]{1,0:T(8,128)(2,1)S(1)}, bf16[336,128]{1,0:T(8,128)(2,1)S(1)}, u32[]{:S(2)}, u32[]{:S(2)}) collective-permute-start(bf16[336,128]{1,0:T(8,128)(2,1)S(1)} %get-tuple-element.29), channel_id=1, source_target_pairs={{0,6},{1,7},{2,4},{3,5},{4,2},{5,3},{6,0},{7,1},{8,14},{9,15},{10,... | collective-permute-start | bytes 258056 | tf_op jit(solution)/shard_map/ppermute | solution.py:643
  26.4 15.4 %collective-permute-start.6 = (bf16[336,128]{1,0:T(8,128)(2,1)S(1)}, bf16[336,128]{1,0:T(8,128)(2,1)S(1)}, u32[]{:S(2)}, u32[]{:S(2)}) collective-permute-start(bf16[336,128]{1,0:T(8,128)(2,1)S(1)} %get-tuple-element.30), channel_id=1, source_target_pairs={{0,20},{1,21},{2,22},{3,23},{4,16},{5,17},{6,18},{7,19},{8,28},{9,... | collective-permute-start | bytes 258056 | tf_op jit(solution)/shard_map/ppermute | solution.py:643
  28.8 14.9 %collective-permute-start.7 = (bf16[336,128]{1,0:T(8,128)(2,1)S(1)}, bf16[336,128]{1,0:T(8,128)(2,1)S(1)}, u32[]{:S(2)}, u32[]{:S(2)}) collective-permute-start(bf16[336,128]{1,0:T(8,128)(2,1)S(1)} %get-tuple-element.31), channel_id=1, source_target_pairs={{0,4},{1,5},{2,6},{3,7},{4,0},{5,1},{6,2},{7,3},{8,12},{9,13},{10,... | collective-permute-start | bytes 258056 | tf_op jit(solution)/shard_map/ppermute | solution.py:643
  29.4 14.3 %collective-permute-start.8 = (bf16[336,128]{1,0:T(8,128)(2,1)S(1)}, bf16[336,128]{1,0:T(8,128)(2,1)S(1)}, u32[]{:S(2)}, u32[]{:S(2)}) collective-permute-start(bf16[336,128]{1,0:T(8,128)(2,1)S(1)} %get-tuple-element.32), channel_id=1, source_target_pairs={{0,18},{1,19},{2,16},{3,17},{4,22},{5,23},{6,20},{7,21},{8,26},{9,... | collective-permute-start | bytes 258056 | tf_op jit(solution)/shard_map/ppermute | solution.py:643
  45.6 12.9 %all-to-all-start.1 = ((bf16[16,8,16,128]{3,2,1,0:T(8,128)(2,1)}), bf16[16,8,16,128]{3,2,1,0:T(8,128)(2,1)S(1)}, u32[]{:S(2)}, u32[]{:S(2)}) async-start(bf16[16,8,16,128]{3,2,1,0:T(8,128)(2,1)} %triangle_product.1), calls=%async_computation.1 | async-start | bytes 1048576 | tf_op jit(solution)/shard_map/all_to_all | solution.py:710
  51.4 0.9 %copy-start.7 = (bf16[8,80,128]{2,1,0:T(8,128)(2,1)}, bf16[8,80,128]{2,1,0:T(8,128)(2,1)S(1)}, u32[]{:S(2)}) copy-start(bf16[8,80,128]{2,1,0:T(8,128)(2,1)S(1)} %fusion.refs_0_) | copy-start | bytes 491524
  51.4 1.5 %copy-start.9 = (bf16[1024,128]{1,0:T(8,128)(2,1)S(1)}, bf16[1024,128]{1,0:T(8,128)(2,1)}, u32[]{:S(2)}) copy-start(bf16[1024,128]{1,0:T(8,128)(2,1)} %refs_2_.1) | copy-start | bytes 786436
  51.4 1.5 %collective-permute-start.9 = (bf16[8,80,128]{2,1,0:T(8,128)(2,1)S(1)}, bf16[8,80,128]{2,1,0:T(8,128)(2,1)S(1)}, u32[]{:S(2)}, u32[]{:S(2)}) collective-permute-start(bf16[8,80,128]{2,1,0:T(8,128)(2,1)S(1)} %fusion.refs_0_), channel_id=1, source_target_pairs={{0,1},{1,0},{2,3},{3,2},{4,5},{5,4},{6,7},{7,6},{8,9},{9,8},{10,11... | collective-permute-start | bytes 491528 | tf_op jit(solution)/shard_map/ppermute | solution.py:643
  52.3 6.2 %copy-start = (bf16[16,128,128]{2,1,0:T(8,128)(2,1)S(1)}, bf16[16,128,128]{2,1,0:T(8,128)(2,1)}, u32[]{:S(2)}) copy-start(bf16[16,128,128]{2,1,0:T(8,128)(2,1)} %x_ref) | copy-start | bytes 1572868
  52.3 6.2 %copy-start.3 = (bf16[128,512]{1,0:T(8,128)(2,1)S(1)}, bf16[128,512]{1,0:T(8,128)(2,1)}, u32[]{:S(2)}) copy-start(bf16[128,512]{1,0:T(8,128)(2,1)} %up_ref.1) | copy-start | bytes 393220
  52.3 6.2 %copy-start.4 = (bf16[512,128]{1,0:T(8,128)(2,1)S(1)}, bf16[512,128]{1,0:T(8,128)(2,1)}, u32[]{:S(2)}) copy-start(bf16[512,128]{1,0:T(8,128)(2,1)} %down_ref.1) | copy-start | bytes 393220
  52.3 6.2 %copy-start.6 = (bf16[128,128]{1,0:T(8,128)(2,1)S(1)}, bf16[128,128]{1,0:T(8,128)(2,1)}, u32[]{:S(2)}) copy-start(bf16[128,128]{1,0:T(8,128)(2,1)} %w_ref.5) | copy-start | bytes 98308
  52.8 0.9 %copy-start.8 = (bf16[8,80,128]{2,1,0:T(8,128)(2,1)S(1)}, bf16[8,80,128]{2,1,0:T(8,128)(2,1)}, u32[]{:S(2)}) copy-start(bf16[8,80,128]{2,1,0:T(8,128)(2,1)} %copy-done.7) | copy-start | bytes 491524

commit v6 on v5

--- a/solution.py
+++ b/solution.py
@@ -14,7 +14,7 @@
 TN = (((0,), (0,)), ((), ()))
 VMEM = pl.BlockSpec(memory_space=pltpu.VMEM)
 SMEM = pl.BlockSpec(memory_space=pltpu.SMEM)
-TARGETS = (0, 1, 4, 7, 3, 6, 2, 5)
+TARGETS = (0, 4, 1, 2, 7, 3, 6, 5)
 HBM = pl.BlockSpec(memory_space=pltpu.HBM)
 PARAMS = pltpu.CompilerParams(vmem_limit_bytes=48 * 1024 * 1024)
 
@@ -310,62 +310,45 @@
 
 
 def msa_kernel(
-    n_branch, rows, seq_hbm, up_hbm, down_hbm, factor_hbm, fresh_ref, sides_ref,
-    seq_ref, up_ref, down_ref, factor_ref, sems
+    n_branch, rows, seq_ref, far_ref, up_ref, down_ref, factor_ref, fresh_ref, *side_refs
 ):
-    pairs = [
-        (seq_hbm, seq_ref),
-        (up_hbm, up_ref),
-        (down_hbm, down_ref),
-        (factor_hbm, factor_ref),
-    ]
-    copies = [pltpu.make_async_copy(a, b, sems.at[k]) for k, (a, b) in enumerate(pairs)]
-    for copy in copies:
-        copy.start()
-    copies[0].wait()
-    x = seq_ref[0].astype(F32)
-    tokens = normed(x, -1)
-    copies[1].wait()
-    hidden = jnp.maximum(dot(tokens, up_ref[...]), 0.0).astype(BF16)
-    copies[2].wait()
-    fresh = (x + dot(hidden, down_ref[...])).astype(BF16)
-    fresh_ref[0] = fresh
-    tokens = normed(fresh.astype(F32), -1)
-    copies[3].wait()
+    x = [ref[0].astype(F32) for ref in (seq_ref, far_ref)]
+    tokens = [normed(v, -1) for v in x]
+    hidden = [jnp.maximum(dot(t, up_ref[...]).astype(BF16), 0.0) for t in tokens]
+    fresh = [(v + dot(h, down_ref[...])).astype(BF16) for v, h in zip(x, hidden)]
+    fresh_ref[0] = fresh[0]
     factor = factor_ref[...]
     depth = factor.shape[0] // 2
-    left = dot(tokens, factor[:depth], NT).astype(BF16)
-    right = dot(factor[depth:], tokens, NT).astype(BF16)
-    width = sides_ref.shape[1]
-    for b in range(n_branch):
-        sides_ref[b * depth : (b + 1) * depth] = right[:, b * width : (b + 1) * width]
-    tiles = left.reshape(-1, 2, rows, depth)
-    blank = jnp.zeros((rows, width - 2 * depth), BF16)
-    base = n_branch * depth
-    for t in range(tiles.shape[0]):
-        sides_ref[base + t * rows : base + (t + 1) * rows] = jnp.concatenate(
-            [tiles[t, 0], tiles[t, 1], blank], axis=1
-        )
-
-
-def msa(seq, up, down, factor, rows, width):
+    for row, sides_ref in zip(fresh, side_refs):
+        tokens = normed(row.astype(F32), -1)
+        left = dot(tokens, factor[:depth], NT).astype(BF16)
+        right = dot(factor[depth:], tokens, NT).astype(BF16)
+        width = sides_ref.shape[1]
+        for b in range(n_branch):
+            sides_ref[b * depth : (b + 1) * depth] = right[:, b * width : (b + 1) * width]
+        tiles = left.reshape(-1, 2, rows, depth)
+        blank = jnp.zeros((rows, width - 2 * depth), BF16)
+        base = n_branch * depth
+        for t in range(tiles.shape[0]):
+            sides_ref[base + t * rows : base + (t + 1) * rows] = jnp.concatenate(
+                [tiles[t, 0], tiles[t, 1], blank], axis=1
+            )
+
+
+def msa(seq, far, up, down, factor, rows, width):
     _, length, feats = seq.shape
     depth = factor.shape[0] // 2
     n_branch = length // width
-    operands = (seq, up, down, factor)
+    sides = jax.ShapeDtypeStruct((n_branch * depth + length // 2, width), BF16)
     return pl.pallas_call(
         functools.partial(msa_kernel, n_branch, rows),
-        out_shape=[
-            jax.ShapeDtypeStruct(seq.shape, BF16),
-            jax.ShapeDtypeStruct((n_branch * depth + length // 2, width), BF16),
-        ],
-        in_specs=[HBM] * 4,
-        out_specs=[VMEM] * 2,
-        scratch_shapes=[pltpu.VMEM(array.shape, BF16) for array in operands]
-        + [pltpu.SemaphoreType.DMA((4,))],
-        cost_estimate=cost(4 * length * feats * up.shape[1], 4 * feats * up.shape[1]),
+        out_shape=[jax.ShapeDtypeStruct(seq.shape, BF16), sides, sides],
+        in_specs=[VMEM] * 5,
+        out_specs=[VMEM] * 3,
+        compiler_params=PARAMS,
+        cost_estimate=cost(8 * length * feats * up.shape[1], 4 * feats * up.shape[1]),
         name="msa_transition",
-    )(*operands)
+    )(seq, far, up, down, factor)
 
 
 def beside_kernel(
@@ -430,7 +413,7 @@
         out_specs=[VMEM] * count,
         scratch_shapes=[pltpu.VMEM((2, count * per * rows, width), F32)],
         compiler_params=PARAMS,
-        cost_estimate=cost(4 * x.size * 2 * chans, x.size * 8),
+        cost_estimate=cost(2 * 10**10, x.size * 8),
         name="left_operand",
     )(where, x, other, w, sides, far_sides)
 
@@ -664,23 +647,22 @@
     per = chans // (n_branch * near)
     where = jnp.stack([lax.axis_index("branch"), lax.axis_index("rows")]).astype(jnp.int32)
 
-    fresh, sides = msa(
+    far_row = swap(homolog_features, n_branch, n_rows, near)
+    sent, tokens = right_operand(
+        pairwise_input, triangle_projection_weight, n_branch, n_branch * n_rows, per
+    )
+    received = lax.all_to_all(sent, AXES, 0, 0, tiled=True)
+
+    other = swap(tokens, n_branch, n_rows, 1)
+    fresh, sides, far_sides = msa(
         homolog_features,
+        far_row,
         transition_expand_matrix,
         transition_contract_matrix,
         jnp.transpose(factor_pair_matrices),
         rows,
         pairwise_input.shape[1],
     )
-    far_sides = swap(sides, n_branch, n_rows, near)
-    pairwise_input, _ = lax.optimization_barrier((pairwise_input, sides))
-    sent, tokens = right_operand(
-        pairwise_input, triangle_projection_weight, n_branch, n_branch * n_rows, per
-    )
-    sent, far_sides = lax.optimization_barrier((sent, far_sides))
-    received = lax.all_to_all(sent, AXES, 0, 0, tiled=True)
-
-    other = swap(tokens, n_branch, n_rows, 1)
     pieces = beside(
         where,
         tokens,

time: 62.1 us -> 58.6 us (0.944); the launches traced: 61.7 us -> 57.5 us
  waiting for transfers between devices: 16.9 us -> 13.5 us
    ppermute x10, waiting for transfers between devices: 14.9 us -> 11.9 us  [swap(): return lax.ppermute(x, AXES, [(d, d ^ mask) for d in range(count)])]
    all_to_all x1, starting transfers between devices: 5.53 us -> 3.82 us  [own_channels_device(): received = lax.all_to_all(sent, AXES, 0, 0, tiled=True)]
    ppermute x10, starting transfers between devices: 15.2 us -> 16.9 us  [swap(): return lax.ppermute(x, AXES, [(d, d ^ mask) for d in range(count)])]
    pallas_call x1, Pallas kernels: 2.95 us -> 2.1 us  [msa(): pl.pallas_call(functools.partial(msa_kernel, n_branch, rows), out_shape=[...]
  transfers between devices with their start and end apart: 12 -> 12, of which waited for: 8 -> 7; matrix products, arithmetic and copies ran while one was open for 0% -> 0% of each run, Pallas kernels for 14% -> 14%
where the time goes in v6:
time: 58.6 us; the launch traced here: 57.5 us
  starting transfers between devices  25.9 us (44%)
  Pallas kernels  16.2 us (28%)
  waiting for transfers between devices  13.5 us (23%)
  local copies, waits for them, and re-layouts  1.05 us (2%)
  between operations  0.81 us (1%)
    ppermute x10, starting transfers between devices, swap(): return lax.ppermute(x, AXES, [(d, d ^ mask) for d in range(count)])  16.9 us
    ppermute x10, waiting for transfers between devices, swap(): return lax.ppermute(x, AXES, [(d, d ^ mask) for d in range(count)])  11.9 us
    all_to_all x1, starting transfers between devices, own_channels_device(): lax.all_to_all(product, AXES, 0, 0, axis_index_groups=members, tiled=True)  5.15 us
    all_to_all x1, starting transfers between devices, own_channels_device(): received = lax.all_to_all(sent, AXES, 0, 0, tiled=True)  3.82 us
    pallas_call x1, Pallas kernels, right_operand(): pl.pallas_call(functools.partial(right_kernel, n_branch), out_shape=[jax....  3.32 us
    pallas_call x1, Pallas kernels, pair_output(): pl.pallas_call(pair_output_kernel, out_shape=jax.ShapeDtypeStruct(x.shape...  3.22 us
    pallas_call x1, Pallas kernels, outer_update(): pl.pallas_call(outer_kernel, out_shape=jax.ShapeDtypeStruct((rows, width,...  2.91 us
    pallas_call x1, Pallas kernels, beside(): pl.pallas_call(functools.partial(beside_kernel, n_branch, near), out_shap...  2.14 us
  transfers between devices with their start and end apart: 12, of which 7 were waited for; matrix products, arithmetic and copies ran while one was open for 0% of the time, Pallas kernels for 14%

profile of v6, /device:TPU:0, one launch (start us, length us, event | category | flops | bytes accessed | tf_op | source)
XLA Modules:
  0.0 57.5 jit_solution(18085306834085883060)
XLA Ops:
  0.6 3.3 %right_operand.1 = (bf16[32,8,16,128]{3,2,1,0:T(8,128)(2,1)}, bf16[16,128,128]{2,1,0:T(8,128)(2,1)}) custom-call(bf16[16,128,128]{2,1,0:T(8,128)(2,1)} %x_ref.1, bf16[128,640]{1,0:T(8,128)(2,1)} %w_ref.4), custom_call_target="tpu_custom_call" | custom-call | flops 134217728 | bytes 1572864 | tf_op jit(solution)/shard_map/right_operand/pallas_call | solution.py:291
  4.0 0.5 collective-permute-start.1
  4.5 3.7 %collective-permute-start = (bf16[1,256,256]{2,1,0:T(8,128)(2,1)S(1)}, bf16[1,256,256]{2,1,0:T(8,128)(2,1)S(1)}, u32[]{:S(2)}, u32[]{:S(2)}) collective-permute-start(bf16[1,256,256]{2,1,0:T(8,128)(2,1)S(1)} %copy-done.11), channel_id=1, source_target_pairs={{0,8},{1,9},{2,10},{3,11},{4,12},{5,13},{6,14},{7,15},{8,0},{9,1},... | collective-permute-start | bytes 393224 | tf_op jit(solution)/shard_map/ppermute | solution.py:626
  8.2 3.8 %all-to-all-start = ((bf16[32,8,16,128]{3,2,1,0:T(8,128)(2,1)}), bf16[32,8,16,128]{3,2,1,0:T(8,128)(2,1)S(1)}, u32[]{:S(2)}, u32[]{:S(2)}) async-start(bf16[32,8,16,128]{3,2,1,0:T(8,128)(2,1)} %get-tuple-element.17), calls=%async_computation | async-start | bytes 2097152 | tf_op jit(solution)/shard_map/all_to_all | solution.py:654
  12.0 0.1 pad_add_fusion.where_ref
  12.1 3.0 %collective-permute-done.far_ref = bf16[1,256,256]{2,1,0:T(8,128)(2,1)S(1)} collective-permute-done((bf16[1,256,256]{2,1,0:T(8,128)(2,1)S(1)}, bf16[1,256,256]{2,1,0:T(8,128)(2,1)S(1)}, u32[]{:S(2)}, u32[]{:S(2)}) %collective-permute-start) | collective-permute-done | bytes 131104 | tf_op jit(solution)/shard_map/ppermute | solution.py:626
  15.1 0.0 copy-start.1
  15.1 0.0 copy-start.2
  15.1 2.1 %msa_transition.1 = (bf16[1,256,256]{2,1,0:T(8,128)(2,1)}, bf16[192,128]{1,0:T(8,128)(2,1)S(1)}, bf16[192,128]{1,0:T(8,128)(2,1)S(1)}) custom-call(bf16[1,256,256]{2,1,0:T(8,128)(2,1)S(1)} %copy-done.11, bf16[1,256,256]{2,1,0:T(8,128)(2,1)S(1)} %collective-permute-done.far_ref, bf16[256,1024]{1,0:T(8,128)(2,1)S(1)} %copy-done.8, ...), custom_call_target="tpu_custom_call" | custom-call | flops 536870912 | bytes 1048576 | tf_op jit(solution)/shard_map/msa_transition/pallas_call | solution.py:343
  17.2 2.1 %left_operand.1 = (bf16[336,128]{1,0:T(8,128)(2,1)S(1)}, bf16[336,128]{1,0:T(8,128)(2,1)S(1)}, bf16[336,128]{1,0:T(8,128)(2,1)S(1)}, bf16[336,128]{1,0:T(8,128)(...) custom-call(s32[2]{0:T(128)S(1)} %pad_add_fusion.where_ref, ...), custom_call_target="tpu_custom_call" | custom-call | flops 20000000000 | bytes 2097152 | tf_op jit(solution)/shard_map/left_operand/pallas_call | solution.py:409
  19.4 1.7 %collective-permute-start.2 = (bf16[336,128]{1,0:T(8,128)(2,1)S(1)}, bf16[336,128]{1,0:T(8,128)(2,1)S(1)}, u32[]{:S(2)}, u32[]{:S(2)}) collective-permute-start(bf16[336,128]{1,0:T(8,128)(2,1)S(1)} %get-tuple-element.22), channel_id=1, source_target_pairs={{0,16},{1,17},{2,18},{3,19},{4,20},{5,21},{6,22},{7,23},{8,24},{9,... | collective-permute-start | bytes 258056 | tf_op jit(solution)/shard_map/ppermute | solution.py:626
  21.0 1.5 %collective-permute-start.3 = (bf16[336,128]{1,0:T(8,128)(2,1)S(1)}, bf16[336,128]{1,0:T(8,128)(2,1)S(1)}, u32[]{:S(2)}, u32[]{:S(2)}) collective-permute-start(bf16[336,128]{1,0:T(8,128)(2,1)S(1)} %get-tuple-element.23), channel_id=1, source_target_pairs={{0,2},{1,3},{2,0},{3,1},{4,6},{5,7},{6,4},{7,5},{8,10},{9,11},{10,... | collective-permute-start | bytes 258056 | tf_op jit(solution)/shard_map/ppermute | solution.py:626
  22.5 4.9 %collective-permute-start.4 = (bf16[336,128]{1,0:T(8,128)(2,1)S(1)}, bf16[336,128]{1,0:T(8,128)(2,1)S(1)}, u32[]{:S(2)}, u32[]{:S(2)}) collective-permute-start(bf16[336,128]{1,0:T(8,128)(2,1)S(1)} %get-tuple-element.24), channel_id=1, source_target_pairs={{0,4},{1,5},{2,6},{3,7},{4,0},{5,1},{6,2},{7,3},{8,12},{9,13},{10,... | collective-permute-start | bytes 258056 | tf_op jit(solution)/shard_map/ppermute | solution.py:626
  27.5 2.8 %collective-permute-start.6 = (bf16[336,128]{1,0:T(8,128)(2,1)S(1)}, bf16[336,128]{1,0:T(8,128)(2,1)S(1)}, u32[]{:S(2)}, u32[]{:S(2)}) collective-permute-start(bf16[336,128]{1,0:T(8,128)(2,1)S(1)} %get-tuple-element.26), channel_id=1, source_target_pairs={{0,6},{1,7},{2,4},{3,5},{4,2},{5,3},{6,0},{7,1},{8,14},{9,15},{10,... | collective-permute-start | bytes 258056 | tf_op jit(solution)/shard_map/ppermute | solution.py:626
  30.3 1.0 %collective-permute-start.7 = (bf16[336,128]{1,0:T(8,128)(2,1)S(1)}, bf16[336,128]{1,0:T(8,128)(2,1)S(1)}, u32[]{:S(2)}, u32[]{:S(2)}) collective-permute-start(bf16[336,128]{1,0:T(8,128)(2,1)S(1)} %get-tuple-element.27), channel_id=1, source_target_pairs={{0,20},{1,21},{2,22},{3,23},{4,16},{5,17},{6,18},{7,19},{8,28},{9,... | collective-permute-start | bytes 258056 | tf_op jit(solution)/shard_map/ppermute | solution.py:626
  31.3 0.6 %collective-permute-start.8 = (bf16[336,128]{1,0:T(8,128)(2,1)S(1)}, bf16[336,128]{1,0:T(8,128)(2,1)S(1)}, u32[]{:S(2)}, u32[]{:S(2)}) collective-permute-start(bf16[336,128]{1,0:T(8,128)(2,1)S(1)} %get-tuple-element.28), channel_id=1, source_target_pairs={{0,18},{1,19},{2,16},{3,17},{4,22},{5,23},{6,20},{7,21},{8,26},{9,... | collective-permute-start | bytes 258056 | tf_op jit(solution)/shard_map/ppermute | solution.py:626
  32.0 1.5 %collective-permute-done.4.rest_3_ = bf16[336,128]{1,0:T(8,128)(2,1)S(1)} collective-permute-done((bf16[336,128]{1,0:T(8,128)(2,1)S(1)}, bf16[336,128]{1,0:T(8,128)(2,1)S(1)}, u32[]{:S(2)}, u32[]{:S(2)}) %collective-permute-start.4) | collective-permute-done | bytes 86048 | tf_op jit(solution)/shard_map/ppermute | solution.py:626
  33.4 3.6 %collective-permute-done.5.rest_4_ = bf16[336,128]{1,0:T(8,128)(2,1)S(1)} collective-permute-done((bf16[336,128]{1,0:T(8,128)(2,1)S(1)}, bf16[336,128]{1,0:T(8,128)(2,1)S(1)}, u32[]{:S(2)}, u32[]{:S(2)}) %collective-permute-start.5) | collective-permute-done | bytes 86048 | tf_op jit(solution)/shard_map/ppermute | solution.py:626
  37.0 2.6 %collective-permute-done.6.rest_5_ = bf16[336,128]{1,0:T(8,128)(2,1)S(1)} collective-permute-done((bf16[336,128]{1,0:T(8,128)(2,1)S(1)}, bf16[336,128]{1,0:T(8,128)(2,1)S(1)}, u32[]{:S(2)}, u32[]{:S(2)}) %collective-permute-start.6) | collective-permute-done | bytes 86048 | tf_op jit(solution)/shard_map/ppermute | solution.py:626
  39.7 0.7 %collective-permute-done.7.rest_6_ = bf16[336,128]{1,0:T(8,128)(2,1)S(1)} collective-permute-done((bf16[336,128]{1,0:T(8,128)(2,1)S(1)}, bf16[336,128]{1,0:T(8,128)(2,1)S(1)}, u32[]{:S(2)}, u32[]{:S(2)}) %collective-permute-start.7) | collective-permute-done | bytes 86048 | tf_op jit(solution)/shard_map/ppermute | solution.py:626
  40.4 1.7 %triangle_product.1 = bf16[16,8,16,128]{3,2,1,0:T(8,128)(2,1)} custom-call(s32[2]{0:T(128)S(1)} %pad_add_fusion.where_ref, bf16[32,8,16,128]{3,2,1,0:T(8,128)(2,1)S(1)} %all-to-all-done.in_ref, bf16[336,128]{1,0:T(8,128)(2,1)S(1)} %get-tuple-element.21.rest_0_, bf16[336,128]{1,0:T(8,128)(2,1)S(1)} %collective-permute-done.2.rest_1_, ...), custom_call_target="tpu_custom_call" | custom-call | flops 134217728 | bytes 2097152 | tf_op jit(solution)/shard_map/triangle_product/pallas_call | solution.py:493
  42.1 5.2 %all-to-all-start.1 = ((bf16[16,8,16,128]{3,2,1,0:T(8,128)(2,1)}), bf16[16,8,16,128]{3,2,1,0:T(8,128)(2,1)S(1)}, u32[]{:S(2)}, u32[]{:S(2)}) async-start(bf16[16,8,16,128]{3,2,1,0:T(8,128)(2,1)} %triangle_product.1), calls=%async_computation.1 | async-start | bytes 1048576 | tf_op jit(solution)/shard_map/all_to_all | solution.py:692
  47.4 0.0 copy-start.10
  47.4 0.1 collective-permute-start.9
  47.5 0.8 %triangle_output_gate.1.gate_ref = f32[16,128,128]{2,1,0:T(8,128)S(1)} custom-call(bf16[16,128,128]{2,1,0:T(8,128)(2,1)S(1)} %copy-done.2, bf16[128,640]{1,0:T(8,128)(2,1)S(1)} %copy-done.1), custom_call_target="tpu_custom_call" | custom-call | flops 67108864 | bytes 1572864 | tf_op jit(solution)/shard_map/triangle_output_gate/pallas_call | solution.py:431
  48.3 0.0 copy-start.4
  48.3 0.0 copy-start.5
  48.3 0.5 collective-permute-done.9.refs_1_
  48.8 0.9 %copy-done.7 = bf16[8,80,128]{2,1,0:T(8,128)(2,1)S(1)} copy-done((bf16[8,80,128]{2,1,0:T(8,128)(2,1)S(1)}, bf16[8,80,128]{2,1,0:T(8,128)(2,1)}, u32[]{:S(2)}) %copy-start.7) | copy-done | bytes 163864
  49.8 2.9 %outer_product_mean.1.outer_ref = f32[16,128,128]{2,1,0:T(8,128)S(1)} custom-call(s32[2]{0:T(128)S(1)} %pad_add_fusion.where_ref, bf16[8,80,128]{2,1,0:T(8,128)(2,1)S(1)} %copy-done.7, bf16[8,80,128]{2,1,0:T(8,128)(2,1)S(1)} %collective-permute-done.9.refs_1_, bf16[1024,128]{1,0:T(8,128)(2,1)S(1)} %copy-done.10), custom_call_target="tpu_custom_call" | custom-call | flops 1073741824 | bytes 1048576 | tf_op jit(solution)/shard_map/outer_product_mean/pallas_call | solution.py:607
  52.7 1.6 %all-to-all-done.1.p_ref = bf16[16,8,16,128]{3,2,1,0:T(8,128)(2,1)S(1)} async-done(((bf16[16,8,16,128]{3,2,1,0:T(8,128)(2,1)}), bf16[16,8,16,128]{3,2,1,0:T(8,128)(2,1)S(1)}, u32[]{:S(2)}, u32[]{:S(2)}) %all-to-all-start.1) | async-done | bytes 524320 | tf_op jit(solution)/shard_map/all_to_all | solution.py:692
  54.3 3.2 %pair_output.1 = bf16[16,128,128]{2,1,0:T(8,128)(2,1)} custom-call(bf16[16,8,16,128]{3,2,1,0:T(8,128)(2,1)S(1)} %all-to-all-done.1.p_ref, bf16[16,128,128]{2,1,0:T(8,128)(2,1)S(1)} %copy-done, f32[16,128,128]{2,1,0:T(8,128)S(1)} %triangle_output_gate.1.gate_ref, f32[16,128,128]{2,1,0:T(8,128)S(1)} %outer_product_mean.1.outer_ref, ...), custom_call_target="tpu_custom_call" | custom-call | flops 603979776 | bytes 3670016 | tf_op jit(solution)/shard_map/pair_output/pallas_call | solution.py:552
  (34 shorter events, 0.1 us)
Async XLA Ops:
  0.6 3.9 %copy-start.11 = (bf16[1,256,256]{2,1,0:T(8,128)(2,1)S(1)}, bf16[1,256,256]{2,1,0:T(8,128)(2,1)}, u32[]{:S(2)}) copy-start(bf16[1,256,256]{2,1,0:T(8,128)(2,1)} %seq_ref.1) | copy-start | bytes 393220
  4.0 13.2 %collective-permute-start.1 = (bf16[16,128,128]{2,1,0:T(8,128)(2,1)}, bf16[16,128,128]{2,1,0:T(8,128)(2,1)}, u32[]{:S(2)}, u32[]{:S(2)}) collective-permute-start(bf16[16,128,128]{2,1,0:T(8,128)(2,1)} %get-tuple-element.29.x_ref), channel_id=1, source_target_pairs={{0,1},{1,0},{2,3},{3,2},{4,5},{5,4},{6,7},{7,6},{8,9},{9,8},{10,11... | collective-permute-start | bytes 1572872 | tf_op jit(solution)/shard_map/ppermute | solution.py:626
  4.5 10.6 %collective-permute-start = (bf16[1,256,256]{2,1,0:T(8,128)(2,1)S(1)}, bf16[1,256,256]{2,1,0:T(8,128)(2,1)S(1)}, u32[]{:S(2)}, u32[]{:S(2)}) collective-permute-start(bf16[1,256,256]{2,1,0:T(8,128)(2,1)S(1)} %copy-done.11), channel_id=1, source_target_pairs={{0,8},{1,9},{2,10},{3,11},{4,12},{5,13},{6,14},{7,15},{8,0},{9,1},... | collective-permute-start | bytes 393224 | tf_op jit(solution)/shard_map/ppermute | solution.py:626
  8.2 6.9 %copy-start.8 = (bf16[256,1024]{1,0:T(8,128)(2,1)S(1)}, bf16[256,1024]{1,0:T(8,128)(2,1)}, u32[]{:S(2)}) copy-start(bf16[256,1024]{1,0:T(8,128)(2,1)} %up_ref.2) | copy-start | bytes 1572868
  8.2 6.9 %copy-start.9 = (bf16[1024,256]{1,0:T(8,128)(2,1)S(1)}, bf16[1024,256]{1,0:T(8,128)(2,1)}, u32[]{:S(2)}) copy-start(bf16[1024,256]{1,0:T(8,128)(2,1)} %down_ref.2) | copy-start | bytes 1572868
  8.2 6.9 %copy-start.12 = (bf16[256,64]{0,1:T(8,128)(2,1)S(1)}, bf16[256,64]{0,1:T(8,128)(2,1)}, u32[]{:S(2)}) copy-start(bf16[256,64]{0,1:T(8,128)(2,1)} %param.14) | copy-start | bytes 98308
  8.2 32.3 %all-to-all-start = ((bf16[32,8,16,128]{3,2,1,0:T(8,128)(2,1)}), bf16[32,8,16,128]{3,2,1,0:T(8,128)(2,1)S(1)}, u32[]{:S(2)}, u32[]{:S(2)}) async-start(bf16[32,8,16,128]{3,2,1,0:T(8,128)(2,1)} %get-tuple-element.17), calls=%async_computation | async-start | bytes 2097152 | tf_op jit(solution)/shard_map/all_to_all | solution.py:654
  15.1 2.1 %copy-start.1 = (bf16[128,640]{1,0:T(8,128)(2,1)S(1)}, bf16[128,640]{1,0:T(8,128)(2,1)}, u32[]{:S(2)}) copy-start(bf16[128,640]{1,0:T(8,128)(2,1)} %w_ref.4) | copy-start | bytes 491524
  15.1 2.1 %copy-start.2 = (bf16[16,128,128]{2,1,0:T(8,128)(2,1)S(1)}, bf16[16,128,128]{2,1,0:T(8,128)(2,1)}, u32[]{:S(2)}) copy-start(bf16[16,128,128]{2,1,0:T(8,128)(2,1)} %get-tuple-element.29.x_ref) | copy-start | bytes 1572868
  19.4 10.9 %collective-permute-start.2 = (bf16[336,128]{1,0:T(8,128)(2,1)S(1)}, bf16[336,128]{1,0:T(8,128)(2,1)S(1)}, u32[]{:S(2)}, u32[]{:S(2)}) collective-permute-start(bf16[336,128]{1,0:T(8,128)(2,1)S(1)} %get-tuple-element.22), channel_id=1, source_target_pairs={{0,16},{1,17},{2,18},{3,19},{4,20},{5,21},{6,22},{7,23},{8,24},{9,... | collective-permute-start | bytes 258056 | tf_op jit(solution)/shard_map/ppermute | solution.py:626
  21.0 10.3 %collective-permute-start.3 = (bf16[336,128]{1,0:T(8,128)(2,1)S(1)}, bf16[336,128]{1,0:T(8,128)(2,1)S(1)}, u32[]{:S(2)}, u32[]{:S(2)}) collective-permute-start(bf16[336,128]{1,0:T(8,128)(2,1)S(1)} %get-tuple-element.23), channel_id=1, source_target_pairs={{0,2},{1,3},{2,0},{3,1},{4,6},{5,7},{6,4},{7,5},{8,10},{9,11},{10,... | collective-permute-start | bytes 258056 | tf_op jit(solution)/shard_map/ppermute | solution.py:626
  22.5 10.9 %collective-permute-start.4 = (bf16[336,128]{1,0:T(8,128)(2,1)S(1)}, bf16[336,128]{1,0:T(8,128)(2,1)S(1)}, u32[]{:S(2)}, u32[]{:S(2)}) collective-permute-start(bf16[336,128]{1,0:T(8,128)(2,1)S(1)} %get-tuple-element.24), channel_id=1, source_target_pairs={{0,4},{1,5},{2,6},{3,7},{4,0},{5,1},{6,2},{7,3},{8,12},{9,13},{10,... | collective-permute-start | bytes 258056 | tf_op jit(solution)/shard_map/ppermute | solution.py:626
  27.5 9.6 %collective-permute-start.5 = (bf16[336,128]{1,0:T(8,128)(2,1)S(1)}, bf16[336,128]{1,0:T(8,128)(2,1)S(1)}, u32[]{:S(2)}, u32[]{:S(2)}) collective-permute-start(bf16[336,128]{1,0:T(8,128)(2,1)S(1)} %get-tuple-element.25), channel_id=1, source_target_pairs={{0,22},{1,23},{2,20},{3,21},{4,18},{5,19},{6,16},{7,17},{8,30},{9,... | collective-permute-start | bytes 258056 | tf_op jit(solution)/shard_map/ppermute | solution.py:626
  27.5 12.2 %collective-permute-start.6 = (bf16[336,128]{1,0:T(8,128)(2,1)S(1)}, bf16[336,128]{1,0:T(8,128)(2,1)S(1)}, u32[]{:S(2)}, u32[]{:S(2)}) collective-permute-start(bf16[336,128]{1,0:T(8,128)(2,1)S(1)} %get-tuple-element.26), channel_id=1, source_target_pairs={{0,6},{1,7},{2,4},{3,5},{4,2},{5,3},{6,0},{7,1},{8,14},{9,15},{10,... | collective-permute-start | bytes 258056 | tf_op jit(solution)/shard_map/ppermute | solution.py:626
  30.3 10.1 %collective-permute-start.7 = (bf16[336,128]{1,0:T(8,128)(2,1)S(1)}, bf16[336,128]{1,0:T(8,128)(2,1)S(1)}, u32[]{:S(2)}, u32[]{:S(2)}) collective-permute-start(bf16[336,128]{1,0:T(8,128)(2,1)S(1)} %get-tuple-element.27), channel_id=1, source_target_pairs={{0,20},{1,21},{2,22},{3,23},{4,16},{5,17},{6,18},{7,19},{8,28},{9,... | collective-permute-start | bytes 258056 | tf_op jit(solution)/shard_map/ppermute | solution.py:626
  31.3 9.1 %collective-permute-start.8 = (bf16[336,128]{1,0:T(8,128)(2,1)S(1)}, bf16[336,128]{1,0:T(8,128)(2,1)S(1)}, u32[]{:S(2)}, u32[]{:S(2)}) collective-permute-start(bf16[336,128]{1,0:T(8,128)(2,1)S(1)} %get-tuple-element.28), channel_id=1, source_target_pairs={{0,18},{1,19},{2,16},{3,17},{4,22},{5,23},{6,20},{7,21},{8,26},{9,... | collective-permute-start | bytes 258056 | tf_op jit(solution)/shard_map/ppermute | solution.py:626
  42.1 12.1 %all-to-all-start.1 = ((bf16[16,8,16,128]{3,2,1,0:T(8,128)(2,1)}), bf16[16,8,16,128]{3,2,1,0:T(8,128)(2,1)S(1)}, u32[]{:S(2)}, u32[]{:S(2)}) async-start(bf16[16,8,16,128]{3,2,1,0:T(8,128)(2,1)} %triangle_product.1), calls=%async_computation.1 | async-start | bytes 1048576 | tf_op jit(solution)/shard_map/all_to_all | solution.py:692
  47.4 0.9 %copy-start.6 = (bf16[8,80,128]{2,1,0:T(8,128)(2,1)}, bf16[8,80,128]{2,1,0:T(8,128)(2,1)S(1)}, u32[]{:S(2)}) copy-start(bf16[8,80,128]{2,1,0:T(8,128)(2,1)S(1)} %fusion.refs_0_) | copy-start | bytes 491524
  47.4 1.5 %copy-start.10 = (bf16[1024,128]{1,0:T(8,128)(2,1)S(1)}, bf16[1024,128]{1,0:T(8,128)(2,1)}, u32[]{:S(2)}) copy-start(bf16[1024,128]{1,0:T(8,128)(2,1)} %refs_2_.1) | copy-start | bytes 786436
  47.4 1.5 %collective-permute-start.9 = (bf16[8,80,128]{2,1,0:T(8,128)(2,1)S(1)}, bf16[8,80,128]{2,1,0:T(8,128)(2,1)S(1)}, u32[]{:S(2)}, u32[]{:S(2)}) collective-permute-start(bf16[8,80,128]{2,1,0:T(8,128)(2,1)S(1)} %fusion.refs_0_), channel_id=1, source_target_pairs={{0,1},{1,0},{2,3},{3,2},{4,5},{5,4},{6,7},{7,6},{8,9},{9,8},{10,11... | collective-permute-start | bytes 491528 | tf_op jit(solution)/shard_map/ppermute | solution.py:626
  48.3 6.0 %copy-start = (bf16[16,128,128]{2,1,0:T(8,128)(2,1)S(1)}, bf16[16,128,128]{2,1,0:T(8,128)(2,1)}, u32[]{:S(2)}) copy-start(bf16[16,128,128]{2,1,0:T(8,128)(2,1)} %x_ref.1) | copy-start | bytes 1572868
  48.3 6.0 %copy-start.3 = (bf16[128,512]{1,0:T(8,128)(2,1)S(1)}, bf16[128,512]{1,0:T(8,128)(2,1)}, u32[]{:S(2)}) copy-start(bf16[128,512]{1,0:T(8,128)(2,1)} %up_ref.3) | copy-start | bytes 393220
  48.3 6.0 %copy-start.4 = (bf16[512,128]{1,0:T(8,128)(2,1)S(1)}, bf16[512,128]{1,0:T(8,128)(2,1)}, u32[]{:S(2)}) copy-start(bf16[512,128]{1,0:T(8,128)(2,1)} %down_ref.3) | copy-start | bytes 393220
  48.3 5.9 %copy-start.5 = (bf16[128,128]{1,0:T(8,128)(2,1)S(1)}, bf16[128,128]{1,0:T(8,128)(2,1)}, u32[]{:S(2)}) copy-start(bf16[128,128]{1,0:T(8,128)(2,1)} %w_ref.5) | copy-start | bytes 98308
  48.8 0.9 %copy-start.7 = (bf16[8,80,128]{2,1,0:T(8,128)(2,1)S(1)}, bf16[8,80,128]{2,1,0:T(8,128)(2,1)}, u32[]{:S(2)}) copy-start(bf16[8,80,128]{2,1,0:T(8,128)(2,1)} %copy-done.6) | copy-start | bytes 491524

commit v7 on v6

--- a/solution.py
+++ b/solution.py
@@ -309,9 +309,69 @@
     )(x, w)
 
 
-def msa_kernel(
-    n_branch, rows, seq_ref, far_ref, up_ref, down_ref, factor_ref, fresh_ref, *side_refs
+def left_kernel(n_branch, near, where_ref, x_ref, other_ref, w_ref, out_ref, scr, norm_scr):
+    rows, _, chans = x_ref.shape
+    branch, row_at = where_ref[0], where_ref[1]
+    core = lax.bitwise_and(row_at, 1)
+    place = lax.shift_right_logical(lax.bitwise_and(row_at, near - 1), 1)
+    count = out_ref.shape[0]
+    places = count // n_branch
+    per = chans // (n_branch * near)
+
+    total = count * per
+    q = lax.broadcasted_iota(jnp.int32, (total, chans), 0)
+    t = q // per
+    group = lax.bitwise_xor(t // places, branch) * near + (
+        lax.bitwise_xor(t % places, place) * 2 + core
+    )
+    values, gates = channel_order(w_ref[...], (0, 1), group * per + q % per, total)
+
+    def store_at(at):
+        def store(i, block):
+            scr[at, pl.ds(i, total, stride=rows), :] = block
+
+        return store
+
+    gated_rows(values, gates, x_ref, store_at(core))
+    for i in range(0, rows, 4):
+        norm_scr[i : i + 4] = normed(other_ref[i : i + 4].astype(F32), -1)
+    gated_rows(values, gates, norm_scr, store_at(1 - core))
+    for t in range(count):
+        for c in range(per):
+            for k in range(2):
+                start = (t * per + c) * rows
+                out_ref[t, pl.ds((c * 2 + k) * rows, rows)] = scr[
+                    k, start : start + rows, :
+                ].astype(BF16)
+
+
+def left_operand(where, x, other, w, n_branch, near):
+    rows, width, chans = x.shape
+    count = n_branch * near // 2
+    per = chans // (n_branch * near)
+    return pl.pallas_call(
+        functools.partial(left_kernel, n_branch, near),
+        out_shape=jax.ShapeDtypeStruct((count, per * 2 * rows, width), BF16),
+        in_specs=[SMEM] + [VMEM] * 3,
+        out_specs=VMEM,
+        scratch_shapes=[
+            pltpu.VMEM((2, count * per * rows, width), F32),
+            pltpu.VMEM(x.shape, BF16),
+        ],
+        compiler_params=PARAMS,
+        cost_estimate=cost(4 * x.size * 2 * chans, x.size * 8),
+        name="left_operand",
+    )(where, x, other, w)
+
+
+def message_kernel(
+    n_branch, near, rows, where_ref, left_ref, seq_ref, far_ref, up_ref, down_ref, factor_ref,
+    fresh_ref, *rest
 ):
+    out_refs, (right_scr, left_scr) = rest[:-2], rest[-2:]
+    count, size, width = left_ref.shape
+    for t, out_ref in zip(TARGETS, out_refs):
+        out_ref[:size] = left_ref[t]
     x = [ref[0].astype(F32) for ref in (seq_ref, far_ref)]
     tokens = [normed(v, -1) for v in x]
     hidden = [jnp.maximum(dot(t, up_ref[...]).astype(BF16), 0.0) for t in tokens]
@@ -319,103 +379,42 @@
     fresh_ref[0] = fresh[0]
     factor = factor_ref[...]
     depth = factor.shape[0] // 2
-    for row, sides_ref in zip(fresh, side_refs):
-        tokens = normed(row.astype(F32), -1)
-        left = dot(tokens, factor[:depth], NT).astype(BF16)
-        right = dot(factor[depth:], tokens, NT).astype(BF16)
-        width = sides_ref.shape[1]
+    tokens = [normed(v.astype(F32), -1) for v in fresh]
+    for k, row in enumerate(tokens):
+        right = dot(factor[depth:], row, NT).astype(BF16)
         for b in range(n_branch):
-            sides_ref[b * depth : (b + 1) * depth] = right[:, b * width : (b + 1) * width]
-        tiles = left.reshape(-1, 2, rows, depth)
-        blank = jnp.zeros((rows, width - 2 * depth), BF16)
-        base = n_branch * depth
-        for t in range(tiles.shape[0]):
-            sides_ref[base + t * rows : base + (t + 1) * rows] = jnp.concatenate(
-                [tiles[t, 0], tiles[t, 1], blank], axis=1
-            )
-
-
-def msa(seq, far, up, down, factor, rows, width):
+            right_scr[b, k * depth : (k + 1) * depth] = right[:, b * width : (b + 1) * width]
+    tiles = [dot(row, factor[:depth], NT).astype(BF16).reshape(-1, 2, rows, depth) for row in tokens]
+    for t in range(left_scr.shape[0]):
+        left_scr[t] = jnp.concatenate([tile[t, c] for tile in tiles for c in range(2)], axis=1)
+    branch, row_at = where_ref[0], where_ref[1]
+    place = lax.shift_right_logical(lax.bitwise_and(row_at, near - 1), 1)
+    places = count // n_branch
+    first = row_at // near * places
+    for t, out_ref in zip(TARGETS, out_refs):
+        out_ref[size : size + 2 * depth] = right_scr[lax.bitwise_xor(branch, t // places)]
+        out_ref[size + 2 * depth :] = left_scr[first + lax.bitwise_xor(place, t % places)]
+
+
+def messages(where, left, seq, far, up, down, factor, rows, n_branch, near):
     _, length, feats = seq.shape
     depth = factor.shape[0] // 2
-    n_branch = length // width
-    sides = jax.ShapeDtypeStruct((n_branch * depth + length // 2, width), BF16)
-    return pl.pallas_call(
-        functools.partial(msa_kernel, n_branch, rows),
-        out_shape=[jax.ShapeDtypeStruct(seq.shape, BF16), sides, sides],
-        in_specs=[VMEM] * 5,
-        out_specs=[VMEM] * 3,
+    count, size, width = left.shape
+    piece = jax.ShapeDtypeStruct((size + 2 * depth + rows, width), BF16)
+    fresh, *pieces = pl.pallas_call(
+        functools.partial(message_kernel, n_branch, near, rows),
+        out_shape=[jax.ShapeDtypeStruct(seq.shape, BF16)] + [piece] * count,
+        in_specs=[SMEM] + [VMEM] * 6,
+        out_specs=[VMEM] * (1 + count),
+        scratch_shapes=[
+            pltpu.VMEM((n_branch, 2 * depth, width), BF16),
+            pltpu.VMEM((length // rows // 2, rows, width), BF16),
+        ],
         compiler_params=PARAMS,
-        cost_estimate=cost(8 * length * feats * up.shape[1], 4 * feats * up.shape[1]),
-        name="msa_transition",
-    )(seq, far, up, down, factor)
-
-
-def beside_kernel(
-    n_branch, near, where_ref, x_ref, other_ref, w_ref, sides_ref, far_ref, *rest
-):
-    out_refs, scr = rest[:-1], rest[-1]
-    rows, _, chans = x_ref.shape
-    branch, row_at = where_ref[0], where_ref[1]
-    core = lax.bitwise_and(row_at, 1)
-    place = lax.shift_right_logical(lax.bitwise_and(row_at, near - 1), 1)
-    half = row_at // near
-    count = len(out_refs)
-    places = count // n_branch
-    per = chans // (n_branch * near)
-
-    total = count * per
-    q = lax.broadcasted_iota(jnp.int32, (total, chans), 0)
-    t = q // per
-    group = lax.bitwise_xor(t // places, branch) * near + (
-        lax.bitwise_xor(t % places, place) * 2 + core
-    )
-    values, gates = channel_order(w_ref[...], (0, 1), group * per + q % per, total)
-
-    def store_at(at):
-        def store(i, block):
-            scr[at, pl.ds(i, total, stride=rows), :] = block
-
-        return store
-
-    gated_rows(values, gates, x_ref, store_at(core))
-    gated_rows(values, gates, other_ref, store_at(1 - core))
-    depth = (out_refs[0].shape[0] - per * 2 * rows - rows) // 2
-    base = per * 2 * rows
-    for t, out_ref in zip(TARGETS, out_refs):
-        for c in range(per):
-            for k in range(2):
-                start = (t * per + c) * rows
-                out_ref[pl.ds((c * 2 + k) * rows, rows)] = scr[k, start : start + rows, :].astype(
-                    BF16
-                )
-        b = lax.bitwise_xor(branch, t // places)
-        p = lax.bitwise_xor(place, t % places)
-        right = pl.ds(pl.multiple_of(b * depth, depth), depth)
-        start = n_branch * depth + (half * places + p) * rows
-        left = pl.ds(pl.multiple_of(start, rows), rows)
-        out_ref[base : base + depth] = sides_ref[right]
-        out_ref[base + depth : base + 2 * depth] = far_ref[right]
-        out_ref[base + 2 * depth :] = jnp.concatenate(
-            [sides_ref[left][:, : 2 * depth], far_ref[left][:, : 2 * depth]], axis=1
-        )
-
-
-def beside(where, x, other, w, sides, far_sides, depth, n_branch, near):
-    rows, width, chans = x.shape
-    count = n_branch * near // 2
-    per = chans // (n_branch * near)
-    piece = jax.ShapeDtypeStruct((per * 2 * rows + 2 * depth + rows, width), BF16)
-    return pl.pallas_call(
-        functools.partial(beside_kernel, n_branch, near),
-        out_shape=[piece] * count,
-        in_specs=[SMEM] + [VMEM] * 5,
-        out_specs=[VMEM] * count,
-        scratch_shapes=[pltpu.VMEM((2, count * per * rows, width), F32)],
-        compiler_params=PARAMS,
-        cost_estimate=cost(2 * 10**10, x.size * 8),
-        name="left_operand",
-    )(where, x, other, w, sides, far_sides)
+        cost_estimate=cost(2 * 10**10, 4 * feats * up.shape[1]),
+        name="msa_transition_and_messages",
+    )(where, left, seq, far, up, down, factor)
+    return fresh, pieces
 
 
 def gate_kernel(x_ref, w_ref, out_ref):
@@ -653,24 +652,17 @@
     )
     received = lax.all_to_all(sent, AXES, 0, 0, tiled=True)
 
-    other = swap(tokens, n_branch, n_rows, 1)
-    fresh, sides, far_sides = msa(
+    other = swap(pairwise_input, n_branch, n_rows, 1)
+    left = left_operand(where, tokens, other, triangle_projection_weight, n_branch, near)
+    fresh, pieces = messages(
+        where,
+        left,
         homolog_features,
         far_row,
         transition_expand_matrix,
         transition_contract_matrix,
         jnp.transpose(factor_pair_matrices),
         rows,
-        pairwise_input.shape[1],
-    )
-    pieces = beside(
-        where,
-        tokens,
-        other,
-        triangle_projection_weight,
-        sides,
-        far_sides,
-        factor_pair_matrices.shape[1] // 2,
         n_branch,
         near,
     )

time: 58.6 us -> 57.1 us (0.974); the launches traced: 57.5 us -> 56.8 us
  starting transfers between devices: 25.9 us -> 23.6 us
  waiting for transfers between devices: 13.5 us -> 14.9 us
    ppermute x10, starting transfers between devices: 16.9 us -> 14.9 us  [swap(): return lax.ppermute(x, AXES, [(d, d ^ mask) for d in range(count)])]
    ppermute x10, waiting for transfers between devices: 11.9 us -> 13.3 us  [swap(): return lax.ppermute(x, AXES, [(d, d ^ mask) for d in range(count)])]
  transfers between devices with their start and end apart: 12 -> 12, of which waited for: 7 -> 6; matrix products, arithmetic and copies ran while one was open for 0% -> 0% of each run, Pallas kernels for 14% -> 20%
where the time goes in v7:
time: 57.1 us; the launch traced here: 56.8 us
  starting transfers between devices  23.6 us (41%)
  Pallas kernels  16.2 us (28%)
  waiting for transfers between devices  14.9 us (26%)
  local copies, waits for them, and re-layouts  1.06 us (2%)
  between operations  0.87 us (2%)
    ppermute x10, starting transfers between devices, swap(): return lax.ppermute(x, AXES, [(d, d ^ mask) for d in range(count)])  14.9 us
    ppermute x10, waiting for transfers between devices, swap(): return lax.ppermute(x, AXES, [(d, d ^ mask) for d in range(count)])  13.3 us
    all_to_all x1, starting transfers between devices, own_channels_device(): lax.all_to_all(product, AXES, 0, 0, axis_index_groups=members, tiled=True)  4.89 us
    all_to_all x1, starting transfers between devices, own_channels_device(): received = lax.all_to_all(sent, AXES, 0, 0, tiled=True)  3.83 us
    pallas_call x1, Pallas kernels, right_operand(): pl.pallas_call(functools.partial(right_kernel, n_branch), out_shape=[jax....  3.28 us
    pallas_call x1, Pallas kernels, pair_output(): pl.pallas_call(pair_output_kernel, out_shape=jax.ShapeDtypeStruct(x.shape...  3.22 us
    pallas_call x1, Pallas kernels, outer_update(): pl.pallas_call(outer_kernel, out_shape=jax.ShapeDtypeStruct((rows, width,...  2.91 us
    pallas_call x1, Pallas kernels, messages(): pl.pallas_call(functools.partial(message_kernel, n_branch, near, rows), o...  2.55 us
  transfers between devices with their start and end apart: 12, of which 6 were waited for; matrix products, arithmetic and copies ran while one was open for 0% of the time, Pallas kernels for 20%

profile of v7, /device:TPU:0, one launch (start us, length us, event | category | flops | bytes accessed | tf_op | source)
XLA Modules:
  0.0 56.8 jit_solution(11994126859924364782)
XLA Ops:
  0.6 0.5 collective-permute-start
  1.1 3.7 %collective-permute-start.1 = (bf16[1,256,256]{2,1,0:T(8,128)(2,1)}, bf16[1,256,256]{2,1,0:T(8,128)(2,1)S(1)}, u32[]{:S(2)}, u32[]{:S(2)}) collective-permute-start(bf16[1,256,256]{2,1,0:T(8,128)(2,1)} %seq_ref.1), channel_id=1, source_target_pairs={{0,8},{1,9},{2,10},{3,11},{4,12},{5,13},{6,14},{7,15},{8,0},{9,1},... | collective-permute-start | bytes 393224 | tf_op jit(solution)/shard_map/ppermute | solution.py:625
  4.8 3.3 %right_operand.1 = (bf16[32,8,16,128]{3,2,1,0:T(8,128)(2,1)}, bf16[16,128,128]{2,1,0:T(8,128)(2,1)}) custom-call(bf16[16,128,128]{2,1,0:T(8,128)(2,1)} %x_ref.1, bf16[128,640]{1,0:T(8,128)(2,1)} %w_ref.4), custom_call_target="tpu_custom_call" | custom-call | flops 134217728 | bytes 1572864 | tf_op jit(solution)/shard_map/right_operand/pallas_call | solution.py:291
  8.1 0.0 copy-start.1
  8.1 0.0 copy-start.2
  8.1 3.8 %all-to-all-start = ((bf16[32,8,16,128]{3,2,1,0:T(8,128)(2,1)}), bf16[32,8,16,128]{3,2,1,0:T(8,128)(2,1)S(1)}, u32[]{:S(2)}, u32[]{:S(2)}) async-start(bf16[32,8,16,128]{3,2,1,0:T(8,128)(2,1)} %get-tuple-element.16), calls=%async_computation | async-start | bytes 2097152 | tf_op jit(solution)/shard_map/all_to_all | solution.py:653
  12.0 0.1 pad_add_fusion.where_ref
  12.1 0.0 copy-start.8
  12.1 0.0 copy-start.9
  12.1 1.8 %left_operand.1.left_ref = bf16[8,256,128]{2,1,0:T(8,128)(2,1)S(1)} custom-call(s32[2]{0:T(128)S(1)} %pad_add_fusion.where_ref, bf16[16,128,128]{2,1,0:T(8,128)(2,1)S(1)} %copy-done.1, bf16[16,128,128]{2,1,0:T(8,128)(2,1)S(1)} %collective-permute-done.other_ref, bf16[128,640]{1,0:T(8,128)(2,1)S(1)} %copy-done.2), custom_call_target="tpu_custom_call" | custom-call | flops 268435456 | bytes 2097152 | tf_op jit(solution)/shard_map/left_operand/pallas_call | solution.py:352
  13.9 2.5 %msa_transition_and_messages.1 = (bf16[1,256,256]{2,1,0:T(8,128)(2,1)}, bf16[336,128]{1,0:T(8,128)(2,1)S(1)}, bf16[336,128]{1,0:T(8,128)(2,1)S(1)}, bf16[336,128...) custom-call(s32[2]{0:T(128)S(1)} %pad_add_fusion.where_ref, ...), custom_call_target="tpu_custom_call" | custom-call | flops 20000000000 | bytes 1048576 | tf_op jit(solution)/shard_map/msa_transition_and_messages/pallas_call | solution.py:404
  16.5 1.8 %collective-permute-start.2 = (bf16[336,128]{1,0:T(8,128)(2,1)S(1)}, bf16[336,128]{1,0:T(8,128)(2,1)S(1)}, u32[]{:S(2)}, u32[]{:S(2)}) collective-permute-start(bf16[336,128]{1,0:T(8,128)(2,1)S(1)} %get-tuple-element.18), channel_id=1, source_target_pairs={{0,16},{1,17},{2,18},{3,19},{4,20},{5,21},{6,22},{7,23},{8,24},{9,... | collective-permute-start | bytes 258056 | tf_op jit(solution)/shard_map/ppermute | solution.py:625
  18.2 1.5 %collective-permute-start.3 = (bf16[336,128]{1,0:T(8,128)(2,1)S(1)}, bf16[336,128]{1,0:T(8,128)(2,1)S(1)}, u32[]{:S(2)}, u32[]{:S(2)}) collective-permute-start(bf16[336,128]{1,0:T(8,128)(2,1)S(1)} %get-tuple-element.19), channel_id=1, source_target_pairs={{0,2},{1,3},{2,0},{3,1},{4,6},{5,7},{6,4},{7,5},{8,10},{9,11},{10,... | collective-permute-start | bytes 258056 | tf_op jit(solution)/shard_map/ppermute | solution.py:625
  19.7 1.5 %collective-permute-start.4 = (bf16[336,128]{1,0:T(8,128)(2,1)S(1)}, bf16[336,128]{1,0:T(8,128)(2,1)S(1)}, u32[]{:S(2)}, u32[]{:S(2)}) collective-permute-start(bf16[336,128]{1,0:T(8,128)(2,1)S(1)} %get-tuple-element.20), channel_id=1, source_target_pairs={{0,4},{1,5},{2,6},{3,7},{4,0},{5,1},{6,2},{7,3},{8,12},{9,13},{10,... | collective-permute-start | bytes 258056 | tf_op jit(solution)/shard_map/ppermute | solution.py:625
  21.2 0.2 collective-permute-start.5
  21.4 2.7 %collective-permute-start.6 = (bf16[336,128]{1,0:T(8,128)(2,1)S(1)}, bf16[336,128]{1,0:T(8,128)(2,1)S(1)}, u32[]{:S(2)}, u32[]{:S(2)}) collective-permute-start(bf16[336,128]{1,0:T(8,128)(2,1)S(1)} %get-tuple-element.22), channel_id=1, source_target_pairs={{0,6},{1,7},{2,4},{3,5},{4,2},{5,3},{6,0},{7,1},{8,14},{9,15},{10,... | collective-permute-start | bytes 258056 | tf_op jit(solution)/shard_map/ppermute | solution.py:625
  24.1 1.5 %collective-permute-start.7 = (bf16[336,128]{1,0:T(8,128)(2,1)S(1)}, bf16[336,128]{1,0:T(8,128)(2,1)S(1)}, u32[]{:S(2)}, u32[]{:S(2)}) collective-permute-start(bf16[336,128]{1,0:T(8,128)(2,1)S(1)} %get-tuple-element.23), channel_id=1, source_target_pairs={{0,20},{1,21},{2,22},{3,23},{4,16},{5,17},{6,18},{7,19},{8,28},{9,... | collective-permute-start | bytes 258056 | tf_op jit(solution)/shard_map/ppermute | solution.py:625
  25.6 1.5 %collective-permute-start.8 = (bf16[336,128]{1,0:T(8,128)(2,1)S(1)}, bf16[336,128]{1,0:T(8,128)(2,1)S(1)}, u32[]{:S(2)}, u32[]{:S(2)}) collective-permute-start(bf16[336,128]{1,0:T(8,128)(2,1)S(1)} %get-tuple-element.24), channel_id=1, source_target_pairs={{0,18},{1,19},{2,16},{3,17},{4,22},{5,23},{6,20},{7,21},{8,26},{9,... | collective-permute-start | bytes 258056 | tf_op jit(solution)/shard_map/ppermute | solution.py:625
  27.1 4.8 %collective-permute-done.4.rest_3_ = bf16[336,128]{1,0:T(8,128)(2,1)S(1)} collective-permute-done((bf16[336,128]{1,0:T(8,128)(2,1)S(1)}, bf16[336,128]{1,0:T(8,128)(2,1)S(1)}, u32[]{:S(2)}, u32[]{:S(2)}) %collective-permute-start.4) | collective-permute-done | bytes 86048 | tf_op jit(solution)/shard_map/ppermute | solution.py:625
  31.9 2.2 %collective-permute-done.5.rest_4_ = bf16[336,128]{1,0:T(8,128)(2,1)S(1)} collective-permute-done((bf16[336,128]{1,0:T(8,128)(2,1)S(1)}, bf16[336,128]{1,0:T(8,128)(2,1)S(1)}, u32[]{:S(2)}, u32[]{:S(2)}) %collective-permute-start.5) | collective-permute-done | bytes 86048 | tf_op jit(solution)/shard_map/ppermute | solution.py:625
  34.1 3.7 %collective-permute-done.6.rest_5_ = bf16[336,128]{1,0:T(8,128)(2,1)S(1)} collective-permute-done((bf16[336,128]{1,0:T(8,128)(2,1)S(1)}, bf16[336,128]{1,0:T(8,128)(2,1)S(1)}, u32[]{:S(2)}, u32[]{:S(2)}) %collective-permute-start.6) | collective-permute-done | bytes 86048 | tf_op jit(solution)/shard_map/ppermute | solution.py:625
  37.8 2.2 %collective-permute-done.7.rest_6_ = bf16[336,128]{1,0:T(8,128)(2,1)S(1)} collective-permute-done((bf16[336,128]{1,0:T(8,128)(2,1)S(1)}, bf16[336,128]{1,0:T(8,128)(2,1)S(1)}, u32[]{:S(2)}, u32[]{:S(2)}) %collective-permute-start.7) | collective-permute-done | bytes 86048 | tf_op jit(solution)/shard_map/ppermute | solution.py:625
  40.0 1.7 %triangle_product.1 = bf16[16,8,16,128]{3,2,1,0:T(8,128)(2,1)} custom-call(s32[2]{0:T(128)S(1)} %pad_add_fusion.where_ref, bf16[32,8,16,128]{3,2,1,0:T(8,128)(2,1)S(1)} %all-to-all-done.in_ref, bf16[336,128]{1,0:T(8,128)(2,1)S(1)} %get-tuple-element.17.rest_0_, bf16[336,128]{1,0:T(8,128)(2,1)S(1)} %collective-permute-done.2.rest_1_, ...), custom_call_target="tpu_custom_call" | custom-call | flops 134217728 | bytes 2097152 | tf_op jit(solution)/shard_map/triangle_product/pallas_call | solution.py:492
  41.7 4.9 %all-to-all-start.1 = ((bf16[16,8,16,128]{3,2,1,0:T(8,128)(2,1)}), bf16[16,8,16,128]{3,2,1,0:T(8,128)(2,1)S(1)}, u32[]{:S(2)}, u32[]{:S(2)}) async-start(bf16[16,8,16,128]{3,2,1,0:T(8,128)(2,1)} %triangle_product.1), calls=%async_computation.1 | async-start | bytes 1048576 | tf_op jit(solution)/shard_map/all_to_all | solution.py:684
  46.7 0.1 collective-permute-start.9
  46.8 0.8 %triangle_output_gate.1.gate_ref = f32[16,128,128]{2,1,0:T(8,128)S(1)} custom-call(bf16[16,128,128]{2,1,0:T(8,128)(2,1)S(1)} %copy-done.1, bf16[128,640]{1,0:T(8,128)(2,1)S(1)} %copy-done.2), custom_call_target="tpu_custom_call" | custom-call | flops 67108864 | bytes 1572864 | tf_op jit(solution)/shard_map/triangle_output_gate/pallas_call | solution.py:430
  47.6 0.0 copy-start
  47.6 0.5 collective-permute-done.9.refs_1_
  48.1 0.9 %copy-done.7 = bf16[8,80,128]{2,1,0:T(8,128)(2,1)S(1)} copy-done((bf16[8,80,128]{2,1,0:T(8,128)(2,1)S(1)}, bf16[8,80,128]{2,1,0:T(8,128)(2,1)}, u32[]{:S(2)}) %copy-start.7) | copy-done | bytes 163864
  49.0 2.9 %outer_product_mean.1.outer_ref = f32[16,128,128]{2,1,0:T(8,128)S(1)} custom-call(s32[2]{0:T(128)S(1)} %pad_add_fusion.where_ref, bf16[8,80,128]{2,1,0:T(8,128)(2,1)S(1)} %copy-done.7, bf16[8,80,128]{2,1,0:T(8,128)(2,1)S(1)} %collective-permute-done.9.refs_1_, bf16[1024,128]{1,0:T(8,128)(2,1)S(1)} %copy-done.10), custom_call_target="tpu_custom_call" | custom-call | flops 1073741824 | bytes 1048576 | tf_op jit(solution)/shard_map/outer_product_mean/pallas_call | solution.py:606
  52.0 1.6 %all-to-all-done.1.p_ref = bf16[16,8,16,128]{3,2,1,0:T(8,128)(2,1)S(1)} async-done(((bf16[16,8,16,128]{3,2,1,0:T(8,128)(2,1)}), bf16[16,8,16,128]{3,2,1,0:T(8,128)(2,1)S(1)}, u32[]{:S(2)}, u32[]{:S(2)}) %all-to-all-start.1) | async-done | bytes 524320 | tf_op jit(solution)/shard_map/all_to_all | solution.py:684
  53.6 3.2 %pair_output.1 = bf16[16,128,128]{2,1,0:T(8,128)(2,1)} custom-call(bf16[16,8,16,128]{3,2,1,0:T(8,128)(2,1)S(1)} %all-to-all-done.1.p_ref, bf16[16,128,128]{2,1,0:T(8,128)(2,1)S(1)} %copy-done, f32[16,128,128]{2,1,0:T(8,128)S(1)} %triangle_output_gate.1.gate_ref, f32[16,128,128]{2,1,0:T(8,128)S(1)} %outer_product_mean.1.outer_ref, ...), custom_call_target="tpu_custom_call" | custom-call | flops 603979776 | bytes 3670016 | tf_op jit(solution)/shard_map/pair_output/pallas_call | solution.py:551
  (34 shorter events, 0.1 us)
Async XLA Ops:
  0.6 11.4 %collective-permute-start = (bf16[16,128,128]{2,1,0:T(8,128)(2,1)}, bf16[16,128,128]{2,1,0:T(8,128)(2,1)S(1)}, u32[]{:S(2)}, u32[]{:S(2)}) collective-permute-start(bf16[16,128,128]{2,1,0:T(8,128)(2,1)} %x_ref.1), channel_id=1, source_target_pairs={{0,1},{1,0},{2,3},{3,2},{4,5},{5,4},{6,7},{7,6},{8,9},{9,8},{10,11... | collective-permute-start | bytes 1572872 | tf_op jit(solution)/shard_map/ppermute | solution.py:625
  1.1 12.7 %collective-permute-start.1 = (bf16[1,256,256]{2,1,0:T(8,128)(2,1)}, bf16[1,256,256]{2,1,0:T(8,128)(2,1)S(1)}, u32[]{:S(2)}, u32[]{:S(2)}) collective-permute-start(bf16[1,256,256]{2,1,0:T(8,128)(2,1)} %seq_ref.1), channel_id=1, source_target_pairs={{0,8},{1,9},{2,10},{3,11},{4,12},{5,13},{6,14},{7,15},{8,0},{9,1},... | collective-permute-start | bytes 393224 | tf_op jit(solution)/shard_map/ppermute | solution.py:625
  8.1 3.9 %copy-start.1 = (bf16[16,128,128]{2,1,0:T(8,128)(2,1)S(1)}, bf16[16,128,128]{2,1,0:T(8,128)(2,1)}, u32[]{:S(2)}) copy-start(bf16[16,128,128]{2,1,0:T(8,128)(2,1)} %get-tuple-element.25.x_ref) | copy-start | bytes 1572868
  8.1 3.9 %copy-start.2 = (bf16[128,640]{1,0:T(8,128)(2,1)S(1)}, bf16[128,640]{1,0:T(8,128)(2,1)}, u32[]{:S(2)}) copy-start(bf16[128,640]{1,0:T(8,128)(2,1)} %w_ref.4) | copy-start | bytes 491524
  8.1 31.8 %all-to-all-start = ((bf16[32,8,16,128]{3,2,1,0:T(8,128)(2,1)}), bf16[32,8,16,128]{3,2,1,0:T(8,128)(2,1)S(1)}, u32[]{:S(2)}, u32[]{:S(2)}) async-start(bf16[32,8,16,128]{3,2,1,0:T(8,128)(2,1)} %get-tuple-element.16), calls=%async_computation | async-start | bytes 2097152 | tf_op jit(solution)/shard_map/all_to_all | solution.py:653
  12.1 1.8 %copy-start.8 = (bf16[256,1024]{1,0:T(8,128)(2,1)S(1)}, bf16[256,1024]{1,0:T(8,128)(2,1)}, u32[]{:S(2)}) copy-start(bf16[256,1024]{1,0:T(8,128)(2,1)} %up_ref.2) | copy-start | bytes 1572868
  12.1 1.8 %copy-start.9 = (bf16[1024,256]{1,0:T(8,128)(2,1)S(1)}, bf16[1024,256]{1,0:T(8,128)(2,1)}, u32[]{:S(2)}) copy-start(bf16[1024,256]{1,0:T(8,128)(2,1)} %down_ref.2) | copy-start | bytes 1572868
  12.1 1.8 %copy-start.11 = (bf16[1,256,256]{2,1,0:T(8,128)(2,1)S(1)}, bf16[1,256,256]{2,1,0:T(8,128)(2,1)}, u32[]{:S(2)}) copy-start(bf16[1,256,256]{2,1,0:T(8,128)(2,1)} %seq_ref.1) | copy-start | bytes 393220
  12.1 1.8 %copy-start.12 = (bf16[256,64]{0,1:T(8,128)(2,1)S(1)}, bf16[256,64]{0,1:T(8,128)(2,1)}, u32[]{:S(2)}) copy-start(bf16[256,64]{0,1:T(8,128)(2,1)} %param.14) | copy-start | bytes 98308
  16.5 7.6 %collective-permute-start.2 = (bf16[336,128]{1,0:T(8,128)(2,1)S(1)}, bf16[336,128]{1,0:T(8,128)(2,1)S(1)}, u32[]{:S(2)}, u32[]{:S(2)}) collective-permute-start(bf16[336,128]{1,0:T(8,128)(2,1)S(1)} %get-tuple-element.18), channel_id=1, source_target_pairs={{0,16},{1,17},{2,18},{3,19},{4,20},{5,21},{6,22},{7,23},{8,24},{9,... | collective-permute-start | bytes 258056 | tf_op jit(solution)/shard_map/ppermute | solution.py:625
  18.2 7.3 %collective-permute-start.3 = (bf16[336,128]{1,0:T(8,128)(2,1)S(1)}, bf16[336,128]{1,0:T(8,128)(2,1)S(1)}, u32[]{:S(2)}, u32[]{:S(2)}) collective-permute-start(bf16[336,128]{1,0:T(8,128)(2,1)S(1)} %get-tuple-element.19), channel_id=1, source_target_pairs={{0,2},{1,3},{2,0},{3,1},{4,6},{5,7},{6,4},{7,5},{8,10},{9,11},{10,... | collective-permute-start | bytes 258056 | tf_op jit(solution)/shard_map/ppermute | solution.py:625
  19.7 12.2 %collective-permute-start.4 = (bf16[336,128]{1,0:T(8,128)(2,1)S(1)}, bf16[336,128]{1,0:T(8,128)(2,1)S(1)}, u32[]{:S(2)}, u32[]{:S(2)}) collective-permute-start(bf16[336,128]{1,0:T(8,128)(2,1)S(1)} %get-tuple-element.20), channel_id=1, source_target_pairs={{0,4},{1,5},{2,6},{3,7},{4,0},{5,1},{6,2},{7,3},{8,12},{9,13},{10,... | collective-permute-start | bytes 258056 | tf_op jit(solution)/shard_map/ppermute | solution.py:625
  21.2 12.9 %collective-permute-start.5 = (bf16[336,128]{1,0:T(8,128)(2,1)S(1)}, bf16[336,128]{1,0:T(8,128)(2,1)S(1)}, u32[]{:S(2)}, u32[]{:S(2)}) collective-permute-start(bf16[336,128]{1,0:T(8,128)(2,1)S(1)} %get-tuple-element.21), channel_id=1, source_target_pairs={{0,22},{1,23},{2,20},{3,21},{4,18},{5,19},{6,16},{7,17},{8,30},{9,... | collective-permute-start | bytes 258056 | tf_op jit(solution)/shard_map/ppermute | solution.py:625
  21.4 16.4 %collective-permute-start.6 = (bf16[336,128]{1,0:T(8,128)(2,1)S(1)}, bf16[336,128]{1,0:T(8,128)(2,1)S(1)}, u32[]{:S(2)}, u32[]{:S(2)}) collective-permute-start(bf16[336,128]{1,0:T(8,128)(2,1)S(1)} %get-tuple-element.22), channel_id=1, source_target_pairs={{0,6},{1,7},{2,4},{3,5},{4,2},{5,3},{6,0},{7,1},{8,14},{9,15},{10,... | collective-permute-start | bytes 258056 | tf_op jit(solution)/shard_map/ppermute | solution.py:625
  24.1 15.9 %collective-permute-start.7 = (bf16[336,128]{1,0:T(8,128)(2,1)S(1)}, bf16[336,128]{1,0:T(8,128)(2,1)S(1)}, u32[]{:S(2)}, u32[]{:S(2)}) collective-permute-start(bf16[336,128]{1,0:T(8,128)(2,1)S(1)} %get-tuple-element.23), channel_id=1, source_target_pairs={{0,20},{1,21},{2,22},{3,23},{4,16},{5,17},{6,18},{7,19},{8,28},{9,... | collective-permute-start | bytes 258056 | tf_op jit(solution)/shard_map/ppermute | solution.py:625
  25.6 14.4 %collective-permute-start.8 = (bf16[336,128]{1,0:T(8,128)(2,1)S(1)}, bf16[336,128]{1,0:T(8,128)(2,1)S(1)}, u32[]{:S(2)}, u32[]{:S(2)}) collective-permute-start(bf16[336,128]{1,0:T(8,128)(2,1)S(1)} %get-tuple-element.24), channel_id=1, source_target_pairs={{0,18},{1,19},{2,16},{3,17},{4,22},{5,23},{6,20},{7,21},{8,26},{9,... | collective-permute-start | bytes 258056 | tf_op jit(solution)/shard_map/ppermute | solution.py:625
  41.7 11.8 %all-to-all-start.1 = ((bf16[16,8,16,128]{3,2,1,0:T(8,128)(2,1)}), bf16[16,8,16,128]{3,2,1,0:T(8,128)(2,1)S(1)}, u32[]{:S(2)}, u32[]{:S(2)}) async-start(bf16[16,8,16,128]{3,2,1,0:T(8,128)(2,1)} %triangle_product.1), calls=%async_computation.1 | async-start | bytes 1048576 | tf_op jit(solution)/shard_map/all_to_all | solution.py:684
  46.6 0.9 %copy-start.6 = (bf16[8,80,128]{2,1,0:T(8,128)(2,1)}, bf16[8,80,128]{2,1,0:T(8,128)(2,1)S(1)}, u32[]{:S(2)}) copy-start(bf16[8,80,128]{2,1,0:T(8,128)(2,1)S(1)} %fusion.refs_0_) | copy-start | bytes 491524
  46.6 1.5 %copy-start.10 = (bf16[1024,128]{1,0:T(8,128)(2,1)S(1)}, bf16[1024,128]{1,0:T(8,128)(2,1)}, u32[]{:S(2)}) copy-start(bf16[1024,128]{1,0:T(8,128)(2,1)} %refs_2_.1) | copy-start | bytes 786436
  46.7 1.5 %collective-permute-start.9 = (bf16[8,80,128]{2,1,0:T(8,128)(2,1)S(1)}, bf16[8,80,128]{2,1,0:T(8,128)(2,1)S(1)}, u32[]{:S(2)}, u32[]{:S(2)}) collective-permute-start(bf16[8,80,128]{2,1,0:T(8,128)(2,1)S(1)} %fusion.refs_0_), channel_id=1, source_target_pairs={{0,1},{1,0},{2,3},{3,2},{4,5},{5,4},{6,7},{7,6},{8,9},{9,8},{10,11... | collective-permute-start | bytes 491528 | tf_op jit(solution)/shard_map/ppermute | solution.py:625
  47.6 6.0 %copy-start = (bf16[16,128,128]{2,1,0:T(8,128)(2,1)S(1)}, bf16[16,128,128]{2,1,0:T(8,128)(2,1)}, u32[]{:S(2)}) copy-start(bf16[16,128,128]{2,1,0:T(8,128)(2,1)} %x_ref.1) | copy-start | bytes 1572868
  47.6 6.0 %copy-start.3 = (bf16[128,512]{1,0:T(8,128)(2,1)S(1)}, bf16[128,512]{1,0:T(8,128)(2,1)}, u32[]{:S(2)}) copy-start(bf16[128,512]{1,0:T(8,128)(2,1)} %up_ref.3) | copy-start | bytes 393220
  47.6 6.0 %copy-start.4 = (bf16[512,128]{1,0:T(8,128)(2,1)S(1)}, bf16[512,128]{1,0:T(8,128)(2,1)}, u32[]{:S(2)}) copy-start(bf16[512,128]{1,0:T(8,128)(2,1)} %down_ref.3) | copy-start | bytes 393220
  47.6 6.0 %copy-start.5 = (bf16[128,128]{1,0:T(8,128)(2,1)S(1)}, bf16[128,128]{1,0:T(8,128)(2,1)}, u32[]{:S(2)}) copy-start(bf16[128,128]{1,0:T(8,128)(2,1)} %w_ref.5) | copy-start | bytes 98308
  48.1 0.9 %copy-start.7 = (bf16[8,80,128]{2,1,0:T(8,128)(2,1)S(1)}, bf16[8,80,128]{2,1,0:T(8,128)(2,1)}, u32[]{:S(2)}) copy-start(bf16[8,80,128]{2,1,0:T(8,128)(2,1)} %copy-done.6) | copy-start | bytes 491524

commit v8 on v7

--- a/solution.py
+++ b/solution.py
@@ -510,15 +510,14 @@
     shape = (step * width, chans)
     share = up_ref.shape[1] // 4
 
-    def place(i):
-        for g in range(devices):
-            for c in range(per):
-                tile = p_ref[devices - 1 - g, c].astype(F32)[i : i + step]
-                scr[pl.ds(i * chans + g * per + c, step, stride=chans), :] = tile
+    for g in range(devices):
+        for c in range(per):
+            k = (g * per + c) * rows
+            scr[k : k + rows, :] = p_ref[devices - 1 - g, c].astype(F32)
 
     def triangle(i):
         parts = [
-            normed(scr[(i + k) * chans : (i + k + 1) * chans, :], 0) for k in range(step)
+            normed(scr[pl.ds(i + k, chans, stride=rows), :], 0) for k in range(step)
         ]
         update = dot(jnp.concatenate(parts, axis=1), w_ref[...], TN)
         x = x_ref[i : i + step].astype(F32).reshape(shape)
@@ -536,10 +535,7 @@
         copy.start()
         return copy
 
-    middles = []
-    for i in range(0, rows, step):
-        place(i)
-        middles.append(triangle(i))
+    middles = [triangle(i) for i in range(0, rows, step)]
     copies = [transition(i * step, *middle) for i, middle in enumerate(middles)]
     for copy in copies:
         copy.wait()

time: 57.1 us -> 56.8 us (level)
  no operation moved by 1% of the time
where the time goes in v8:
time: 56.8 us; the launch traced here: 56.5 us
  starting transfers between devices  23.6 us (42%)
  Pallas kernels  15.9 us (28%)
  waiting for transfers between devices  14.9 us (26%)
  local copies, waits for them, and re-layouts  1.06 us (2%)
  between operations  0.87 us (2%)
    ppermute x10, starting transfers between devices, swap(): return lax.ppermute(x, AXES, [(d, d ^ mask) for d in range(count)])  14.9 us
    ppermute x10, waiting for transfers between devices, swap(): return lax.ppermute(x, AXES, [(d, d ^ mask) for d in range(count)])  13.3 us
    all_to_all x1, starting transfers between devices, own_channels_device(): lax.all_to_all(product, AXES, 0, 0, axis_index_groups=members, tiled=True)  4.89 us
    all_to_all x1, starting transfers between devices, own_channels_device(): received = lax.all_to_all(sent, AXES, 0, 0, tiled=True)  3.83 us
    pallas_call x1, Pallas kernels, right_operand(): pl.pallas_call(functools.partial(right_kernel, n_branch), out_shape=[jax....  3.28 us
    pallas_call x1, Pallas kernels, pair_output(): pl.pallas_call(pair_output_kernel, out_shape=jax.ShapeDtypeStruct(x.shape...  2.93 us
    pallas_call x1, Pallas kernels, outer_update(): pl.pallas_call(outer_kernel, out_shape=jax.ShapeDtypeStruct((rows, width,...  2.91 us
    pallas_call x1, Pallas kernels, messages(): pl.pallas_call(functools.partial(message_kernel, n_branch, near, rows), o...  2.55 us
  transfers between devices with their start and end apart: 12, of which 6 were waited for; matrix products, arithmetic and copies ran while one was open for 0% of the time, Pallas kernels for 20%

profile of v8, /device:TPU:0, one launch (start us, length us, event | category | flops | bytes accessed | tf_op | source)
XLA Modules:
  0.0 56.5 jit_solution(15437536395617425052)
XLA Ops:
  0.6 0.5 collective-permute-start
  1.1 3.7 %collective-permute-start.1 = (bf16[1,256,256]{2,1,0:T(8,128)(2,1)}, bf16[1,256,256]{2,1,0:T(8,128)(2,1)S(1)}, u32[]{:S(2)}, u32[]{:S(2)}) collective-permute-start(bf16[1,256,256]{2,1,0:T(8,128)(2,1)} %seq_ref.1), channel_id=1, source_target_pairs={{0,8},{1,9},{2,10},{3,11},{4,12},{5,13},{6,14},{7,15},{8,0},{9,1},... | collective-permute-start | bytes 393224 | tf_op jit(solution)/shard_map/ppermute | solution.py:621
  4.8 3.3 %right_operand.1 = (bf16[32,8,16,128]{3,2,1,0:T(8,128)(2,1)}, bf16[16,128,128]{2,1,0:T(8,128)(2,1)}) custom-call(bf16[16,128,128]{2,1,0:T(8,128)(2,1)} %x_ref.1, bf16[128,640]{1,0:T(8,128)(2,1)} %w_ref.4), custom_call_target="tpu_custom_call" | custom-call | flops 134217728 | bytes 1572864 | tf_op jit(solution)/shard_map/right_operand/pallas_call | solution.py:291
  8.1 0.0 copy-start.2
  8.1 3.8 %all-to-all-start = ((bf16[32,8,16,128]{3,2,1,0:T(8,128)(2,1)}), bf16[32,8,16,128]{3,2,1,0:T(8,128)(2,1)S(1)}, u32[]{:S(2)}, u32[]{:S(2)}) async-start(bf16[32,8,16,128]{3,2,1,0:T(8,128)(2,1)} %get-tuple-element.16), calls=%async_computation | async-start | bytes 2097152 | tf_op jit(solution)/shard_map/all_to_all | solution.py:649
  12.0 0.1 pad_add_fusion.where_ref
  12.1 0.0 copy-start.11
  12.1 0.0 copy-start.12
  12.1 1.8 %left_operand.1.left_ref = bf16[8,256,128]{2,1,0:T(8,128)(2,1)S(1)} custom-call(s32[2]{0:T(128)S(1)} %pad_add_fusion.where_ref, bf16[16,128,128]{2,1,0:T(8,128)(2,1)S(1)} %copy-done.1, bf16[16,128,128]{2,1,0:T(8,128)(2,1)S(1)} %collective-permute-done.other_ref, bf16[128,640]{1,0:T(8,128)(2,1)S(1)} %copy-done.2), custom_call_target="tpu_custom_call" | custom-call | flops 268435456 | bytes 2097152 | tf_op jit(solution)/shard_map/left_operand/pallas_call | solution.py:352
  13.9 2.5 %msa_transition_and_messages.1 = (bf16[1,256,256]{2,1,0:T(8,128)(2,1)}, bf16[336,128]{1,0:T(8,128)(2,1)S(1)}, bf16[336,128]{1,0:T(8,128)(2,1)S(1)}, bf16[336,128...) custom-call(s32[2]{0:T(128)S(1)} %pad_add_fusion.where_ref, ...), custom_call_target="tpu_custom_call" | custom-call | flops 20000000000 | bytes 1048576 | tf_op jit(solution)/shard_map/msa_transition_and_messages/pallas_call | solution.py:404
  16.5 1.8 %collective-permute-start.2 = (bf16[336,128]{1,0:T(8,128)(2,1)S(1)}, bf16[336,128]{1,0:T(8,128)(2,1)S(1)}, u32[]{:S(2)}, u32[]{:S(2)}) collective-permute-start(bf16[336,128]{1,0:T(8,128)(2,1)S(1)} %get-tuple-element.18), channel_id=1, source_target_pairs={{0,16},{1,17},{2,18},{3,19},{4,20},{5,21},{6,22},{7,23},{8,24},{9,... | collective-permute-start | bytes 258056 | tf_op jit(solution)/shard_map/ppermute | solution.py:621
  18.2 1.5 %collective-permute-start.3 = (bf16[336,128]{1,0:T(8,128)(2,1)S(1)}, bf16[336,128]{1,0:T(8,128)(2,1)S(1)}, u32[]{:S(2)}, u32[]{:S(2)}) collective-permute-start(bf16[336,128]{1,0:T(8,128)(2,1)S(1)} %get-tuple-element.19), channel_id=1, source_target_pairs={{0,2},{1,3},{2,0},{3,1},{4,6},{5,7},{6,4},{7,5},{8,10},{9,11},{10,... | collective-permute-start | bytes 258056 | tf_op jit(solution)/shard_map/ppermute | solution.py:621
  19.7 1.5 %collective-permute-start.4 = (bf16[336,128]{1,0:T(8,128)(2,1)S(1)}, bf16[336,128]{1,0:T(8,128)(2,1)S(1)}, u32[]{:S(2)}, u32[]{:S(2)}) collective-permute-start(bf16[336,128]{1,0:T(8,128)(2,1)S(1)} %get-tuple-element.20), channel_id=1, source_target_pairs={{0,4},{1,5},{2,6},{3,7},{4,0},{5,1},{6,2},{7,3},{8,12},{9,13},{10,... | collective-permute-start | bytes 258056 | tf_op jit(solution)/shard_map/ppermute | solution.py:621
  21.2 0.2 collective-permute-start.5
  21.4 2.7 %collective-permute-start.6 = (bf16[336,128]{1,0:T(8,128)(2,1)S(1)}, bf16[336,128]{1,0:T(8,128)(2,1)S(1)}, u32[]{:S(2)}, u32[]{:S(2)}) collective-permute-start(bf16[336,128]{1,0:T(8,128)(2,1)S(1)} %get-tuple-element.22), channel_id=1, source_target_pairs={{0,6},{1,7},{2,4},{3,5},{4,2},{5,3},{6,0},{7,1},{8,14},{9,15},{10,... | collective-permute-start | bytes 258056 | tf_op jit(solution)/shard_map/ppermute | solution.py:621
  24.1 1.5 %collective-permute-start.7 = (bf16[336,128]{1,0:T(8,128)(2,1)S(1)}, bf16[336,128]{1,0:T(8,128)(2,1)S(1)}, u32[]{:S(2)}, u32[]{:S(2)}) collective-permute-start(bf16[336,128]{1,0:T(8,128)(2,1)S(1)} %get-tuple-element.23), channel_id=1, source_target_pairs={{0,20},{1,21},{2,22},{3,23},{4,16},{5,17},{6,18},{7,19},{8,28},{9,... | collective-permute-start | bytes 258056 | tf_op jit(solution)/shard_map/ppermute | solution.py:621
  25.6 1.5 %collective-permute-start.8 = (bf16[336,128]{1,0:T(8,128)(2,1)S(1)}, bf16[336,128]{1,0:T(8,128)(2,1)S(1)}, u32[]{:S(2)}, u32[]{:S(2)}) collective-permute-start(bf16[336,128]{1,0:T(8,128)(2,1)S(1)} %get-tuple-element.24), channel_id=1, source_target_pairs={{0,18},{1,19},{2,16},{3,17},{4,22},{5,23},{6,20},{7,21},{8,26},{9,... | collective-permute-start | bytes 258056 | tf_op jit(solution)/shard_map/ppermute | solution.py:621
  27.1 4.8 %collective-permute-done.4.rest_3_ = bf16[336,128]{1,0:T(8,128)(2,1)S(1)} collective-permute-done((bf16[336,128]{1,0:T(8,128)(2,1)S(1)}, bf16[336,128]{1,0:T(8,128)(2,1)S(1)}, u32[]{:S(2)}, u32[]{:S(2)}) %collective-permute-start.4) | collective-permute-done | bytes 86048 | tf_op jit(solution)/shard_map/ppermute | solution.py:621
  31.9 2.2 %collective-permute-done.5.rest_4_ = bf16[336,128]{1,0:T(8,128)(2,1)S(1)} collective-permute-done((bf16[336,128]{1,0:T(8,128)(2,1)S(1)}, bf16[336,128]{1,0:T(8,128)(2,1)S(1)}, u32[]{:S(2)}, u32[]{:S(2)}) %collective-permute-start.5) | collective-permute-done | bytes 86048 | tf_op jit(solution)/shard_map/ppermute | solution.py:621
  34.1 3.7 %collective-permute-done.6.rest_5_ = bf16[336,128]{1,0:T(8,128)(2,1)S(1)} collective-permute-done((bf16[336,128]{1,0:T(8,128)(2,1)S(1)}, bf16[336,128]{1,0:T(8,128)(2,1)S(1)}, u32[]{:S(2)}, u32[]{:S(2)}) %collective-permute-start.6) | collective-permute-done | bytes 86048 | tf_op jit(solution)/shard_map/ppermute | solution.py:621
  37.8 2.2 %collective-permute-done.7.rest_6_ = bf16[336,128]{1,0:T(8,128)(2,1)S(1)} collective-permute-done((bf16[336,128]{1,0:T(8,128)(2,1)S(1)}, bf16[336,128]{1,0:T(8,128)(2,1)S(1)}, u32[]{:S(2)}, u32[]{:S(2)}) %collective-permute-start.7) | collective-permute-done | bytes 86048 | tf_op jit(solution)/shard_map/ppermute | solution.py:621
  40.0 1.7 %triangle_product.1 = bf16[16,8,16,128]{3,2,1,0:T(8,128)(2,1)} custom-call(s32[2]{0:T(128)S(1)} %pad_add_fusion.where_ref, bf16[32,8,16,128]{3,2,1,0:T(8,128)(2,1)S(1)} %all-to-all-done.in_ref, bf16[336,128]{1,0:T(8,128)(2,1)S(1)} %get-tuple-element.17.rest_0_, bf16[336,128]{1,0:T(8,128)(2,1)S(1)} %collective-permute-done.2.rest_1_, ...), custom_call_target="tpu_custom_call" | custom-call | flops 134217728 | bytes 2097152 | tf_op jit(solution)/shard_map/triangle_product/pallas_call | solution.py:492
  41.7 4.9 %all-to-all-start.1 = ((bf16[16,8,16,128]{3,2,1,0:T(8,128)(2,1)}), bf16[16,8,16,128]{3,2,1,0:T(8,128)(2,1)S(1)}, u32[]{:S(2)}, u32[]{:S(2)}) async-start(bf16[16,8,16,128]{3,2,1,0:T(8,128)(2,1)} %triangle_product.1), calls=%async_computation.1 | async-start | bytes 1048576 | tf_op jit(solution)/shard_map/all_to_all | solution.py:680
  46.6 0.0 copy-start.10
  46.7 0.1 collective-permute-start.9
  46.8 0.8 %triangle_output_gate.1.gate_ref = f32[16,128,128]{2,1,0:T(8,128)S(1)} custom-call(bf16[16,128,128]{2,1,0:T(8,128)(2,1)S(1)} %copy-done.1, bf16[128,640]{1,0:T(8,128)(2,1)S(1)} %copy-done.2), custom_call_target="tpu_custom_call" | custom-call | flops 67108864 | bytes 1572864 | tf_op jit(solution)/shard_map/triangle_output_gate/pallas_call | solution.py:430
  47.6 0.0 copy-start.3
  47.6 0.5 collective-permute-done.9.refs_1_
  48.1 0.9 %copy-done.7 = bf16[8,80,128]{2,1,0:T(8,128)(2,1)S(1)} copy-done((bf16[8,80,128]{2,1,0:T(8,128)(2,1)S(1)}, bf16[8,80,128]{2,1,0:T(8,128)(2,1)}, u32[]{:S(2)}) %copy-start.7) | copy-done | bytes 163864
  49.0 2.9 %outer_product_mean.1.outer_ref = f32[16,128,128]{2,1,0:T(8,128)S(1)} custom-call(s32[2]{0:T(128)S(1)} %pad_add_fusion.where_ref, bf16[8,80,128]{2,1,0:T(8,128)(2,1)S(1)} %copy-done.7, bf16[8,80,128]{2,1,0:T(8,128)(2,1)S(1)} %collective-permute-done.9.refs_1_, bf16[1024,128]{1,0:T(8,128)(2,1)S(1)} %copy-done.10), custom_call_target="tpu_custom_call" | custom-call | flops 1073741824 | bytes 1048576 | tf_op jit(solution)/shard_map/outer_product_mean/pallas_call | solution.py:602
  52.0 1.6 %all-to-all-done.1.p_ref = bf16[16,8,16,128]{3,2,1,0:T(8,128)(2,1)S(1)} async-done(((bf16[16,8,16,128]{3,2,1,0:T(8,128)(2,1)}), bf16[16,8,16,128]{3,2,1,0:T(8,128)(2,1)S(1)}, u32[]{:S(2)}, u32[]{:S(2)}) %all-to-all-start.1) | async-done | bytes 524320 | tf_op jit(solution)/shard_map/all_to_all | solution.py:680
  53.6 2.9 %pair_output.1 = bf16[16,128,128]{2,1,0:T(8,128)(2,1)} custom-call(bf16[16,8,16,128]{3,2,1,0:T(8,128)(2,1)S(1)} %all-to-all-done.1.p_ref, bf16[16,128,128]{2,1,0:T(8,128)(2,1)S(1)} %copy-done, f32[16,128,128]{2,1,0:T(8,128)S(1)} %triangle_output_gate.1.gate_ref, f32[16,128,128]{2,1,0:T(8,128)S(1)} %outer_product_mean.1.outer_ref, ...), custom_call_target="tpu_custom_call" | custom-call | flops 603979776 | bytes 3670016 | tf_op jit(solution)/shard_map/pair_output/pallas_call | solution.py:547
  (34 shorter events, 0.1 us)
Async XLA Ops:
  0.6 11.4 %collective-permute-start = (bf16[16,128,128]{2,1,0:T(8,128)(2,1)}, bf16[16,128,128]{2,1,0:T(8,128)(2,1)S(1)}, u32[]{:S(2)}, u32[]{:S(2)}) collective-permute-start(bf16[16,128,128]{2,1,0:T(8,128)(2,1)} %x_ref.1), channel_id=1, source_target_pairs={{0,1},{1,0},{2,3},{3,2},{4,5},{5,4},{6,7},{7,6},{8,9},{9,8},{10,11... | collective-permute-start | bytes 1572872 | tf_op jit(solution)/shard_map/ppermute | solution.py:621
  1.1 12.7 %collective-permute-start.1 = (bf16[1,256,256]{2,1,0:T(8,128)(2,1)}, bf16[1,256,256]{2,1,0:T(8,128)(2,1)S(1)}, u32[]{:S(2)}, u32[]{:S(2)}) collective-permute-start(bf16[1,256,256]{2,1,0:T(8,128)(2,1)} %seq_ref.1), channel_id=1, source_target_pairs={{0,8},{1,9},{2,10},{3,11},{4,12},{5,13},{6,14},{7,15},{8,0},{9,1},... | collective-permute-start | bytes 393224 | tf_op jit(solution)/shard_map/ppermute | solution.py:621
  8.1 3.9 %copy-start.1 = (bf16[16,128,128]{2,1,0:T(8,128)(2,1)S(1)}, bf16[16,128,128]{2,1,0:T(8,128)(2,1)}, u32[]{:S(2)}) copy-start(bf16[16,128,128]{2,1,0:T(8,128)(2,1)} %get-tuple-element.25.x_ref) | copy-start | bytes 1572868
  8.1 3.9 %copy-start.2 = (bf16[128,640]{1,0:T(8,128)(2,1)S(1)}, bf16[128,640]{1,0:T(8,128)(2,1)}, u32[]{:S(2)}) copy-start(bf16[128,640]{1,0:T(8,128)(2,1)} %w_ref.4) | copy-start | bytes 491524
  8.1 31.8 %all-to-all-start = ((bf16[32,8,16,128]{3,2,1,0:T(8,128)(2,1)}), bf16[32,8,16,128]{3,2,1,0:T(8,128)(2,1)S(1)}, u32[]{:S(2)}, u32[]{:S(2)}) async-start(bf16[32,8,16,128]{3,2,1,0:T(8,128)(2,1)} %get-tuple-element.16), calls=%async_computation | async-start | bytes 2097152 | tf_op jit(solution)/shard_map/all_to_all | solution.py:649
  12.1 1.8 %copy-start.8 = (bf16[256,1024]{1,0:T(8,128)(2,1)S(1)}, bf16[256,1024]{1,0:T(8,128)(2,1)}, u32[]{:S(2)}) copy-start(bf16[256,1024]{1,0:T(8,128)(2,1)} %up_ref.2) | copy-start | bytes 1572868
  12.1 1.8 %copy-start.9 = (bf16[1024,256]{1,0:T(8,128)(2,1)S(1)}, bf16[1024,256]{1,0:T(8,128)(2,1)}, u32[]{:S(2)}) copy-start(bf16[1024,256]{1,0:T(8,128)(2,1)} %down_ref.2) | copy-start | bytes 1572868
  12.1 1.8 %copy-start.11 = (bf16[1,256,256]{2,1,0:T(8,128)(2,1)S(1)}, bf16[1,256,256]{2,1,0:T(8,128)(2,1)}, u32[]{:S(2)}) copy-start(bf16[1,256,256]{2,1,0:T(8,128)(2,1)} %seq_ref.1) | copy-start | bytes 393220
  12.1 1.8 %copy-start.12 = (bf16[256,64]{0,1:T(8,128)(2,1)S(1)}, bf16[256,64]{0,1:T(8,128)(2,1)}, u32[]{:S(2)}) copy-start(bf16[256,64]{0,1:T(8,128)(2,1)} %param.14) | copy-start | bytes 98308
  16.5 7.6 %collective-permute-start.2 = (bf16[336,128]{1,0:T(8,128)(2,1)S(1)}, bf16[336,128]{1,0:T(8,128)(2,1)S(1)}, u32[]{:S(2)}, u32[]{:S(2)}) collective-permute-start(bf16[336,128]{1,0:T(8,128)(2,1)S(1)} %get-tuple-element.18), channel_id=1, source_target_pairs={{0,16},{1,17},{2,18},{3,19},{4,20},{5,21},{6,22},{7,23},{8,24},{9,... | collective-permute-start | bytes 258056 | tf_op jit(solution)/shard_map/ppermute | solution.py:621
  18.2 7.3 %collective-permute-start.3 = (bf16[336,128]{1,0:T(8,128)(2,1)S(1)}, bf16[336,128]{1,0:T(8,128)(2,1)S(1)}, u32[]{:S(2)}, u32[]{:S(2)}) collective-permute-start(bf16[336,128]{1,0:T(8,128)(2,1)S(1)} %get-tuple-element.19), channel_id=1, source_target_pairs={{0,2},{1,3},{2,0},{3,1},{4,6},{5,7},{6,4},{7,5},{8,10},{9,11},{10,... | collective-permute-start | bytes 258056 | tf_op jit(solution)/shard_map/ppermute | solution.py:621
  19.7 12.2 %collective-permute-start.4 = (bf16[336,128]{1,0:T(8,128)(2,1)S(1)}, bf16[336,128]{1,0:T(8,128)(2,1)S(1)}, u32[]{:S(2)}, u32[]{:S(2)}) collective-permute-start(bf16[336,128]{1,0:T(8,128)(2,1)S(1)} %get-tuple-element.20), channel_id=1, source_target_pairs={{0,4},{1,5},{2,6},{3,7},{4,0},{5,1},{6,2},{7,3},{8,12},{9,13},{10,... | collective-permute-start | bytes 258056 | tf_op jit(solution)/shard_map/ppermute | solution.py:621
  21.2 12.9 %collective-permute-start.5 = (bf16[336,128]{1,0:T(8,128)(2,1)S(1)}, bf16[336,128]{1,0:T(8,128)(2,1)S(1)}, u32[]{:S(2)}, u32[]{:S(2)}) collective-permute-start(bf16[336,128]{1,0:T(8,128)(2,1)S(1)} %get-tuple-element.21), channel_id=1, source_target_pairs={{0,22},{1,23},{2,20},{3,21},{4,18},{5,19},{6,16},{7,17},{8,30},{9,... | collective-permute-start | bytes 258056 | tf_op jit(solution)/shard_map/ppermute | solution.py:621
  21.4 16.4 %collective-permute-start.6 = (bf16[336,128]{1,0:T(8,128)(2,1)S(1)}, bf16[336,128]{1,0:T(8,128)(2,1)S(1)}, u32[]{:S(2)}, u32[]{:S(2)}) collective-permute-start(bf16[336,128]{1,0:T(8,128)(2,1)S(1)} %get-tuple-element.22), channel_id=1, source_target_pairs={{0,6},{1,7},{2,4},{3,5},{4,2},{5,3},{6,0},{7,1},{8,14},{9,15},{10,... | collective-permute-start | bytes 258056 | tf_op jit(solution)/shard_map/ppermute | solution.py:621
  24.1 15.9 %collective-permute-start.7 = (bf16[336,128]{1,0:T(8,128)(2,1)S(1)}, bf16[336,128]{1,0:T(8,128)(2,1)S(1)}, u32[]{:S(2)}, u32[]{:S(2)}) collective-permute-start(bf16[336,128]{1,0:T(8,128)(2,1)S(1)} %get-tuple-element.23), channel_id=1, source_target_pairs={{0,20},{1,21},{2,22},{3,23},{4,16},{5,17},{6,18},{7,19},{8,28},{9,... | collective-permute-start | bytes 258056 | tf_op jit(solution)/shard_map/ppermute | solution.py:621
  25.6 14.4 %collective-permute-start.8 = (bf16[336,128]{1,0:T(8,128)(2,1)S(1)}, bf16[336,128]{1,0:T(8,128)(2,1)S(1)}, u32[]{:S(2)}, u32[]{:S(2)}) collective-permute-start(bf16[336,128]{1,0:T(8,128)(2,1)S(1)} %get-tuple-element.24), channel_id=1, source_target_pairs={{0,18},{1,19},{2,16},{3,17},{4,22},{5,23},{6,20},{7,21},{8,26},{9,... | collective-permute-start | bytes 258056 | tf_op jit(solution)/shard_map/ppermute | solution.py:621
  41.7 11.8 %all-to-all-start.1 = ((bf16[16,8,16,128]{3,2,1,0:T(8,128)(2,1)}), bf16[16,8,16,128]{3,2,1,0:T(8,128)(2,1)S(1)}, u32[]{:S(2)}, u32[]{:S(2)}) async-start(bf16[16,8,16,128]{3,2,1,0:T(8,128)(2,1)} %triangle_product.1), calls=%async_computation.1 | async-start | bytes 1048576 | tf_op jit(solution)/shard_map/all_to_all | solution.py:680
  46.6 0.9 %copy-start.6 = (bf16[8,80,128]{2,1,0:T(8,128)(2,1)}, bf16[8,80,128]{2,1,0:T(8,128)(2,1)S(1)}, u32[]{:S(2)}) copy-start(bf16[8,80,128]{2,1,0:T(8,128)(2,1)S(1)} %fusion.refs_0_) | copy-start | bytes 491524
  46.6 1.5 %copy-start.10 = (bf16[1024,128]{1,0:T(8,128)(2,1)S(1)}, bf16[1024,128]{1,0:T(8,128)(2,1)}, u32[]{:S(2)}) copy-start(bf16[1024,128]{1,0:T(8,128)(2,1)} %refs_2_.1) | copy-start | bytes 786436
  46.7 1.5 %collective-permute-start.9 = (bf16[8,80,128]{2,1,0:T(8,128)(2,1)S(1)}, bf16[8,80,128]{2,1,0:T(8,128)(2,1)S(1)}, u32[]{:S(2)}, u32[]{:S(2)}) collective-permute-start(bf16[8,80,128]{2,1,0:T(8,128)(2,1)S(1)} %fusion.refs_0_), channel_id=1, source_target_pairs={{0,1},{1,0},{2,3},{3,2},{4,5},{5,4},{6,7},{7,6},{8,9},{9,8},{10,11... | collective-permute-start | bytes 491528 | tf_op jit(solution)/shard_map/ppermute | solution.py:621
  47.6 6.0 %copy-start = (bf16[16,128,128]{2,1,0:T(8,128)(2,1)S(1)}, bf16[16,128,128]{2,1,0:T(8,128)(2,1)}, u32[]{:S(2)}) copy-start(bf16[16,128,128]{2,1,0:T(8,128)(2,1)} %x_ref.1) | copy-start | bytes 1572868
  47.6 6.0 %copy-start.3 = (bf16[128,512]{1,0:T(8,128)(2,1)S(1)}, bf16[128,512]{1,0:T(8,128)(2,1)}, u32[]{:S(2)}) copy-start(bf16[128,512]{1,0:T(8,128)(2,1)} %up_ref.3) | copy-start | bytes 393220
  47.6 6.0 %copy-start.4 = (bf16[512,128]{1,0:T(8,128)(2,1)S(1)}, bf16[512,128]{1,0:T(8,128)(2,1)}, u32[]{:S(2)}) copy-start(bf16[512,128]{1,0:T(8,128)(2,1)} %down_ref.3) | copy-start | bytes 393220
  47.6 6.0 %copy-start.5 = (bf16[128,128]{1,0:T(8,128)(2,1)S(1)}, bf16[128,128]{1,0:T(8,128)(2,1)}, u32[]{:S(2)}) copy-start(bf16[128,128]{1,0:T(8,128)(2,1)} %w_ref.5) | copy-start | bytes 98308
  48.1 0.9 %copy-start.7 = (bf16[8,80,128]{2,1,0:T(8,128)(2,1)S(1)}, bf16[8,80,128]{2,1,0:T(8,128)(2,1)}, u32[]{:S(2)}) copy-start(bf16[8,80,128]{2,1,0:T(8,128)(2,1)} %copy-done.6) | copy-start | bytes 491524

commit v9 on v8

--- a/solution.py
+++ b/solution.py
@@ -301,7 +301,7 @@
             pltpu.VMEM((chans, 2 * chans), BF16),
             pltpu.VMEM((groups, per, rows, width), BF16),
             pltpu.VMEM(x.shape, BF16),
-            pltpu.VMEM((chans * rows, width), F32),
+            pltpu.VMEM(((chans + 1) * rows, width), F32),
             pltpu.SemaphoreType.DMA((3 + devices // 4,)),
         ],
         cost_estimate=cost(2 * rows * width * chans * 2 * chans, 3 * rows * width * chans * 2),
@@ -355,7 +355,7 @@
         in_specs=[SMEM] + [VMEM] * 3,
         out_specs=VMEM,
         scratch_shapes=[
-            pltpu.VMEM((2, count * per * rows, width), F32),
+            pltpu.VMEM((2, (count * per + 1) * rows, width), F32),
             pltpu.VMEM(x.shape, BF16),
         ],
         compiler_params=PARAMS,
@@ -550,7 +550,7 @@
         in_specs=[VMEM] * 7,
         out_specs=HBM,
         scratch_shapes=[
-            pltpu.VMEM((rows * chans, width), F32),
+            pltpu.VMEM((rows * (chans + 1), width), F32),
             pltpu.VMEM(x.shape, BF16),
             pltpu.SemaphoreType.DMA((2,)),
         ],
@@ -575,14 +575,14 @@
                 right_scr[pl.ds(at, depth, stride=total), :] = side
                 left_scr[pl.ds(at, rows, stride=total), :] = both
             s += 1
-    right = jnp.transpose(right_scr[...]).astype(BF16)
-    both = left_scr[...]
+    right = jnp.transpose(right_scr[: depth * total]).astype(BF16)
+    both = left_scr[: rows * total]
     shift = lax.bitwise_and(where_ref[1], 1) * depth
     first = pltpu.roll(both, width - shift, 1)[:, :depth]
     second = pltpu.roll(both, width - 2 * depth - shift, 1)[:, :depth]
     row = lax.broadcasted_iota(jnp.int32, first.shape, 0)
     left = jnp.where(row % total < total // 2, first, second).astype(BF16)
-    w_scr[...] = w_ref[...].astype(F32)
+    w_scr[: depth * depth] = w_ref[...].astype(F32)
     for d in range(depth):
         part = w_scr[pl.ds(d, depth, stride=depth), :].astype(BF16)
         m_scr[:, d * total : (d + 1) * total] = (
@@ -605,9 +605,9 @@
         in_specs=[SMEM] + [VMEM] * (len(groups) + 1),
         out_specs=VMEM,
         scratch_shapes=[
-            pltpu.VMEM((depth * total, width), F32),
-            pltpu.VMEM((rows * total, width), F32),
-            pltpu.VMEM((depth * depth, chans), F32),
+            pltpu.VMEM(((depth + 1) * total, width), F32),
+            pltpu.VMEM(((rows + 1) * total, width), F32),
+            pltpu.VMEM((depth * (depth + 1), chans), F32),
             pltpu.VMEM((rows, depth * total, chans), BF16),
         ],
         compiler_params=PARAMS,

time: 56.8 us -> 56.8 us (level)
  no operation moved by 1% of the time
where the time goes in v9:
time: 56.8 us; the launch traced here: 56.5 us
  starting transfers between devices  23.7 us (42%)
  Pallas kernels  15.9 us (28%)
  waiting for transfers between devices  14.9 us (26%)
  local copies, waits for them, and re-layouts  1.06 us (2%)
  between operations  0.87 us (2%)
    ppermute x10, starting transfers between devices, swap(): return lax.ppermute(x, AXES, [(d, d ^ mask) for d in range(count)])  14.9 us
    ppermute x10, waiting for transfers between devices, swap(): return lax.ppermute(x, AXES, [(d, d ^ mask) for d in range(count)])  13.3 us
    all_to_all x1, starting transfers between devices, own_channels_device(): lax.all_to_all(product, AXES, 0, 0, axis_index_groups=members, tiled=True)  4.89 us
    all_to_all x1, starting transfers between devices, own_channels_device(): received = lax.all_to_all(sent, AXES, 0, 0, tiled=True)  3.83 us
    pallas_call x1, Pallas kernels, right_operand(): pl.pallas_call(functools.partial(right_kernel, n_branch), out_shape=[jax....  3.28 us
    pallas_call x1, Pallas kernels, pair_output(): pl.pallas_call(pair_output_kernel, out_shape=jax.ShapeDtypeStruct(x.shape...  2.93 us
    pallas_call x1, Pallas kernels, outer_update(): pl.pallas_call(outer_kernel, out_shape=jax.ShapeDtypeStruct((rows, width,...  2.91 us
    pallas_call x1, Pallas kernels, messages(): pl.pallas_call(functools.partial(message_kernel, n_branch, near, rows), o...  2.55 us
  transfers between devices with their start and end apart: 12, of which 6 were waited for; matrix products, arithmetic and copies ran while one was open for 0% of the time, Pallas kernels for 20%

profile of v9, /device:TPU:0, one launch (start us, length us, event | category | flops | bytes accessed | tf_op | source)
XLA Modules:
  0.0 56.5 jit_solution(11608888708544458044)
XLA Ops:
  0.6 0.5 collective-permute-start
  1.1 3.7 %collective-permute-start.1 = (bf16[1,256,256]{2,1,0:T(8,128)(2,1)}, bf16[1,256,256]{2,1,0:T(8,128)(2,1)S(1)}, u32[]{:S(2)}, u32[]{:S(2)}) collective-permute-start(bf16[1,256,256]{2,1,0:T(8,128)(2,1)} %seq_ref.1), channel_id=1, source_target_pairs={{0,8},{1,9},{2,10},{3,11},{4,12},{5,13},{6,14},{7,15},{8,0},{9,1},... | collective-permute-start | bytes 393224 | tf_op jit(solution)/shard_map/ppermute | solution.py:621
  4.8 3.3 %right_operand.1 = (bf16[32,8,16,128]{3,2,1,0:T(8,128)(2,1)}, bf16[16,128,128]{2,1,0:T(8,128)(2,1)}) custom-call(bf16[16,128,128]{2,1,0:T(8,128)(2,1)} %x_ref.1, bf16[128,640]{1,0:T(8,128)(2,1)} %w_ref.4), custom_call_target="tpu_custom_call" | custom-call | flops 134217728 | bytes 1572864 | tf_op jit(solution)/shard_map/right_operand/pallas_call | solution.py:291
  8.1 0.0 copy-start.1
  8.1 3.8 %all-to-all-start = ((bf16[32,8,16,128]{3,2,1,0:T(8,128)(2,1)}), bf16[32,8,16,128]{3,2,1,0:T(8,128)(2,1)S(1)}, u32[]{:S(2)}, u32[]{:S(2)}) async-start(bf16[32,8,16,128]{3,2,1,0:T(8,128)(2,1)} %get-tuple-element.16), calls=%async_computation | async-start | bytes 2097152 | tf_op jit(solution)/shard_map/all_to_all | solution.py:649
  12.0 0.1 pad_add_fusion.where_ref
  12.1 0.0 copy-start.9
  12.1 0.0 copy-start.11
  12.1 1.8 %left_operand.1.left_ref = bf16[8,256,128]{2,1,0:T(8,128)(2,1)S(1)} custom-call(s32[2]{0:T(128)S(1)} %pad_add_fusion.where_ref, bf16[16,128,128]{2,1,0:T(8,128)(2,1)S(1)} %copy-done.1, bf16[16,128,128]{2,1,0:T(8,128)(2,1)S(1)} %collective-permute-done.other_ref, bf16[128,640]{1,0:T(8,128)(2,1)S(1)} %copy-done.2), custom_call_target="tpu_custom_call" | custom-call | flops 268435456 | bytes 2097152 | tf_op jit(solution)/shard_map/left_operand/pallas_call | solution.py:352
  13.9 2.5 %msa_transition_and_messages.1 = (bf16[1,256,256]{2,1,0:T(8,128)(2,1)}, bf16[336,128]{1,0:T(8,128)(2,1)S(1)}, bf16[336,128]{1,0:T(8,128)(2,1)S(1)}, bf16[336,128...) custom-call(s32[2]{0:T(128)S(1)} %pad_add_fusion.where_ref, ...), custom_call_target="tpu_custom_call" | custom-call | flops 20000000000 | bytes 1048576 | tf_op jit(solution)/shard_map/msa_transition_and_messages/pallas_call | solution.py:404
  16.5 1.8 %collective-permute-start.2 = (bf16[336,128]{1,0:T(8,128)(2,1)S(1)}, bf16[336,128]{1,0:T(8,128)(2,1)S(1)}, u32[]{:S(2)}, u32[]{:S(2)}) collective-permute-start(bf16[336,128]{1,0:T(8,128)(2,1)S(1)} %get-tuple-element.18), channel_id=1, source_target_pairs={{0,16},{1,17},{2,18},{3,19},{4,20},{5,21},{6,22},{7,23},{8,24},{9,... | collective-permute-start | bytes 258056 | tf_op jit(solution)/shard_map/ppermute | solution.py:621
  18.2 1.5 %collective-permute-start.3 = (bf16[336,128]{1,0:T(8,128)(2,1)S(1)}, bf16[336,128]{1,0:T(8,128)(2,1)S(1)}, u32[]{:S(2)}, u32[]{:S(2)}) collective-permute-start(bf16[336,128]{1,0:T(8,128)(2,1)S(1)} %get-tuple-element.19), channel_id=1, source_target_pairs={{0,2},{1,3},{2,0},{3,1},{4,6},{5,7},{6,4},{7,5},{8,10},{9,11},{10,... | collective-permute-start | bytes 258056 | tf_op jit(solution)/shard_map/ppermute | solution.py:621
  19.7 1.5 %collective-permute-start.4 = (bf16[336,128]{1,0:T(8,128)(2,1)S(1)}, bf16[336,128]{1,0:T(8,128)(2,1)S(1)}, u32[]{:S(2)}, u32[]{:S(2)}) collective-permute-start(bf16[336,128]{1,0:T(8,128)(2,1)S(1)} %get-tuple-element.20), channel_id=1, source_target_pairs={{0,4},{1,5},{2,6},{3,7},{4,0},{5,1},{6,2},{7,3},{8,12},{9,13},{10,... | collective-permute-start | bytes 258056 | tf_op jit(solution)/shard_map/ppermute | solution.py:621
  21.2 0.2 collective-permute-start.5
  21.4 2.7 %collective-permute-start.6 = (bf16[336,128]{1,0:T(8,128)(2,1)S(1)}, bf16[336,128]{1,0:T(8,128)(2,1)S(1)}, u32[]{:S(2)}, u32[]{:S(2)}) collective-permute-start(bf16[336,128]{1,0:T(8,128)(2,1)S(1)} %get-tuple-element.22), channel_id=1, source_target_pairs={{0,6},{1,7},{2,4},{3,5},{4,2},{5,3},{6,0},{7,1},{8,14},{9,15},{10,... | collective-permute-start | bytes 258056 | tf_op jit(solution)/shard_map/ppermute | solution.py:621
  24.1 1.5 %collective-permute-start.7 = (bf16[336,128]{1,0:T(8,128)(2,1)S(1)}, bf16[336,128]{1,0:T(8,128)(2,1)S(1)}, u32[]{:S(2)}, u32[]{:S(2)}) collective-permute-start(bf16[336,128]{1,0:T(8,128)(2,1)S(1)} %get-tuple-element.23), channel_id=1, source_target_pairs={{0,20},{1,21},{2,22},{3,23},{4,16},{5,17},{6,18},{7,19},{8,28},{9,... | collective-permute-start | bytes 258056 | tf_op jit(solution)/shard_map/ppermute | solution.py:621
  25.6 1.5 %collective-permute-start.8 = (bf16[336,128]{1,0:T(8,128)(2,1)S(1)}, bf16[336,128]{1,0:T(8,128)(2,1)S(1)}, u32[]{:S(2)}, u32[]{:S(2)}) collective-permute-start(bf16[336,128]{1,0:T(8,128)(2,1)S(1)} %get-tuple-element.24), channel_id=1, source_target_pairs={{0,18},{1,19},{2,16},{3,17},{4,22},{5,23},{6,20},{7,21},{8,26},{9,... | collective-permute-start | bytes 258056 | tf_op jit(solution)/shard_map/ppermute | solution.py:621
  27.1 4.8 %collective-permute-done.4.rest_3_ = bf16[336,128]{1,0:T(8,128)(2,1)S(1)} collective-permute-done((bf16[336,128]{1,0:T(8,128)(2,1)S(1)}, bf16[336,128]{1,0:T(8,128)(2,1)S(1)}, u32[]{:S(2)}, u32[]{:S(2)}) %collective-permute-start.4) | collective-permute-done | bytes 86048 | tf_op jit(solution)/shard_map/ppermute | solution.py:621
  31.9 2.2 %collective-permute-done.5.rest_4_ = bf16[336,128]{1,0:T(8,128)(2,1)S(1)} collective-permute-done((bf16[336,128]{1,0:T(8,128)(2,1)S(1)}, bf16[336,128]{1,0:T(8,128)(2,1)S(1)}, u32[]{:S(2)}, u32[]{:S(2)}) %collective-permute-start.5) | collective-permute-done | bytes 86048 | tf_op jit(solution)/shard_map/ppermute | solution.py:621
  34.1 3.7 %collective-permute-done.6.rest_5_ = bf16[336,128]{1,0:T(8,128)(2,1)S(1)} collective-permute-done((bf16[336,128]{1,0:T(8,128)(2,1)S(1)}, bf16[336,128]{1,0:T(8,128)(2,1)S(1)}, u32[]{:S(2)}, u32[]{:S(2)}) %collective-permute-start.6) | collective-permute-done | bytes 86048 | tf_op jit(solution)/shard_map/ppermute | solution.py:621
  37.8 2.2 %collective-permute-done.7.rest_6_ = bf16[336,128]{1,0:T(8,128)(2,1)S(1)} collective-permute-done((bf16[336,128]{1,0:T(8,128)(2,1)S(1)}, bf16[336,128]{1,0:T(8,128)(2,1)S(1)}, u32[]{:S(2)}, u32[]{:S(2)}) %collective-permute-start.7) | collective-permute-done | bytes 86048 | tf_op jit(solution)/shard_map/ppermute | solution.py:621
  40.0 1.7 %triangle_product.1 = bf16[16,8,16,128]{3,2,1,0:T(8,128)(2,1)} custom-call(s32[2]{0:T(128)S(1)} %pad_add_fusion.where_ref, bf16[32,8,16,128]{3,2,1,0:T(8,128)(2,1)S(1)} %all-to-all-done.in_ref, bf16[336,128]{1,0:T(8,128)(2,1)S(1)} %get-tuple-element.17.rest_0_, bf16[336,128]{1,0:T(8,128)(2,1)S(1)} %collective-permute-done.2.rest_1_, ...), custom_call_target="tpu_custom_call" | custom-call | flops 134217728 | bytes 2097152 | tf_op jit(solution)/shard_map/triangle_product/pallas_call | solution.py:492
  41.7 4.9 %all-to-all-start.1 = ((bf16[16,8,16,128]{3,2,1,0:T(8,128)(2,1)}), bf16[16,8,16,128]{3,2,1,0:T(8,128)(2,1)S(1)}, u32[]{:S(2)}, u32[]{:S(2)}) async-start(bf16[16,8,16,128]{3,2,1,0:T(8,128)(2,1)} %triangle_product.1), calls=%async_computation.1 | async-start | bytes 1048576 | tf_op jit(solution)/shard_map/all_to_all | solution.py:680
  46.6 0.0 copy-start.10
  46.7 0.1 collective-permute-start.9
  46.8 0.8 %triangle_output_gate.1.gate_ref = f32[16,128,128]{2,1,0:T(8,128)S(1)} custom-call(bf16[16,128,128]{2,1,0:T(8,128)(2,1)S(1)} %copy-done.1, bf16[128,640]{1,0:T(8,128)(2,1)S(1)} %copy-done.2), custom_call_target="tpu_custom_call" | custom-call | flops 67108864 | bytes 1572864 | tf_op jit(solution)/shard_map/triangle_output_gate/pallas_call | solution.py:430
  47.6 0.0 copy-start.3
  47.6 0.5 collective-permute-done.9.refs_1_
  48.1 0.9 %copy-done.7 = bf16[8,80,128]{2,1,0:T(8,128)(2,1)S(1)} copy-done((bf16[8,80,128]{2,1,0:T(8,128)(2,1)S(1)}, bf16[8,80,128]{2,1,0:T(8,128)(2,1)}, u32[]{:S(2)}) %copy-start.7) | copy-done | bytes 163864
  49.0 2.9 %outer_product_mean.1.outer_ref = f32[16,128,128]{2,1,0:T(8,128)S(1)} custom-call(s32[2]{0:T(128)S(1)} %pad_add_fusion.where_ref, bf16[8,80,128]{2,1,0:T(8,128)(2,1)S(1)} %copy-done.7, bf16[8,80,128]{2,1,0:T(8,128)(2,1)S(1)} %collective-permute-done.9.refs_1_, bf16[1024,128]{1,0:T(8,128)(2,1)S(1)} %copy-done.10), custom_call_target="tpu_custom_call" | custom-call | flops 1073741824 | bytes 1048576 | tf_op jit(solution)/shard_map/outer_product_mean/pallas_call | solution.py:602
  52.0 1.6 %all-to-all-done.1.p_ref = bf16[16,8,16,128]{3,2,1,0:T(8,128)(2,1)S(1)} async-done(((bf16[16,8,16,128]{3,2,1,0:T(8,128)(2,1)}), bf16[16,8,16,128]{3,2,1,0:T(8,128)(2,1)S(1)}, u32[]{:S(2)}, u32[]{:S(2)}) %all-to-all-start.1) | async-done | bytes 524320 | tf_op jit(solution)/shard_map/all_to_all | solution.py:680
  53.6 2.9 %pair_output.1 = bf16[16,128,128]{2,1,0:T(8,128)(2,1)} custom-call(bf16[16,8,16,128]{3,2,1,0:T(8,128)(2,1)S(1)} %all-to-all-done.1.p_ref, bf16[16,128,128]{2,1,0:T(8,128)(2,1)S(1)} %copy-done, f32[16,128,128]{2,1,0:T(8,128)S(1)} %triangle_output_gate.1.gate_ref, f32[16,128,128]{2,1,0:T(8,128)S(1)} %outer_product_mean.1.outer_ref, ...), custom_call_target="tpu_custom_call" | custom-call | flops 603979776 | bytes 3670016 | tf_op jit(solution)/shard_map/pair_output/pallas_call | solution.py:547
  (34 shorter events, 0.1 us)
Async XLA Ops:
  0.6 11.4 %collective-permute-start = (bf16[16,128,128]{2,1,0:T(8,128)(2,1)}, bf16[16,128,128]{2,1,0:T(8,128)(2,1)S(1)}, u32[]{:S(2)}, u32[]{:S(2)}) collective-permute-start(bf16[16,128,128]{2,1,0:T(8,128)(2,1)} %x_ref.1), channel_id=1, source_target_pairs={{0,1},{1,0},{2,3},{3,2},{4,5},{5,4},{6,7},{7,6},{8,9},{9,8},{10,11... | collective-permute-start | bytes 1572872 | tf_op jit(solution)/shard_map/ppermute | solution.py:621
  1.1 12.7 %collective-permute-start.1 = (bf16[1,256,256]{2,1,0:T(8,128)(2,1)}, bf16[1,256,256]{2,1,0:T(8,128)(2,1)S(1)}, u32[]{:S(2)}, u32[]{:S(2)}) collective-permute-start(bf16[1,256,256]{2,1,0:T(8,128)(2,1)} %seq_ref.1), channel_id=1, source_target_pairs={{0,8},{1,9},{2,10},{3,11},{4,12},{5,13},{6,14},{7,15},{8,0},{9,1},... | collective-permute-start | bytes 393224 | tf_op jit(solution)/shard_map/ppermute | solution.py:621
  8.1 3.9 %copy-start.1 = (bf16[16,128,128]{2,1,0:T(8,128)(2,1)S(1)}, bf16[16,128,128]{2,1,0:T(8,128)(2,1)}, u32[]{:S(2)}) copy-start(bf16[16,128,128]{2,1,0:T(8,128)(2,1)} %get-tuple-element.25.x_ref) | copy-start | bytes 1572868
  8.1 3.9 %copy-start.2 = (bf16[128,640]{1,0:T(8,128)(2,1)S(1)}, bf16[128,640]{1,0:T(8,128)(2,1)}, u32[]{:S(2)}) copy-start(bf16[128,640]{1,0:T(8,128)(2,1)} %w_ref.4) | copy-start | bytes 491524
  8.1 31.8 %all-to-all-start = ((bf16[32,8,16,128]{3,2,1,0:T(8,128)(2,1)}), bf16[32,8,16,128]{3,2,1,0:T(8,128)(2,1)S(1)}, u32[]{:S(2)}, u32[]{:S(2)}) async-start(bf16[32,8,16,128]{3,2,1,0:T(8,128)(2,1)} %get-tuple-element.16), calls=%async_computation | async-start | bytes 2097152 | tf_op jit(solution)/shard_map/all_to_all | solution.py:649
  12.1 1.8 %copy-start.8 = (bf16[256,1024]{1,0:T(8,128)(2,1)S(1)}, bf16[256,1024]{1,0:T(8,128)(2,1)}, u32[]{:S(2)}) copy-start(bf16[256,1024]{1,0:T(8,128)(2,1)} %up_ref.2) | copy-start | bytes 1572868
  12.1 1.8 %copy-start.9 = (bf16[1024,256]{1,0:T(8,128)(2,1)S(1)}, bf16[1024,256]{1,0:T(8,128)(2,1)}, u32[]{:S(2)}) copy-start(bf16[1024,256]{1,0:T(8,128)(2,1)} %down_ref.2) | copy-start | bytes 1572868
  12.1 1.8 %copy-start.11 = (bf16[1,256,256]{2,1,0:T(8,128)(2,1)S(1)}, bf16[1,256,256]{2,1,0:T(8,128)(2,1)}, u32[]{:S(2)}) copy-start(bf16[1,256,256]{2,1,0:T(8,128)(2,1)} %seq_ref.1) | copy-start | bytes 393220
  12.1 1.8 %copy-start.12 = (bf16[256,64]{0,1:T(8,128)(2,1)S(1)}, bf16[256,64]{0,1:T(8,128)(2,1)}, u32[]{:S(2)}) copy-start(bf16[256,64]{0,1:T(8,128)(2,1)} %param.14) | copy-start | bytes 98308
  16.5 7.6 %collective-permute-start.2 = (bf16[336,128]{1,0:T(8,128)(2,1)S(1)}, bf16[336,128]{1,0:T(8,128)(2,1)S(1)}, u32[]{:S(2)}, u32[]{:S(2)}) collective-permute-start(bf16[336,128]{1,0:T(8,128)(2,1)S(1)} %get-tuple-element.18), channel_id=1, source_target_pairs={{0,16},{1,17},{2,18},{3,19},{4,20},{5,21},{6,22},{7,23},{8,24},{9,... | collective-permute-start | bytes 258056 | tf_op jit(solution)/shard_map/ppermute | solution.py:621
  18.2 7.3 %collective-permute-start.3 = (bf16[336,128]{1,0:T(8,128)(2,1)S(1)}, bf16[336,128]{1,0:T(8,128)(2,1)S(1)}, u32[]{:S(2)}, u32[]{:S(2)}) collective-permute-start(bf16[336,128]{1,0:T(8,128)(2,1)S(1)} %get-tuple-element.19), channel_id=1, source_target_pairs={{0,2},{1,3},{2,0},{3,1},{4,6},{5,7},{6,4},{7,5},{8,10},{9,11},{10,... | collective-permute-start | bytes 258056 | tf_op jit(solution)/shard_map/ppermute | solution.py:621
  19.7 12.2 %collective-permute-start.4 = (bf16[336,128]{1,0:T(8,128)(2,1)S(1)}, bf16[336,128]{1,0:T(8,128)(2,1)S(1)}, u32[]{:S(2)}, u32[]{:S(2)}) collective-permute-start(bf16[336,128]{1,0:T(8,128)(2,1)S(1)} %get-tuple-element.20), channel_id=1, source_target_pairs={{0,4},{1,5},{2,6},{3,7},{4,0},{5,1},{6,2},{7,3},{8,12},{9,13},{10,... | collective-permute-start | bytes 258056 | tf_op jit(solution)/shard_map/ppermute | solution.py:621
  21.2 12.9 %collective-permute-start.5 = (bf16[336,128]{1,0:T(8,128)(2,1)S(1)}, bf16[336,128]{1,0:T(8,128)(2,1)S(1)}, u32[]{:S(2)}, u32[]{:S(2)}) collective-permute-start(bf16[336,128]{1,0:T(8,128)(2,1)S(1)} %get-tuple-element.21), channel_id=1, source_target_pairs={{0,22},{1,23},{2,20},{3,21},{4,18},{5,19},{6,16},{7,17},{8,30},{9,... | collective-permute-start | bytes 258056 | tf_op jit(solution)/shard_map/ppermute | solution.py:621
  21.4 16.4 %collective-permute-start.6 = (bf16[336,128]{1,0:T(8,128)(2,1)S(1)}, bf16[336,128]{1,0:T(8,128)(2,1)S(1)}, u32[]{:S(2)}, u32[]{:S(2)}) collective-permute-start(bf16[336,128]{1,0:T(8,128)(2,1)S(1)} %get-tuple-element.22), channel_id=1, source_target_pairs={{0,6},{1,7},{2,4},{3,5},{4,2},{5,3},{6,0},{7,1},{8,14},{9,15},{10,... | collective-permute-start | bytes 258056 | tf_op jit(solution)/shard_map/ppermute | solution.py:621
  24.1 15.8 %collective-permute-start.7 = (bf16[336,128]{1,0:T(8,128)(2,1)S(1)}, bf16[336,128]{1,0:T(8,128)(2,1)S(1)}, u32[]{:S(2)}, u32[]{:S(2)}) collective-permute-start(bf16[336,128]{1,0:T(8,128)(2,1)S(1)} %get-tuple-element.23), channel_id=1, source_target_pairs={{0,20},{1,21},{2,22},{3,23},{4,16},{5,17},{6,18},{7,19},{8,28},{9,... | collective-permute-start | bytes 258056 | tf_op jit(solution)/shard_map/ppermute | solution.py:621
  25.6 14.4 %collective-permute-start.8 = (bf16[336,128]{1,0:T(8,128)(2,1)S(1)}, bf16[336,128]{1,0:T(8,128)(2,1)S(1)}, u32[]{:S(2)}, u32[]{:S(2)}) collective-permute-start(bf16[336,128]{1,0:T(8,128)(2,1)S(1)} %get-tuple-element.24), channel_id=1, source_target_pairs={{0,18},{1,19},{2,16},{3,17},{4,22},{5,23},{6,20},{7,21},{8,26},{9,... | collective-permute-start | bytes 258056 | tf_op jit(solution)/shard_map/ppermute | solution.py:621
  41.7 11.9 %all-to-all-start.1 = ((bf16[16,8,16,128]{3,2,1,0:T(8,128)(2,1)}), bf16[16,8,16,128]{3,2,1,0:T(8,128)(2,1)S(1)}, u32[]{:S(2)}, u32[]{:S(2)}) async-start(bf16[16,8,16,128]{3,2,1,0:T(8,128)(2,1)} %triangle_product.1), calls=%async_computation.1 | async-start | bytes 1048576 | tf_op jit(solution)/shard_map/all_to_all | solution.py:680
  46.6 0.9 %copy-start.6 = (bf16[8,80,128]{2,1,0:T(8,128)(2,1)}, bf16[8,80,128]{2,1,0:T(8,128)(2,1)S(1)}, u32[]{:S(2)}) copy-start(bf16[8,80,128]{2,1,0:T(8,128)(2,1)S(1)} %fusion.refs_0_) | copy-start | bytes 491524
  46.6 1.5 %copy-start.10 = (bf16[1024,128]{1,0:T(8,128)(2,1)S(1)}, bf16[1024,128]{1,0:T(8,128)(2,1)}, u32[]{:S(2)}) copy-start(bf16[1024,128]{1,0:T(8,128)(2,1)} %refs_2_.1) | copy-start | bytes 786436
  46.7 1.5 %collective-permute-start.9 = (bf16[8,80,128]{2,1,0:T(8,128)(2,1)S(1)}, bf16[8,80,128]{2,1,0:T(8,128)(2,1)S(1)}, u32[]{:S(2)}, u32[]{:S(2)}) collective-permute-start(bf16[8,80,128]{2,1,0:T(8,128)(2,1)S(1)} %fusion.refs_0_), channel_id=1, source_target_pairs={{0,1},{1,0},{2,3},{3,2},{4,5},{5,4},{6,7},{7,6},{8,9},{9,8},{10,11... | collective-permute-start | bytes 491528 | tf_op jit(solution)/shard_map/ppermute | solution.py:621
  47.6 6.0 %copy-start = (bf16[16,128,128]{2,1,0:T(8,128)(2,1)S(1)}, bf16[16,128,128]{2,1,0:T(8,128)(2,1)}, u32[]{:S(2)}) copy-start(bf16[16,128,128]{2,1,0:T(8,128)(2,1)} %x_ref.1) | copy-start | bytes 1572868
  47.6 6.0 %copy-start.3 = (bf16[128,512]{1,0:T(8,128)(2,1)S(1)}, bf16[128,512]{1,0:T(8,128)(2,1)}, u32[]{:S(2)}) copy-start(bf16[128,512]{1,0:T(8,128)(2,1)} %up_ref.3) | copy-start | bytes 393220
  47.6 6.0 %copy-start.4 = (bf16[512,128]{1,0:T(8,128)(2,1)S(1)}, bf16[512,128]{1,0:T(8,128)(2,1)}, u32[]{:S(2)}) copy-start(bf16[512,128]{1,0:T(8,128)(2,1)} %down_ref.3) | copy-start | bytes 393220
  47.6 6.0 %copy-start.5 = (bf16[128,128]{1,0:T(8,128)(2,1)S(1)}, bf16[128,128]{1,0:T(8,128)(2,1)}, u32[]{:S(2)}) copy-start(bf16[128,128]{1,0:T(8,128)(2,1)} %w_ref.5) | copy-start | bytes 98308
  48.1 0.9 %copy-start.7 = (bf16[8,80,128]{2,1,0:T(8,128)(2,1)S(1)}, bf16[8,80,128]{2,1,0:T(8,128)(2,1)}, u32[]{:S(2)}) copy-start(bf16[8,80,128]{2,1,0:T(8,128)(2,1)} %copy-done.6) | copy-start | bytes 491524

commit v10 on v9

--- a/solution.py
+++ b/solution.py
@@ -236,7 +236,7 @@
 
 
 def right_kernel(
-    n_branch, x_hbm, w_hbm, sent_hbm, tokens_hbm, x_ref, w_ref, sent_ref, tokens_ref, scr, sems
+    n_branch, x_hbm, w_hbm, sent_hbm, x_ref, w_ref, sent_ref, scr, sems
 ):
     rows, width, chans = x_ref.shape
     groups, per = sent_ref.shape[:2]
@@ -257,10 +257,8 @@
     parts = []
     for i in range(0, rows, step):
         tokens = normed(x_ref[i : i + step].astype(F32), -1)
-        tokens_ref[i : i + step] = tokens
         parts.append(tokens.reshape(step * width, chans))
-    outs = [pltpu.make_async_copy(tokens_ref, tokens_hbm, sems.at[2])]
-    outs[0].start()
+    outs = []
     for i, tokens in zip(range(0, rows, step), parts):
         result = dot(values, tokens, NT) * sigmoid(dot(gates, tokens, NT))
         for k in range(step):
@@ -290,17 +288,13 @@
     groups = chans // per
     return pl.pallas_call(
         functools.partial(right_kernel, n_branch),
-        out_shape=[
-            jax.ShapeDtypeStruct((devices, per, rows, width), BF16),
-            jax.ShapeDtypeStruct(x.shape, BF16),
-        ],
+        out_shape=jax.ShapeDtypeStruct((devices, per, rows, width), BF16),
         in_specs=[HBM] * 2,
-        out_specs=[HBM] * 2,
+        out_specs=HBM,
         scratch_shapes=[
             pltpu.VMEM(x.shape, BF16),
             pltpu.VMEM((chans, 2 * chans), BF16),
             pltpu.VMEM((groups, per, rows, width), BF16),
-            pltpu.VMEM(x.shape, BF16),
             pltpu.VMEM(((chans + 1) * rows, width), F32),
             pltpu.SemaphoreType.DMA((3 + devices // 4,)),
         ],
@@ -332,10 +326,10 @@
 
         return store
 
-    gated_rows(values, gates, x_ref, store_at(core))
-    for i in range(0, rows, 4):
-        norm_scr[i : i + 4] = normed(other_ref[i : i + 4].astype(F32), -1)
-    gated_rows(values, gates, norm_scr, store_at(1 - core))
+    for k, ref, at in ((0, x_ref, core), (1, other_ref, 1 - core)):
+        for i in range(0, rows, 4):
+            norm_scr[k, i : i + 4] = normed(ref[i : i + 4].astype(F32), -1)
+        gated_rows(values, gates, norm_scr.at[k], store_at(at))
     for t in range(count):
         for c in range(per):
             for k in range(2):
@@ -356,7 +350,7 @@
         out_specs=VMEM,
         scratch_shapes=[
             pltpu.VMEM((2, (count * per + 1) * rows, width), F32),
-            pltpu.VMEM(x.shape, BF16),
+            pltpu.VMEM((2,) + x.shape, BF16),
         ],
         compiler_params=PARAMS,
         cost_estimate=cost(4 * x.size * 2 * chans, x.size * 8),
@@ -419,7 +413,7 @@
 
 def gate_kernel(x_ref, w_ref, out_ref):
     rows, width, chans = x_ref.shape
-    tokens = x_ref[...].reshape(rows * width, chans)
+    tokens = normed(x_ref[...].astype(F32).reshape(rows * width, chans), -1)
     out_ref[...] = sigmoid(dot(tokens, w_ref[:, 4 * chans :])).reshape(rows, width, chans)
 
 
@@ -643,13 +637,13 @@
     where = jnp.stack([lax.axis_index("branch"), lax.axis_index("rows")]).astype(jnp.int32)
 
     far_row = swap(homolog_features, n_branch, n_rows, near)
-    sent, tokens = right_operand(
+    sent = right_operand(
         pairwise_input, triangle_projection_weight, n_branch, n_branch * n_rows, per
     )
     received = lax.all_to_all(sent, AXES, 0, 0, tiled=True)
 
     other = swap(pairwise_input, n_branch, n_rows, 1)
-    left = left_operand(where, tokens, other, triangle_projection_weight, n_branch, near)
+    left = left_operand(where, pairwise_input, other, triangle_projection_weight, n_branch, near)
     fresh, pieces = messages(
         where,
         left,
@@ -669,8 +663,8 @@
     mine = jnp.stack([piece[per * 2 * rows :] for piece in moved])
     groups = [mine, swap(mine, n_branch, n_rows, 1)]
     outer = outer_update(where, groups, outer_output_weight, rows, chans)
-    gate_tokens, _ = lax.optimization_barrier((tokens, moved[0]))
-    gate = output_gate(gate_tokens, triangle_projection_weight)
+    gate_tile, _ = lax.optimization_barrier((pairwise_input, moved[0]))
+    gate = output_gate(gate_tile, triangle_projection_weight)
 
     product = triangle_product(where, received, moved, n_branch, near)
     members = [

time: 56.8 us -> 56.9 us (level)
  waiting for transfers between devices: 14.9 us -> 12.7 us
  Pallas kernels: 15.9 us -> 17.4 us
  starting transfers between devices: 23.7 us -> 24.4 us
    ppermute x10, waiting for transfers between devices: 13.3 us -> 11.4 us  [swap(): return lax.ppermute(x, AXES, [(d, d ^ mask) for d in range(count)])]
    pallas_call x1, Pallas kernels: 0.75 us -> 1.48 us  [output_gate(): pl.pallas_call(gate_kernel, grid=(rows // step,), out_shape=jax.ShapeDtyp...]
    ppermute x10, starting transfers between devices: 14.9 us -> 15.6 us  [swap(): return lax.ppermute(x, AXES, [(d, d ^ mask) for d in range(count)])]
    pallas_call x1, Pallas kernels: 1.76 us -> 2.48 us  [left_operand(): pl.pallas_call(functools.partial(left_kernel, n_branch, near), out_shape=...]
  transfers between devices with their start and end apart: 12 -> 12, of which waited for: 6 -> 5; matrix products, arithmetic and copies ran while one was open for 0% -> 0% of each run, Pallas kernels for 20% -> 23%
where the time goes in v10:
time: 56.9 us; the launch traced here: 56.5 us
  starting transfers between devices  24.4 us (43%)
  Pallas kernels  17.4 us (31%)
  waiting for transfers between devices  12.7 us (22%)
  local copies, waits for them, and re-layouts  1.11 us (2%)
  between operations  0.87 us (2%)
    ppermute x10, starting transfers between devices, swap(): return lax.ppermute(x, AXES, [(d, d ^ mask) for d in range(count)])  15.6 us
    ppermute x10, waiting for transfers between devices, swap(): return lax.ppermute(x, AXES, [(d, d ^ mask) for d in range(count)])  11.4 us
    all_to_all x1, starting transfers between devices, own_channels_device(): lax.all_to_all(product, AXES, 0, 0, axis_index_groups=members, tiled=True)  4.89 us
    all_to_all x1, starting transfers between devices, own_channels_device(): received = lax.all_to_all(sent, AXES, 0, 0, tiled=True)  3.83 us
    pallas_call x1, Pallas kernels, right_operand(): pl.pallas_call(functools.partial(right_kernel, n_branch), out_shape=jax.S...  3.34 us
    pallas_call x1, Pallas kernels, pair_output(): pl.pallas_call(pair_output_kernel, out_shape=jax.ShapeDtypeStruct(x.shape...  2.93 us
    pallas_call x1, Pallas kernels, outer_update(): pl.pallas_call(outer_kernel, out_shape=jax.ShapeDtypeStruct((rows, width,...  2.91 us
    pallas_call x1, Pallas kernels, messages(): pl.pallas_call(functools.partial(message_kernel, n_branch, near, rows), o...  2.55 us
  transfers between devices with their start and end apart: 12, of which 5 were waited for; matrix products, arithmetic and copies ran while one was open for 0% of the time, Pallas kernels for 23%

profile of v10, /device:TPU:0, one launch (start us, length us, event | category | flops | bytes accessed | tf_op | source)
XLA Modules:
  0.0 56.5 jit_solution(8694433857215225559)
XLA Ops:
  0.6 0.5 collective-permute-start
  1.1 3.7 %collective-permute-start.1 = (bf16[1,256,256]{2,1,0:T(8,128)(2,1)}, bf16[1,256,256]{2,1,0:T(8,128)(2,1)S(1)}, u32[]{:S(2)}, u32[]{:S(2)}) collective-permute-start(bf16[1,256,256]{2,1,0:T(8,128)(2,1)} %seq_ref.1), channel_id=1, source_target_pairs={{0,8},{1,9},{2,10},{3,11},{4,12},{5,13},{6,14},{7,15},{8,0},{9,1},... | collective-permute-start | bytes 393224 | tf_op jit(solution)/shard_map/ppermute | solution.py:615
  4.8 3.3 %right_operand.1 = bf16[32,8,16,128]{3,2,1,0:T(8,128)(2,1)} custom-call(bf16[16,128,128]{2,1,0:T(8,128)(2,1)} %x_ref.4, bf16[128,640]{1,0:T(8,128)(2,1)} %w_ref.4), custom_call_target="tpu_custom_call" | custom-call | flops 134217728 | bytes 1572864 | tf_op jit(solution)/shard_map/right_operand/pallas_call | solution.py:289
  8.2 0.0 copy-start
  8.2 0.0 copy-start.1
  8.2 3.8 %all-to-all-start = ((bf16[32,8,16,128]{3,2,1,0:T(8,128)(2,1)}), bf16[32,8,16,128]{3,2,1,0:T(8,128)(2,1)S(1)}, u32[]{:S(2)}, u32[]{:S(2)}) async-start(bf16[32,8,16,128]{3,2,1,0:T(8,128)(2,1)} %right_operand.1), calls=%async_computation | async-start | bytes 2097152 | tf_op jit(solution)/shard_map/all_to_all | solution.py:643
  12.0 0.1 pad_add_fusion.where_ref
  12.1 2.5 %left_operand.1.left_ref = bf16[8,256,128]{2,1,0:T(8,128)(2,1)S(1)} custom-call(s32[2]{0:T(128)S(1)} %pad_add_fusion.where_ref, bf16[16,128,128]{2,1,0:T(8,128)(2,1)S(1)} %copy-done, bf16[16,128,128]{2,1,0:T(8,128)(2,1)S(1)} %collective-permute-done.other_ref, bf16[128,640]{1,0:T(8,128)(2,1)S(1)} %copy-done.1), custom_call_target="tpu_custom_call" | custom-call | flops 268435456 | bytes 2097152 | tf_op jit(solution)/shard_map/left_operand/pallas_call | solution.py:346
  14.7 2.6 %msa_transition_and_messages.1 = (bf16[1,256,256]{2,1,0:T(8,128)(2,1)}, bf16[336,128]{1,0:T(8,128)(2,1)S(1)}, bf16[336,128]{1,0:T(8,128)(2,1)S(1)}, bf16[336,128...) custom-call(s32[2]{0:T(128)S(1)} %pad_add_fusion.where_ref, ...), custom_call_target="tpu_custom_call" | custom-call | flops 20000000000 | bytes 1048576 | tf_op jit(solution)/shard_map/msa_transition_and_messages/pallas_call | solution.py:398
  17.2 1.8 %collective-permute-start.2 = (bf16[336,128]{1,0:T(8,128)(2,1)S(1)}, bf16[336,128]{1,0:T(8,128)(2,1)S(1)}, u32[]{:S(2)}, u32[]{:S(2)}) collective-permute-start(bf16[336,128]{1,0:T(8,128)(2,1)S(1)} %get-tuple-element.14), channel_id=1, source_target_pairs={{0,16},{1,17},{2,18},{3,19},{4,20},{5,21},{6,22},{7,23},{8,24},{9,... | collective-permute-start | bytes 258056 | tf_op jit(solution)/shard_map/ppermute | solution.py:615
  19.0 1.5 %collective-permute-start.3 = (bf16[336,128]{1,0:T(8,128)(2,1)S(1)}, bf16[336,128]{1,0:T(8,128)(2,1)S(1)}, u32[]{:S(2)}, u32[]{:S(2)}) collective-permute-start(bf16[336,128]{1,0:T(8,128)(2,1)S(1)} %get-tuple-element.15), channel_id=1, source_target_pairs={{0,2},{1,3},{2,0},{3,1},{4,6},{5,7},{6,4},{7,5},{8,10},{9,11},{10,... | collective-permute-start | bytes 258056 | tf_op jit(solution)/shard_map/ppermute | solution.py:615
  20.5 1.5 %collective-permute-start.4 = (bf16[336,128]{1,0:T(8,128)(2,1)S(1)}, bf16[336,128]{1,0:T(8,128)(2,1)S(1)}, u32[]{:S(2)}, u32[]{:S(2)}) collective-permute-start(bf16[336,128]{1,0:T(8,128)(2,1)S(1)} %get-tuple-element.16), channel_id=1, source_target_pairs={{0,4},{1,5},{2,6},{3,7},{4,0},{5,1},{6,2},{7,3},{8,12},{9,13},{10,... | collective-permute-start | bytes 258056 | tf_op jit(solution)/shard_map/ppermute | solution.py:615
  21.9 0.2 collective-permute-start.5
  22.2 2.7 %collective-permute-start.6 = (bf16[336,128]{1,0:T(8,128)(2,1)S(1)}, bf16[336,128]{1,0:T(8,128)(2,1)S(1)}, u32[]{:S(2)}, u32[]{:S(2)}) collective-permute-start(bf16[336,128]{1,0:T(8,128)(2,1)S(1)} %get-tuple-element.18), channel_id=1, source_target_pairs={{0,6},{1,7},{2,4},{3,5},{4,2},{5,3},{6,0},{7,1},{8,14},{9,15},{10,... | collective-permute-start | bytes 258056 | tf_op jit(solution)/shard_map/ppermute | solution.py:615
  24.9 1.5 %collective-permute-start.7 = (bf16[336,128]{1,0:T(8,128)(2,1)S(1)}, bf16[336,128]{1,0:T(8,128)(2,1)S(1)}, u32[]{:S(2)}, u32[]{:S(2)}) collective-permute-start(bf16[336,128]{1,0:T(8,128)(2,1)S(1)} %get-tuple-element.19), channel_id=1, source_target_pairs={{0,20},{1,21},{2,22},{3,23},{4,16},{5,17},{6,18},{7,19},{8,28},{9,... | collective-permute-start | bytes 258056 | tf_op jit(solution)/shard_map/ppermute | solution.py:615
  26.3 2.2 %collective-permute-start.8 = (bf16[336,128]{1,0:T(8,128)(2,1)S(1)}, bf16[336,128]{1,0:T(8,128)(2,1)S(1)}, u32[]{:S(2)}, u32[]{:S(2)}) collective-permute-start(bf16[336,128]{1,0:T(8,128)(2,1)S(1)} %get-tuple-element.20), channel_id=1, source_target_pairs={{0,18},{1,19},{2,16},{3,17},{4,22},{5,23},{6,20},{7,21},{8,26},{9,... | collective-permute-start | bytes 258056 | tf_op jit(solution)/shard_map/ppermute | solution.py:615
  28.6 3.4 %collective-permute-done.4.rest_3_ = bf16[336,128]{1,0:T(8,128)(2,1)S(1)} collective-permute-done((bf16[336,128]{1,0:T(8,128)(2,1)S(1)}, bf16[336,128]{1,0:T(8,128)(2,1)S(1)}, u32[]{:S(2)}, u32[]{:S(2)}) %collective-permute-start.4) | collective-permute-done | bytes 86048 | tf_op jit(solution)/shard_map/ppermute | solution.py:615
  32.0 2.2 %collective-permute-done.5.rest_4_ = bf16[336,128]{1,0:T(8,128)(2,1)S(1)} collective-permute-done((bf16[336,128]{1,0:T(8,128)(2,1)S(1)}, bf16[336,128]{1,0:T(8,128)(2,1)S(1)}, u32[]{:S(2)}, u32[]{:S(2)}) %collective-permute-start.5) | collective-permute-done | bytes 86048 | tf_op jit(solution)/shard_map/ppermute | solution.py:615
  34.3 3.6 %collective-permute-done.6.rest_5_ = bf16[336,128]{1,0:T(8,128)(2,1)S(1)} collective-permute-done((bf16[336,128]{1,0:T(8,128)(2,1)S(1)}, bf16[336,128]{1,0:T(8,128)(2,1)S(1)}, u32[]{:S(2)}, u32[]{:S(2)}) %collective-permute-start.6) | collective-permute-done | bytes 86048 | tf_op jit(solution)/shard_map/ppermute | solution.py:615
  37.9 2.2 %collective-permute-done.7.rest_6_ = bf16[336,128]{1,0:T(8,128)(2,1)S(1)} collective-permute-done((bf16[336,128]{1,0:T(8,128)(2,1)S(1)}, bf16[336,128]{1,0:T(8,128)(2,1)S(1)}, u32[]{:S(2)}, u32[]{:S(2)}) %collective-permute-start.7) | collective-permute-done | bytes 86048 | tf_op jit(solution)/shard_map/ppermute | solution.py:615
  40.0 1.7 %triangle_product.1 = bf16[16,8,16,128]{3,2,1,0:T(8,128)(2,1)} custom-call(s32[2]{0:T(128)S(1)} %pad_add_fusion.where_ref, bf16[32,8,16,128]{3,2,1,0:T(8,128)(2,1)S(1)} %all-to-all-done.in_ref, bf16[336,128]{1,0:T(8,128)(2,1)S(1)} %get-tuple-element.13.rest_0_, bf16[336,128]{1,0:T(8,128)(2,1)S(1)} %collective-permute-done.2.rest_1_, ...), custom_call_target="tpu_custom_call" | custom-call | flops 134217728 | bytes 2097152 | tf_op jit(solution)/shard_map/triangle_product/pallas_call | solution.py:486
  41.8 4.9 %all-to-all-start.1 = ((bf16[16,8,16,128]{3,2,1,0:T(8,128)(2,1)}), bf16[16,8,16,128]{3,2,1,0:T(8,128)(2,1)S(1)}, u32[]{:S(2)}, u32[]{:S(2)}) async-start(bf16[16,8,16,128]{3,2,1,0:T(8,128)(2,1)} %triangle_product.1), calls=%async_computation.1 | async-start | bytes 1048576 | tf_op jit(solution)/shard_map/all_to_all | solution.py:674
  46.7 0.0 copy-start.9
  46.7 0.1 collective-permute-start.9
  46.9 1.5 %triangle_output_gate.1.gate_ref = f32[16,128,128]{2,1,0:T(8,128)S(1)} custom-call(bf16[16,128,128]{2,1,0:T(8,128)(2,1)S(1)} %copy-done, bf16[128,640]{1,0:T(8,128)(2,1)S(1)} %copy-done.1), custom_call_target="tpu_custom_call" | custom-call | flops 67108864 | bytes 1572864 | tf_op jit(solution)/shard_map/triangle_output_gate/pallas_call | solution.py:424
  48.4 0.0 copy-start.2
  48.4 0.0 copy-start.3
  48.4 0.0 copy-start.4
  48.4 1.0 %copy-done.6 = bf16[8,80,128]{2,1,0:T(8,128)(2,1)S(1)} copy-done((bf16[8,80,128]{2,1,0:T(8,128)(2,1)S(1)}, bf16[8,80,128]{2,1,0:T(8,128)(2,1)}, u32[]{:S(2)}) %copy-start.6) | copy-done | bytes 163864
  49.4 2.9 %outer_product_mean.1.outer_ref = f32[16,128,128]{2,1,0:T(8,128)S(1)} custom-call(s32[2]{0:T(128)S(1)} %pad_add_fusion.where_ref, bf16[8,80,128]{2,1,0:T(8,128)(2,1)S(1)} %copy-done.6, bf16[8,80,128]{2,1,0:T(8,128)(2,1)S(1)} %collective-permute-done.9.refs_1_, bf16[1024,128]{1,0:T(8,128)(2,1)S(1)} %copy-done.9), custom_call_target="tpu_custom_call" | custom-call | flops 1073741824 | bytes 1048576 | tf_op jit(solution)/shard_map/outer_product_mean/pallas_call | solution.py:596
  52.3 1.3 %all-to-all-done.1.p_ref = bf16[16,8,16,128]{3,2,1,0:T(8,128)(2,1)S(1)} async-done(((bf16[16,8,16,128]{3,2,1,0:T(8,128)(2,1)}), bf16[16,8,16,128]{3,2,1,0:T(8,128)(2,1)S(1)}, u32[]{:S(2)}, u32[]{:S(2)}) %all-to-all-start.1) | async-done | bytes 524320 | tf_op jit(solution)/shard_map/all_to_all | solution.py:674
  53.6 2.9 %pair_output.1 = bf16[16,128,128]{2,1,0:T(8,128)(2,1)} custom-call(bf16[16,8,16,128]{3,2,1,0:T(8,128)(2,1)S(1)} %all-to-all-done.1.p_ref, bf16[16,128,128]{2,1,0:T(8,128)(2,1)S(1)} %copy-done, f32[16,128,128]{2,1,0:T(8,128)S(1)} %triangle_output_gate.1.gate_ref, f32[16,128,128]{2,1,0:T(8,128)S(1)} %outer_product_mean.1.outer_ref, ...), custom_call_target="tpu_custom_call" | custom-call | flops 603979776 | bytes 3670016 | tf_op jit(solution)/shard_map/pair_output/pallas_call | solution.py:541
  (32 shorter events, 0.1 us)
Async XLA Ops:
  0.6 11.5 %collective-permute-start = (bf16[16,128,128]{2,1,0:T(8,128)(2,1)}, bf16[16,128,128]{2,1,0:T(8,128)(2,1)S(1)}, u32[]{:S(2)}, u32[]{:S(2)}) collective-permute-start(bf16[16,128,128]{2,1,0:T(8,128)(2,1)} %x_ref.4), channel_id=1, source_target_pairs={{0,1},{1,0},{2,3},{3,2},{4,5},{5,4},{6,7},{7,6},{8,9},{9,8},{10,11... | collective-permute-start | bytes 1572872 | tf_op jit(solution)/shard_map/ppermute | solution.py:615
  1.1 13.5 %collective-permute-start.1 = (bf16[1,256,256]{2,1,0:T(8,128)(2,1)}, bf16[1,256,256]{2,1,0:T(8,128)(2,1)S(1)}, u32[]{:S(2)}, u32[]{:S(2)}) collective-permute-start(bf16[1,256,256]{2,1,0:T(8,128)(2,1)} %seq_ref.1), channel_id=1, source_target_pairs={{0,8},{1,9},{2,10},{3,11},{4,12},{5,13},{6,14},{7,15},{8,0},{9,1},... | collective-permute-start | bytes 393224 | tf_op jit(solution)/shard_map/ppermute | solution.py:615
  8.2 4.0 %copy-start = (bf16[16,128,128]{2,1,0:T(8,128)(2,1)S(1)}, bf16[16,128,128]{2,1,0:T(8,128)(2,1)}, u32[]{:S(2)}) copy-start(bf16[16,128,128]{2,1,0:T(8,128)(2,1)} %x_ref.4) | copy-start | bytes 1572868
  8.2 4.0 %copy-start.1 = (bf16[128,640]{1,0:T(8,128)(2,1)S(1)}, bf16[128,640]{1,0:T(8,128)(2,1)}, u32[]{:S(2)}) copy-start(bf16[128,640]{1,0:T(8,128)(2,1)} %w_ref.4) | copy-start | bytes 491524
  8.2 31.8 %all-to-all-start = ((bf16[32,8,16,128]{3,2,1,0:T(8,128)(2,1)}), bf16[32,8,16,128]{3,2,1,0:T(8,128)(2,1)S(1)}, u32[]{:S(2)}, u32[]{:S(2)}) async-start(bf16[32,8,16,128]{3,2,1,0:T(8,128)(2,1)} %right_operand.1), calls=%async_computation | async-start | bytes 2097152 | tf_op jit(solution)/shard_map/all_to_all | solution.py:643
  12.1 2.5 %copy-start.7 = (bf16[256,1024]{1,0:T(8,128)(2,1)S(1)}, bf16[256,1024]{1,0:T(8,128)(2,1)}, u32[]{:S(2)}) copy-start(bf16[256,1024]{1,0:T(8,128)(2,1)} %up_ref.2) | copy-start | bytes 1572868
  12.1 2.5 %copy-start.8 = (bf16[1024,256]{1,0:T(8,128)(2,1)S(1)}, bf16[1024,256]{1,0:T(8,128)(2,1)}, u32[]{:S(2)}) copy-start(bf16[1024,256]{1,0:T(8,128)(2,1)} %down_ref.2) | copy-start | bytes 1572868
  12.1 2.6 %copy-start.10 = (bf16[1,256,256]{2,1,0:T(8,128)(2,1)S(1)}, bf16[1,256,256]{2,1,0:T(8,128)(2,1)}, u32[]{:S(2)}) copy-start(bf16[1,256,256]{2,1,0:T(8,128)(2,1)} %seq_ref.1) | copy-start | bytes 393220
  12.1 2.6 %copy-start.11 = (bf16[256,64]{0,1:T(8,128)(2,1)S(1)}, bf16[256,64]{0,1:T(8,128)(2,1)}, u32[]{:S(2)}) copy-start(bf16[256,64]{0,1:T(8,128)(2,1)} %param.14) | copy-start | bytes 98308
  17.2 7.6 %collective-permute-start.2 = (bf16[336,128]{1,0:T(8,128)(2,1)S(1)}, bf16[336,128]{1,0:T(8,128)(2,1)S(1)}, u32[]{:S(2)}, u32[]{:S(2)}) collective-permute-start(bf16[336,128]{1,0:T(8,128)(2,1)S(1)} %get-tuple-element.14), channel_id=1, source_target_pairs={{0,16},{1,17},{2,18},{3,19},{4,20},{5,21},{6,22},{7,23},{8,24},{9,... | collective-permute-start | bytes 258056 | tf_op jit(solution)/shard_map/ppermute | solution.py:615
  19.0 7.3 %collective-permute-start.3 = (bf16[336,128]{1,0:T(8,128)(2,1)S(1)}, bf16[336,128]{1,0:T(8,128)(2,1)S(1)}, u32[]{:S(2)}, u32[]{:S(2)}) collective-permute-start(bf16[336,128]{1,0:T(8,128)(2,1)S(1)} %get-tuple-element.15), channel_id=1, source_target_pairs={{0,2},{1,3},{2,0},{3,1},{4,6},{5,7},{6,4},{7,5},{8,10},{9,11},{10,... | collective-permute-start | bytes 258056 | tf_op jit(solution)/shard_map/ppermute | solution.py:615
  20.5 11.5 %collective-permute-start.4 = (bf16[336,128]{1,0:T(8,128)(2,1)S(1)}, bf16[336,128]{1,0:T(8,128)(2,1)S(1)}, u32[]{:S(2)}, u32[]{:S(2)}) collective-permute-start(bf16[336,128]{1,0:T(8,128)(2,1)S(1)} %get-tuple-element.16), channel_id=1, source_target_pairs={{0,4},{1,5},{2,6},{3,7},{4,0},{5,1},{6,2},{7,3},{8,12},{9,13},{10,... | collective-permute-start | bytes 258056 | tf_op jit(solution)/shard_map/ppermute | solution.py:615
  21.9 12.3 %collective-permute-start.5 = (bf16[336,128]{1,0:T(8,128)(2,1)S(1)}, bf16[336,128]{1,0:T(8,128)(2,1)S(1)}, u32[]{:S(2)}, u32[]{:S(2)}) collective-permute-start(bf16[336,128]{1,0:T(8,128)(2,1)S(1)} %get-tuple-element.17), channel_id=1, source_target_pairs={{0,22},{1,23},{2,20},{3,21},{4,18},{5,19},{6,16},{7,17},{8,30},{9,... | collective-permute-start | bytes 258056 | tf_op jit(solution)/shard_map/ppermute | solution.py:615
  22.2 15.7 %collective-permute-start.6 = (bf16[336,128]{1,0:T(8,128)(2,1)S(1)}, bf16[336,128]{1,0:T(8,128)(2,1)S(1)}, u32[]{:S(2)}, u32[]{:S(2)}) collective-permute-start(bf16[336,128]{1,0:T(8,128)(2,1)S(1)} %get-tuple-element.18), channel_id=1, source_target_pairs={{0,6},{1,7},{2,4},{3,5},{4,2},{5,3},{6,0},{7,1},{8,14},{9,15},{10,... | collective-permute-start | bytes 258056 | tf_op jit(solution)/shard_map/ppermute | solution.py:615
  24.9 15.2 %collective-permute-start.7 = (bf16[336,128]{1,0:T(8,128)(2,1)S(1)}, bf16[336,128]{1,0:T(8,128)(2,1)S(1)}, u32[]{:S(2)}, u32[]{:S(2)}) collective-permute-start(bf16[336,128]{1,0:T(8,128)(2,1)S(1)} %get-tuple-element.19), channel_id=1, source_target_pairs={{0,20},{1,21},{2,22},{3,23},{4,16},{5,17},{6,18},{7,19},{8,28},{9,... | collective-permute-start | bytes 258056 | tf_op jit(solution)/shard_map/ppermute | solution.py:615
  26.3 13.7 %collective-permute-start.8 = (bf16[336,128]{1,0:T(8,128)(2,1)S(1)}, bf16[336,128]{1,0:T(8,128)(2,1)S(1)}, u32[]{:S(2)}, u32[]{:S(2)}) collective-permute-start(bf16[336,128]{1,0:T(8,128)(2,1)S(1)} %get-tuple-element.20), channel_id=1, source_target_pairs={{0,18},{1,19},{2,16},{3,17},{4,22},{5,23},{6,20},{7,21},{8,26},{9,... | collective-permute-start | bytes 258056 | tf_op jit(solution)/shard_map/ppermute | solution.py:615
  41.8 11.8 %all-to-all-start.1 = ((bf16[16,8,16,128]{3,2,1,0:T(8,128)(2,1)}), bf16[16,8,16,128]{3,2,1,0:T(8,128)(2,1)S(1)}, u32[]{:S(2)}, u32[]{:S(2)}) async-start(bf16[16,8,16,128]{3,2,1,0:T(8,128)(2,1)} %triangle_product.1), calls=%async_computation.1 | async-start | bytes 1048576 | tf_op jit(solution)/shard_map/all_to_all | solution.py:674
  46.7 1.7 %copy-start.5 = (bf16[8,80,128]{2,1,0:T(8,128)(2,1)}, bf16[8,80,128]{2,1,0:T(8,128)(2,1)S(1)}, u32[]{:S(2)}) copy-start(bf16[8,80,128]{2,1,0:T(8,128)(2,1)S(1)} %fusion.refs_0_) | copy-start | bytes 491524
  46.7 1.7 %copy-start.9 = (bf16[1024,128]{1,0:T(8,128)(2,1)S(1)}, bf16[1024,128]{1,0:T(8,128)(2,1)}, u32[]{:S(2)}) copy-start(bf16[1024,128]{1,0:T(8,128)(2,1)} %refs_2_.1) | copy-start | bytes 786436
  46.7 1.7 %collective-permute-start.9 = (bf16[8,80,128]{2,1,0:T(8,128)(2,1)S(1)}, bf16[8,80,128]{2,1,0:T(8,128)(2,1)S(1)}, u32[]{:S(2)}, u32[]{:S(2)}) collective-permute-start(bf16[8,80,128]{2,1,0:T(8,128)(2,1)S(1)} %fusion.refs_0_), channel_id=1, source_target_pairs={{0,1},{1,0},{2,3},{3,2},{4,5},{5,4},{6,7},{7,6},{8,9},{9,8},{10,11... | collective-permute-start | bytes 491528 | tf_op jit(solution)/shard_map/ppermute | solution.py:615
  48.4 5.2 %copy-start.2 = (bf16[128,512]{1,0:T(8,128)(2,1)S(1)}, bf16[128,512]{1,0:T(8,128)(2,1)}, u32[]{:S(2)}) copy-start(bf16[128,512]{1,0:T(8,128)(2,1)} %up_ref.3) | copy-start | bytes 393220
  48.4 5.2 %copy-start.3 = (bf16[512,128]{1,0:T(8,128)(2,1)S(1)}, bf16[512,128]{1,0:T(8,128)(2,1)}, u32[]{:S(2)}) copy-start(bf16[512,128]{1,0:T(8,128)(2,1)} %down_ref.3) | copy-start | bytes 393220
  48.4 5.2 %copy-start.4 = (bf16[128,128]{1,0:T(8,128)(2,1)S(1)}, bf16[128,128]{1,0:T(8,128)(2,1)}, u32[]{:S(2)}) copy-start(bf16[128,128]{1,0:T(8,128)(2,1)} %w_ref.5) | copy-start | bytes 98308
  48.4 1.0 %copy-start.6 = (bf16[8,80,128]{2,1,0:T(8,128)(2,1)S(1)}, bf16[8,80,128]{2,1,0:T(8,128)(2,1)}, u32[]{:S(2)}) copy-start(bf16[8,80,128]{2,1,0:T(8,128)(2,1)} %copy-done.5) | copy-start | bytes 491524

commit v11 on v10

--- a/solution.py
+++ b/solution.py
@@ -442,6 +442,7 @@
     branch, row_at = where_ref[0], where_ref[1]
     place = lax.shift_right_logical(lax.bitwise_and(row_at, near - 1), 1)
     outs = []
+    ends = (0, per // 2, per * 3 // 4, per)
     for c in range(per):
         span = slice(c * 2 * rows, (c + 1) * 2 * rows)
         left = jnp.concatenate(
@@ -469,10 +470,10 @@
                     out_ref[n_branch * near - 1 - (b * near + at + k), c] = part[
                         k * rows : (k + 1) * rows, b * width : (b + 1) * width
                     ]
-        if c % 2 == 1:
-            half = pl.ds(c - 1, 2)
+        if c + 1 in ends:
+            done = pl.ds(ends[len(outs)], c + 1 - ends[len(outs)])
             copy = pltpu.make_async_copy(
-                out_ref.at[:, half], out_hbm.at[:, half], sems.at[c // 2]
+                out_ref.at[:, done], out_hbm.at[:, done], sems.at[len(outs)]
             )
             copy.start()
             outs.append(copy)

time: 56.9 us -> 56.9 us (level)
  no operation moved by 1% of the time
where the time goes in v11:
time: 56.9 us; the launch traced here: 56.5 us
  starting transfers between devices  24.4 us (43%)
  Pallas kernels  17.4 us (31%)
  waiting for transfers between devices  12.7 us (22%)
  local copies, waits for them, and re-layouts  1.11 us (2%)
  between operations  0.87 us (2%)
    ppermute x10, starting transfers between devices, swap(): return lax.ppermute(x, AXES, [(d, d ^ mask) for d in range(count)])  15.6 us
    ppermute x10, waiting for transfers between devices, swap(): return lax.ppermute(x, AXES, [(d, d ^ mask) for d in range(count)])  11.4 us
    all_to_all x1, starting transfers between devices, own_channels_device(): lax.all_to_all(product, AXES, 0, 0, axis_index_groups=members, tiled=True)  4.89 us
    all_to_all x1, starting transfers between devices, own_channels_device(): received = lax.all_to_all(sent, AXES, 0, 0, tiled=True)  3.83 us
    pallas_call x1, Pallas kernels, right_operand(): pl.pallas_call(functools.partial(right_kernel, n_branch), out_shape=jax.S...  3.34 us
    pallas_call x1, Pallas kernels, pair_output(): pl.pallas_call(pair_output_kernel, out_shape=jax.ShapeDtypeStruct(x.shape...  2.93 us
    pallas_call x1, Pallas kernels, outer_update(): pl.pallas_call(outer_kernel, out_shape=jax.ShapeDtypeStruct((rows, width,...  2.91 us
    pallas_call x1, Pallas kernels, messages(): pl.pallas_call(functools.partial(message_kernel, n_branch, near, rows), o...  2.55 us
  transfers between devices with their start and end apart: 12, of which 5 were waited for; matrix products, arithmetic and copies ran while one was open for 0% of the time, Pallas kernels for 23%

profile of v11, /device:TPU:0, one launch (start us, length us, event | category | flops | bytes accessed | tf_op | source)
XLA Modules:
  0.0 56.5 jit_solution(1150559342140249680)
XLA Ops:
  0.6 0.5 collective-permute-start
  1.1 3.7 %collective-permute-start.1 = (bf16[1,256,256]{2,1,0:T(8,128)(2,1)}, bf16[1,256,256]{2,1,0:T(8,128)(2,1)S(1)}, u32[]{:S(2)}, u32[]{:S(2)}) collective-permute-start(bf16[1,256,256]{2,1,0:T(8,128)(2,1)} %seq_ref.1), channel_id=1, source_target_pairs={{0,8},{1,9},{2,10},{3,11},{4,12},{5,13},{6,14},{7,15},{8,0},{9,1},... | collective-permute-start | bytes 393224 | tf_op jit(solution)/shard_map/ppermute | solution.py:616
  4.8 3.3 %right_operand.1 = bf16[32,8,16,128]{3,2,1,0:T(8,128)(2,1)} custom-call(bf16[16,128,128]{2,1,0:T(8,128)(2,1)} %x_ref.4, bf16[128,640]{1,0:T(8,128)(2,1)} %w_ref.4), custom_call_target="tpu_custom_call" | custom-call | flops 134217728 | bytes 1572864 | tf_op jit(solution)/shard_map/right_operand/pallas_call | solution.py:289
  8.2 0.0 copy-start
  8.2 0.0 copy-start.1
  8.2 3.8 %all-to-all-start = ((bf16[32,8,16,128]{3,2,1,0:T(8,128)(2,1)}), bf16[32,8,16,128]{3,2,1,0:T(8,128)(2,1)S(1)}, u32[]{:S(2)}, u32[]{:S(2)}) async-start(bf16[32,8,16,128]{3,2,1,0:T(8,128)(2,1)} %right_operand.1), calls=%async_computation | async-start | bytes 2097152 | tf_op jit(solution)/shard_map/all_to_all | solution.py:644
  12.0 0.1 pad_add_fusion.where_ref
  12.1 2.5 %left_operand.1.left_ref = bf16[8,256,128]{2,1,0:T(8,128)(2,1)S(1)} custom-call(s32[2]{0:T(128)S(1)} %pad_add_fusion.where_ref, bf16[16,128,128]{2,1,0:T(8,128)(2,1)S(1)} %copy-done, bf16[16,128,128]{2,1,0:T(8,128)(2,1)S(1)} %collective-permute-done.other_ref, bf16[128,640]{1,0:T(8,128)(2,1)S(1)} %copy-done.1), custom_call_target="tpu_custom_call" | custom-call | flops 268435456 | bytes 2097152 | tf_op jit(solution)/shard_map/left_operand/pallas_call | solution.py:346
  14.7 2.6 %msa_transition_and_messages.1 = (bf16[1,256,256]{2,1,0:T(8,128)(2,1)}, bf16[336,128]{1,0:T(8,128)(2,1)S(1)}, bf16[336,128]{1,0:T(8,128)(2,1)S(1)}, bf16[336,128...) custom-call(s32[2]{0:T(128)S(1)} %pad_add_fusion.where_ref, ...), custom_call_target="tpu_custom_call" | custom-call | flops 20000000000 | bytes 1048576 | tf_op jit(solution)/shard_map/msa_transition_and_messages/pallas_call | solution.py:398
  17.2 1.8 %collective-permute-start.2 = (bf16[336,128]{1,0:T(8,128)(2,1)S(1)}, bf16[336,128]{1,0:T(8,128)(2,1)S(1)}, u32[]{:S(2)}, u32[]{:S(2)}) collective-permute-start(bf16[336,128]{1,0:T(8,128)(2,1)S(1)} %get-tuple-element.14), channel_id=1, source_target_pairs={{0,16},{1,17},{2,18},{3,19},{4,20},{5,21},{6,22},{7,23},{8,24},{9,... | collective-permute-start | bytes 258056 | tf_op jit(solution)/shard_map/ppermute | solution.py:616
  19.0 1.5 %collective-permute-start.3 = (bf16[336,128]{1,0:T(8,128)(2,1)S(1)}, bf16[336,128]{1,0:T(8,128)(2,1)S(1)}, u32[]{:S(2)}, u32[]{:S(2)}) collective-permute-start(bf16[336,128]{1,0:T(8,128)(2,1)S(1)} %get-tuple-element.15), channel_id=1, source_target_pairs={{0,2},{1,3},{2,0},{3,1},{4,6},{5,7},{6,4},{7,5},{8,10},{9,11},{10,... | collective-permute-start | bytes 258056 | tf_op jit(solution)/shard_map/ppermute | solution.py:616
  20.5 1.5 %collective-permute-start.4 = (bf16[336,128]{1,0:T(8,128)(2,1)S(1)}, bf16[336,128]{1,0:T(8,128)(2,1)S(1)}, u32[]{:S(2)}, u32[]{:S(2)}) collective-permute-start(bf16[336,128]{1,0:T(8,128)(2,1)S(1)} %get-tuple-element.16), channel_id=1, source_target_pairs={{0,4},{1,5},{2,6},{3,7},{4,0},{5,1},{6,2},{7,3},{8,12},{9,13},{10,... | collective-permute-start | bytes 258056 | tf_op jit(solution)/shard_map/ppermute | solution.py:616
  21.9 0.2 collective-permute-start.5
  22.2 2.7 %collective-permute-start.6 = (bf16[336,128]{1,0:T(8,128)(2,1)S(1)}, bf16[336,128]{1,0:T(8,128)(2,1)S(1)}, u32[]{:S(2)}, u32[]{:S(2)}) collective-permute-start(bf16[336,128]{1,0:T(8,128)(2,1)S(1)} %get-tuple-element.18), channel_id=1, source_target_pairs={{0,6},{1,7},{2,4},{3,5},{4,2},{5,3},{6,0},{7,1},{8,14},{9,15},{10,... | collective-permute-start | bytes 258056 | tf_op jit(solution)/shard_map/ppermute | solution.py:616
  24.9 1.5 %collective-permute-start.7 = (bf16[336,128]{1,0:T(8,128)(2,1)S(1)}, bf16[336,128]{1,0:T(8,128)(2,1)S(1)}, u32[]{:S(2)}, u32[]{:S(2)}) collective-permute-start(bf16[336,128]{1,0:T(8,128)(2,1)S(1)} %get-tuple-element.19), channel_id=1, source_target_pairs={{0,20},{1,21},{2,22},{3,23},{4,16},{5,17},{6,18},{7,19},{8,28},{9,... | collective-permute-start | bytes 258056 | tf_op jit(solution)/shard_map/ppermute | solution.py:616
  26.3 2.2 %collective-permute-start.8 = (bf16[336,128]{1,0:T(8,128)(2,1)S(1)}, bf16[336,128]{1,0:T(8,128)(2,1)S(1)}, u32[]{:S(2)}, u32[]{:S(2)}) collective-permute-start(bf16[336,128]{1,0:T(8,128)(2,1)S(1)} %get-tuple-element.20), channel_id=1, source_target_pairs={{0,18},{1,19},{2,16},{3,17},{4,22},{5,23},{6,20},{7,21},{8,26},{9,... | collective-permute-start | bytes 258056 | tf_op jit(solution)/shard_map/ppermute | solution.py:616
  28.6 3.4 %collective-permute-done.4.rest_3_ = bf16[336,128]{1,0:T(8,128)(2,1)S(1)} collective-permute-done((bf16[336,128]{1,0:T(8,128)(2,1)S(1)}, bf16[336,128]{1,0:T(8,128)(2,1)S(1)}, u32[]{:S(2)}, u32[]{:S(2)}) %collective-permute-start.4) | collective-permute-done | bytes 86048 | tf_op jit(solution)/shard_map/ppermute | solution.py:616
  32.0 2.2 %collective-permute-done.5.rest_4_ = bf16[336,128]{1,0:T(8,128)(2,1)S(1)} collective-permute-done((bf16[336,128]{1,0:T(8,128)(2,1)S(1)}, bf16[336,128]{1,0:T(8,128)(2,1)S(1)}, u32[]{:S(2)}, u32[]{:S(2)}) %collective-permute-start.5) | collective-permute-done | bytes 86048 | tf_op jit(solution)/shard_map/ppermute | solution.py:616
  34.3 3.6 %collective-permute-done.6.rest_5_ = bf16[336,128]{1,0:T(8,128)(2,1)S(1)} collective-permute-done((bf16[336,128]{1,0:T(8,128)(2,1)S(1)}, bf16[336,128]{1,0:T(8,128)(2,1)S(1)}, u32[]{:S(2)}, u32[]{:S(2)}) %collective-permute-start.6) | collective-permute-done | bytes 86048 | tf_op jit(solution)/shard_map/ppermute | solution.py:616
  37.9 2.2 %collective-permute-done.7.rest_6_ = bf16[336,128]{1,0:T(8,128)(2,1)S(1)} collective-permute-done((bf16[336,128]{1,0:T(8,128)(2,1)S(1)}, bf16[336,128]{1,0:T(8,128)(2,1)S(1)}, u32[]{:S(2)}, u32[]{:S(2)}) %collective-permute-start.7) | collective-permute-done | bytes 86048 | tf_op jit(solution)/shard_map/ppermute | solution.py:616
  40.0 1.7 %triangle_product.1 = bf16[16,8,16,128]{3,2,1,0:T(8,128)(2,1)} custom-call(s32[2]{0:T(128)S(1)} %pad_add_fusion.where_ref, bf16[32,8,16,128]{3,2,1,0:T(8,128)(2,1)S(1)} %all-to-all-done.in_ref, bf16[336,128]{1,0:T(8,128)(2,1)S(1)} %get-tuple-element.13.rest_0_, bf16[336,128]{1,0:T(8,128)(2,1)S(1)} %collective-permute-done.2.rest_1_, ...), custom_call_target="tpu_custom_call" | custom-call | flops 134217728 | bytes 2097152 | tf_op jit(solution)/shard_map/triangle_product/pallas_call | solution.py:487
  41.8 4.9 %all-to-all-start.1 = ((bf16[16,8,16,128]{3,2,1,0:T(8,128)(2,1)}), bf16[16,8,16,128]{3,2,1,0:T(8,128)(2,1)S(1)}, u32[]{:S(2)}, u32[]{:S(2)}) async-start(bf16[16,8,16,128]{3,2,1,0:T(8,128)(2,1)} %triangle_product.1), calls=%async_computation.1 | async-start | bytes 1048576 | tf_op jit(solution)/shard_map/all_to_all | solution.py:675
  46.7 0.0 copy-start.9
  46.7 0.1 collective-permute-start.9
  46.9 1.5 %triangle_output_gate.1.gate_ref = f32[16,128,128]{2,1,0:T(8,128)S(1)} custom-call(bf16[16,128,128]{2,1,0:T(8,128)(2,1)S(1)} %copy-done, bf16[128,640]{1,0:T(8,128)(2,1)S(1)} %copy-done.1), custom_call_target="tpu_custom_call" | custom-call | flops 67108864 | bytes 1572864 | tf_op jit(solution)/shard_map/triangle_output_gate/pallas_call | solution.py:424
  48.4 0.0 copy-start.2
  48.4 0.0 copy-start.3
  48.4 0.0 copy-start.4
  48.4 1.0 %copy-done.6 = bf16[8,80,128]{2,1,0:T(8,128)(2,1)S(1)} copy-done((bf16[8,80,128]{2,1,0:T(8,128)(2,1)S(1)}, bf16[8,80,128]{2,1,0:T(8,128)(2,1)}, u32[]{:S(2)}) %copy-start.6) | copy-done | bytes 163864
  49.4 2.9 %outer_product_mean.1.outer_ref = f32[16,128,128]{2,1,0:T(8,128)S(1)} custom-call(s32[2]{0:T(128)S(1)} %pad_add_fusion.where_ref, bf16[8,80,128]{2,1,0:T(8,128)(2,1)S(1)} %copy-done.6, bf16[8,80,128]{2,1,0:T(8,128)(2,1)S(1)} %collective-permute-done.9.refs_1_, bf16[1024,128]{1,0:T(8,128)(2,1)S(1)} %copy-done.9), custom_call_target="tpu_custom_call" | custom-call | flops 1073741824 | bytes 1048576 | tf_op jit(solution)/shard_map/outer_product_mean/pallas_call | solution.py:597
  52.3 1.3 %all-to-all-done.1.p_ref = bf16[16,8,16,128]{3,2,1,0:T(8,128)(2,1)S(1)} async-done(((bf16[16,8,16,128]{3,2,1,0:T(8,128)(2,1)}), bf16[16,8,16,128]{3,2,1,0:T(8,128)(2,1)S(1)}, u32[]{:S(2)}, u32[]{:S(2)}) %all-to-all-start.1) | async-done | bytes 524320 | tf_op jit(solution)/shard_map/all_to_all | solution.py:675
  53.6 2.9 %pair_output.1 = bf16[16,128,128]{2,1,0:T(8,128)(2,1)} custom-call(bf16[16,8,16,128]{3,2,1,0:T(8,128)(2,1)S(1)} %all-to-all-done.1.p_ref, bf16[16,128,128]{2,1,0:T(8,128)(2,1)S(1)} %copy-done, f32[16,128,128]{2,1,0:T(8,128)S(1)} %triangle_output_gate.1.gate_ref, f32[16,128,128]{2,1,0:T(8,128)S(1)} %outer_product_mean.1.outer_ref, ...), custom_call_target="tpu_custom_call" | custom-call | flops 603979776 | bytes 3670016 | tf_op jit(solution)/shard_map/pair_output/pallas_call | solution.py:542
  (32 shorter events, 0.1 us)
Async XLA Ops:
  0.6 11.5 %collective-permute-start = (bf16[16,128,128]{2,1,0:T(8,128)(2,1)}, bf16[16,128,128]{2,1,0:T(8,128)(2,1)S(1)}, u32[]{:S(2)}, u32[]{:S(2)}) collective-permute-start(bf16[16,128,128]{2,1,0:T(8,128)(2,1)} %x_ref.4), channel_id=1, source_target_pairs={{0,1},{1,0},{2,3},{3,2},{4,5},{5,4},{6,7},{7,6},{8,9},{9,8},{10,11... | collective-permute-start | bytes 1572872 | tf_op jit(solution)/shard_map/ppermute | solution.py:616
  1.1 13.5 %collective-permute-start.1 = (bf16[1,256,256]{2,1,0:T(8,128)(2,1)}, bf16[1,256,256]{2,1,0:T(8,128)(2,1)S(1)}, u32[]{:S(2)}, u32[]{:S(2)}) collective-permute-start(bf16[1,256,256]{2,1,0:T(8,128)(2,1)} %seq_ref.1), channel_id=1, source_target_pairs={{0,8},{1,9},{2,10},{3,11},{4,12},{5,13},{6,14},{7,15},{8,0},{9,1},... | collective-permute-start | bytes 393224 | tf_op jit(solution)/shard_map/ppermute | solution.py:616
  8.2 4.0 %copy-start = (bf16[16,128,128]{2,1,0:T(8,128)(2,1)S(1)}, bf16[16,128,128]{2,1,0:T(8,128)(2,1)}, u32[]{:S(2)}) copy-start(bf16[16,128,128]{2,1,0:T(8,128)(2,1)} %x_ref.4) | copy-start | bytes 1572868
  8.2 4.0 %copy-start.1 = (bf16[128,640]{1,0:T(8,128)(2,1)S(1)}, bf16[128,640]{1,0:T(8,128)(2,1)}, u32[]{:S(2)}) copy-start(bf16[128,640]{1,0:T(8,128)(2,1)} %w_ref.4) | copy-start | bytes 491524
  8.2 31.8 %all-to-all-start = ((bf16[32,8,16,128]{3,2,1,0:T(8,128)(2,1)}), bf16[32,8,16,128]{3,2,1,0:T(8,128)(2,1)S(1)}, u32[]{:S(2)}, u32[]{:S(2)}) async-start(bf16[32,8,16,128]{3,2,1,0:T(8,128)(2,1)} %right_operand.1), calls=%async_computation | async-start | bytes 2097152 | tf_op jit(solution)/shard_map/all_to_all | solution.py:644
  12.1 2.5 %copy-start.7 = (bf16[256,1024]{1,0:T(8,128)(2,1)S(1)}, bf16[256,1024]{1,0:T(8,128)(2,1)}, u32[]{:S(2)}) copy-start(bf16[256,1024]{1,0:T(8,128)(2,1)} %up_ref.2) | copy-start | bytes 1572868
  12.1 2.5 %copy-start.8 = (bf16[1024,256]{1,0:T(8,128)(2,1)S(1)}, bf16[1024,256]{1,0:T(8,128)(2,1)}, u32[]{:S(2)}) copy-start(bf16[1024,256]{1,0:T(8,128)(2,1)} %down_ref.2) | copy-start | bytes 1572868
  12.1 2.6 %copy-start.10 = (bf16[1,256,256]{2,1,0:T(8,128)(2,1)S(1)}, bf16[1,256,256]{2,1,0:T(8,128)(2,1)}, u32[]{:S(2)}) copy-start(bf16[1,256,256]{2,1,0:T(8,128)(2,1)} %seq_ref.1) | copy-start | bytes 393220
  12.1 2.6 %copy-start.11 = (bf16[256,64]{0,1:T(8,128)(2,1)S(1)}, bf16[256,64]{0,1:T(8,128)(2,1)}, u32[]{:S(2)}) copy-start(bf16[256,64]{0,1:T(8,128)(2,1)} %param.14) | copy-start | bytes 98308
  17.2 7.6 %collective-permute-start.2 = (bf16[336,128]{1,0:T(8,128)(2,1)S(1)}, bf16[336,128]{1,0:T(8,128)(2,1)S(1)}, u32[]{:S(2)}, u32[]{:S(2)}) collective-permute-start(bf16[336,128]{1,0:T(8,128)(2,1)S(1)} %get-tuple-element.14), channel_id=1, source_target_pairs={{0,16},{1,17},{2,18},{3,19},{4,20},{5,21},{6,22},{7,23},{8,24},{9,... | collective-permute-start | bytes 258056 | tf_op jit(solution)/shard_map/ppermute | solution.py:616
  19.0 7.3 %collective-permute-start.3 = (bf16[336,128]{1,0:T(8,128)(2,1)S(1)}, bf16[336,128]{1,0:T(8,128)(2,1)S(1)}, u32[]{:S(2)}, u32[]{:S(2)}) collective-permute-start(bf16[336,128]{1,0:T(8,128)(2,1)S(1)} %get-tuple-element.15), channel_id=1, source_target_pairs={{0,2},{1,3},{2,0},{3,1},{4,6},{5,7},{6,4},{7,5},{8,10},{9,11},{10,... | collective-permute-start | bytes 258056 | tf_op jit(solution)/shard_map/ppermute | solution.py:616
  20.5 11.5 %collective-permute-start.4 = (bf16[336,128]{1,0:T(8,128)(2,1)S(1)}, bf16[336,128]{1,0:T(8,128)(2,1)S(1)}, u32[]{:S(2)}, u32[]{:S(2)}) collective-permute-start(bf16[336,128]{1,0:T(8,128)(2,1)S(1)} %get-tuple-element.16), channel_id=1, source_target_pairs={{0,4},{1,5},{2,6},{3,7},{4,0},{5,1},{6,2},{7,3},{8,12},{9,13},{10,... | collective-permute-start | bytes 258056 | tf_op jit(solution)/shard_map/ppermute | solution.py:616
  21.9 12.3 %collective-permute-start.5 = (bf16[336,128]{1,0:T(8,128)(2,1)S(1)}, bf16[336,128]{1,0:T(8,128)(2,1)S(1)}, u32[]{:S(2)}, u32[]{:S(2)}) collective-permute-start(bf16[336,128]{1,0:T(8,128)(2,1)S(1)} %get-tuple-element.17), channel_id=1, source_target_pairs={{0,22},{1,23},{2,20},{3,21},{4,18},{5,19},{6,16},{7,17},{8,30},{9,... | collective-permute-start | bytes 258056 | tf_op jit(solution)/shard_map/ppermute | solution.py:616
  22.2 15.7 %collective-permute-start.6 = (bf16[336,128]{1,0:T(8,128)(2,1)S(1)}, bf16[336,128]{1,0:T(8,128)(2,1)S(1)}, u32[]{:S(2)}, u32[]{:S(2)}) collective-permute-start(bf16[336,128]{1,0:T(8,128)(2,1)S(1)} %get-tuple-element.18), channel_id=1, source_target_pairs={{0,6},{1,7},{2,4},{3,5},{4,2},{5,3},{6,0},{7,1},{8,14},{9,15},{10,... | collective-permute-start | bytes 258056 | tf_op jit(solution)/shard_map/ppermute | solution.py:616
  24.9 15.2 %collective-permute-start.7 = (bf16[336,128]{1,0:T(8,128)(2,1)S(1)}, bf16[336,128]{1,0:T(8,128)(2,1)S(1)}, u32[]{:S(2)}, u32[]{:S(2)}) collective-permute-start(bf16[336,128]{1,0:T(8,128)(2,1)S(1)} %get-tuple-element.19), channel_id=1, source_target_pairs={{0,20},{1,21},{2,22},{3,23},{4,16},{5,17},{6,18},{7,19},{8,28},{9,... | collective-permute-start | bytes 258056 | tf_op jit(solution)/shard_map/ppermute | solution.py:616
  26.3 13.7 %collective-permute-start.8 = (bf16[336,128]{1,0:T(8,128)(2,1)S(1)}, bf16[336,128]{1,0:T(8,128)(2,1)S(1)}, u32[]{:S(2)}, u32[]{:S(2)}) collective-permute-start(bf16[336,128]{1,0:T(8,128)(2,1)S(1)} %get-tuple-element.20), channel_id=1, source_target_pairs={{0,18},{1,19},{2,16},{3,17},{4,22},{5,23},{6,20},{7,21},{8,26},{9,... | collective-permute-start | bytes 258056 | tf_op jit(solution)/shard_map/ppermute | solution.py:616
  41.8 11.8 %all-to-all-start.1 = ((bf16[16,8,16,128]{3,2,1,0:T(8,128)(2,1)}), bf16[16,8,16,128]{3,2,1,0:T(8,128)(2,1)S(1)}, u32[]{:S(2)}, u32[]{:S(2)}) async-start(bf16[16,8,16,128]{3,2,1,0:T(8,128)(2,1)} %triangle_product.1), calls=%async_computation.1 | async-start | bytes 1048576 | tf_op jit(solution)/shard_map/all_to_all | solution.py:675
  46.7 1.7 %copy-start.5 = (bf16[8,80,128]{2,1,0:T(8,128)(2,1)}, bf16[8,80,128]{2,1,0:T(8,128)(2,1)S(1)}, u32[]{:S(2)}) copy-start(bf16[8,80,128]{2,1,0:T(8,128)(2,1)S(1)} %fusion.refs_0_) | copy-start | bytes 491524
  46.7 1.7 %copy-start.9 = (bf16[1024,128]{1,0:T(8,128)(2,1)S(1)}, bf16[1024,128]{1,0:T(8,128)(2,1)}, u32[]{:S(2)}) copy-start(bf16[1024,128]{1,0:T(8,128)(2,1)} %refs_2_.1) | copy-start | bytes 786436
  46.7 1.7 %collective-permute-start.9 = (bf16[8,80,128]{2,1,0:T(8,128)(2,1)S(1)}, bf16[8,80,128]{2,1,0:T(8,128)(2,1)S(1)}, u32[]{:S(2)}, u32[]{:S(2)}) collective-permute-start(bf16[8,80,128]{2,1,0:T(8,128)(2,1)S(1)} %fusion.refs_0_), channel_id=1, source_target_pairs={{0,1},{1,0},{2,3},{3,2},{4,5},{5,4},{6,7},{7,6},{8,9},{9,8},{10,11... | collective-permute-start | bytes 491528 | tf_op jit(solution)/shard_map/ppermute | solution.py:616
  48.4 5.2 %copy-start.2 = (bf16[128,512]{1,0:T(8,128)(2,1)S(1)}, bf16[128,512]{1,0:T(8,128)(2,1)}, u32[]{:S(2)}) copy-start(bf16[128,512]{1,0:T(8,128)(2,1)} %up_ref.3) | copy-start | bytes 393220
  48.4 5.2 %copy-start.3 = (bf16[512,128]{1,0:T(8,128)(2,1)S(1)}, bf16[512,128]{1,0:T(8,128)(2,1)}, u32[]{:S(2)}) copy-start(bf16[512,128]{1,0:T(8,128)(2,1)} %down_ref.3) | copy-start | bytes 393220
  48.4 5.2 %copy-start.4 = (bf16[128,128]{1,0:T(8,128)(2,1)S(1)}, bf16[128,128]{1,0:T(8,128)(2,1)}, u32[]{:S(2)}) copy-start(bf16[128,128]{1,0:T(8,128)(2,1)} %w_ref.5) | copy-start | bytes 98308
  48.4 1.0 %copy-start.6 = (bf16[8,80,128]{2,1,0:T(8,128)(2,1)S(1)}, bf16[8,80,128]{2,1,0:T(8,128)(2,1)}, u32[]{:S(2)}) copy-start(bf16[8,80,128]{2,1,0:T(8,128)(2,1)} %copy-done.5) | copy-start | bytes 491524
